TPU v7x, 32 devices: a whole 2x2x4 slice. The times are simulated.
32 devices in a mesh: tx: 8 (over z, x), ty: 4 (over y, core).
Axes of the slice: x: 2, y: 2, z: 4, core: 2. Of those that a mesh axis runs over, the one named last changes fastest.
Arguments:
- features: bfloat16 [128, 128, 128], P(('tx', 'ty')), may hold values from -6 to 6
- occupancy: int32 [128, 128], P(('tx', 'ty')), may hold values from 0 to 1, as said below
- neighbors: int32 [27, 128], P(None, ('tx', 'ty')), may hold values from -1 to 127, as said below
- point_voxel: int32 [32768], P(('tx', 'ty')), may hold values from 0 to 511, as said below
- conv_weight: bfloat16 [27, 128, 128], replicated, may hold values from -0.109375 to 0.109375
- head_weight: bfloat16 [16, 128], replicated, may hold values from -0.5 to 0.5
- teacher: bfloat16 [16, 32768], P(None, ('tx', 'ty')), may hold values from -15 to 15
Outputs:
- grad_features: bfloat16 [128, 128, 128], P(('tx', 'ty'))
- grad_weight: float32 [27, 128, 128], replicated
Inputs may be any that keep to these rules, and one draw needn't show every extreme that they name: `occupancy`: every voxel of a slot that holds no active brick is 0; every active brick has one or more occupied voxels. A brick's global slot is 4 times its tile's index (tx index times the number of ty devices plus ty index) plus (2 i + j) + k for its place (i, j, k) in the tile's 2 x 2 x 1 grid of bricks. neighbors[o, b] is the global slot of the brick at brick offset o from b if that brick is active and b is active, else -1; neighbors[13, b] is b exactly when b is active. At most 3 bricks of a tile are active, and some tile has exactly 3. `point_voxel`: each entry is 128 s + v for an occupied voxel v of slot s of the point's own tile.
All inputs are finite; a program needn't handle non-finite values.
Results may differ from a plain program's by a relative error of at most 0.0052.
Values may be sent and summed in bfloat16 or wider, within the bound.
No kernel may reach another device: no remote copies, remote signals or barrier semaphores. Data moves between devices by JAX's collectives and lax.ppermute only.
A program may use at most 64 MiB of HBM per device.

v0:
```python
import jax
import jax.numpy as jnp
from jax import lax
from jax.sharding import PartitionSpec as P

GX = 2
GY = 2
GZ = 1


def with_halo(cells, sides, width):
    for axis, dim in sides:
        count = lax.axis_size(axis)
        ends = count - 1
        head = lax.slice_in_dim(cells, 0, width, axis=dim)
        tail = lax.slice_in_dim(cells, cells.shape[dim] - width, cells.shape[dim], axis=dim)
        cells = jnp.concatenate(
            [
                lax.ppermute(tail, axis, [(i, (i + 1) % count) for i in range(ends)]),
                cells,
                lax.ppermute(head, axis, [((i + 1) % count, i) for i in range(ends)]),
            ],
            axis=dim,
        )
    return cells


def plane_columns(padded, move_x, transpose):
    channels = padded.shape[-1]
    windows = []
    for move_y in (-1, 0, 1):
        for move_z in (-1, 0, 1):
            if transpose:
                anchor = (1 - move_x, 1 - move_y, 1 - move_z)
            else:
                anchor = (1 + move_x, 1 + move_y, 1 + move_z)
            window = padded[
                :,
                anchor[0] : anchor[0] + 4,
                anchor[1] : anchor[1] + 4,
                anchor[2] : anchor[2] + 8,
                :,
            ]
            windows.append(window.reshape(-1, channels))
    return jnp.concatenate(windows, axis=1)


def convolve(padded, weight, transpose):
    channels = padded.shape[-1]
    summed = jnp.zeros((padded.shape[0] * 128, channels), jnp.float32)
    for move_x in (-1, 0, 1):
        first = 9 * (move_x + 1)
        if transpose:
            matrix = jnp.concatenate([weight[first + inner].T for inner in range(9)], axis=0)
        else:
            matrix = weight[first : first + 9].reshape(9 * channels, channels)
        columns = plane_columns(padded, move_x, transpose)
        summed = summed + jnp.dot(columns, matrix, preferred_element_type=jnp.float32)
    return summed


def weight_terms(padded, gradient):
    channels = padded.shape[-1]
    flat_grad = gradient.reshape(-1, channels)
    terms = []
    for move_x in (-1, 0, 1):
        columns = plane_columns(padded, move_x, False)
        product = lax.dot_general(
            columns, flat_grad, (((0,), (0,)), ((), ())), preferred_element_type=jnp.float32
        )
        terms.append(product.reshape(9, channels, channels))
    return jnp.concatenate(terms, axis=0)


def silu_slope(value):
    logistic = jax.nn.sigmoid(value)
    return logistic * (1.0 + value * (1.0 - logistic))


def tile_gradient(pre, occupied, voxel_index, teacher_block, head_weight):
    channels = pre.shape[-1]
    occupied_cells = occupied[..., None]
    hidden = (jax.nn.silu(pre) * occupied_cells).astype(jnp.bfloat16)
    chosen = jnp.take(hidden.reshape(-1, channels), voxel_index, axis=0)
    logits = lax.dot_general(
        head_weight, chosen, (((1,), (1,)), ((), ())), preferred_element_type=jnp.float32
    )
    student = jnp.exp(logits)
    student = student / jnp.sum(student, axis=0, keepdims=True)
    target = jnp.exp(teacher_block.astype(jnp.float32))
    target = target / jnp.sum(target, axis=0, keepdims=True)
    slope_logits = student - target
    per_point = jnp.dot(
        slope_logits.T, head_weight.astype(jnp.float32), precision=lax.Precision.HIGHEST
    )
    per_voxel = (
        jnp.zeros((pre.shape[0] * 128, channels), jnp.float32).at[voxel_index].add(per_point)
    )
    return (per_voxel.reshape(pre.shape) * silu_slope(pre) * occupied_cells).astype(jnp.bfloat16)


def neighbourhood(block, chosen_rows):
    channels = block.shape[2]
    voxel_grid = (
        block.reshape(GX, GY, GZ, 4, 4, 8, channels)
        .transpose(0, 3, 1, 4, 2, 5, 6)
        .reshape(GX * 4, GY * 4, GZ * 8, channels)
    )
    extended = with_halo(voxel_grid, (("tx", 0), ("ty", 1)), 1)
    extended = jnp.pad(extended, ((0, 0), (0, 0), (1, 1), (0, 0)))
    place_i = chosen_rows // (GY * GZ)
    place_j = chosen_rows // GZ % GY
    place_k = chosen_rows % GZ

    def cut_block(first_i, first_j, first_k):
        return lax.dynamic_slice(
            extended, (4 * first_i, 4 * first_j, 8 * first_k, 0), (6, 6, 10, channels)
        )

    return jax.vmap(cut_block)(place_i, place_j, place_k)


def normalise_terms(local_terms):
    summed = lax.psum(local_terms, ("tx", "ty"))
    return summed / jnp.sqrt(jnp.mean(summed * summed) + 1e-06)


def on_device(features, occupancy, neighbors, point_voxel, conv_weight, head_weight, teacher):
    slots = features.shape[0]
    channels = features.shape[2]
    occupied = occupancy.astype(jnp.float32)
    masked = features * occupancy.astype(jnp.bfloat16)[..., None]
    chosen_rows = jnp.arange(slots, dtype=jnp.int32)
    padded_x = neighbourhood(masked, chosen_rows)
    pre_rows = convolve(padded_x, conv_weight, False).reshape(-1, 128, channels)
    gradient = tile_gradient(pre_rows, occupied, point_voxel, teacher, head_weight)
    padded_g = neighbourhood(gradient, chosen_rows)
    back_rows = convolve(padded_g, conv_weight, True).reshape(-1, 128, channels)
    grad_features = (back_rows * occupied[..., None]).astype(jnp.bfloat16)
    local_terms = weight_terms(padded_x, jnp.take(gradient, chosen_rows, axis=0))
    grad_weight = normalise_terms(local_terms)
    return (grad_features, grad_weight)


def solution(mesh):
    in_specs = (
        P(("tx", "ty"), None, None),
        P(("tx", "ty"), None),
        P(None, ("tx", "ty")),
        P(("tx", "ty")),
        P(),
        P(),
        P(None, ("tx", "ty")),
    )
    out_specs = (P(("tx", "ty"), None, None), P())
    return jax.shard_map(
        on_device, mesh=mesh, in_specs=in_specs, out_specs=out_specs, check_vma=False
    )
```

profile of v0, /device:TPU:0, one launch (start us, length us, event | category | flops | bytes accessed | tf_op | source)
XLA Modules:
  0.0 262.3 jit_solution(11752471083295711286)
XLA Ops:
  7.2 1.4 convert_bitcast_fusion
  8.6 1.0 broadcast_multiply_fusion
  9.7 1.3 collective-permute-start.1
  11.0 5.5 %collective-permute-start = (bf16[1,8,8,128]{3,2,1,0:T(8,128)(2,1)S(1)}, bf16[1,8,8,128]{3,2,1,0:T(8,128)(2,1)S(1)}, u32[]{:S(2)}, u32[]{:S(2)}) collective-permute-start(bf16[1,8,8,128]{3,2,1,0:T(8,128)(2,1)S(1)} %get-tuple-element.92), channel_id=1, source_target_pairs={{0,4},{4,8},{8,12},{12,16},{16,20},{20,24},{24,28},{1,5},{5,9},{9,... | collective-permute-start | bytes 49160 | tf_op jit(solution)/shard_map/ppermute | solution.py:19
  16.4 2.1 fusion.21
  26.4 1.3 collective-permute-start.3
  27.7 3.0 %collective-permute-start.2 = (bf16[10,1,8,128]{3,2,1,0:T(8,128)(2,1)S(1)}, bf16[10,1,8,128]{3,2,1,0:T(8,128)(2,1)S(1)}, u32[]{:S(2)}, u32[]{:S(2)}) collective-permute-start(bf16[10,1,8,128]{3,2,1,0:T(8,128)(2,1)S(1)} %get-tuple-element.88), channel_id=1, source_target_pairs={{0,1},{1,2},{2,3},{4,5},{5,6},{6,7},{8,9},{9,10},{10,11},{12,13},{... | collective-permute-start | bytes 61448 | tf_op jit(solution)/shard_map/ppermute | solution.py:19
  33.0 1.3 pad_slice_fusion.18
  36.8 1.7 copy.11
  52.5 1.7 copy.28
  54.2 1.6 copy.29
  55.8 1.7 copy.30
  57.5 1.7 copy.31
  59.2 1.7 copy.32
  60.8 1.7 copy.33
  62.5 1.6 copy.34
  64.1 1.7 copy.35
  65.8 1.0 constant_dynamic-update-slice_fusion.7
  66.8 0.9 constant_dynamic-update-slice_fusion.6
  74.5 1.8 multiply_convert_fusion.3
  76.3 3.2 %gather_fusion.1 = bf16[1024,128]{1,0:T(8,128)(2,1)S(1)} fusion(bf16[512,128]{1,0:T(8,128)(2,1)S(1)} %get-tuple-element.101, s32[1024]{0:T(1024)S(1)} %copy-done.34), kind=kCustom, calls=%fused_computation.1 | custom fusion | bytes 528384 | tf_op jit(solution)/shard_map/jit(_take)/gather | solution.py:84
  80.6 6.2 %scatter_custom_fusion = f32[512,128]{1,0:T(8,128)S(1)} fusion(s32[1024]{0:T(1024)} %get-tuple-element.95, f32[1024,128]{1,0:T(8,128)S(1)} %fusion.6, f32[]{:T(128)} %constant.98.clone.1), kind=kCustom, calls=%fused_computation.139 | custom fusion | flops 131072 | bytes 262656 | tf_op jit(solution)/shard_map/scatter-add | solution.py:97
  87.0 1.3 collective-permute-start.5
  88.3 5.4 %collective-permute-start.4 = (bf16[1,8,8,128]{3,2,1,0:T(8,128)(2,1)S(1)}, bf16[1,8,8,128]{3,2,1,0:T(8,128)(2,1)S(1)}, u32[]{:S(2)}, u32[]{:S(2)}) collective-permute-start(bf16[1,8,8,128]{3,2,1,0:T(8,128)(2,1)S(1)} %get-tuple-element.90), channel_id=1, source_target_pairs={{0,4},{4,8},{8,12},{12,16},{16,20},{20,24},{24,28},{1,5},{5,9},{9,... | collective-permute-start | bytes 49160 | tf_op jit(solution)/shard_map/ppermute | solution.py:19
  93.7 1.5 constant_dynamic-update-slice_fusion.72
  95.2 1.3 collective-permute-start.7
  96.5 3.6 %collective-permute-start.6 = (bf16[10,1,8,128]{3,2,1,0:T(8,128)(2,1)S(1)}, bf16[10,1,8,128]{3,2,1,0:T(8,128)(2,1)S(1)}, u32[]{:S(2)}, u32[]{:S(2)}) collective-permute-start(bf16[10,1,8,128]{3,2,1,0:T(8,128)(2,1)S(1)} %get-tuple-element.86), channel_id=1, source_target_pairs={{0,1},{1,2},{2,3},{4,5},{5,6},{6,7},{8,9},{9,10},{10,11},{12,13},{... | collective-permute-start | bytes 61448 | tf_op jit(solution)/shard_map/ppermute | solution.py:19
  107.5 1.7 fusion.31
  110.1 1.3 pad_maximum_fusion
  111.5 139.1 %all-reduce.4.cloned.1.call-done = f32[27,128,128]{2,1,0:T(8,128)} async-done(((f32[27,128,128]{2,1,0:T(8,128)}), f32[27,128,128]{2,1,0:T(8,128)}) %all-reduce.4.cloned.1.call-update) | async-done | bytes 1769488 | tf_op jit(solution)/shard_map/psum | solution.py:124
  250.6 2.7 %multiply_reduce_fusion = f32[]{:T(128)} fusion(f32[27,128,128]{2,1,0:T(8,128)} %all-reduce.4.cloned.1.call-done), kind=kLoop, calls=%fused_computation.42 | loop fusion | flops 884735 | bytes 1769476 | tf_op jit(solution)/shard_map/reduce_sum | solution.py:125
  254.0 1.5 broadcast_divide_fusion
  (197 shorter events, 42.3 us)
Async XLA Ops:
  7.2 72.4 %copy-start = (bf16[16,128]{1,0:T(8,128)(2,1)S(1)}, bf16[16,128]{1,0:T(8,128)(2,1)}, u32[]{:S(2)}) copy-start(bf16[16,128]{1,0:T(8,128)(2,1)} %param.11) | copy-start | bytes 12292
  7.2 243.4 %all-reduce.4.cloned.1.call-start = ((), (), s32[]{:S(2)}) async-start(), calls=%async_computation | async-start | bytes 3538944 | tf_op jit(solution)/shard_map/psum | solution.py:124
  9.6 9.7 %copy-start.35 = (s32[1024]{0:T(1024)S(1)}, s32[1024]{0:T(1024)}, u32[]{:S(2)}) copy-start(s32[1024]{0:T(1024)} %param.9) | copy-start | bytes 12292
  9.7 16.7 %collective-permute-start.1 = (bf16[1,8,8,128]{3,2,1,0:T(8,128)(2,1)S(1)}, bf16[1,8,8,128]{3,2,1,0:T(8,128)(2,1)S(1)}, u32[]{:S(2)}, u32[]{:S(2)}) collective-permute-start(bf16[1,8,8,128]{3,2,1,0:T(8,128)(2,1)S(1)} %get-tuple-element.93), channel_id=1, source_target_pairs={{4,0},{8,4},{12,8},{16,12},{20,16},{24,20},{28,24},{5,1},{9,5},{13... | collective-permute-start | bytes 49160 | tf_op jit(solution)/shard_map/ppermute | solution.py:21
  11.0 15.4 %collective-permute-start = (bf16[1,8,8,128]{3,2,1,0:T(8,128)(2,1)S(1)}, bf16[1,8,8,128]{3,2,1,0:T(8,128)(2,1)S(1)}, u32[]{:S(2)}, u32[]{:S(2)}) collective-permute-start(bf16[1,8,8,128]{3,2,1,0:T(8,128)(2,1)S(1)} %get-tuple-element.92), channel_id=1, source_target_pairs={{0,4},{4,8},{8,12},{12,16},{16,20},{20,24},{24,28},{1,5},{5,9},{9,... | collective-permute-start | bytes 49160 | tf_op jit(solution)/shard_map/ppermute | solution.py:19
  18.5 7.8 %copy-start.31 = (bf16[16,1024]{1,0:T(8,128)(2,1)S(1)}, bf16[16,1024]{1,0:T(8,128)(2,1)}, u32[]{:S(2)}) copy-start(bf16[16,1024]{1,0:T(8,128)(2,1)} %param.12) | copy-start | bytes 98308
  26.3 5.2 %copy-start.24 = (bf16[1152,128]{0,1:T(8,128)(2,1)}, bf16[1152,128]{0,1:T(8,128)(2,1)S(1)}, u32[]{:S(2)}) copy-start(bf16[1152,128]{0,1:T(8,128)(2,1)S(1)} %get-tuple-element.5) | copy-start | bytes 884740
  26.3 5.2 %copy-start.26 = (bf16[1152,128]{0,1:T(8,128)(2,1)}, bf16[1152,128]{0,1:T(8,128)(2,1)S(1)}, u32[]{:S(2)}) copy-start(bf16[1152,128]{0,1:T(8,128)(2,1)S(1)} %get-tuple-element.6) | copy-start | bytes 884740
  26.3 6.7 %copy-start.28 = (bf16[1152,128]{0,1:T(8,128)(2,1)}, bf16[1152,128]{0,1:T(8,128)(2,1)S(1)}, u32[]{:S(2)}) copy-start(bf16[1152,128]{0,1:T(8,128)(2,1)S(1)} %get-tuple-element.7) | copy-start | bytes 884740
  26.4 5.1 %collective-permute-start.3 = (bf16[10,1,8,128]{3,2,1,0:T(8,128)(2,1)S(1)}, bf16[10,1,8,128]{3,2,1,0:T(8,128)(2,1)S(1)}, u32[]{:S(2)}, u32[]{:S(2)}) collective-permute-start(bf16[10,1,8,128]{3,2,1,0:T(8,128)(2,1)S(1)} %get-tuple-element.89), channel_id=1, source_target_pairs={{1,0},{2,1},{3,2},{5,4},{6,5},{7,6},{9,8},{10,9},{11,10},{13,12},{... | collective-permute-start | bytes 61448 | tf_op jit(solution)/shard_map/ppermute | solution.py:21
  27.7 3.9 %collective-permute-start.2 = (bf16[10,1,8,128]{3,2,1,0:T(8,128)(2,1)S(1)}, bf16[10,1,8,128]{3,2,1,0:T(8,128)(2,1)S(1)}, u32[]{:S(2)}, u32[]{:S(2)}) collective-permute-start(bf16[10,1,8,128]{3,2,1,0:T(8,128)(2,1)S(1)} %get-tuple-element.88), channel_id=1, source_target_pairs={{0,1},{1,2},{2,3},{4,5},{5,6},{6,7},{8,9},{9,10},{10,11},{12,13},{... | collective-permute-start | bytes 61448 | tf_op jit(solution)/shard_map/ppermute | solution.py:19
  65.8 4.7 %copy-start.23 = (bf16[512,128]{0,1:T(8,128)(2,1)S(1)}, bf16[512,128]{0,1:T(8,128)(2,1)}, u32[]{:S(2)}) copy-start(bf16[512,128]{0,1:T(8,128)(2,1)} %copy.15) | copy-start | bytes 393220
  65.8 4.7 %copy-start.22 = (bf16[512,128]{0,1:T(8,128)(2,1)S(1)}, bf16[512,128]{0,1:T(8,128)(2,1)}, u32[]{:S(2)}) copy-start(bf16[512,128]{0,1:T(8,128)(2,1)} %copy.16) | copy-start | bytes 393220
  65.8 4.7 %copy-start.19 = (bf16[512,128]{0,1:T(8,128)(2,1)S(1)}, bf16[512,128]{0,1:T(8,128)(2,1)}, u32[]{:S(2)}) copy-start(bf16[512,128]{0,1:T(8,128)(2,1)} %copy.17) | copy-start | bytes 393220
  65.8 4.8 %copy-start.4 = (bf16[9,128,128]{2,1,0:T(8,128)(2,1)S(1)}, bf16[9,128,128]{2,1,0:T(8,128)(2,1)}, u32[]{:S(2)}) copy-start(bf16[9,128,128]{2,1,0:T(8,128)(2,1)} %get-tuple-element.31) | copy-start | bytes 884740
  70.6 1.1 copy-start.16
  70.6 1.1 copy-start.13
  71.4 1.0 copy-start.14
  71.4 1.1 copy-start.15
  71.5 1.0 copy-start.12
  73.4 1.1 copy-start.30
  73.4 1.1 copy-start.36
  74.5 1.8 copy-start.34
  76.3 3.2 %copy-start.37 = (pred[1024]{0:T(1024)(128)(4,1)S(1)}, pred[1024]{0:T(1024)(128)(4,1)}, u32[]{:S(2)}) copy-start(pred[1024]{0:T(1024)(128)(4,1)} %compare_and_fusion) | copy-start | bytes 3076
  76.3 3.6 %copy-start.32 = (bf16[16,1024]{1,0:T(8,128)(2,1)S(1)}, bf16[16,1024]{1,0:T(8,128)(2,1)}, u32[]{:S(2)}) copy-start(bf16[16,1024]{1,0:T(8,128)(2,1)} %param.12) | copy-start | bytes 98308
  79.6 7.2 %copy-start.33 = (f32[2,2,4,4,8]{4,3,2,1,0:T(4,128)S(1)}, f32[2,2,4,4,8]{4,3,2,1,0:T(4,128)}, u32[]{:S(2)}) copy-start(f32[2,2,4,4,8]{4,3,2,1,0:T(4,128)} %mul.127) | copy-start | bytes 6148
  87.0 8.2 %collective-permute-start.5 = (bf16[1,8,8,128]{3,2,1,0:T(8,128)(2,1)S(1)}, bf16[1,8,8,128]{3,2,1,0:T(8,128)(2,1)S(1)}, u32[]{:S(2)}, u32[]{:S(2)}) collective-permute-start(bf16[1,8,8,128]{3,2,1,0:T(8,128)(2,1)S(1)} %get-tuple-element.91), channel_id=1, source_target_pairs={{4,0},{8,4},{12,8},{16,12},{20,16},{24,20},{28,24},{5,1},{9,5},{13... | collective-permute-start | bytes 49160 | tf_op jit(solution)/shard_map/ppermute | solution.py:21
  88.3 6.9 %collective-permute-start.4 = (bf16[1,8,8,128]{3,2,1,0:T(8,128)(2,1)S(1)}, bf16[1,8,8,128]{3,2,1,0:T(8,128)(2,1)S(1)}, u32[]{:S(2)}, u32[]{:S(2)}) collective-permute-start(bf16[1,8,8,128]{3,2,1,0:T(8,128)(2,1)S(1)} %get-tuple-element.90), channel_id=1, source_target_pairs={{0,4},{4,8},{8,12},{12,16},{16,20},{20,24},{24,28},{1,5},{5,9},{9,... | collective-permute-start | bytes 49160 | tf_op jit(solution)/shard_map/ppermute | solution.py:19
  95.2 5.0 %collective-permute-start.7 = (bf16[10,1,8,128]{3,2,1,0:T(8,128)(2,1)S(1)}, bf16[10,1,8,128]{3,2,1,0:T(8,128)(2,1)S(1)}, u32[]{:S(2)}, u32[]{:S(2)}) collective-permute-start(bf16[10,1,8,128]{3,2,1,0:T(8,128)(2,1)S(1)} %get-tuple-element.87), channel_id=1, source_target_pairs={{1,0},{2,1},{3,2},{5,4},{6,5},{7,6},{9,8},{10,9},{11,10},{13,12},{... | collective-permute-start | bytes 61448 | tf_op jit(solution)/shard_map/ppermute | solution.py:21
  96.5 4.3 %collective-permute-start.6 = (bf16[10,1,8,128]{3,2,1,0:T(8,128)(2,1)S(1)}, bf16[10,1,8,128]{3,2,1,0:T(8,128)(2,1)S(1)}, u32[]{:S(2)}, u32[]{:S(2)}) collective-permute-start(bf16[10,1,8,128]{3,2,1,0:T(8,128)(2,1)S(1)} %get-tuple-element.86), channel_id=1, source_target_pairs={{0,1},{1,2},{2,3},{4,5},{5,6},{6,7},{8,9},{9,10},{10,11},{12,13},{... | collective-permute-start | bytes 61448 | tf_op jit(solution)/shard_map/ppermute | solution.py:19
  104.3 1.1 copy-start.25
  250.6 3.4 %copy-start.1 = (f32[27,128,128]{2,1,0:T(8,128)S(1)}, f32[27,128,128]{2,1,0:T(8,128)}, u32[]{:S(2)}) copy-start(f32[27,128,128]{2,1,0:T(8,128)} %all-reduce.4.cloned.1.call-done) | copy-start | bytes 5308420
  (15 other events, 14.7 us)
Sparse Core Ops, SparseCore 0:
  111.6 138.9 all-reduce.3
where the time goes:
time: 264 us; the launch traced here: 262 us
  waiting for transfers between devices  140 us (53%)
  local copies, waits for them, and re-layouts  59.7 us (23%)
  starting transfers between devices  22.8 us (9%)
  other arithmetic  16.4 us (6%)
  between operations  15.7 us (6%)
  matrix products  7.85 us (3%)
    psum x1, waiting for transfers between devices, normalise_terms(): summed = lax.psum(local_terms, ('tx', 'ty'))  139 us
    reshape x27, local copies, waits for them, and re-layouts, plane_columns(): windows.append(window.reshape(-1, channels))  28.7 us
    unnamed x132, local copies, waits for them, and re-layouts  18.7 us
    ppermute x4, starting transfers between devices, with_halo(): lax.ppermute(tail, axis, [(i, (i + 1) % count) for i in range(ends)])  17.6 us
    scatter-add x1, other arithmetic, tile_gradient(): jnp.zeros((pre.shape[0] * 128, channels), jnp.float32).at[voxel_index]  6.21 us
  transfers between devices with their start and end apart: 9, of which 3 were waited for; matrix products, arithmetic and copies ran while one was open for 5% of the time, Pallas kernels for 0%

commit v1 on v0

v1 whole, which is shorter than its diff:
```python
import jax
import jax.numpy as jnp
from jax import lax
from jax.experimental import pallas as pl
from jax.experimental.pallas import tpu as pltpu
from jax.sharding import PartitionSpec as P

GX = 2
GY = 2
BX = 4
BY = 4
SIDE = 8
PLANE = SIDE * SIDE
TAPS = 9
BF16 = jnp.bfloat16
F32 = jnp.float32
PARTS = 8


def vmem(count):
    return [pl.BlockSpec(memory_space=pltpu.VMEM)] * count


def call(body, outs, inputs, scratch=(), limit=32 * 2**20, name=None):
    return pl.pallas_call(
        body,
        out_shape=outs,
        in_specs=vmem(len(inputs)),
        out_specs=jax.tree.map(lambda _: pl.BlockSpec(memory_space=pltpu.VMEM), outs),
        scratch_shapes=list(scratch),
        compiler_params=pltpu.CompilerParams(vmem_limit_bytes=limit),
        name=name,
    )(*inputs)


def shape(dims, dtype):
    return jax.ShapeDtypeStruct(dims, dtype)


def slot_planes(slot):
    return BX * (slot // GY), (slot % GY) * BY * SIDE


def parity(axis):
    return lax.rem(lax.axis_index(axis), 2) == 0


def occupancy_columns(occ_ref, rows):
    occ = occ_ref[...].astype(F32)
    padded = jnp.concatenate([occ, jnp.zeros((8 - occ.shape[0], occ.shape[1]), F32)], axis=0)
    return padded.T


def write_grid(grid_ref, planes):
    for x in range(SIDE):
        grid_ref[x + 1, SIDE : SIDE + PLANE, :] = planes(x)


def y_faces(planes):
    low = jnp.concatenate([planes(x)[:SIDE] for x in range(SIDE)], axis=0)
    high = jnp.concatenate([planes(x)[PLANE - SIDE :] for x in range(SIDE)], axis=0)
    return low, high


def send_faces(low_plane, high_plane, low_y, high_y, a_ref, b_ref, edge_ref):
    even = parity("tx")
    a_ref[...] = jnp.where(even, high_plane, low_plane).astype(BF16)
    b_ref[...] = jnp.where(even, low_plane, high_plane).astype(BF16)
    edge_ref[0] = low_y.astype(BF16)
    edge_ref[1] = high_y.astype(BF16)


def first_faces_kernel(feat_ref, occ_ref, a_ref, b_ref, edge_ref):
    columns = occupancy_columns(occ_ref, 8)
    channels = feat_ref.shape[2]

    def masked(slot, first, rows):
        mask = jnp.broadcast_to(columns[first : first + rows, slot : slot + 1], (rows, channels))
        return feat_ref[slot, first : first + rows, :].astype(F32) * mask

    def plane(x):
        i, a = x // BX, x % BX
        return jnp.concatenate(
            [masked(i * GY + j, a * BY * SIDE, BY * SIDE) for j in range(GY)], axis=0
        )

    every = [plane(x) for x in range(SIDE)]
    low_y, high_y = y_faces(lambda x: every[x])
    send_faces(every[0], every[SIDE - 1], low_y, high_y, a_ref, b_ref, edge_ref)


def edge_kernel(edge_ref, got_a_ref, got_b_ref, a_ref, b_ref):
    even_x, even_y = parity("tx"), parity("ty")
    got_a, got_b = got_a_ref[...].astype(F32), got_b_ref[...].astype(F32)
    low, high = jnp.where(even_x, got_b, got_a), jnp.where(even_x, got_a, got_b)
    bottom = jnp.concatenate([low[:SIDE], edge_ref[0].astype(F32), high[:SIDE]], axis=0)
    last = PLANE - SIDE
    top = jnp.concatenate([low[last:], edge_ref[1].astype(F32), high[last:]], axis=0)
    a_ref[...] = jnp.where(even_y, top, bottom).astype(BF16)
    b_ref[...] = jnp.where(even_y, bottom, top).astype(BF16)


def write_halo(grid_ref, x_a_ref, x_b_ref, y_a_ref, y_b_ref):
    even_x, even_y = parity("tx"), parity("ty")
    x_a, x_b = x_a_ref[...].astype(F32), x_b_ref[...].astype(F32)
    grid_ref[0, SIDE : SIDE + PLANE, :] = jnp.where(even_x, x_b, x_a)
    grid_ref[SIDE + 1, SIDE : SIDE + PLANE, :] = jnp.where(even_x, x_a, x_b)
    y_a, y_b = y_a_ref[...].astype(F32), y_b_ref[...].astype(F32)
    low, high = jnp.where(even_y, y_b, y_a), jnp.where(even_y, y_a, y_b)
    for x in range(SIDE + 2):
        grid_ref[x, :SIDE, :] = low[x * SIDE : (x + 1) * SIDE]
        grid_ref[x, SIDE + PLANE :, :] = high[x * SIDE : (x + 1) * SIDE]


def write_columns(grid_ref, cols_ref):
    channels = grid_ref.shape[2]
    z = lax.broadcasted_iota(jnp.int32, ((SIDE + 2) * SIDE, channels), 0) % SIDE
    for x in range(SIDE + 2):
        plane = grid_ref[x]
        zeros = jnp.zeros((1, channels), F32)
        before = jnp.where(z == 0, 0.0, jnp.concatenate([zeros, plane[:-1]], axis=0))
        after = jnp.where(z == SIDE - 1, 0.0, jnp.concatenate([plane[1:], zeros], axis=0))
        for dz, moved in enumerate((before, plane, after)):
            for dy in range(3):
                tap = 3 * dy + dz
                cols_ref[x, :, tap * channels : (tap + 1) * channels] = moved[
                    dy * SIDE : dy * SIDE + PLANE
                ].astype(BF16)


def split3(value):
    high = value.astype(BF16)
    rest = value - high.astype(F32)
    middle = rest.astype(BF16)
    low = (rest - middle.astype(F32)).astype(BF16)
    return high, middle, low


def contract(a, b, dim_a, dim_b):
    return lax.dot_general(a, b, (((dim_a,), (dim_b,)), ((), ())), preferred_element_type=F32)


def write_mask(occ_ref, mask_ref):
    columns = occupancy_columns(occ_ref, 8)
    rows, channels = BY * SIDE, mask_ref.shape[2]
    for slot in range(GX * GY):
        x0, row0 = slot_planes(slot)
        wide = jnp.broadcast_to(columns[:, slot : slot + 1], (columns.shape[0], channels))
        for a in range(BX):
            mask_ref[x0 + a, row0 : row0 + rows, :] = wide[a * rows : (a + 1) * rows]


def tile_kernel(
    feat_ref, occ_ref, x_a_ref, x_b_ref, y_a_ref, y_b_ref, weight_ref, head_ref, point_ref, teach_ref,
    grad_ref, a_ref, b_ref, edge_ref, keep_ref, send_ref,
    grid_ref, cols_ref, mask_ref, terms_ref,
):
    channels = feat_ref.shape[2]
    classes = head_ref.shape[0]
    voxels = SIDE * PLANE
    write_mask(occ_ref, mask_ref)
    rows = BY * SIDE
    for slot in range(GX * GY):
        x0, row0 = slot_planes(slot)
        for a in range(BX):
            part = feat_ref[slot, a * rows : (a + 1) * rows, :].astype(F32)
            part = part * mask_ref[x0 + a, row0 : row0 + rows, :]
            grid_ref[x0 + a + 1, SIDE + row0 : SIDE + row0 + rows, :] = part
    write_halo(grid_ref, x_a_ref, x_b_ref, y_a_ref, y_b_ref)
    write_columns(grid_ref, cols_ref)

    pre = jnp.zeros((voxels, channels), F32)
    for dx in range(3):
        window = cols_ref[dx : dx + SIDE].reshape(voxels, TAPS * channels)
        matrix = weight_ref[TAPS * dx : TAPS * (dx + 1)].reshape(TAPS * channels, channels)
        pre = pre + jnp.dot(window, matrix, preferred_element_type=F32)
    mask = mask_ref[...].reshape(voxels, channels)
    logistic = 1.0 / (1.0 + jnp.exp(-pre))
    slope = logistic * (1.0 + pre * (1.0 - logistic)) * mask
    hidden = (pre / (1.0 + jnp.exp(-pre)) * mask).astype(BF16)

    logits = contract(head_ref[...], hidden, 1, 1)
    student = jnp.exp(logits)
    student = student / jnp.sum(student, axis=0, keepdims=True)
    target = jnp.exp(teach_ref[...].astype(F32))
    target = target / jnp.sum(target, axis=0, keepdims=True)
    points = target.shape[1]
    place = point_ref[...]
    place = (place & 0x11F) | ((place & 0x80) >> 2) | ((place & 0x60) << 1)
    chosen = lax.broadcasted_iota(jnp.int32, (voxels, points), 0) == place
    chosen = jnp.where(chosen, 1.0, 0.0).astype(BF16)
    stack = jnp.concatenate([*split3(target), jnp.ones((classes, points), BF16)], axis=0)
    sums = contract(stack, chosen, 1, 1)
    target_sum = sums[:classes] + sums[classes : 2 * classes] + sums[2 * classes : 3 * classes]
    count = sums[3 * classes :]
    slope_logits = jnp.where(count > 0.0, count * student, 0.0) - target_sum
    heads = jnp.concatenate([head_ref[...]] * 3, axis=0)
    pieces = jnp.concatenate([piece.astype(F32) for piece in split3(slope_logits)], axis=0)
    dhidden = contract(pieces.T.astype(BF16), heads, 1, 0)
    gradient = dhidden * slope
    rounded = gradient.astype(BF16)
    grad_ref[...] = rounded.reshape(SIDE, PLANE, channels)
    low_y, high_y = y_faces(lambda x: gradient[x * PLANE : (x + 1) * PLANE])
    send_faces(gradient[:PLANE], gradient[voxels - PLANE :], low_y, high_y, a_ref, b_ref, edge_ref)

    for dx in range(3):
        window = cols_ref[dx : dx + SIDE].reshape(voxels, TAPS * channels)
        product = contract(window, rounded, 0, 0)
        terms_ref[TAPS * dx : TAPS * (dx + 1)] = product.reshape(TAPS, channels, channels)
    length = channels // PARTS
    for r in range(PARTS):
        first = pl.multiple_of(part_index(r) * length, length)
        part = terms_ref[:, pl.ds(first, length), :].reshape(-1, channels)
        if r < PARTS // 2:
            keep_ref[r] = part
        else:
            send_ref[r - PARTS // 2] = part.astype(BF16)


def part_index(r):
    tx, ty = lax.axis_index("tx"), lax.axis_index("ty")
    core, across, along = (ty & 1) ^ (r >> 2), (ty >> 1) & 1, tx & 1
    first = jnp.where(core == 0, across, along)
    second = jnp.where(core == 0, along, across)
    return core * 4 + ((first * 2 + second) ^ (r & 3))


def back_kernel(
    grad_ref, occ_ref, x_a_ref, x_b_ref, y_a_ref, y_b_ref, weight_ref, out_ref,
    grid_ref, cols_ref, mask_ref,
):
    channels = grad_ref.shape[2]
    voxels = SIDE * PLANE
    write_mask(occ_ref, mask_ref)
    write_grid(grid_ref, lambda x: grad_ref[x].astype(F32))
    write_halo(grid_ref, x_a_ref, x_b_ref, y_a_ref, y_b_ref)
    write_columns(grid_ref, cols_ref)
    total = jnp.zeros((voxels, channels), F32)
    for dx in range(3):
        window = cols_ref[dx : dx + SIDE].reshape(voxels, TAPS * channels)
        taps = [weight_ref[3 * TAPS - 1 - (TAPS * dx + tap)] for tap in range(TAPS)]
        total = total + contract(window, jnp.concatenate(taps, axis=1), 1, 1)
    total = (total * mask_ref[...].reshape(voxels, channels)).reshape(SIDE, PLANE, channels)
    rows = BY * SIDE
    for slot in range(GX * GY):
        x0, row0 = slot_planes(slot)
        for a in range(BX):
            part = total[x0 + a, row0 : row0 + rows].astype(BF16)
            out_ref[slot, a * rows : (a + 1) * rows, :] = part


def norm_kernel(*refs):
    pieces, out_ref = refs[:-1], refs[-1]
    kernels, channels = out_ref.shape[0], out_ref.shape[2]
    length = channels // PARTS
    squares = jnp.zeros((kernels * length, channels), F32)
    for piece in pieces:
        value = piece[...].astype(F32)
        squares = squares + value * value
    mean = jnp.sum(squares) / (kernels * channels * channels)
    scale = 1.0 / jnp.sqrt(jnp.broadcast_to(mean, (1, channels)) + 1e-06)
    for r, piece in enumerate(pieces):
        value = piece[...].astype(F32) * scale
        first = pl.multiple_of(part_index(r) * length, length)
        out_ref[:, pl.ds(first, length), :] = value.reshape(kernels, length, channels)


def swap_pairs(first, count):
    return [pair for i in range(first, count - 1, 2) for pair in ((i, i + 1), (i + 1, i))]


def exchange(axis, a, b):
    count = lax.axis_size(axis)
    return (
        lax.ppermute(a, axis, swap_pairs(0, count)),
        lax.ppermute(b, axis, swap_pairs(1, count)),
    )


def halo(a, b, edges):
    channels = a.shape[1]
    x_a, x_b = exchange("tx", a, b)
    face = shape(((SIDE + 2) * SIDE, channels), BF16)
    ya, yb = call(edge_kernel, (face, face), (edges, x_a, x_b), name="edge_faces")
    return (x_a, x_b, *exchange("ty", ya, yb))


def exchange_with(value, partner):
    n_tx, n_ty = lax.axis_size("tx"), lax.axis_size("ty")
    pairs = []
    for tx in range(n_tx):
        for ty in range(n_ty):
            other_tx, other_ty = partner(tx, ty)
            pairs.append((tx * n_ty + ty, other_tx * n_ty + other_ty))
    return lax.ppermute(value, ("tx", "ty"), pairs)


def on_device(features, occupancy, neighbors, point_voxel, conv_weight, head_weight, teacher):
    slots, brick, channels = features.shape
    kernels = conv_weight.shape[0]
    plane = shape((PLANE, channels), BF16)
    edges = shape((2, PLANE, channels), BF16)
    ext = (SIDE + 2, (SIDE + 2) * SIDE, channels)
    grid = pltpu.VMEM(ext, F32)
    cols = pltpu.VMEM((SIDE + 2, PLANE, TAPS * channels), BF16)
    mask = pltpu.VMEM((SIDE, PLANE, channels), F32)

    x_faces = call(
        first_faces_kernel, (plane, plane, edges), (features, occupancy), name="first_faces"
    )
    x_halo = halo(*x_faces)
    part = kernels * channels // PARTS
    gradient, ga, gb, g_edges, keep, send = call(
        tile_kernel,
        (
            shape((SIDE, PLANE, channels), BF16),
            plane,
            plane,
            edges,
            shape((PARTS // 2, part, channels), F32),
            shape((PARTS // 2, part, channels), BF16),
        ),
        (features, occupancy, *x_halo, conv_weight, head_weight, point_voxel.reshape(1, -1), teacher),
        (grid, cols, mask, pltpu.VMEM((kernels, channels, channels), F32)),
        name="tile",
    )

    n_tx, n_ty = lax.axis_size("tx"), lax.axis_size("ty")

    def by_core(tx, ty):
        return tx, ty ^ 1

    def first_way(tx, ty):
        return (tx, ty ^ 2) if ty % 2 == 0 else (tx ^ 1, ty)

    def second_way(tx, ty):
        return (tx ^ 1, ty) if ty % 2 == 0 else (tx, ty ^ 2)

    got0 = exchange_with(send, by_core).astype(F32)
    send1 = (keep[2:4] + got0[2:4]).astype(BF16)
    got1 = exchange_with(send1, first_way).astype(F32)
    send2 = (keep[1] + got0[1] + got1[1]).astype(BF16)
    got2 = exchange_with(send2, second_way).astype(F32)
    total = (keep[0] + got0[0] + got1[0] + got2).astype(BF16)
    bit = 2
    while bit < n_tx:
        flip = 2 * bit - 2
        got = exchange_with(total, lambda tx, ty, flip=flip: (tx ^ flip, ty))
        total = (total.astype(F32) + got.astype(F32)).astype(BF16)
        bit *= 2
    bit = 4
    while bit < n_ty:
        flip = 2 * bit - 4
        got = exchange_with(total, lambda tx, ty, flip=flip: (tx, ty ^ flip))
        total = (total.astype(F32) + got.astype(F32)).astype(BF16)
        bit *= 2
    piece1 = exchange_with(total, second_way)
    piece2 = exchange_with(total, first_way)
    piece3 = exchange_with(piece1, first_way)
    pieces = [total, piece1, piece2, piece3]
    pieces = pieces + [exchange_with(piece, by_core) for piece in pieces]
    grad_weight = call(
        norm_kernel, shape((kernels, channels, channels), F32), tuple(pieces), name="normalise"
    )

    g_halo = halo(ga, gb, g_edges)
    grad_features = call(
        back_kernel,
        shape((slots, brick, channels), BF16),
        (gradient, occupancy, *g_halo, conv_weight),
        (grid, cols, mask),
        name="back",
    )
    return (grad_features, grad_weight)


def solution(mesh):
    in_specs = (
        P(("tx", "ty"), None, None),
        P(("tx", "ty"), None),
        P(None, ("tx", "ty")),
        P(("tx", "ty")),
        P(),
        P(),
        P(None, ("tx", "ty")),
    )
    out_specs = (P(("tx", "ty"), None, None), P())
    return jax.shard_map(
        on_device, mesh=mesh, in_specs=in_specs, out_specs=out_specs, check_vma=False
    )
```

time: 264 us -> 78.7 us (0.30)
  the two profiles are of different devices: /device:TPU:0 before, /device:TPU:25 now
where the time goes in v1:
time: 78.7 us; the launch traced here: 78.3 us
  waiting for transfers between devices  35.6 us (45%)
  starting transfers between devices  28.5 us (36%)
  Pallas kernels  7.34 us (9%)
  local copies, waits for them, and re-layouts  5.79 us (7%)
  between operations  0.81 us (1%)
    ppermute x12, waiting for transfers between devices, exchange_with(): return lax.ppermute(value, ('tx', 'ty'), pairs)  21.4 us
    ppermute x12, starting transfers between devices, exchange_with(): return lax.ppermute(value, ('tx', 'ty'), pairs)  12.6 us
    ppermute x4, waiting for transfers between devices, exchange(): lax.ppermute(b, axis, swap_pairs(1, count))  10.8 us
    ppermute x4, starting transfers between devices, exchange(): lax.ppermute(b, axis, swap_pairs(1, count))  10.1 us
    pallas_call x6, Pallas kernels, call(): pl.pallas_call(body, out_shape=outs, in_specs=vmem(len(inputs)), out_spec...  7.34 us
    ppermute x4, starting transfers between devices, exchange(): lax.ppermute(a, axis, swap_pairs(0, count))  5.82 us
    unnamed x18, local copies, waits for them, and re-layouts  5.79 us
    ppermute x4, waiting for transfers between devices, exchange(): lax.ppermute(a, axis, swap_pairs(0, count))  3.44 us
  transfers between devices with their start and end apart: 20, of which 12 were waited for; matrix products, arithmetic and copies ran while one was open for 0% of the time, Pallas kernels for 2%

profile of v1, /device:TPU:25, one launch (start us, length us, event | category | flops | bytes accessed | tf_op | source)
XLA Modules:
  0.0 78.3 jit_solution(16615705973948131743)
XLA Ops:
  0.6 0.9 %copy-done.2 = bf16[4,128,128]{2,1,0:T(8,128)(2,1)S(1)} copy-done((bf16[4,128,128]{2,1,0:T(8,128)(2,1)S(1)}, bf16[4,128,128]{2,1,0:T(8,128)(2,1)}, u32[]{:S(2)}) %copy-start.2) | copy-done | bytes 131096
  2.4 1.3 %collective-permute-start = (bf16[64,128]{1,0:T(8,128)(2,1)S(1)}, bf16[64,128]{1,0:T(8,128)(2,1)S(1)}, u32[]{:S(2)}, u32[]{:S(2)}) collective-permute-start(bf16[64,128]{1,0:T(8,128)(2,1)S(1)} %get-tuple-element.15), channel_id=1, source_target_pairs={{0,4},{4,0},{8,12},{12,8},{16,20},{20,16},{24,28},{28,24},{1,5},{5... | collective-permute-start | bytes 49160 | tf_op jit(solution)/shard_map/ppermute | solution.py:275
  3.7 2.0 %collective-permute-start.1 = (bf16[64,128]{1,0:T(8,128)(2,1)S(1)}, bf16[64,128]{1,0:T(8,128)(2,1)S(1)}, u32[]{:S(2)}, u32[]{:S(2)}) collective-permute-start(bf16[64,128]{1,0:T(8,128)(2,1)S(1)} %get-tuple-element.16), channel_id=1, source_target_pairs={{4,8},{8,4},{12,16},{16,12},{20,24},{24,20},{5,9},{9,5},{13,17},{1... | collective-permute-start | bytes 49160 | tf_op jit(solution)/shard_map/ppermute | solution.py:276
  5.8 3.3 %collective-permute-done.1.got_b_ref.x_b_ref = bf16[64,128]{1,0:T(8,128)(2,1)S(1)} collective-permute-done((bf16[64,128]{1,0:T(8,128)(2,1)S(1)}, bf16[64,128]{1,0:T(8,128)(2,1)S(1)}, u32[]{:S(2)}, u32[]{:S(2)}) %collective-permute-start.1) | collective-permute-done | bytes 16416 | tf_op jit(solution)/shard_map/ppermute | solution.py:276
  9.1 2.2 %collective-permute-start.2 = (bf16[80,128]{1,0:T(8,128)(2,1)S(1)}, bf16[80,128]{1,0:T(8,128)(2,1)S(1)}, u32[]{:S(2)}, u32[]{:S(2)}) collective-permute-start(bf16[80,128]{1,0:T(8,128)(2,1)S(1)} %get-tuple-element.18), channel_id=1, source_target_pairs={{0,1},{1,0},{2,3},{3,2},{4,5},{5,4},{6,7},{7,6},{8,9},{9,8},{10,11... | collective-permute-start | bytes 61448 | tf_op jit(solution)/shard_map/ppermute | solution.py:275
  11.3 3.0 %collective-permute-start.3 = (bf16[80,128]{1,0:T(8,128)(2,1)S(1)}, bf16[80,128]{1,0:T(8,128)(2,1)S(1)}, u32[]{:S(2)}, u32[]{:S(2)}) collective-permute-start(bf16[80,128]{1,0:T(8,128)(2,1)S(1)} %get-tuple-element.19), channel_id=1, source_target_pairs={{1,2},{2,1},{5,6},{6,5},{9,10},{10,9},{13,14},{14,13},{17,18},{18,... | collective-permute-start | bytes 61448 | tf_op jit(solution)/shard_map/ppermute | solution.py:276
  14.3 2.0 %collective-permute-done.3.y_b_ref = bf16[80,128]{1,0:T(8,128)(2,1)S(1)} collective-permute-done((bf16[80,128]{1,0:T(8,128)(2,1)S(1)}, bf16[80,128]{1,0:T(8,128)(2,1)S(1)}, u32[]{:S(2)}, u32[]{:S(2)}) %collective-permute-start.3) | collective-permute-done | bytes 20512 | tf_op jit(solution)/shard_map/ppermute | solution.py:276
  16.4 1.2 %copy-done = bf16[27,128,128]{2,1,0:T(8,128)(2,1)S(1)} copy-done((bf16[27,128,128]{2,1,0:T(8,128)(2,1)S(1)}, bf16[27,128,128]{2,1,0:T(8,128)(2,1)}, u32[]{:S(2)}) %copy-start) | copy-done | bytes 884760
  17.5 0.9 %copy-done.3 = bf16[4,128,128]{2,1,0:T(8,128)(2,1)S(1)} copy-done((bf16[4,128,128]{2,1,0:T(8,128)(2,1)S(1)}, bf16[4,128,128]{2,1,0:T(8,128)(2,1)}, u32[]{:S(2)}) %copy-start.3) | copy-done | bytes 131096
  18.4 0.8 copy-done.4
  19.2 0.7 copy-done.7
  19.9 0.7 copy-done.8
  20.6 3.7 %tile.1 = (bf16[8,64,128]{2,1,0:T(8,128)(2,1)S(1)}, bf16[64,128]{1,0:T(8,128)(2,1)S(1)}, bf16[64,128]{1,0:T(8,128)(2,1)S(1)}, bf16[2,64,128]{2,1,0:T(8,128)(2,1)...) custom-call(bf16[4,128,128]{2,1,0:T(8,128)(2,1)S(1)} %copy-done.3, s32[4,128]{1,0:T(4,128)S(1)} %copy-done.5, ...), custom_call_target="tpu_custom_call" | custom-call | tf_op jit(solution)/shard_map/tile/pallas_call | solution.py:25
  24.3 1.8 %collective-permute-done.8 = bf16[4,432,128]{2,1,0:T(8,128)(2,1)S(1)} collective-permute-done((bf16[4,432,128]{2,1,0:T(8,128)(2,1)S(1)}, bf16[4,432,128]{2,1,0:T(8,128)(2,1)S(1)}, u32[]{:S(2)}, u32[]{:S(2)}) %collective-permute-start.8) | collective-permute-done | bytes 442400 | tf_op jit(solution)/shard_map/ppermute | solution.py:295
  26.3 5.1 %collective-permute-done.9 = bf16[2,432,128]{2,1,0:T(8,128)(2,1)S(1)} collective-permute-done((bf16[2,432,128]{2,1,0:T(8,128)(2,1)S(1)}, bf16[2,432,128]{2,1,0:T(8,128)(2,1)S(1)}, u32[]{:S(2)}, u32[]{:S(2)}) %collective-permute-start.9) | collective-permute-done | bytes 221216 | tf_op jit(solution)/shard_map/ppermute | solution.py:295
  31.5 1.0 %collective-permute-start.10 = (bf16[432,128]{1,0:T(8,128)(2,1)S(1)}, bf16[432,128]{1,0:T(8,128)(2,1)S(1)}, u32[]{:S(2)}, u32[]{:S(2)}) collective-permute-start(bf16[432,128]{1,0:T(8,128)(2,1)S(1)} %fusion.5), channel_id=1, source_target_pairs={{0,4},{1,3},{2,6},{3,1},{4,0},{5,7},{6,2},{7,5},{8,12},{9,11},{10,... | collective-permute-start | bytes 331784 | tf_op jit(solution)/shard_map/ppermute | solution.py:295
  32.4 2.7 %collective-permute-done.10 = bf16[432,128]{1,0:T(8,128)(2,1)S(1)} collective-permute-done((bf16[432,128]{1,0:T(8,128)(2,1)S(1)}, bf16[432,128]{1,0:T(8,128)(2,1)S(1)}, u32[]{:S(2)}, u32[]{:S(2)}) %collective-permute-start.10) | collective-permute-done | bytes 110624 | tf_op jit(solution)/shard_map/ppermute | solution.py:295
  35.4 3.4 %collective-permute-done.11 = bf16[432,128]{1,0:T(8,128)(2,1)S(1)} collective-permute-done((bf16[432,128]{1,0:T(8,128)(2,1)S(1)}, bf16[432,128]{1,0:T(8,128)(2,1)S(1)}, u32[]{:S(2)}, u32[]{:S(2)}) %collective-permute-start.11) | collective-permute-done | bytes 110624 | tf_op jit(solution)/shard_map/ppermute | solution.py:295
  39.0 5.4 %collective-permute-done.12 = bf16[432,128]{1,0:T(8,128)(2,1)S(1)} collective-permute-done((bf16[432,128]{1,0:T(8,128)(2,1)S(1)}, bf16[432,128]{1,0:T(8,128)(2,1)S(1)}, u32[]{:S(2)}, u32[]{:S(2)}) %collective-permute-start.12) | collective-permute-done | bytes 110624 | tf_op jit(solution)/shard_map/ppermute | solution.py:295
  44.4 1.0 %collective-permute-start.13 = (bf16[432,128]{1,0:T(8,128)(2,1)S(1)}, bf16[432,128]{1,0:T(8,128)(2,1)S(1)}, u32[]{:S(2)}, u32[]{:S(2)}) collective-permute-start(bf16[432,128]{1,0:T(8,128)(2,1)S(1)} %add_convert_fusion.refs_0_), channel_id=1, source_target_pairs={{0,4},{1,3},{2,6},{3,1},{4,0},{5,7},{6,2},{7,5},{8,12},{9,11},{10,... | collective-permute-start | bytes 331784 | tf_op jit(solution)/shard_map/ppermute | solution.py:295
  45.3 3.0 %collective-permute-done.13.refs_1_ = bf16[432,128]{1,0:T(8,128)(2,1)S(1)} collective-permute-done((bf16[432,128]{1,0:T(8,128)(2,1)S(1)}, bf16[432,128]{1,0:T(8,128)(2,1)S(1)}, u32[]{:S(2)}, u32[]{:S(2)}) %collective-permute-start.13) | collective-permute-done | bytes 110624 | tf_op jit(solution)/shard_map/ppermute | solution.py:295
  48.3 6.7 %collective-permute-start.16 = (bf16[432,128]{1,0:T(8,128)(2,1)S(1)}, bf16[432,128]{1,0:T(8,128)(2,1)S(1)}, u32[]{:S(2)}, u32[]{:S(2)}) collective-permute-start(bf16[432,128]{1,0:T(8,128)(2,1)S(1)} %add_convert_fusion.refs_0_), channel_id=1, source_target_pairs={{0,1},{1,0},{2,3},{3,2},{4,5},{5,4},{6,7},{7,6},{8,9},{9,8},{10,11... | collective-permute-start | bytes 331784 | tf_op jit(solution)/shard_map/ppermute | solution.py:295
  55.6 3.0 %collective-permute-start.19 = (bf16[432,128]{1,0:T(8,128)(2,1)S(1)}, bf16[432,128]{1,0:T(8,128)(2,1)S(1)}, u32[]{:S(2)}, u32[]{:S(2)}) collective-permute-start(bf16[432,128]{1,0:T(8,128)(2,1)S(1)} %collective-permute-done.15.refs_3_), channel_id=1, source_target_pairs={{0,1},{1,0},{2,3},{3,2},{4,5},{5,4},{6,7},{7,6},{8,9},{9,8},{10,11... | collective-permute-start | bytes 331784 | tf_op jit(solution)/shard_map/ppermute | solution.py:295
  58.6 2.6 %collective-permute-done.4.got_a_ref.x_a_ref = bf16[64,128]{1,0:T(8,128)(2,1)S(1)} collective-permute-done((bf16[64,128]{1,0:T(8,128)(2,1)S(1)}, bf16[64,128]{1,0:T(8,128)(2,1)S(1)}, u32[]{:S(2)}, u32[]{:S(2)}) %collective-permute-start.4) | collective-permute-done | bytes 16416 | tf_op jit(solution)/shard_map/ppermute | solution.py:275
  61.1 1.9 %collective-permute-start.5 = (bf16[64,128]{1,0:T(8,128)(2,1)S(1)}, bf16[64,128]{1,0:T(8,128)(2,1)S(1)}, u32[]{:S(2)}, u32[]{:S(2)}) collective-permute-start(bf16[64,128]{1,0:T(8,128)(2,1)S(1)} %get-tuple-element.22), channel_id=1, source_target_pairs={{4,8},{8,4},{12,16},{16,12},{20,24},{24,20},{5,9},{9,5},{13,17},{1... | collective-permute-start | bytes 49160 | tf_op jit(solution)/shard_map/ppermute | solution.py:276
  63.1 3.5 %collective-permute-done.5.got_b_ref.x_b_ref = bf16[64,128]{1,0:T(8,128)(2,1)S(1)} collective-permute-done((bf16[64,128]{1,0:T(8,128)(2,1)S(1)}, bf16[64,128]{1,0:T(8,128)(2,1)S(1)}, u32[]{:S(2)}, u32[]{:S(2)}) %collective-permute-start.5) | collective-permute-done | bytes 16416 | tf_op jit(solution)/shard_map/ppermute | solution.py:276
  66.5 2.4 %collective-permute-start.6 = (bf16[80,128]{1,0:T(8,128)(2,1)S(1)}, bf16[80,128]{1,0:T(8,128)(2,1)S(1)}, u32[]{:S(2)}, u32[]{:S(2)}) collective-permute-start(bf16[80,128]{1,0:T(8,128)(2,1)S(1)} %get-tuple-element.24), channel_id=1, source_target_pairs={{0,1},{1,0},{2,3},{3,2},{4,5},{5,4},{6,7},{7,6},{8,9},{9,8},{10,11... | collective-permute-start | bytes 61448 | tf_op jit(solution)/shard_map/ppermute | solution.py:275
  68.9 0.8 %collective-permute-done.6.y_a_ref = bf16[80,128]{1,0:T(8,128)(2,1)S(1)} collective-permute-done((bf16[80,128]{1,0:T(8,128)(2,1)S(1)}, bf16[80,128]{1,0:T(8,128)(2,1)S(1)}, u32[]{:S(2)}, u32[]{:S(2)}) %collective-permute-start.6) | collective-permute-done | bytes 20512 | tf_op jit(solution)/shard_map/ppermute | solution.py:275
  69.7 3.1 %collective-permute-start.7 = (bf16[80,128]{1,0:T(8,128)(2,1)S(1)}, bf16[80,128]{1,0:T(8,128)(2,1)S(1)}, u32[]{:S(2)}, u32[]{:S(2)}) collective-permute-start(bf16[80,128]{1,0:T(8,128)(2,1)S(1)} %get-tuple-element.25), channel_id=1, source_target_pairs={{1,2},{2,1},{5,6},{6,5},{9,10},{10,9},{13,14},{14,13},{17,18},{18,... | collective-permute-start | bytes 61448 | tf_op jit(solution)/shard_map/ppermute | solution.py:276
  72.8 2.0 %collective-permute-done.7.y_b_ref = bf16[80,128]{1,0:T(8,128)(2,1)S(1)} collective-permute-done((bf16[80,128]{1,0:T(8,128)(2,1)S(1)}, bf16[80,128]{1,0:T(8,128)(2,1)S(1)}, u32[]{:S(2)}, u32[]{:S(2)}) %collective-permute-start.7) | collective-permute-done | bytes 20512 | tf_op jit(solution)/shard_map/ppermute | solution.py:276
  74.8 1.8 %back.1 = bf16[4,128,128]{2,1,0:T(8,128)(2,1)} custom-call(bf16[8,64,128]{2,1,0:T(8,128)(2,1)S(1)} %get-tuple-element.20.grad_ref, s32[4,128]{1,0:T(4,128)S(1)} %copy-done.6, bf16[64,128]{1,0:T(8,128)(2,1)S(1)} %collective-permute-done.4.got_a_ref.x_a_ref, bf16[64,128]{1,0:T(8,128)(2,1)S(1)} %collective-permute-done.5.got_b_ref.x_b_ref, ...), custom_call_target="tpu_custom_call" | custom-call | tf_op jit(solution)/shard_map/back/pallas_call | solution.py:25
  76.7 1.7 %normalise.1 = f32[27,128,128]{2,1,0:T(8,128)} custom-call(bf16[432,128]{1,0:T(8,128)(2,1)S(1)} %add_convert_fusion.refs_0_, bf16[432,128]{1,0:T(8,128)(2,1)S(1)} %collective-permute-done.13.refs_1_, bf16[432,128]{1,0:T(8,128)(2,1)S(1)} %collective-permute-done.14.refs_2_, bf16[432,128]{1,0:T(8,128)(2,1)S(1)} %collective-permute-done.15.refs_3_, ...), custom_call_target="tpu_custom_call" | custom-call | tf_op jit(solution)/shard_map/normalise/pallas_call | solution.py:25
  (39 shorter events, 2.2 us)
Async XLA Ops:
  0.6 0.9 %copy-start.2 = (bf16[4,128,128]{2,1,0:T(8,128)(2,1)S(1)}, bf16[4,128,128]{2,1,0:T(8,128)(2,1)}, u32[]{:S(2)}) copy-start(bf16[4,128,128]{2,1,0:T(8,128)(2,1)} %feat_ref.3) | copy-start | bytes 393220
  1.5 0.7 copy-start.5
  2.4 3.3 %collective-permute-start = (bf16[64,128]{1,0:T(8,128)(2,1)S(1)}, bf16[64,128]{1,0:T(8,128)(2,1)S(1)}, u32[]{:S(2)}, u32[]{:S(2)}) collective-permute-start(bf16[64,128]{1,0:T(8,128)(2,1)S(1)} %get-tuple-element.15), channel_id=1, source_target_pairs={{0,4},{4,0},{8,12},{12,8},{16,20},{20,16},{24,28},{28,24},{1,5},{5... | collective-permute-start | bytes 49160 | tf_op jit(solution)/shard_map/ppermute | solution.py:275
  3.7 5.4 %collective-permute-start.1 = (bf16[64,128]{1,0:T(8,128)(2,1)S(1)}, bf16[64,128]{1,0:T(8,128)(2,1)S(1)}, u32[]{:S(2)}, u32[]{:S(2)}) collective-permute-start(bf16[64,128]{1,0:T(8,128)(2,1)S(1)} %get-tuple-element.16), channel_id=1, source_target_pairs={{4,8},{8,4},{12,16},{16,12},{20,24},{24,20},{5,9},{9,5},{13,17},{1... | collective-permute-start | bytes 49160 | tf_op jit(solution)/shard_map/ppermute | solution.py:276
  9.1 5.2 %collective-permute-start.2 = (bf16[80,128]{1,0:T(8,128)(2,1)S(1)}, bf16[80,128]{1,0:T(8,128)(2,1)S(1)}, u32[]{:S(2)}, u32[]{:S(2)}) collective-permute-start(bf16[80,128]{1,0:T(8,128)(2,1)S(1)} %get-tuple-element.18), channel_id=1, source_target_pairs={{0,1},{1,0},{2,3},{3,2},{4,5},{5,4},{6,7},{7,6},{8,9},{9,8},{10,11... | collective-permute-start | bytes 61448 | tf_op jit(solution)/shard_map/ppermute | solution.py:275
  11.3 5.1 %collective-permute-start.3 = (bf16[80,128]{1,0:T(8,128)(2,1)S(1)}, bf16[80,128]{1,0:T(8,128)(2,1)S(1)}, u32[]{:S(2)}, u32[]{:S(2)}) collective-permute-start(bf16[80,128]{1,0:T(8,128)(2,1)S(1)} %get-tuple-element.19), channel_id=1, source_target_pairs={{1,2},{2,1},{5,6},{6,5},{9,10},{10,9},{13,14},{14,13},{17,18},{18,... | collective-permute-start | bytes 61448 | tf_op jit(solution)/shard_map/ppermute | solution.py:276
  16.3 1.2 %copy-start = (bf16[27,128,128]{2,1,0:T(8,128)(2,1)S(1)}, bf16[27,128,128]{2,1,0:T(8,128)(2,1)}, u32[]{:S(2)}) copy-start(bf16[27,128,128]{2,1,0:T(8,128)(2,1)} %weight_ref.3) | copy-start | bytes 2654212
  17.5 0.9 %copy-start.3 = (bf16[4,128,128]{2,1,0:T(8,128)(2,1)S(1)}, bf16[4,128,128]{2,1,0:T(8,128)(2,1)}, u32[]{:S(2)}) copy-start(bf16[4,128,128]{2,1,0:T(8,128)(2,1)} %feat_ref.3) | copy-start | bytes 393220
  18.4 0.8 copy-start.4
  19.2 0.7 copy-start.7
  19.9 0.7 copy-start.8
  24.2 1.9 %collective-permute-start.8 = (bf16[4,432,128]{2,1,0:T(8,128)(2,1)S(1)}, bf16[4,432,128]{2,1,0:T(8,128)(2,1)S(1)}, u32[]{:S(2)}, u32[]{:S(2)}) collective-permute-start(bf16[4,432,128]{2,1,0:T(8,128)(2,1)S(1)} %get-tuple-element.27), channel_id=1, source_target_pairs={{0,1},{1,0},{2,3},{3,2},{4,5},{5,4},{6,7},{7,6},{8,9},{9,8},{10,11... | collective-permute-start | bytes 1327112 | tf_op jit(solution)/shard_map/ppermute | solution.py:295
  26.2 48.6 %copy-start.1 = (bf16[27,128,128]{2,1,0:T(8,128)(2,1)S(1)}, bf16[27,128,128]{2,1,0:T(8,128)(2,1)}, u32[]{:S(2)}) copy-start(bf16[27,128,128]{2,1,0:T(8,128)(2,1)} %weight_ref.3) | copy-start | bytes 2654212
  26.2 48.6 %copy-start.6 = (s32[4,128]{1,0:T(4,128)S(1)}, s32[4,128]{1,0:T(4,128)}, u32[]{:S(2)}) copy-start(s32[4,128]{1,0:T(4,128)} %occ_ref.5) | copy-start | bytes 6148
  26.2 5.1 %collective-permute-start.9 = (bf16[2,432,128]{2,1,0:T(8,128)(2,1)S(1)}, bf16[2,432,128]{2,1,0:T(8,128)(2,1)S(1)}, u32[]{:S(2)}, u32[]{:S(2)}) collective-permute-start(bf16[2,432,128]{2,1,0:T(8,128)(2,1)S(1)} %fusion), channel_id=1, source_target_pairs={{0,2},{1,5},{2,0},{3,7},{4,6},{5,1},{6,4},{7,3},{8,10},{9,13},{10,... | collective-permute-start | bytes 663560 | tf_op jit(solution)/shard_map/ppermute | solution.py:295
  31.5 3.7 %collective-permute-start.10 = (bf16[432,128]{1,0:T(8,128)(2,1)S(1)}, bf16[432,128]{1,0:T(8,128)(2,1)S(1)}, u32[]{:S(2)}, u32[]{:S(2)}) collective-permute-start(bf16[432,128]{1,0:T(8,128)(2,1)S(1)} %fusion.5), channel_id=1, source_target_pairs={{0,4},{1,3},{2,6},{3,1},{4,0},{5,7},{6,2},{7,5},{8,12},{9,11},{10,... | collective-permute-start | bytes 331784 | tf_op jit(solution)/shard_map/ppermute | solution.py:295
  35.2 3.7 %collective-permute-start.11 = (bf16[432,128]{1,0:T(8,128)(2,1)S(1)}, bf16[432,128]{1,0:T(8,128)(2,1)S(1)}, u32[]{:S(2)}, u32[]{:S(2)}) collective-permute-start(bf16[432,128]{1,0:T(8,128)(2,1)S(1)} %fusion.4), channel_id=1, source_target_pairs={{0,8},{1,9},{2,10},{3,11},{4,12},{5,13},{6,14},{7,15},{8,0},{9,1},... | collective-permute-start | bytes 331784 | tf_op jit(solution)/shard_map/ppermute | solution.py:295
  38.9 5.5 %collective-permute-start.12 = (bf16[432,128]{1,0:T(8,128)(2,1)S(1)}, bf16[432,128]{1,0:T(8,128)(2,1)S(1)}, u32[]{:S(2)}, u32[]{:S(2)}) collective-permute-start(bf16[432,128]{1,0:T(8,128)(2,1)S(1)} %add_convert_fusion.1), channel_id=1, source_target_pairs={{0,24},{1,25},{2,26},{3,27},{4,28},{5,29},{6,30},{7,31},{8,16},{9,... | collective-permute-start | bytes 331784 | tf_op jit(solution)/shard_map/ppermute | solution.py:295
  44.4 4.0 %collective-permute-start.13 = (bf16[432,128]{1,0:T(8,128)(2,1)S(1)}, bf16[432,128]{1,0:T(8,128)(2,1)S(1)}, u32[]{:S(2)}, u32[]{:S(2)}) collective-permute-start(bf16[432,128]{1,0:T(8,128)(2,1)S(1)} %add_convert_fusion.refs_0_), channel_id=1, source_target_pairs={{0,4},{1,3},{2,6},{3,1},{4,0},{5,7},{6,2},{7,5},{8,12},{9,11},{10,... | collective-permute-start | bytes 331784 | tf_op jit(solution)/shard_map/ppermute | solution.py:295
  45.3 9.7 %collective-permute-start.14 = (bf16[432,128]{1,0:T(8,128)(2,1)S(1)}, bf16[432,128]{1,0:T(8,128)(2,1)S(1)}, u32[]{:S(2)}, u32[]{:S(2)}) collective-permute-start(bf16[432,128]{1,0:T(8,128)(2,1)S(1)} %add_convert_fusion.refs_0_), channel_id=1, source_target_pairs={{0,2},{1,5},{2,0},{3,7},{4,6},{5,1},{6,4},{7,3},{8,10},{9,13},{10,... | collective-permute-start | bytes 331784 | tf_op jit(solution)/shard_map/ppermute | solution.py:295
  48.3 7.2 %collective-permute-start.15 = (bf16[432,128]{1,0:T(8,128)(2,1)S(1)}, bf16[432,128]{1,0:T(8,128)(2,1)S(1)}, u32[]{:S(2)}, u32[]{:S(2)}) collective-permute-start(bf16[432,128]{1,0:T(8,128)(2,1)S(1)} %collective-permute-done.13.refs_1_), channel_id=1, source_target_pairs={{0,2},{1,5},{2,0},{3,7},{4,6},{5,1},{6,4},{7,3},{8,10},{9,13},{10,... | collective-permute-start | bytes 331784 | tf_op jit(solution)/shard_map/ppermute | solution.py:295
  48.3 28.3 %collective-permute-start.16 = (bf16[432,128]{1,0:T(8,128)(2,1)S(1)}, bf16[432,128]{1,0:T(8,128)(2,1)S(1)}, u32[]{:S(2)}, u32[]{:S(2)}) collective-permute-start(bf16[432,128]{1,0:T(8,128)(2,1)S(1)} %add_convert_fusion.refs_0_), channel_id=1, source_target_pairs={{0,1},{1,0},{2,3},{3,2},{4,5},{5,4},{6,7},{7,6},{8,9},{9,8},{10,11... | collective-permute-start | bytes 331784 | tf_op jit(solution)/shard_map/ppermute | solution.py:295
  55.0 21.6 %collective-permute-start.17 = (bf16[432,128]{1,0:T(8,128)(2,1)S(1)}, bf16[432,128]{1,0:T(8,128)(2,1)S(1)}, u32[]{:S(2)}, u32[]{:S(2)}) collective-permute-start(bf16[432,128]{1,0:T(8,128)(2,1)S(1)} %collective-permute-done.13.refs_1_), channel_id=1, source_target_pairs={{0,1},{1,0},{2,3},{3,2},{4,5},{5,4},{6,7},{7,6},{8,9},{9,8},{10,11... | collective-permute-start | bytes 331784 | tf_op jit(solution)/shard_map/ppermute | solution.py:295
  55.0 21.6 %collective-permute-start.18 = (bf16[432,128]{1,0:T(8,128)(2,1)S(1)}, bf16[432,128]{1,0:T(8,128)(2,1)S(1)}, u32[]{:S(2)}, u32[]{:S(2)}) collective-permute-start(bf16[432,128]{1,0:T(8,128)(2,1)S(1)} %collective-permute-done.14.refs_2_), channel_id=1, source_target_pairs={{0,1},{1,0},{2,3},{3,2},{4,5},{5,4},{6,7},{7,6},{8,9},{9,8},{10,11... | collective-permute-start | bytes 331784 | tf_op jit(solution)/shard_map/ppermute | solution.py:295
  55.6 21.1 %collective-permute-start.19 = (bf16[432,128]{1,0:T(8,128)(2,1)S(1)}, bf16[432,128]{1,0:T(8,128)(2,1)S(1)}, u32[]{:S(2)}, u32[]{:S(2)}) collective-permute-start(bf16[432,128]{1,0:T(8,128)(2,1)S(1)} %collective-permute-done.15.refs_3_), channel_id=1, source_target_pairs={{0,1},{1,0},{2,3},{3,2},{4,5},{5,4},{6,7},{7,6},{8,9},{9,8},{10,11... | collective-permute-start | bytes 331784 | tf_op jit(solution)/shard_map/ppermute | solution.py:295
  58.6 2.6 %collective-permute-start.4 = (bf16[64,128]{1,0:T(8,128)(2,1)S(1)}, bf16[64,128]{1,0:T(8,128)(2,1)S(1)}, u32[]{:S(2)}, u32[]{:S(2)}) collective-permute-start(bf16[64,128]{1,0:T(8,128)(2,1)S(1)} %get-tuple-element.21), channel_id=1, source_target_pairs={{0,4},{4,0},{8,12},{12,8},{16,20},{20,16},{24,28},{28,24},{1,5},{5... | collective-permute-start | bytes 49160 | tf_op jit(solution)/shard_map/ppermute | solution.py:275
  61.1 5.4 %collective-permute-start.5 = (bf16[64,128]{1,0:T(8,128)(2,1)S(1)}, bf16[64,128]{1,0:T(8,128)(2,1)S(1)}, u32[]{:S(2)}, u32[]{:S(2)}) collective-permute-start(bf16[64,128]{1,0:T(8,128)(2,1)S(1)} %get-tuple-element.22), channel_id=1, source_target_pairs={{4,8},{8,4},{12,16},{16,12},{20,24},{24,20},{5,9},{9,5},{13,17},{1... | collective-permute-start | bytes 49160 | tf_op jit(solution)/shard_map/ppermute | solution.py:276
  66.5 3.2 %collective-permute-start.6 = (bf16[80,128]{1,0:T(8,128)(2,1)S(1)}, bf16[80,128]{1,0:T(8,128)(2,1)S(1)}, u32[]{:S(2)}, u32[]{:S(2)}) collective-permute-start(bf16[80,128]{1,0:T(8,128)(2,1)S(1)} %get-tuple-element.24), channel_id=1, source_target_pairs={{0,1},{1,0},{2,3},{3,2},{4,5},{5,4},{6,7},{7,6},{8,9},{9,8},{10,11... | collective-permute-start | bytes 61448 | tf_op jit(solution)/shard_map/ppermute | solution.py:275
  69.7 5.1 %collective-permute-start.7 = (bf16[80,128]{1,0:T(8,128)(2,1)S(1)}, bf16[80,128]{1,0:T(8,128)(2,1)S(1)}, u32[]{:S(2)}, u32[]{:S(2)}) collective-permute-start(bf16[80,128]{1,0:T(8,128)(2,1)S(1)} %get-tuple-element.25), channel_id=1, source_target_pairs={{1,2},{2,1},{5,6},{6,5},{9,10},{10,9},{13,14},{14,13},{17,18},{18,... | collective-permute-start | bytes 61448 | tf_op jit(solution)/shard_map/ppermute | solution.py:276

commit v2 on v1

v2 whole, which is shorter than its diff:
```python
import functools

import jax
import jax.numpy as jnp
from jax import lax
from jax.experimental import pallas as pl
from jax.experimental.pallas import tpu as pltpu
from jax.sharding import PartitionSpec as P

GX = 2
GY = 2
BX = 4
BY = 4
SIDE = 8
PLANE = SIDE * SIDE
TAPS = 9
BF16 = jnp.bfloat16
F32 = jnp.float32
PARTS = 8


def vmem(count):
    return [pl.BlockSpec(memory_space=pltpu.VMEM)] * count


def pin(array):
    return pltpu.with_memory_space_constraint(array, pltpu.HBM)


def call(body, outs, inputs, scratch=(), limit=32 * 2**20, name=None, fetched=0):
    return pl.pallas_call(
        body,
        out_shape=outs,
        in_specs=[pl.BlockSpec(memory_space=pltpu.HBM)] * fetched + vmem(len(inputs) - fetched),
        out_specs=jax.tree.map(lambda _: pl.BlockSpec(memory_space=pltpu.VMEM), outs),
        scratch_shapes=list(scratch),
        compiler_params=pltpu.CompilerParams(vmem_limit_bytes=limit),
        name=name,
    )(*[pin(array) for array in inputs[:fetched]], *inputs[fetched:])


def buffers(*arrays):
    rooms = [pltpu.VMEM(array.shape, array.dtype) for array in arrays]
    return (*rooms, pltpu.SemaphoreType.DMA((len(arrays),)))


def fetch(sources, rooms, semaphores):
    copies = [
        pltpu.make_async_copy(source, room, semaphores.at[i])
        for i, (source, room) in enumerate(zip(sources, rooms))
    ]
    for copy in copies:
        copy.start()
    return copies


def shape(dims, dtype):
    return jax.ShapeDtypeStruct(dims, dtype)


def slot_planes(slot):
    return BX * (slot // GY), (slot % GY) * BY * SIDE


def parity(axis):
    return lax.rem(lax.axis_index(axis), 2) == 0


def occupancy_columns(occ_ref, rows):
    occ = occ_ref[...].astype(F32)
    padded = jnp.concatenate([occ, jnp.zeros((8 - occ.shape[0], occ.shape[1]), F32)], axis=0)
    return padded.T


def write_grid(grid_ref, planes):
    for x in range(SIDE):
        grid_ref[x + 1, SIDE : SIDE + PLANE, :] = planes(x)


def y_faces(planes):
    low = jnp.concatenate([planes(x)[:SIDE] for x in range(SIDE)], axis=0)
    high = jnp.concatenate([planes(x)[PLANE - SIDE :] for x in range(SIDE)], axis=0)
    return low, high


def store_faces(low_plane, high_plane, low_y, high_y, pair_ref, next_ref, edge_ref):
    even = parity("tx")
    pair_ref[...] = jnp.where(even, high_plane, low_plane).astype(BF16)
    next_ref[...] = jnp.where(even, low_plane, high_plane).astype(BF16)
    edge_ref[0] = low_y.astype(BF16)
    edge_ref[1] = high_y.astype(BF16)


def first_faces_kernel(
    feat_hbm, occ_hbm, pair_ref, next_ref, edge_ref, feat_ref, occ_ref, semaphores
):
    for copy in fetch((feat_hbm, occ_hbm), (feat_ref, occ_ref), semaphores):
        copy.wait()
    columns = occupancy_columns(occ_ref, 8)
    channels = feat_ref.shape[2]

    def masked(slot, first, rows):
        mask = jnp.broadcast_to(columns[first : first + rows, slot : slot + 1], (rows, channels))
        return feat_ref[slot, first : first + rows, :].astype(F32) * mask

    def plane(x):
        i, a = x // BX, x % BX
        return jnp.concatenate(
            [masked(i * GY + j, a * BY * SIDE, BY * SIDE) for j in range(GY)], axis=0
        )

    every = [plane(x) for x in range(SIDE)]
    low_y, high_y = y_faces(lambda x: every[x])
    store_faces(every[0], every[SIDE - 1], low_y, high_y, pair_ref, next_ref, edge_ref)


def store_edges(low, high, edge_ref, a_ref, b_ref, planes_ref):
    even_y = parity("ty")
    planes_ref[0] = low.astype(BF16)
    planes_ref[1] = high.astype(BF16)
    last = PLANE - SIDE
    bottom = jnp.concatenate([low[:SIDE], edge_ref[0].astype(F32), high[:SIDE]], axis=0)
    top = jnp.concatenate([low[last:], edge_ref[1].astype(F32), high[last:]], axis=0)
    a_ref[...] = jnp.where(even_y, top, bottom).astype(BF16)
    b_ref[...] = jnp.where(even_y, bottom, top).astype(BF16)


def edge_kernel(edge_ref, next_ref, pair_ref, *refs):
    even = parity("tx")
    pair, other = pair_ref[...].astype(F32), next_ref[...].astype(F32)
    low, high = jnp.where(even, other, pair), jnp.where(even, pair, other)
    store_edges(low, high, edge_ref, *refs[-3:])


def hand_on_edge_kernel(flips, first_row, edge_ref, got1_ref, got2_ref, *refs):
    lines, (a_ref, b_ref, planes_ref) = refs[: len(flips)], refs[-3:]
    even = parity("tx")
    pair = picked_face(got1_ref[first_row[0] : first_row[0] + PLANE], got2_ref[first_row[1] : first_row[1] + PLANE])
    place = lax.axis_index("tx") // 2
    behind = jnp.where(even, place - 1, place + 1)
    other = jnp.zeros(pair.shape, F32)
    for flip, line_ref in zip(flips, lines):
        face = line_ref[first_row[2] : first_row[2] + PLANE].astype(F32)
        other = jnp.where((place ^ behind) == flip, face, other)
    low, high = jnp.where(even, other, pair), jnp.where(even, pair, other)
    store_edges(low, high, edge_ref, a_ref, b_ref, planes_ref)


def picked_face(by_first_way, by_second_way):
    lane = lane_of(lax.axis_index("tx"), lax.axis_index("ty"))
    return jnp.where(lane == 0, by_second_way.astype(F32), by_first_way.astype(F32))


def write_halo(grid_ref, planes_ref, y_a_ref, y_b_ref):
    even_y = parity("ty")
    grid_ref[0, SIDE : SIDE + PLANE, :] = planes_ref[0].astype(F32)
    grid_ref[SIDE + 1, SIDE : SIDE + PLANE, :] = planes_ref[1].astype(F32)
    y_a, y_b = y_a_ref[...].astype(F32), y_b_ref[...].astype(F32)
    low, high = jnp.where(even_y, y_b, y_a), jnp.where(even_y, y_a, y_b)
    for x in range(SIDE + 2):
        grid_ref[x, :SIDE, :] = low[x * SIDE : (x + 1) * SIDE]
        grid_ref[x, SIDE + PLANE :, :] = high[x * SIDE : (x + 1) * SIDE]


def write_columns(grid_ref, cols_ref):
    channels = grid_ref.shape[2]
    z = lax.broadcasted_iota(jnp.int32, ((SIDE + 2) * SIDE, channels), 0) % SIDE
    for x in range(SIDE + 2):
        plane = grid_ref[x]
        zeros = jnp.zeros((1, channels), F32)
        before = jnp.where(z == 0, 0.0, jnp.concatenate([zeros, plane[:-1]], axis=0))
        after = jnp.where(z == SIDE - 1, 0.0, jnp.concatenate([plane[1:], zeros], axis=0))
        for dz, moved in enumerate((before, plane, after)):
            for dy in range(3):
                tap = 3 * dy + dz
                cols_ref[x, :, tap * channels : (tap + 1) * channels] = moved[
                    dy * SIDE : dy * SIDE + PLANE
                ].astype(BF16)


def split3(value):
    high = value.astype(BF16)
    rest = value - high.astype(F32)
    middle = rest.astype(BF16)
    low = (rest - middle.astype(F32)).astype(BF16)
    return high, middle, low


def contract(a, b, dim_a, dim_b):
    return lax.dot_general(a, b, (((dim_a,), (dim_b,)), ((), ())), preferred_element_type=F32)


def write_mask(occ_ref, mask_ref):
    columns = occupancy_columns(occ_ref, 8)
    rows, channels = BY * SIDE, mask_ref.shape[2]
    for slot in range(GX * GY):
        x0, row0 = slot_planes(slot)
        wide = jnp.broadcast_to(columns[:, slot : slot + 1], (columns.shape[0], channels))
        for a in range(BX):
            mask_ref[x0 + a, row0 : row0 + rows, :] = wide[a * rows : (a + 1) * rows]


def prepare_kernel(
    feat_hbm, occ_hbm, point_hbm, teach_hbm, head_hbm, weight_hbm, order_ref,
    masked_ref, mask_ref, sums_ref, head_ref, weight_ref,
    feat_ref, occ_ref, point_ref, teach_ref, semaphores,
):
    del order_ref
    sources = (feat_hbm, occ_hbm, point_hbm, teach_hbm, head_hbm, weight_hbm)
    rooms = (feat_ref, occ_ref, point_ref, teach_ref, head_ref, weight_ref)
    copies = fetch(sources, rooms, semaphores)
    for copy in copies[:4]:
        copy.wait()
    rows = BY * SIDE
    write_mask(occ_ref, mask_ref)
    for slot in range(GX * GY):
        x0, row0 = slot_planes(slot)
        for a in range(BX):
            part = feat_ref[slot, a * rows : (a + 1) * rows, :].astype(F32)
            part = part * mask_ref[x0 + a, row0 : row0 + rows, :]
            masked_ref[x0 + a, row0 : row0 + rows, :] = part
    target = jnp.exp(teach_ref[...].astype(F32))
    target = target / jnp.sum(target, axis=0, keepdims=True)
    classes, points = target.shape
    place = point_ref[...]
    place = (place & 0x11F) | ((place & 0x80) >> 2) | ((place & 0x60) << 1)
    chosen = lax.broadcasted_iota(jnp.int32, (SIDE * PLANE, points), 0) == place
    chosen = jnp.where(chosen, 1.0, 0.0).astype(BF16)
    stack = jnp.concatenate([*split3(target), jnp.ones((classes, points), BF16)], axis=0)
    sums = contract(stack, chosen, 1, 1)
    target_sum = sums[:classes] + sums[classes : 2 * classes] + sums[2 * classes : 3 * classes]
    sums_ref[...] = jnp.concatenate([target_sum, sums[3 * classes :]], axis=0)
    for copy in copies[4:]:
        copy.wait()


def tile_kernel(
    masked_ref, mask_ref, sums_ref, head_ref, weight_ref, planes_ref, y_b_ref, y_a_ref,
    grad_ref, next_ref, edge_ref, keep_ref, send_ref,
    grid_ref, cols_ref, terms_ref,
):
    channels = masked_ref.shape[2]
    classes = head_ref.shape[0]
    voxels = SIDE * PLANE
    write_grid(grid_ref, lambda x: masked_ref[x])
    write_halo(grid_ref, planes_ref, y_a_ref, y_b_ref)
    write_columns(grid_ref, cols_ref)

    pre = jnp.zeros((voxels, channels), F32)
    for dx in range(3):
        window = cols_ref[dx : dx + SIDE].reshape(voxels, TAPS * channels)
        matrix = weight_ref[TAPS * dx : TAPS * (dx + 1)].reshape(TAPS * channels, channels)
        pre = pre + jnp.dot(window, matrix, preferred_element_type=F32)
    mask = mask_ref[...].reshape(voxels, channels)
    logistic = 1.0 / (1.0 + jnp.exp(-pre))
    slope = logistic * (1.0 + pre * (1.0 - logistic)) * mask
    hidden = (pre / (1.0 + jnp.exp(-pre)) * mask).astype(BF16)

    logits = contract(head_ref[...], hidden, 1, 1)
    student = jnp.exp(logits)
    student = student / jnp.sum(student, axis=0, keepdims=True)
    target_sum, count = sums_ref[:classes], sums_ref[classes:]
    slope_logits = jnp.where(count > 0.0, count * student, 0.0) - target_sum
    heads = jnp.concatenate([head_ref[...]] * 3, axis=0)
    pieces = jnp.concatenate([piece.astype(F32) for piece in split3(slope_logits)], axis=0)
    dhidden = contract(pieces.T.astype(BF16), heads, 1, 0)
    gradient = dhidden * slope
    rounded = gradient.astype(BF16)
    grad_ref[...] = rounded.reshape(SIDE, PLANE, channels)
    low_y, high_y = y_faces(lambda x: gradient[x * PLANE : (x + 1) * PLANE])
    ends = gradient[:PLANE], gradient[voxels - PLANE :]
    pair_ref = send_ref.at[send_ref.shape[0] - PLANE :]
    store_faces(*ends, low_y, high_y, pair_ref, next_ref, edge_ref)

    for dx in range(3):
        window = cols_ref[dx : dx + SIDE].reshape(voxels, TAPS * channels)
        product = contract(window, rounded, 0, 0)
        terms_ref[TAPS * dx : TAPS * (dx + 1)] = product.reshape(TAPS, channels, channels)
    length = channels // PARTS
    for r in range(PARTS):
        first = pl.multiple_of(part_index(r) * length, length)
        part = terms_ref[:, pl.ds(first, length), :].reshape(-1, channels)
        row = (r % (PARTS // 2)) * part.shape[0]
        if r < PARTS // 2:
            keep_ref[row : row + part.shape[0]] = part
        else:
            send_ref[row : row + part.shape[0]] = part.astype(BF16)


def lane_of(tx, ty):
    return (ty ^ (ty >> 1) ^ tx ^ (tx >> 1)) & 1


def part_index(r):
    tx, ty = lax.axis_index("tx"), lax.axis_index("ty")
    lane, across, along = lane_of(tx, ty) ^ (r >> 2), (ty >> 1) & 1, tx & 1
    first = jnp.where(lane == 0, across, along)
    second = jnp.where(lane == 0, along, across)
    return lane * 4 + ((first * 2 + second) ^ (r & 3))


def back_kernel(
    mask_ref, weight_ref, grad_ref, planes_ref, y_b_ref, y_a_ref, out_ref, token_ref,
    grid_ref, cols_ref,
):
    channels = grad_ref.shape[2]
    voxels = SIDE * PLANE
    write_grid(grid_ref, lambda x: grad_ref[x].astype(F32))
    write_halo(grid_ref, planes_ref, y_a_ref, y_b_ref)
    write_columns(grid_ref, cols_ref)
    token_ref[...] = jnp.zeros(token_ref.shape, F32)
    total = jnp.zeros((voxels, channels), F32)
    for dx in range(3):
        window = cols_ref[dx : dx + SIDE].reshape(voxels, TAPS * channels)
        taps = [weight_ref[3 * TAPS - 1 - (TAPS * dx + tap)] for tap in range(TAPS)]
        total = total + contract(window, jnp.concatenate(taps, axis=1), 1, 1)
    total = (total * mask_ref[...].reshape(voxels, channels)).reshape(SIDE, PLANE, channels)
    rows = BY * SIDE
    for slot in range(GX * GY):
        x0, row0 = slot_planes(slot)
        for a in range(BX):
            part = total[x0 + a, row0 : row0 + rows].astype(BF16)
            out_ref[slot, a * rows : (a + 1) * rows, :] = part


def norm_kernel(near_ref, far_ref, got_near_ref, got_far_ref, out_ref):
    kernels, channels = out_ref.shape[0], out_ref.shape[2]
    length = channels // PARTS
    refs = (near_ref, far_ref, got_near_ref, got_far_ref)
    rows = kernels * length
    pieces = [ref.at[i * rows : (i + 1) * rows] for ref in refs for i in range(2)]
    squares = jnp.zeros((kernels * length, channels), F32)
    for piece in pieces:
        value = piece[...].astype(F32)
        squares = squares + value * value
    mean = jnp.sum(squares) / (kernels * channels * channels)
    scale = 1.0 / jnp.sqrt(jnp.broadcast_to(mean, (1, channels)) + 1e-06)
    for r, piece in enumerate(pieces):
        value = piece[...].astype(F32) * scale
        first = pl.multiple_of(part_index(r) * length, length)
        out_ref[:, pl.ds(first, length), :] = value.reshape(kernels, length, channels)


def swap_pairs(first, count):
    return [pair for i in range(first, count - 1, 2) for pair in ((i, i + 1), (i + 1, i))]


def swap_along_y(a, b):
    count = lax.axis_size("ty")
    got_b = lax.ppermute(b, "ty", swap_pairs(1, count))
    return lax.ppermute(a, "ty", swap_pairs(0, count)), got_b


def edge_faces(kernel, edges, faces, waits=()):
    face = shape(((SIDE + 2) * SIDE, edges.shape[2]), BF16)
    return pl.pallas_call(
        kernel,
        out_shape=(face, face, shape(edges.shape, BF16)),
        in_specs=vmem(1 + len(faces)) + [pl.BlockSpec(memory_space=pl.ANY)] * len(waits),
        out_specs=tuple(vmem(3)),
        compiler_params=pltpu.CompilerParams(vmem_limit_bytes=16 * 2**20),
        name="edge_faces",
    )(edges, *faces, *waits)


def exchange_with(value, partner):
    n_tx, n_ty = lax.axis_size("tx"), lax.axis_size("ty")
    pairs = []
    for tx in range(n_tx):
        for ty in range(n_ty):
            other = partner(tx, ty)
            if other is not None:
                pairs.append((tx * n_ty + ty, other[0] * n_ty + other[1]))
    return lax.ppermute(value, ("tx", "ty"), pairs)


def by_core(tx, ty):
    return tx, ty ^ 1


def same_lane(tx, ty, other_tx, other_ty):
    return other_tx, other_ty ^ lane_of(tx, ty) ^ lane_of(other_tx, other_ty)


def first_way(tx, ty):
    other = (tx, ty ^ 2) if lane_of(tx, ty) == 0 else (tx ^ 1, ty)
    return same_lane(tx, ty, *other)


def second_way(tx, ty):
    other = (tx ^ 1, ty) if lane_of(tx, ty) == 0 else (tx, ty ^ 2)
    return same_lane(tx, ty, *other)


def along_line(flip):
    return lambda tx, ty: same_lane(tx, ty, tx ^ (2 * flip), ty)


def add(*terms):
    total = terms[0]
    for term in terms[1:]:
        total = total + term
    return total


def message(sections, waits=(), passes=()):
    arrays = []
    for _, _, *terms in sections:
        for array, _ in terms:
            if not any(array is known for known in arrays):
                arrays.append(array)
    place = [[next(i for i, x in enumerate(arrays) if x is array) for array, _ in terms] for _, _, *terms in sections]
    count, others = len(arrays), len(waits) + len(passes)
    total_rows = sum(section[0] for section in sections)

    def body(*refs):
        out_ref, row = refs[count + others], 0
        for places, (rows, fn, *terms) in zip(place, sections):
            values = [refs[i][first : first + rows].astype(F32) for i, (_, first) in zip(places, terms)]
            out_ref[row : row + rows] = fn(*values).astype(BF16)
            row += rows

    plain = pl.BlockSpec(memory_space=pl.ANY)
    outs = [shape((total_rows, arrays[0].shape[1]), BF16)]
    out, *passed = pl.pallas_call(
        body,
        out_shape=outs + [shape(x.shape, x.dtype) for x in passes],
        in_specs=vmem(count) + [plain] * others,
        out_specs=vmem(1) + [plain] * len(passes),
        input_output_aliases={count + len(waits) + i: 1 + i for i in range(len(passes))},
        compiler_params=pltpu.CompilerParams(vmem_limit_bytes=16 * 2**20),
        name="message",
    )(*arrays, *waits, *passes)
    return (out, *passed) if passes else out


def after(value, token):
    plain = pl.BlockSpec(memory_space=pl.ANY)
    return pl.pallas_call(
        lambda value_ref, token_ref, out_ref: None,
        out_shape=shape(value.shape, value.dtype),
        in_specs=[plain] * 2,
        out_specs=plain,
        input_output_aliases={0: 0},
        compiler_params=pltpu.CompilerParams(vmem_limit_bytes=16 * 2**20),
        name="after",
    )(value, token)


def on_device(features, occupancy, neighbors, point_voxel, conv_weight, head_weight, teacher):
    slots, brick, channels = features.shape
    kernels = conv_weight.shape[0]
    n_tx, n_ty = lax.axis_size("tx"), lax.axis_size("ty")
    edges = shape((2, PLANE, channels), BF16)
    ext = (SIDE + 2, (SIDE + 2) * SIDE, channels)
    grid = pltpu.VMEM(ext, F32)
    cols = pltpu.VMEM((SIDE + 2, PLANE, TAPS * channels), BF16)

    fetched = (features, occupancy)
    face = shape((PLANE, channels), BF16)
    pair_face, next_face, x_edges = call(
        first_faces_kernel, (face, face, edges), fetched, buffers(*fetched),
        name="first_faces", fetched=2,
    )
    x_next = lax.ppermute(next_face, "tx", swap_pairs(1, n_tx))
    x_pair = lax.ppermute(pair_face, "tx", swap_pairs(0, n_tx))
    fetched = (
        features, occupancy, point_voxel.reshape(1, -1), teacher, head_weight, conv_weight
    )
    classes = head_weight.shape[0]
    planes = shape((SIDE, PLANE, channels), F32)
    prepared = call(
        prepare_kernel,
        (
            planes,
            planes,
            shape((2 * classes, SIDE * PLANE), F32),
            shape(head_weight.shape, BF16),
            shape(conv_weight.shape, BF16),
        ),
        (*fetched, x_edges),
        (*buffers(*fetched[:4])[:-1], pltpu.SemaphoreType.DMA((len(fetched),))),
        name="prepare",
        fetched=len(fetched),
    )
    y_a, y_b, planes = edge_faces(edge_kernel, x_edges, (x_next, x_pair), prepared[:1])
    y_a, y_b = swap_along_y(y_a, y_b)
    part = kernels * channels // PARTS
    gradient, g_next, g_edges, keep, send = call(
        tile_kernel,
        (
            shape((SIDE, PLANE, channels), BF16),
            face,
            edges,
            shape((PARTS // 2 * part, channels), F32),
            shape((PARTS // 2 * part + PLANE, channels), BF16),
        ),
        (*prepared, planes, y_b, y_a),
        (grid, cols, pltpu.VMEM((kernels, channels, channels), F32)),
        name="tile",
    )
    mask, weight = prepared[1], prepared[4]

    got0 = exchange_with(send, by_core)
    faces = [(PLANE, add, (got0, 4 * part)), (PLANE, add, (g_next, 0))]
    kept = [(2 * part, add, (keep, 2 * part), (got0, 2 * part))]
    got1 = exchange_with(message(kept + faces), first_way)
    kept = [(part, add, (keep, part), (got0, part), (got1, part))]
    got2 = exchange_with(message(kept + faces), second_way)
    at = (2 * part, part, part)
    hand_on = (PLANE, picked_face, (got1, at[0] + PLANE), (got2, at[1] + PLANE))
    total = [(part, add, (keep, 0), (got0, 0), (got1, 0), (got2, 0))]
    flips, lines = [], []
    while 2 ** len(flips) < n_tx // 2:
        flips.append(2 ** (len(flips) + 1) - 1)
        own = message(total + [hand_on])
        lines.append(exchange_with(own, along_line(flips[-1])))
        total = [(part, add, (own, 0), (lines[-1], 0))]
        hand_on = (PLANE, add, (own, part))
    bit = 4
    while bit < n_ty:
        own = message(total)
        flip = 2 * bit - 4
        got = exchange_with(own, lambda tx, ty, flip=flip: same_lane(tx, ty, tx, ty ^ flip))
        total = [(part, add, (own, 0), (got, 0))]
        bit *= 2
    total, g_edges = message(total, (), (g_edges,))
    got3 = exchange_with(total, second_way)
    kernel = functools.partial(hand_on_edge_kernel, flips, at)
    g_a, g_b, planes = edge_faces(kernel, g_edges, (got1, got2, *lines))
    g_a, g_b = swap_along_y(g_a, g_b)
    near, gradient = message(
        [(part, add, (total, 0)), (part, add, (got3, 0))], (g_b, g_a), (gradient,)
    )
    far = exchange_with(near, first_way)
    grad_features, token = call(
        back_kernel,
        (shape((slots, brick, channels), BF16), shape((8, channels), F32)),
        (mask, weight, gradient, planes, g_b, g_a),
        (grid, cols),
        name="back",
    )
    far = after(far, token)
    grad_weight = call(
        norm_kernel,
        shape((kernels, channels, channels), F32),
        (near, far, exchange_with(near, by_core), exchange_with(far, by_core)),
        name="normalise",
    )
    return (grad_features, grad_weight)


def solution(mesh):
    in_specs = (
        P(("tx", "ty"), None, None),
        P(("tx", "ty"), None),
        P(None, ("tx", "ty")),
        P(("tx", "ty")),
        P(),
        P(),
        P(None, ("tx", "ty")),
    )
    out_specs = (P(("tx", "ty"), None, None), P())
    return jax.shard_map(
        on_device, mesh=mesh, in_specs=in_specs, out_specs=out_specs, check_vma=False
    )
```

time: 78.7 us -> 59.1 us (0.75)
  the two profiles are of different devices: /device:TPU:25 before, /device:TPU:0 now
where the time goes in v2:
time: 59.1 us; the launch traced here: 58.5 us
  starting transfers between devices  28.3 us (48%)
  waiting for transfers between devices  20.1 us (34%)
  Pallas kernels  9.33 us (16%)
  between operations  0.73 us (1%)
    ppermute x9, waiting for transfers between devices, exchange_with(): return lax.ppermute(value, ('tx', 'ty'), pairs)  18.1 us
    ppermute x9, starting transfers between devices, exchange_with(): return lax.ppermute(value, ('tx', 'ty'), pairs)  15.8 us
    pallas_call x5, Pallas kernels, call(): pl.pallas_call(body, out_shape=outs, in_specs=[pl.BlockSpec(memory_space=...  9.04 us
    ppermute x1, starting transfers between devices, on_device(): x_pair = lax.ppermute(pair_face, 'tx', swap_pairs(0, n_tx))  5.8 us
    ppermute x2, starting transfers between devices, swap_along_y(): return (lax.ppermute(a, 'ty', swap_pairs(0, count)), got_b)  4.78 us
    ppermute x2, waiting for transfers between devices, swap_along_y(): return (lax.ppermute(a, 'ty', swap_pairs(0, count)), got_b)  1.68 us
    ppermute x2, starting transfers between devices, swap_along_y(): got_b = lax.ppermute(b, 'ty', swap_pairs(1, count))  1.33 us
  transfers between devices with their start and end apart: 15, of which 10 were waited for; matrix products, arithmetic and copies ran while one was open for 0% of the time, Pallas kernels for 6%

profile of v2, /device:TPU:0, one launch (start us, length us, event | category | flops | bytes accessed | tf_op | source)
XLA Modules:
  0.0 58.5 jit_solution(17628654077825447129)
XLA Ops:
  0.6 1.1 %first_faces.1 = (bf16[64,128]{1,0:T(8,128)(2,1)S(1)}, bf16[64,128]{1,0:T(8,128)(2,1)S(1)}, bf16[2,64,128]{2,1,0:T(8,128)(2,1)S(1)}) custom-call(bf16[4,128,128]{2,1,0:T(8,128)(2,1)} %feat_hbm.3, s32[4,128]{1,0:T(4,128)} %occ_hbm.3), custom_call_target="tpu_custom_call" | custom-call | tf_op jit(solution)/shard_map/first_faces/pallas_call | solution.py:31
  1.8 0.7 %collective-permute-start = (bf16[64,128]{1,0:T(8,128)(2,1)S(1)}, bf16[64,128]{1,0:T(8,128)(2,1)S(1)}, u32[]{:S(2)}, u32[]{:S(2)}) collective-permute-start(bf16[64,128]{1,0:T(8,128)(2,1)S(1)} %get-tuple-element.33), channel_id=1, source_target_pairs={{4,8},{8,4},{12,16},{16,12},{20,24},{24,20},{5,9},{9,5},{13,17},{1... | collective-permute-start | bytes 49160 | tf_op jit(solution)/shard_map/ppermute | solution.py:465
  2.4 5.8 %collective-permute-start.1 = (bf16[64,128]{1,0:T(8,128)(2,1)S(1)}, bf16[64,128]{1,0:T(8,128)(2,1)S(1)}, u32[]{:S(2)}, u32[]{:S(2)}) collective-permute-start(bf16[64,128]{1,0:T(8,128)(2,1)S(1)} %get-tuple-element.34), channel_id=1, source_target_pairs={{0,4},{4,0},{8,12},{12,8},{16,20},{20,16},{24,28},{28,24},{1,5},{5... | collective-permute-start | bytes 49160 | tf_op jit(solution)/shard_map/ppermute | solution.py:466
  8.2 1.4 %prepare.1 = (f32[8,64,128]{2,1,0:T(8,128)S(1)}, f32[8,64,128]{2,1,0:T(8,128)S(1)}, f32[32,512]{1,0:T(8,128)S(1)}, bf16[16,128]{1,0:T(8,128)(2,1)S(1)}, bf16[27,128,128]{2,1,0:T(8,128)(2,1)S(1)}) custom-call(bf16[4,128,128]{2,1,0:T(8,128)(2,1)} %feat_hbm.3, s32[4,128]{1,0:T(4,128)} %occ_hbm.3, s32[1,1024]{1,0:T(1,128)} %bitcast.1, ...), custom_call_target="tpu_custom_call" | custom-call | tf_op jit(solution)/shard_map/prepare/pallas_call | solution.py:31
  9.7 0.3 collective-permute-done.1.pair_ref
  10.0 0.7 %collective-permute-start.2 = (bf16[80,128]{1,0:T(8,128)(2,1)S(1)}, bf16[80,128]{1,0:T(8,128)(2,1)S(1)}, u32[]{:S(2)}, u32[]{:S(2)}) collective-permute-start(bf16[80,128]{1,0:T(8,128)(2,1)S(1)} %get-tuple-element.36), channel_id=1, source_target_pairs={{1,2},{2,1},{5,6},{6,5},{9,10},{10,9},{13,14},{14,13},{17,18},{18,... | collective-permute-start | bytes 61448 | tf_op jit(solution)/shard_map/ppermute | solution.py:350
  10.6 2.9 %collective-permute-start.3 = (bf16[80,128]{1,0:T(8,128)(2,1)S(1)}, bf16[80,128]{1,0:T(8,128)(2,1)S(1)}, u32[]{:S(2)}, u32[]{:S(2)}) collective-permute-start(bf16[80,128]{1,0:T(8,128)(2,1)S(1)} %get-tuple-element.37), channel_id=1, source_target_pairs={{0,1},{1,0},{2,3},{3,2},{4,5},{5,4},{6,7},{7,6},{8,9},{9,8},{10,11... | collective-permute-start | bytes 61448 | tf_op jit(solution)/shard_map/ppermute | solution.py:351
  13.6 0.8 %collective-permute-done.3.y_a_ref = bf16[80,128]{1,0:T(8,128)(2,1)S(1)} collective-permute-done((bf16[80,128]{1,0:T(8,128)(2,1)S(1)}, bf16[80,128]{1,0:T(8,128)(2,1)S(1)}, u32[]{:S(2)}, u32[]{:S(2)}) %collective-permute-start.3) | collective-permute-done | bytes 20512 | tf_op jit(solution)/shard_map/ppermute | solution.py:351
  14.4 3.0 %tile.1 = (bf16[8,64,128]{2,1,0:T(8,128)(2,1)S(1)}, bf16[64,128]{1,0:T(8,128)(2,1)S(1)}, bf16[2,64,128]{2,1,0:T(8,128)(2,1)S(1)}, f32[1728,128]{1,0:T(8,128)S(1)}, bf16[1792,128]{1,0:T(8,128)(2,1)S(1)}) custom-call(f32[8,64,128]{2,1,0:T(8,128)S(1)} %get-tuple-element.30.refs_0_.masked_ref, f32[8,64,128]{2,1,0:T(8,128)S(1)} %get-tuple-element.28.mask_ref, ...), custom_call_target="tpu_custom_call" | custom-call | tf_op jit(solution)/shard_map/tile/pallas_call | solution.py:31
  17.5 0.6 %collective-permute-start.4 = (bf16[1792,128]{1,0:T(8,128)(2,1)S(1)}, bf16[1792,128]{1,0:T(8,128)(2,1)S(1)}, u32[]{:S(2)}, u32[]{:S(2)}) collective-permute-start(bf16[1792,128]{1,0:T(8,128)(2,1)S(1)} %get-tuple-element.39), channel_id=1, source_target_pairs={{0,1},{1,0},{2,3},{3,2},{4,5},{5,4},{6,7},{7,6},{8,9},{9,8},{10,11... | collective-permute-start | bytes 1376264 | tf_op jit(solution)/shard_map/ppermute | solution.py:374
  18.1 1.4 %collective-permute-done.4.refs_1_ = bf16[1792,128]{1,0:T(8,128)(2,1)S(1)} collective-permute-done((bf16[1792,128]{1,0:T(8,128)(2,1)S(1)}, bf16[1792,128]{1,0:T(8,128)(2,1)S(1)}, u32[]{:S(2)}, u32[]{:S(2)}) %collective-permute-start.4) | collective-permute-done | bytes 458784 | tf_op jit(solution)/shard_map/ppermute | solution.py:374
  19.5 0.1 message.6
  19.6 1.8 %collective-permute-start.5 = (bf16[992,128]{1,0:T(8,128)(2,1)S(1)}, bf16[992,128]{1,0:T(8,128)(2,1)S(1)}, u32[]{:S(2)}, u32[]{:S(2)}) collective-permute-start(bf16[992,128]{1,0:T(8,128)(2,1)S(1)} %message.6), channel_id=1, source_target_pairs={{0,3},{1,4},{2,7},{3,0},{4,1},{5,6},{6,5},{7,2},{8,13},{9,10},{10,... | collective-permute-start | bytes 761864 | tf_op jit(solution)/shard_map/ppermute | solution.py:374
  21.4 4.0 %collective-permute-done.5.refs_2_.got1_ref = bf16[992,128]{1,0:T(8,128)(2,1)S(1)} collective-permute-done((bf16[992,128]{1,0:T(8,128)(2,1)S(1)}, bf16[992,128]{1,0:T(8,128)(2,1)S(1)}, u32[]{:S(2)}, u32[]{:S(2)}) %collective-permute-start.5) | collective-permute-done | bytes 253984 | tf_op jit(solution)/shard_map/ppermute | solution.py:374
  25.4 2.1 %collective-permute-start.6 = (bf16[560,128]{1,0:T(8,128)(2,1)S(1)}, bf16[560,128]{1,0:T(8,128)(2,1)S(1)}, u32[]{:S(2)}, u32[]{:S(2)}) collective-permute-start(bf16[560,128]{1,0:T(8,128)(2,1)S(1)} %message.7), channel_id=1, source_target_pairs={{0,5},{1,2},{2,1},{3,6},{4,7},{5,0},{6,3},{7,4},{8,11},{9,12},{10,... | collective-permute-start | bytes 430088 | tf_op jit(solution)/shard_map/ppermute | solution.py:374
  27.5 2.8 %collective-permute-done.6.refs_3_.got2_ref = bf16[560,128]{1,0:T(8,128)(2,1)S(1)} collective-permute-done((bf16[560,128]{1,0:T(8,128)(2,1)S(1)}, bf16[560,128]{1,0:T(8,128)(2,1)S(1)}, u32[]{:S(2)}, u32[]{:S(2)}) %collective-permute-start.6) | collective-permute-done | bytes 143392 | tf_op jit(solution)/shard_map/ppermute | solution.py:374
  30.3 0.1 message.8.refs_0_
  30.3 1.7 %collective-permute-start.7 = (bf16[496,128]{1,0:T(8,128)(2,1)S(1)}, bf16[496,128]{1,0:T(8,128)(2,1)S(1)}, u32[]{:S(2)}, u32[]{:S(2)}) collective-permute-start(bf16[496,128]{1,0:T(8,128)(2,1)S(1)} %message.8.refs_0_), channel_id=1, source_target_pairs={{0,9},{1,8},{2,11},{3,10},{4,13},{5,12},{6,15},{7,14},{8,1},{9,0},... | collective-permute-start | bytes 380936 | tf_op jit(solution)/shard_map/ppermute | solution.py:374
  32.1 3.7 %collective-permute-done.7.refs_1_.refs_0_ = bf16[496,128]{1,0:T(8,128)(2,1)S(1)} collective-permute-done((bf16[496,128]{1,0:T(8,128)(2,1)S(1)}, bf16[496,128]{1,0:T(8,128)(2,1)S(1)}, u32[]{:S(2)}, u32[]{:S(2)}) %collective-permute-start.7) | collective-permute-done | bytes 127008 | tf_op jit(solution)/shard_map/ppermute | solution.py:374
  35.8 3.5 %collective-permute-start.8 = (bf16[496,128]{1,0:T(8,128)(2,1)S(1)}, bf16[496,128]{1,0:T(8,128)(2,1)S(1)}, u32[]{:S(2)}, u32[]{:S(2)}) collective-permute-start(bf16[496,128]{1,0:T(8,128)(2,1)S(1)} %message.9.refs_0_), channel_id=1, source_target_pairs={{0,25},{1,24},{2,27},{3,26},{4,29},{5,28},{6,31},{7,30},{8,17},{9,... | collective-permute-start | bytes 380936 | tf_op jit(solution)/shard_map/ppermute | solution.py:374
  39.3 3.8 %collective-permute-done.8.refs_1_ = bf16[496,128]{1,0:T(8,128)(2,1)S(1)} collective-permute-done((bf16[496,128]{1,0:T(8,128)(2,1)S(1)}, bf16[496,128]{1,0:T(8,128)(2,1)S(1)}, u32[]{:S(2)}, u32[]{:S(2)}) %collective-permute-start.8) | collective-permute-done | bytes 127008 | tf_op jit(solution)/shard_map/ppermute | solution.py:374
  43.2 1.4 %collective-permute-start.9 = (bf16[432,128]{1,0:T(8,128)(2,1)S(1)}, bf16[432,128]{1,0:T(8,128)(2,1)S(1)}, u32[]{:S(2)}, u32[]{:S(2)}) collective-permute-start(bf16[432,128]{1,0:T(8,128)(2,1)S(1)} %get-tuple-element.42.refs_0_), channel_id=1, source_target_pairs={{0,5},{1,2},{2,1},{3,6},{4,7},{5,0},{6,3},{7,4},{8,11},{9,12},{10,... | collective-permute-start | bytes 331784 | tf_op jit(solution)/shard_map/ppermute | solution.py:374
  44.7 0.7 %collective-permute-start.10 = (bf16[80,128]{1,0:T(8,128)(2,1)S(1)}, bf16[80,128]{1,0:T(8,128)(2,1)S(1)}, u32[]{:S(2)}, u32[]{:S(2)}) collective-permute-start(bf16[80,128]{1,0:T(8,128)(2,1)S(1)} %get-tuple-element.44), channel_id=1, source_target_pairs={{1,2},{2,1},{5,6},{6,5},{9,10},{10,9},{13,14},{14,13},{17,18},{18,... | collective-permute-start | bytes 61448 | tf_op jit(solution)/shard_map/ppermute | solution.py:350
  45.3 1.8 %collective-permute-start.11 = (bf16[80,128]{1,0:T(8,128)(2,1)S(1)}, bf16[80,128]{1,0:T(8,128)(2,1)S(1)}, u32[]{:S(2)}, u32[]{:S(2)}) collective-permute-start(bf16[80,128]{1,0:T(8,128)(2,1)S(1)} %get-tuple-element.45), channel_id=1, source_target_pairs={{0,1},{1,0},{2,3},{3,2},{4,5},{5,4},{6,7},{7,6},{8,9},{9,8},{10,11... | collective-permute-start | bytes 61448 | tf_op jit(solution)/shard_map/ppermute | solution.py:351
  47.2 0.8 %collective-permute-done.11.refs_3_.y_a_ref = bf16[80,128]{1,0:T(8,128)(2,1)S(1)} collective-permute-done((bf16[80,128]{1,0:T(8,128)(2,1)S(1)}, bf16[80,128]{1,0:T(8,128)(2,1)S(1)}, u32[]{:S(2)}, u32[]{:S(2)}) %collective-permute-start.11) | collective-permute-done | bytes 20512 | tf_op jit(solution)/shard_map/ppermute | solution.py:351
  48.1 1.8 %collective-permute-start.12 = (bf16[864,128]{1,0:T(8,128)(2,1)S(1)}, bf16[864,128]{1,0:T(8,128)(2,1)S(1)}, u32[]{:S(2)}, u32[]{:S(2)}) collective-permute-start(bf16[864,128]{1,0:T(8,128)(2,1)S(1)} %get-tuple-element.50.near_ref), channel_id=1, source_target_pairs={{0,3},{1,4},{2,7},{3,0},{4,1},{5,6},{6,5},{7,2},{8,13},{9,10},{10,... | collective-permute-start | bytes 663560 | tf_op jit(solution)/shard_map/ppermute | solution.py:374
  49.8 0.6 %collective-permute-start.13 = (bf16[864,128]{1,0:T(8,128)(2,1)S(1)}, bf16[864,128]{1,0:T(8,128)(2,1)S(1)}, u32[]{:S(2)}, u32[]{:S(2)}) collective-permute-start(bf16[864,128]{1,0:T(8,128)(2,1)S(1)} %get-tuple-element.50.near_ref), channel_id=1, source_target_pairs={{0,1},{1,0},{2,3},{3,2},{4,5},{5,4},{6,7},{7,6},{8,9},{9,8},{10,11... | collective-permute-start | bytes 663560 | tf_op jit(solution)/shard_map/ppermute | solution.py:374
  50.5 1.8 %back.1 = (bf16[4,128,128]{2,1,0:T(8,128)(2,1)}, f32[8,128]{1,0:T(8,128)S(1)}) custom-call(f32[8,64,128]{2,1,0:T(8,128)S(1)} %get-tuple-element.28.mask_ref, bf16[27,128,128]{2,1,0:T(8,128)(2,1)S(1)} %get-tuple-element.29.weight_ref, bf16[8,64,128]{2,1,0:T(8,128)(2,1)S(1)} %get-tuple-element.47.grad_ref, ...), custom_call_target="tpu_custom_call" | custom-call | tf_op jit(solution)/shard_map/back/pallas_call | solution.py:31
  52.2 1.3 %collective-permute-done.12.value_ref = bf16[864,128]{1,0:T(8,128)(2,1)S(1)} collective-permute-done((bf16[864,128]{1,0:T(8,128)(2,1)S(1)}, bf16[864,128]{1,0:T(8,128)(2,1)S(1)}, u32[]{:S(2)}, u32[]{:S(2)}) %collective-permute-start.12) | collective-permute-done | bytes 221216 | tf_op jit(solution)/shard_map/ppermute | solution.py:374
  53.5 2.2 %collective-permute-start.14 = (bf16[864,128]{1,0:T(8,128)(2,1)S(1)}, bf16[864,128]{1,0:T(8,128)(2,1)S(1)}, u32[]{:S(2)}, u32[]{:S(2)}) collective-permute-start(bf16[864,128]{1,0:T(8,128)(2,1)S(1)} %after.1.far_ref), channel_id=1, source_target_pairs={{0,1},{1,0},{2,3},{3,2},{4,5},{5,4},{6,7},{7,6},{8,9},{9,8},{10,11... | collective-permute-start | bytes 663560 | tf_op jit(solution)/shard_map/ppermute | solution.py:374
  55.7 1.1 %collective-permute-done.14.got_far_ref = bf16[864,128]{1,0:T(8,128)(2,1)S(1)} collective-permute-done((bf16[864,128]{1,0:T(8,128)(2,1)S(1)}, bf16[864,128]{1,0:T(8,128)(2,1)S(1)}, u32[]{:S(2)}, u32[]{:S(2)}) %collective-permute-start.14) | collective-permute-done | bytes 221216 | tf_op jit(solution)/shard_map/ppermute | solution.py:374
  56.8 1.6 %normalise.1 = f32[27,128,128]{2,1,0:T(8,128)} custom-call(bf16[864,128]{1,0:T(8,128)(2,1)S(1)} %get-tuple-element.50.near_ref, bf16[864,128]{1,0:T(8,128)(2,1)S(1)} %after.1.far_ref, bf16[864,128]{1,0:T(8,128)(2,1)S(1)} %collective-permute-done.13.got_near_ref, bf16[864,128]{1,0:T(8,128)(2,1)S(1)} %collective-permute-done.14.got_far_ref), custom_call_target="tpu_custom_call" | custom-call | tf_op jit(solution)/shard_map/normalise/pallas_call | solution.py:31
  (12 shorter events, 0.2 us)
Async XLA Ops:
  1.8 7.9 %collective-permute-start = (bf16[64,128]{1,0:T(8,128)(2,1)S(1)}, bf16[64,128]{1,0:T(8,128)(2,1)S(1)}, u32[]{:S(2)}, u32[]{:S(2)}) collective-permute-start(bf16[64,128]{1,0:T(8,128)(2,1)S(1)} %get-tuple-element.33), channel_id=1, source_target_pairs={{4,8},{8,4},{12,16},{16,12},{20,24},{24,20},{5,9},{9,5},{13,17},{1... | collective-permute-start | bytes 49160 | tf_op jit(solution)/shard_map/ppermute | solution.py:465
  2.4 7.5 %collective-permute-start.1 = (bf16[64,128]{1,0:T(8,128)(2,1)S(1)}, bf16[64,128]{1,0:T(8,128)(2,1)S(1)}, u32[]{:S(2)}, u32[]{:S(2)}) collective-permute-start(bf16[64,128]{1,0:T(8,128)(2,1)S(1)} %get-tuple-element.34), channel_id=1, source_target_pairs={{0,4},{4,0},{8,12},{12,8},{16,20},{20,16},{24,28},{28,24},{1,5},{5... | collective-permute-start | bytes 49160 | tf_op jit(solution)/shard_map/ppermute | solution.py:466
  10.0 3.6 %collective-permute-start.2 = (bf16[80,128]{1,0:T(8,128)(2,1)S(1)}, bf16[80,128]{1,0:T(8,128)(2,1)S(1)}, u32[]{:S(2)}, u32[]{:S(2)}) collective-permute-start(bf16[80,128]{1,0:T(8,128)(2,1)S(1)} %get-tuple-element.36), channel_id=1, source_target_pairs={{1,2},{2,1},{5,6},{6,5},{9,10},{10,9},{13,14},{14,13},{17,18},{18,... | collective-permute-start | bytes 61448 | tf_op jit(solution)/shard_map/ppermute | solution.py:350
  10.6 3.8 %collective-permute-start.3 = (bf16[80,128]{1,0:T(8,128)(2,1)S(1)}, bf16[80,128]{1,0:T(8,128)(2,1)S(1)}, u32[]{:S(2)}, u32[]{:S(2)}) collective-permute-start(bf16[80,128]{1,0:T(8,128)(2,1)S(1)} %get-tuple-element.37), channel_id=1, source_target_pairs={{0,1},{1,0},{2,3},{3,2},{4,5},{5,4},{6,7},{7,6},{8,9},{9,8},{10,11... | collective-permute-start | bytes 61448 | tf_op jit(solution)/shard_map/ppermute | solution.py:351
  17.5 2.1 %collective-permute-start.4 = (bf16[1792,128]{1,0:T(8,128)(2,1)S(1)}, bf16[1792,128]{1,0:T(8,128)(2,1)S(1)}, u32[]{:S(2)}, u32[]{:S(2)}) collective-permute-start(bf16[1792,128]{1,0:T(8,128)(2,1)S(1)} %get-tuple-element.39), channel_id=1, source_target_pairs={{0,1},{1,0},{2,3},{3,2},{4,5},{5,4},{6,7},{7,6},{8,9},{9,8},{10,11... | collective-permute-start | bytes 1376264 | tf_op jit(solution)/shard_map/ppermute | solution.py:374
  19.6 5.8 %collective-permute-start.5 = (bf16[992,128]{1,0:T(8,128)(2,1)S(1)}, bf16[992,128]{1,0:T(8,128)(2,1)S(1)}, u32[]{:S(2)}, u32[]{:S(2)}) collective-permute-start(bf16[992,128]{1,0:T(8,128)(2,1)S(1)} %message.6), channel_id=1, source_target_pairs={{0,3},{1,4},{2,7},{3,0},{4,1},{5,6},{6,5},{7,2},{8,13},{9,10},{10,... | collective-permute-start | bytes 761864 | tf_op jit(solution)/shard_map/ppermute | solution.py:374
  25.4 4.9 %collective-permute-start.6 = (bf16[560,128]{1,0:T(8,128)(2,1)S(1)}, bf16[560,128]{1,0:T(8,128)(2,1)S(1)}, u32[]{:S(2)}, u32[]{:S(2)}) collective-permute-start(bf16[560,128]{1,0:T(8,128)(2,1)S(1)} %message.7), channel_id=1, source_target_pairs={{0,5},{1,2},{2,1},{3,6},{4,7},{5,0},{6,3},{7,4},{8,11},{9,12},{10,... | collective-permute-start | bytes 430088 | tf_op jit(solution)/shard_map/ppermute | solution.py:374
  30.3 5.5 %collective-permute-start.7 = (bf16[496,128]{1,0:T(8,128)(2,1)S(1)}, bf16[496,128]{1,0:T(8,128)(2,1)S(1)}, u32[]{:S(2)}, u32[]{:S(2)}) collective-permute-start(bf16[496,128]{1,0:T(8,128)(2,1)S(1)} %message.8.refs_0_), channel_id=1, source_target_pairs={{0,9},{1,8},{2,11},{3,10},{4,13},{5,12},{6,15},{7,14},{8,1},{9,0},... | collective-permute-start | bytes 380936 | tf_op jit(solution)/shard_map/ppermute | solution.py:374
  35.8 7.3 %collective-permute-start.8 = (bf16[496,128]{1,0:T(8,128)(2,1)S(1)}, bf16[496,128]{1,0:T(8,128)(2,1)S(1)}, u32[]{:S(2)}, u32[]{:S(2)}) collective-permute-start(bf16[496,128]{1,0:T(8,128)(2,1)S(1)} %message.9.refs_0_), channel_id=1, source_target_pairs={{0,25},{1,24},{2,27},{3,26},{4,29},{5,28},{6,31},{7,30},{8,17},{9,... | collective-permute-start | bytes 380936 | tf_op jit(solution)/shard_map/ppermute | solution.py:374
  43.2 4.8 %collective-permute-start.9 = (bf16[432,128]{1,0:T(8,128)(2,1)S(1)}, bf16[432,128]{1,0:T(8,128)(2,1)S(1)}, u32[]{:S(2)}, u32[]{:S(2)}) collective-permute-start(bf16[432,128]{1,0:T(8,128)(2,1)S(1)} %get-tuple-element.42.refs_0_), channel_id=1, source_target_pairs={{0,5},{1,2},{2,1},{3,6},{4,7},{5,0},{6,3},{7,4},{8,11},{9,12},{10,... | collective-permute-start | bytes 331784 | tf_op jit(solution)/shard_map/ppermute | solution.py:374
  44.7 2.5 %collective-permute-start.10 = (bf16[80,128]{1,0:T(8,128)(2,1)S(1)}, bf16[80,128]{1,0:T(8,128)(2,1)S(1)}, u32[]{:S(2)}, u32[]{:S(2)}) collective-permute-start(bf16[80,128]{1,0:T(8,128)(2,1)S(1)} %get-tuple-element.44), channel_id=1, source_target_pairs={{1,2},{2,1},{5,6},{6,5},{9,10},{10,9},{13,14},{14,13},{17,18},{18,... | collective-permute-start | bytes 61448 | tf_op jit(solution)/shard_map/ppermute | solution.py:350
  45.3 2.7 %collective-permute-start.11 = (bf16[80,128]{1,0:T(8,128)(2,1)S(1)}, bf16[80,128]{1,0:T(8,128)(2,1)S(1)}, u32[]{:S(2)}, u32[]{:S(2)}) collective-permute-start(bf16[80,128]{1,0:T(8,128)(2,1)S(1)} %get-tuple-element.45), channel_id=1, source_target_pairs={{0,1},{1,0},{2,3},{3,2},{4,5},{5,4},{6,7},{7,6},{8,9},{9,8},{10,11... | collective-permute-start | bytes 61448 | tf_op jit(solution)/shard_map/ppermute | solution.py:351
  48.1 5.4 %collective-permute-start.12 = (bf16[864,128]{1,0:T(8,128)(2,1)S(1)}, bf16[864,128]{1,0:T(8,128)(2,1)S(1)}, u32[]{:S(2)}, u32[]{:S(2)}) collective-permute-start(bf16[864,128]{1,0:T(8,128)(2,1)S(1)} %get-tuple-element.50.near_ref), channel_id=1, source_target_pairs={{0,3},{1,4},{2,7},{3,0},{4,1},{5,6},{6,5},{7,2},{8,13},{9,10},{10,... | collective-permute-start | bytes 663560 | tf_op jit(solution)/shard_map/ppermute | solution.py:374
  49.8 5.9 %collective-permute-start.13 = (bf16[864,128]{1,0:T(8,128)(2,1)S(1)}, bf16[864,128]{1,0:T(8,128)(2,1)S(1)}, u32[]{:S(2)}, u32[]{:S(2)}) collective-permute-start(bf16[864,128]{1,0:T(8,128)(2,1)S(1)} %get-tuple-element.50.near_ref), channel_id=1, source_target_pairs={{0,1},{1,0},{2,3},{3,2},{4,5},{5,4},{6,7},{7,6},{8,9},{9,8},{10,11... | collective-permute-start | bytes 663560 | tf_op jit(solution)/shard_map/ppermute | solution.py:374
  53.5 3.3 %collective-permute-start.14 = (bf16[864,128]{1,0:T(8,128)(2,1)S(1)}, bf16[864,128]{1,0:T(8,128)(2,1)S(1)}, u32[]{:S(2)}, u32[]{:S(2)}) collective-permute-start(bf16[864,128]{1,0:T(8,128)(2,1)S(1)} %after.1.far_ref), channel_id=1, source_target_pairs={{0,1},{1,0},{2,3},{3,2},{4,5},{5,4},{6,7},{7,6},{8,9},{9,8},{10,11... | collective-permute-start | bytes 663560 | tf_op jit(solution)/shard_map/ppermute | solution.py:374

commit v3 on v2

--- a/solution.py
+++ b/solution.py
@@ -92,26 +92,43 @@
 
 
 def first_faces_kernel(
-    feat_hbm, occ_hbm, pair_ref, next_ref, edge_ref, feat_ref, occ_ref, semaphores
+    feat_hbm, occ_hbm, b_ref, a_ref, ends_ref, masked_ref, mask_ref, feat_ref, occ_ref, semaphores
 ):
     for copy in fetch((feat_hbm, occ_hbm), (feat_ref, occ_ref), semaphores):
         copy.wait()
     columns = occupancy_columns(occ_ref, 8)
-    channels = feat_ref.shape[2]
-
-    def masked(slot, first, rows):
-        mask = jnp.broadcast_to(columns[first : first + rows, slot : slot + 1], (rows, channels))
-        return feat_ref[slot, first : first + rows, :].astype(F32) * mask
-
-    def plane(x):
-        i, a = x // BX, x % BX
-        return jnp.concatenate(
-            [masked(i * GY + j, a * BY * SIDE, BY * SIDE) for j in range(GY)], axis=0
-        )
-
-    every = [plane(x) for x in range(SIDE)]
-    low_y, high_y = y_faces(lambda x: every[x])
-    store_faces(every[0], every[SIDE - 1], low_y, high_y, pair_ref, next_ref, edge_ref)
+    rows, channels = BY * SIDE, mask_ref.shape[2]
+    for slot in range(GX * GY):
+        x0, row0 = slot_planes(slot)
+        wide = jnp.broadcast_to(columns[:, slot : slot + 1], (columns.shape[0], channels))
+        for a in range(BX):
+            mask = wide[a * rows : (a + 1) * rows]
+            part = feat_ref[slot, a * rows : (a + 1) * rows, :].astype(F32)
+            mask_ref[x0 + a, row0 : row0 + rows, :] = mask
+            masked_ref[x0 + a, row0 : row0 + rows, :] = part * mask
+    low_y, high_y = y_faces(lambda x: masked_ref[x])
+    even = parity("ty")
+    a_ref[...] = jnp.where(even, high_y, low_y).astype(BF16)
+    b_ref[...] = jnp.where(even, low_y, high_y).astype(BF16)
+    ends_ref[0] = masked_ref[0].astype(BF16)
+    ends_ref[1] = masked_ref[SIDE - 1].astype(BF16)
+
+
+def halo_along_y(b_ref, a_ref):
+    even = parity("ty")
+    a, b = a_ref[...].astype(F32), b_ref[...].astype(F32)
+    return jnp.where(even, b, a), jnp.where(even, a, b)
+
+
+def x_faces_kernel(ends_ref, y_b_ref, y_a_ref, *refs):
+    pair_ref, next_ref = refs[-2:]
+    low, high = halo_along_y(y_b_ref, y_a_ref)
+    last = PLANE - SIDE
+    first = jnp.concatenate([low[:SIDE], ends_ref[0].astype(F32), high[:SIDE]], axis=0)
+    final = jnp.concatenate([low[last:], ends_ref[1].astype(F32), high[last:]], axis=0)
+    even = parity("tx")
+    pair_ref[...] = jnp.where(even, final, first).astype(BF16)
+    next_ref[...] = jnp.where(even, first, final).astype(BF16)
 
 
 def store_edges(low, high, edge_ref, a_ref, b_ref, planes_ref):
@@ -125,13 +142,6 @@
     b_ref[...] = jnp.where(even_y, bottom, top).astype(BF16)
 
 
-def edge_kernel(edge_ref, next_ref, pair_ref, *refs):
-    even = parity("tx")
-    pair, other = pair_ref[...].astype(F32), next_ref[...].astype(F32)
-    low, high = jnp.where(even, other, pair), jnp.where(even, pair, other)
-    store_edges(low, high, edge_ref, *refs[-3:])
-
-
 def hand_on_edge_kernel(flips, first_row, edge_ref, got1_ref, got2_ref, *refs):
     lines, (a_ref, b_ref, planes_ref) = refs[: len(flips)], refs[-3:]
     even = parity("tx")
@@ -139,7 +149,9 @@
     place = lax.axis_index("tx") // 2
     behind = jnp.where(even, place - 1, place + 1)
     other = jnp.zeros(pair.shape, F32)
-    for flip, line_ref in zip(flips, lines):
+    lane = lane_of(lax.axis_index("tx"), lax.axis_index("ty"))
+    for both, line_ref in zip(flips, lines):
+        flip = jnp.where(lane == 0, *both)
         face = line_ref[first_row[2] : first_row[2] + PLANE].astype(F32)
         other = jnp.where((place ^ behind) == flip, face, other)
     low, high = jnp.where(even, other, pair), jnp.where(even, pair, other)
@@ -151,31 +163,17 @@
     return jnp.where(lane == 0, by_second_way.astype(F32), by_first_way.astype(F32))
 
 
-def write_halo(grid_ref, planes_ref, y_a_ref, y_b_ref):
-    even_y = parity("ty")
-    grid_ref[0, SIDE : SIDE + PLANE, :] = planes_ref[0].astype(F32)
-    grid_ref[SIDE + 1, SIDE : SIDE + PLANE, :] = planes_ref[1].astype(F32)
-    y_a, y_b = y_a_ref[...].astype(F32), y_b_ref[...].astype(F32)
-    low, high = jnp.where(even_y, y_b, y_a), jnp.where(even_y, y_a, y_b)
-    for x in range(SIDE + 2):
-        grid_ref[x, :SIDE, :] = low[x * SIDE : (x + 1) * SIDE]
-        grid_ref[x, SIDE + PLANE :, :] = high[x * SIDE : (x + 1) * SIDE]
-
-
-def write_columns(grid_ref, cols_ref):
-    channels = grid_ref.shape[2]
-    z = lax.broadcasted_iota(jnp.int32, ((SIDE + 2) * SIDE, channels), 0) % SIDE
-    for x in range(SIDE + 2):
-        plane = grid_ref[x]
-        zeros = jnp.zeros((1, channels), F32)
-        before = jnp.where(z == 0, 0.0, jnp.concatenate([zeros, plane[:-1]], axis=0))
-        after = jnp.where(z == SIDE - 1, 0.0, jnp.concatenate([plane[1:], zeros], axis=0))
-        for dz, moved in enumerate((before, plane, after)):
-            for dy in range(3):
-                tap = 3 * dy + dz
-                cols_ref[x, :, tap * channels : (tap + 1) * channels] = moved[
-                    dy * SIDE : dy * SIDE + PLANE
-                ].astype(BF16)
+def write_columns(plane, cols_ref):
+    channels = plane.shape[1]
+    z = lax.broadcasted_iota(jnp.int32, plane.shape, 0) % SIDE
+    zeros = jnp.zeros((1, channels), F32)
+    before = jnp.where(z == 0, 0.0, jnp.concatenate([zeros, plane[:-1]], axis=0))
+    after = jnp.where(z == SIDE - 1, 0.0, jnp.concatenate([plane[1:], zeros], axis=0))
+    for dz, moved in enumerate((before, plane, after)):
+        for dy in range(3):
+            tap = 3 * dy + dz
+            window = moved[dy * SIDE : dy * SIDE + PLANE]
+            cols_ref[:, tap * channels : (tap + 1) * channels] = window.astype(BF16)
 
 
 def split3(value):
@@ -190,35 +188,7 @@
     return lax.dot_general(a, b, (((dim_a,), (dim_b,)), ((), ())), preferred_element_type=F32)
 
 
-def write_mask(occ_ref, mask_ref):
-    columns = occupancy_columns(occ_ref, 8)
-    rows, channels = BY * SIDE, mask_ref.shape[2]
-    for slot in range(GX * GY):
-        x0, row0 = slot_planes(slot)
-        wide = jnp.broadcast_to(columns[:, slot : slot + 1], (columns.shape[0], channels))
-        for a in range(BX):
-            mask_ref[x0 + a, row0 : row0 + rows, :] = wide[a * rows : (a + 1) * rows]
-
-
-def prepare_kernel(
-    feat_hbm, occ_hbm, point_hbm, teach_hbm, head_hbm, weight_hbm, order_ref,
-    masked_ref, mask_ref, sums_ref, head_ref, weight_ref,
-    feat_ref, occ_ref, point_ref, teach_ref, semaphores,
-):
-    del order_ref
-    sources = (feat_hbm, occ_hbm, point_hbm, teach_hbm, head_hbm, weight_hbm)
-    rooms = (feat_ref, occ_ref, point_ref, teach_ref, head_ref, weight_ref)
-    copies = fetch(sources, rooms, semaphores)
-    for copy in copies[:4]:
-        copy.wait()
-    rows = BY * SIDE
-    write_mask(occ_ref, mask_ref)
-    for slot in range(GX * GY):
-        x0, row0 = slot_planes(slot)
-        for a in range(BX):
-            part = feat_ref[slot, a * rows : (a + 1) * rows, :].astype(F32)
-            part = part * mask_ref[x0 + a, row0 : row0 + rows, :]
-            masked_ref[x0 + a, row0 : row0 + rows, :] = part
+def voxel_sums(point_ref, teach_ref):
     target = jnp.exp(teach_ref[...].astype(F32))
     target = target / jnp.sum(target, axis=0, keepdims=True)
     classes, points = target.shape
@@ -229,28 +199,57 @@
     stack = jnp.concatenate([*split3(target), jnp.ones((classes, points), BF16)], axis=0)
     sums = contract(stack, chosen, 1, 1)
     target_sum = sums[:classes] + sums[classes : 2 * classes] + sums[2 * classes : 3 * classes]
-    sums_ref[...] = jnp.concatenate([target_sum, sums[3 * classes :]], axis=0)
-    for copy in copies[4:]:
+    return jnp.concatenate([target_sum, sums[3 * classes :]], axis=0)
+
+
+def main_kernel(
+    point_hbm, teach_hbm, head_hbm, weight_hbm, masked_ref, y_b_ref, y_a_ref,
+    cols_ref, pre_ref, sums_ref, head_ref, weight_ref,
+    point_ref, teach_ref, semaphores,
+):
+    sources = (point_hbm, teach_hbm, head_hbm, weight_hbm)
+    copies = fetch(sources, (point_ref, teach_ref, head_ref, weight_ref), semaphores)
+    channels = masked_ref.shape[2]
+    low, high = halo_along_y(y_b_ref, y_a_ref)
+    for x in range(SIDE):
+        rows = slice(x * SIDE, (x + 1) * SIDE)
+        plane = jnp.concatenate([low[rows], masked_ref[x], high[rows]], axis=0)
+        write_columns(plane, cols_ref.at[x])
+    wide, inner = TAPS * channels, SIDE - 1
+    for copy in copies[:2]:
         copy.wait()
+    sums_ref[...] = voxel_sums(point_ref, teach_ref)
+    for copy in copies[2:]:
+        copy.wait()
+
+    def product(planes, dx):
+        window = cols_ref[planes].reshape(-1, wide)
+        matrix = weight_ref[TAPS * dx : TAPS * (dx + 1)].reshape(wide, channels)
+        return jnp.dot(window, matrix, preferred_element_type=F32)
+
+    edge = jnp.zeros((PLANE, channels), F32)
+    pre = product(slice(0, SIDE), 1)
+    pre = pre + jnp.concatenate([edge, product(slice(0, inner), 0)], axis=0)
+    pre_ref[...] = pre + jnp.concatenate([product(slice(1, SIDE), 2), edge], axis=0)
 
 
 def tile_kernel(
-    masked_ref, mask_ref, sums_ref, head_ref, weight_ref, planes_ref, y_b_ref, y_a_ref,
+    cols_ref, pre_ref, mask_ref, sums_ref, head_ref, weight_ref, x_next_ref, x_pair_ref,
     grad_ref, next_ref, edge_ref, keep_ref, send_ref,
-    grid_ref, cols_ref, terms_ref,
+    ends_ref, terms_ref,
 ):
-    channels = masked_ref.shape[2]
+    channels = cols_ref.shape[2] // TAPS
     classes = head_ref.shape[0]
-    voxels = SIDE * PLANE
-    write_grid(grid_ref, lambda x: masked_ref[x])
-    write_halo(grid_ref, planes_ref, y_a_ref, y_b_ref)
-    write_columns(grid_ref, cols_ref)
-
-    pre = jnp.zeros((voxels, channels), F32)
-    for dx in range(3):
-        window = cols_ref[dx : dx + SIDE].reshape(voxels, TAPS * channels)
-        matrix = weight_ref[TAPS * dx : TAPS * (dx + 1)].reshape(TAPS * channels, channels)
-        pre = pre + jnp.dot(window, matrix, preferred_element_type=F32)
+    voxels, wide, inner = SIDE * PLANE, TAPS * channels, (SIDE - 1) * PLANE
+    even = parity("tx")
+    pair, other = x_pair_ref[...].astype(F32), x_next_ref[...].astype(F32)
+    write_columns(jnp.where(even, other, pair), ends_ref.at[0])
+    write_columns(jnp.where(even, pair, other), ends_ref.at[1])
+    first = weight_ref[:TAPS].reshape(wide, channels)
+    final = weight_ref[2 * TAPS :].reshape(wide, channels)
+    low = pre_ref[:PLANE] + jnp.dot(ends_ref[0], first, preferred_element_type=F32)
+    high = pre_ref[inner:] + jnp.dot(ends_ref[1], final, preferred_element_type=F32)
+    pre = jnp.concatenate([low, pre_ref[PLANE:inner], high], axis=0)
     mask = mask_ref[...].reshape(voxels, channels)
     logistic = 1.0 / (1.0 + jnp.exp(-pre))
     slope = logistic * (1.0 + pre * (1.0 - logistic)) * mask
@@ -272,10 +271,16 @@
     pair_ref = send_ref.at[send_ref.shape[0] - PLANE :]
     store_faces(*ends, low_y, high_y, pair_ref, next_ref, edge_ref)
 
-    for dx in range(3):
-        window = cols_ref[dx : dx + SIDE].reshape(voxels, TAPS * channels)
-        product = contract(window, rounded, 0, 0)
-        terms_ref[TAPS * dx : TAPS * (dx + 1)] = product.reshape(TAPS, channels, channels)
+    def term(planes, gradient):
+        return contract(planes.reshape(-1, wide), gradient, 0, 0).reshape(TAPS, channels, channels)
+
+    terms_ref[:TAPS] = term(cols_ref[: SIDE - 1], rounded[PLANE:]) + term(
+        ends_ref[0], rounded[:PLANE]
+    )
+    terms_ref[TAPS : 2 * TAPS] = term(cols_ref[...], rounded)
+    terms_ref[2 * TAPS :] = term(cols_ref[1:], rounded[:inner]) + term(
+        ends_ref[1], rounded[inner:]
+    )
     length = channels // PARTS
     for r in range(PARTS):
         first = pl.multiple_of(part_index(r) * length, length)
@@ -299,31 +304,54 @@
     return lane * 4 + ((first * 2 + second) ^ (r & 3))
 
 
-def back_kernel(
-    mask_ref, weight_ref, grad_ref, planes_ref, y_b_ref, y_a_ref, out_ref, token_ref,
-    grid_ref, cols_ref,
-):
+def moved_weights(weight_ref, taps):
+    return jnp.concatenate([weight_ref[3 * TAPS - 1 - tap] for tap in taps], axis=1)
+
+
+def back_kernel(grad_ref, planes_ref, weight_ref, part_ref, cols_ref):
     channels = grad_ref.shape[2]
-    voxels = SIDE * PLANE
-    write_grid(grid_ref, lambda x: grad_ref[x].astype(F32))
-    write_halo(grid_ref, planes_ref, y_a_ref, y_b_ref)
-    write_columns(grid_ref, cols_ref)
+    edge = jnp.zeros((SIDE, channels), F32)
+    for x in range(SIDE + 2):
+        plane = planes_ref[0 if x == 0 else 1] if x in (0, SIDE + 1) else grad_ref[x - 1]
+        write_columns(jnp.concatenate([edge, plane.astype(F32), edge], axis=0), cols_ref.at[x])
+    total = jnp.zeros(part_ref.shape, F32)
+    for dx in range(3):
+        window = cols_ref[dx : dx + SIDE].reshape(-1, TAPS * channels)
+        taps = range(TAPS * dx, TAPS * (dx + 1))
+        total = total + contract(window, moved_weights(weight_ref, taps), 1, 1)
+    part_ref[...] = total
+
+
+def y_faces_kernel(extra_ref, part_ref, mask_ref, weight_ref, near_ref, far_ref, line_ref, out_ref, token_ref, cols_ref):
+    channels, rows = part_ref.shape[1], (SIDE + 2) * SIDE
+    tx, ty = lax.axis_index("tx"), lax.axis_index("ty")
     token_ref[...] = jnp.zeros(token_ref.shape, F32)
-    total = jnp.zeros((voxels, channels), F32)
-    for dx in range(3):
-        window = cols_ref[dx : dx + SIDE].reshape(voxels, TAPS * channels)
-        taps = [weight_ref[3 * TAPS - 1 - (TAPS * dx + tap)] for tap in range(TAPS)]
-        total = total + contract(window, jnp.concatenate(taps, axis=1), 1, 1)
-    total = (total * mask_ref[...].reshape(voxels, channels)).reshape(SIDE, PLANE, channels)
+    by_first, by_second = far_ref[far_ref.shape[0] - rows :], line_ref[line_ref.shape[0] - rows :]
+    other = jnp.where(lane_of(tx, ty) == 0, by_first.astype(F32), by_second.astype(F32))
+    beyond = jnp.zeros(other.shape, F32) if extra_ref is None else extra_ref[...].astype(F32)
+    other = jnp.where(((ty + 1) & 2) == 2, other, beyond)
+    pair = near_ref[near_ref.shape[0] - rows :].astype(F32)
+    even = parity("ty")
+    added = []
+    for dy, face in ((0, jnp.where(even, other, pair)), (2, jnp.where(even, pair, other))):
+        write_columns(face, cols_ref)
+        taps = [TAPS * dx + 3 * dy + dz for dx in range(3) for dz in range(3)]
+        added.append(contract(cols_ref[...], moved_weights(weight_ref, taps), 1, 1))
+    low, high = added
     rows = BY * SIDE
-    for slot in range(GX * GY):
-        x0, row0 = slot_planes(slot)
-        for a in range(BX):
-            part = total[x0 + a, row0 : row0 + rows].astype(BF16)
-            out_ref[slot, a * rows : (a + 1) * rows, :] = part
-
-
-def norm_kernel(near_ref, far_ref, got_near_ref, got_far_ref, out_ref):
+    for x in range(SIDE):
+        here = slice(x * SIDE, (x + 1) * SIDE)
+        total = part_ref[x * PLANE : (x + 1) * PLANE]
+        first, final = total[:SIDE] + low[here], total[PLANE - SIDE :] + high[here]
+        total = jnp.concatenate([first, total[SIDE : PLANE - SIDE], final], axis=0)
+        total = (total * mask_ref[x]).astype(BF16)
+        for j in range(GY):
+            slot, a = x // BX * GY + j, x % BX
+            out_ref[slot, a * rows : (a + 1) * rows, :] = total[j * rows : (j + 1) * rows]
+
+
+def norm_kernel(near_ref, far_ref, got_near_ref, got_far_ref, token_ref, out_ref):
+    del token_ref
     kernels, channels = out_ref.shape[0], out_ref.shape[2]
     length = channels // PARTS
     refs = (near_ref, far_ref, got_near_ref, got_far_ref)
@@ -345,10 +373,10 @@
     return [pair for i in range(first, count - 1, 2) for pair in ((i, i + 1), (i + 1, i))]
 
 
-def swap_along_y(a, b):
+def swap_along_y(b, a):
     count = lax.axis_size("ty")
     got_b = lax.ppermute(b, "ty", swap_pairs(1, count))
-    return lax.ppermute(a, "ty", swap_pairs(0, count)), got_b
+    return got_b, lax.ppermute(a, "ty", swap_pairs(0, count))
 
 
 def edge_faces(kernel, edges, faces, waits=()):
@@ -392,8 +420,8 @@
     return same_lane(tx, ty, *other)
 
 
-def along_line(flip):
-    return lambda tx, ty: same_lane(tx, ty, tx ^ (2 * flip), ty)
+def along_line(flips):
+    return lambda tx, ty: same_lane(tx, ty, tx ^ (2 * flips[lane_of(tx, ty)]), ty)
 
 
 def add(*terms):
@@ -458,33 +486,33 @@
 
     fetched = (features, occupancy)
     face = shape((PLANE, channels), BF16)
-    pair_face, next_face, x_edges = call(
-        first_faces_kernel, (face, face, edges), fetched, buffers(*fetched),
+    planes = shape((SIDE, PLANE, channels), F32)
+    y_b, y_a, x_ends, masked, mask = call(
+        first_faces_kernel, (face, face, edges, planes, planes), fetched, buffers(*fetched),
         name="first_faces", fetched=2,
     )
-    x_next = lax.ppermute(next_face, "tx", swap_pairs(1, n_tx))
-    x_pair = lax.ppermute(pair_face, "tx", swap_pairs(0, n_tx))
-    fetched = (
-        features, occupancy, point_voxel.reshape(1, -1), teacher, head_weight, conv_weight
-    )
-    classes = head_weight.shape[0]
-    planes = shape((SIDE, PLANE, channels), F32)
-    prepared = call(
-        prepare_kernel,
+    y_b, y_a = swap_along_y(y_b, y_a)
+    wide_face = shape(((SIDE + 2) * SIDE, channels), BF16)
+    x_pair, x_next = call(
+        x_faces_kernel, (wide_face, wide_face), (x_ends, y_b, y_a), name="x_faces"
+    )
+    x_next = lax.ppermute(x_next, "tx", swap_pairs(1, n_tx))
+    x_pair = lax.ppermute(x_pair, "tx", swap_pairs(0, n_tx))
+    fetched = (point_voxel.reshape(1, -1), teacher, head_weight, conv_weight)
+    tile_cols, pre, sums, head, weight = call(
+        main_kernel,
         (
-            planes,
-            planes,
-            shape((2 * classes, SIDE * PLANE), F32),
+            shape((SIDE, PLANE, TAPS * channels), BF16),
+            shape((SIDE * PLANE, channels), F32),
+            shape((2 * head_weight.shape[0], SIDE * PLANE), F32),
             shape(head_weight.shape, BF16),
             shape(conv_weight.shape, BF16),
         ),
-        (*fetched, x_edges),
-        (*buffers(*fetched[:4])[:-1], pltpu.SemaphoreType.DMA((len(fetched),))),
-        name="prepare",
+        (*fetched, masked, y_b, y_a),
+        (*buffers(*fetched[:2])[:-1], pltpu.SemaphoreType.DMA((len(fetched),))),
+        name="main",
         fetched=len(fetched),
     )
-    y_a, y_b, planes = edge_faces(edge_kernel, x_edges, (x_next, x_pair), prepared[:1])
-    y_a, y_b = swap_along_y(y_a, y_b)
     part = kernels * channels // PARTS
     gradient, g_next, g_edges, keep, send = call(
         tile_kernel,
@@ -495,11 +523,13 @@
             shape((PARTS // 2 * part, channels), F32),
             shape((PARTS // 2 * part + PLANE, channels), BF16),
         ),
-        (*prepared, planes, y_b, y_a),
-        (grid, cols, pltpu.VMEM((kernels, channels, channels), F32)),
+        (tile_cols, pre, mask, sums, head, weight, x_next, x_pair),
+        (
+            pltpu.VMEM((2, PLANE, TAPS * channels), BF16),
+            pltpu.VMEM((kernels, channels, channels), F32),
+        ),
         name="tile",
     )
-    mask, weight = prepared[1], prepared[4]
 
     got0 = exchange_with(send, by_core)
     faces = [(PLANE, add, (got0, 4 * part)), (PLANE, add, (g_next, 0))]
@@ -513,8 +543,10 @@
     flips, lines = [], []
     while 2 ** len(flips) < n_tx // 2:
         flips.append(2 ** (len(flips) + 1) - 1)
+    flips = list(zip(flips, flips[::-1]))
+    for both in flips:
         own = message(total + [hand_on])
-        lines.append(exchange_with(own, along_line(flips[-1])))
+        lines.append(exchange_with(own, along_line(both)))
         total = [(part, add, (own, 0), (lines[-1], 0))]
         hand_on = (PLANE, add, (own, part))
     bit = 4
@@ -524,27 +556,42 @@
         got = exchange_with(own, lambda tx, ty, flip=flip: same_lane(tx, ty, tx, ty ^ flip))
         total = [(part, add, (own, 0), (got, 0))]
         bit *= 2
-    total, g_edges = message(total, (), (g_edges,))
-    got3 = exchange_with(total, second_way)
     kernel = functools.partial(hand_on_edge_kernel, flips, at)
     g_a, g_b, planes = edge_faces(kernel, g_edges, (got1, got2, *lines))
-    g_a, g_b = swap_along_y(g_a, g_b)
-    near, gradient = message(
-        [(part, add, (total, 0)), (part, add, (got3, 0))], (g_b, g_a), (gradient,)
-    )
+    rows = g_a.shape[0]
+    total = message(total + [(rows, add, (g_b, 0))])
+    got3 = exchange_with(total, second_way)
+    near = [(part, add, (total, 0)), (part, add, (got3, 0)), (rows, add, (g_b, 0))]
+    near, gradient = message(near, (), (gradient,))
     far = exchange_with(near, first_way)
+    back_part = call(
+        back_kernel,
+        shape((SIDE * PLANE, channels), F32),
+        (gradient, planes, weight),
+        (cols,),
+        name="back",
+    )
+    got_near = exchange_with(
+        message([(2 * part, add, (near, 0)), (rows, add, (g_a, 0))], (back_part,)), by_core
+    )
+    got_far = exchange_with(far, by_core)
+    faces = (back_part, mask, weight, got_near, far, got3)
+    kernel = functools.partial(y_faces_kernel, None)
+    if n_ty > 4:
+        pairs = [pair for i in range(3, n_ty - 1, 4) for pair in ((i, i + 1), (i + 1, i))]
+        faces = (lax.ppermute(g_b, "ty", pairs), *faces)
+        kernel = y_faces_kernel
     grad_features, token = call(
-        back_kernel,
+        kernel,
         (shape((slots, brick, channels), BF16), shape((8, channels), F32)),
-        (mask, weight, gradient, planes, g_b, g_a),
-        (grid, cols),
-        name="back",
-    )
-    far = after(far, token)
+        faces,
+        (pltpu.VMEM((PLANE, TAPS * channels), BF16),),
+        name="y_faces",
+    )
     grad_weight = call(
         norm_kernel,
         shape((kernels, channels, channels), F32),
-        (near, far, exchange_with(near, by_core), exchange_with(far, by_core)),
+        (near, far, got_near, got_far, token),
         name="normalise",
     )
     return (grad_features, grad_weight)

time: 59.1 us -> 55.6 us (0.941)
  starting transfers between devices: 28.3 us -> 24.8 us
    ppermute x4 -> x3, starting transfers between devices: 11.2 us -> 9.41 us  [the longest x1 4.39 us: swap_along_y(): return (got_b, lax.ppermute(a, 'ty', swap_pairs(0, count)))]
    ppermute x9, waiting for transfers between devices: 18.1 us -> 19.4 us  [exchange_with(): return lax.ppermute(value, ('tx', 'ty'), pairs)]
    ppermute x4 -> x3, waiting for transfers between devices: 1.96 us -> 0.84 us  [the longest x1 0.84 us: swap_along_y(): return (got_b, lax.ppermute(a, 'ty', swap_pairs(0, count)))]
    ppermute x9, starting transfers between devices: 15.8 us -> 14.7 us  [exchange_with(): return lax.ppermute(value, ('tx', 'ty'), pairs)]
    ppermute x2 -> x1, starting transfers between devices: 1.33 us -> 0.66 us  [swap_along_y(): got_b = lax.ppermute(b, 'ty', swap_pairs(1, count))]
    pallas_call x5 -> x7, Pallas kernels: 9.04 us -> 9.3 us  [call(): pl.pallas_call(body, out_shape=outs, in_specs=[pl.BlockSpec(memory_space=...]
  transfers between devices with their start and end apart: 15 -> 13, of which waited for: 10 -> 9; matrix products, arithmetic and copies ran while one was open for 0% -> 0% of each run, Pallas kernels for 6% -> 8%
where the time goes in v3:
time: 55.6 us; the launch traced here: 55.4 us
  starting transfers between devices  24.8 us (45%)
  waiting for transfers between devices  20.3 us (37%)
  Pallas kernels  9.62 us (17%)
  between operations  0.75 us (1%)
    ppermute x9, waiting for transfers between devices, exchange_with(): return lax.ppermute(value, ('tx', 'ty'), pairs)  19.4 us
    ppermute x9, starting transfers between devices, exchange_with(): return lax.ppermute(value, ('tx', 'ty'), pairs)  14.7 us
    pallas_call x7, Pallas kernels, call(): pl.pallas_call(body, out_shape=outs, in_specs=[pl.BlockSpec(memory_space=...  9.3 us
    ppermute x1, starting transfers between devices, swap_along_y(): return (got_b, lax.ppermute(a, 'ty', swap_pairs(0, count)))  4.39 us
    ppermute x1, starting transfers between devices, on_device(): x_pair = lax.ppermute(x_pair, 'tx', swap_pairs(0, n_tx))  4.35 us
  transfers between devices with their start and end apart: 13, of which 9 were waited for; matrix products, arithmetic and copies ran while one was open for 0% of the time, Pallas kernels for 8%

profile of v3, /device:TPU:0, one launch (start us, length us, event | category | flops | bytes accessed | tf_op | source)
XLA Modules:
  0.0 55.4 jit_solution(13550297266056597725)
XLA Ops:
  0.6 1.2 %first_faces.1 = (bf16[64,128]{1,0:T(8,128)(2,1)S(1)}, bf16[64,128]{1,0:T(8,128)(2,1)S(1)}, bf16[2,64,128]{2,1,0:T(8,128)(2,1)S(1)}, f32[8,64,128]{2,1,0:T(8,128)S(1)}, f32[8,64,128]{2,1,0:T(8,128)S(1)}) custom-call(bf16[4,128,128]{2,1,0:T(8,128)(2,1)} %feat_hbm.1, s32[4,128]{1,0:T(4,128)} %occ_hbm.1), custom_call_target="tpu_custom_call" | custom-call | tf_op jit(solution)/shard_map/first_faces/pallas_call | solution.py:31
  1.8 0.7 %collective-permute-start = (bf16[64,128]{1,0:T(8,128)(2,1)S(1)}, bf16[64,128]{1,0:T(8,128)(2,1)S(1)}, u32[]{:S(2)}, u32[]{:S(2)}) collective-permute-start(bf16[64,128]{1,0:T(8,128)(2,1)S(1)} %get-tuple-element.27), channel_id=1, source_target_pairs={{1,2},{2,1},{5,6},{6,5},{9,10},{10,9},{13,14},{14,13},{17,18},{18,... | collective-permute-start | bytes 49160 | tf_op jit(solution)/shard_map/ppermute | solution.py:378
  2.5 4.4 %collective-permute-start.1 = (bf16[64,128]{1,0:T(8,128)(2,1)S(1)}, bf16[64,128]{1,0:T(8,128)(2,1)S(1)}, u32[]{:S(2)}, u32[]{:S(2)}) collective-permute-start(bf16[64,128]{1,0:T(8,128)(2,1)S(1)} %get-tuple-element.28), channel_id=1, source_target_pairs={{0,1},{1,0},{2,3},{3,2},{4,5},{5,4},{6,7},{7,6},{8,9},{9,8},{10,11... | collective-permute-start | bytes 49160 | tf_op jit(solution)/shard_map/ppermute | solution.py:379
  6.9 0.0 collective-permute-done.y_b_ref
  6.9 0.8 %collective-permute-done.1.y_a_ref = bf16[64,128]{1,0:T(8,128)(2,1)S(1)} collective-permute-done((bf16[64,128]{1,0:T(8,128)(2,1)S(1)}, bf16[64,128]{1,0:T(8,128)(2,1)S(1)}, u32[]{:S(2)}, u32[]{:S(2)}) %collective-permute-start.1) | collective-permute-done | bytes 16416 | tf_op jit(solution)/shard_map/ppermute | solution.py:379
  7.7 0.7 %collective-permute-start.2 = (bf16[80,128]{1,0:T(8,128)(2,1)S(1)}, bf16[80,128]{1,0:T(8,128)(2,1)S(1)}, u32[]{:S(2)}, u32[]{:S(2)}) collective-permute-start(bf16[80,128]{1,0:T(8,128)(2,1)S(1)} %get-tuple-element.36), channel_id=1, source_target_pairs={{4,8},{8,4},{12,16},{16,12},{20,24},{24,20},{5,9},{9,5},{13,17},{1... | collective-permute-start | bytes 61448 | tf_op jit(solution)/shard_map/ppermute | solution.py:499
  8.4 4.3 %collective-permute-start.3 = (bf16[80,128]{1,0:T(8,128)(2,1)S(1)}, bf16[80,128]{1,0:T(8,128)(2,1)S(1)}, u32[]{:S(2)}, u32[]{:S(2)}) collective-permute-start(bf16[80,128]{1,0:T(8,128)(2,1)S(1)} %get-tuple-element.37), channel_id=1, source_target_pairs={{0,4},{4,0},{8,12},{12,8},{16,20},{20,16},{24,28},{28,24},{1,5},{5... | collective-permute-start | bytes 61448 | tf_op jit(solution)/shard_map/ppermute | solution.py:500
  12.8 2.3 %main.1 = (bf16[8,64,1152]{2,1,0:T(8,128)(2,1)S(1)}, f32[512,128]{1,0:T(8,128)S(1)}, f32[32,512]{1,0:T(8,128)S(1)}, bf16[16,128]{1,0:T(8,128)(2,1)S(1)}, bf16[27,128,128]{2,1,0:T(8,128)(2,1)S(1)}) custom-call(s32[1,1024]{1,0:T(1,128)} %bitcast.1, bf16[16,1024]{1,0:T(8,128)(2,1)} %teach_hbm.1, bf16[16,128]{1,0:T(8,128)(2,1)} %head_hbm.1, ...), custom_call_target="tpu_custom_call" | custom-call | tf_op jit(solution)/shard_map/main/pallas_call | solution.py:31
  15.0 0.0 collective-permute-done.2.x_next_ref
  15.1 2.0 %tile.1 = (bf16[8,64,128]{2,1,0:T(8,128)(2,1)S(1)}, bf16[64,128]{1,0:T(8,128)(2,1)S(1)}, bf16[2,64,128]{2,1,0:T(8,128)(2,1)S(1)}, f32[1728,128]{1,0:T(8,128)S(1)}, bf16[1792,128]{1,0:T(8,128)(2,1)S(1)}) custom-call(bf16[8,64,1152]{2,1,0:T(8,128)(2,1)S(1)} %get-tuple-element.29.cols_ref, f32[512,128]{1,0:T(8,128)S(1)} %get-tuple-element.30.pre_ref, ...), custom_call_target="tpu_custom_call" | custom-call | tf_op jit(solution)/shard_map/tile/pallas_call | solution.py:31
  17.1 0.1 collective-permute-start.4
  17.2 1.8 %collective-permute-done.4.refs_1_ = bf16[1792,128]{1,0:T(8,128)(2,1)S(1)} collective-permute-done((bf16[1792,128]{1,0:T(8,128)(2,1)S(1)}, bf16[1792,128]{1,0:T(8,128)(2,1)S(1)}, u32[]{:S(2)}, u32[]{:S(2)}) %collective-permute-start.4) | collective-permute-done | bytes 458784 | tf_op jit(solution)/shard_map/ppermute | solution.py:402
  19.0 1.9 %collective-permute-start.5 = (bf16[992,128]{1,0:T(8,128)(2,1)S(1)}, bf16[992,128]{1,0:T(8,128)(2,1)S(1)}, u32[]{:S(2)}, u32[]{:S(2)}) collective-permute-start(bf16[992,128]{1,0:T(8,128)(2,1)S(1)} %message.7), channel_id=1, source_target_pairs={{0,3},{1,4},{2,7},{3,0},{4,1},{5,6},{6,5},{7,2},{8,13},{9,10},{10,... | collective-permute-start | bytes 761864 | tf_op jit(solution)/shard_map/ppermute | solution.py:402
  21.0 4.0 %collective-permute-done.5.refs_2_.got1_ref = bf16[992,128]{1,0:T(8,128)(2,1)S(1)} collective-permute-done((bf16[992,128]{1,0:T(8,128)(2,1)S(1)}, bf16[992,128]{1,0:T(8,128)(2,1)S(1)}, u32[]{:S(2)}, u32[]{:S(2)}) %collective-permute-start.5) | collective-permute-done | bytes 253984 | tf_op jit(solution)/shard_map/ppermute | solution.py:402
  25.0 1.5 %collective-permute-start.6 = (bf16[560,128]{1,0:T(8,128)(2,1)S(1)}, bf16[560,128]{1,0:T(8,128)(2,1)S(1)}, u32[]{:S(2)}, u32[]{:S(2)}) collective-permute-start(bf16[560,128]{1,0:T(8,128)(2,1)S(1)} %message.8), channel_id=1, source_target_pairs={{0,5},{1,2},{2,1},{3,6},{4,7},{5,0},{6,3},{7,4},{8,11},{9,12},{10,... | collective-permute-start | bytes 430088 | tf_op jit(solution)/shard_map/ppermute | solution.py:402
  26.5 3.1 %collective-permute-done.6.refs_3_.got2_ref = bf16[560,128]{1,0:T(8,128)(2,1)S(1)} collective-permute-done((bf16[560,128]{1,0:T(8,128)(2,1)S(1)}, bf16[560,128]{1,0:T(8,128)(2,1)S(1)}, u32[]{:S(2)}, u32[]{:S(2)}) %collective-permute-start.6) | collective-permute-done | bytes 143392 | tf_op jit(solution)/shard_map/ppermute | solution.py:402
  29.6 0.1 message.9.refs_0_
  29.6 1.6 %collective-permute-start.7 = (bf16[496,128]{1,0:T(8,128)(2,1)S(1)}, bf16[496,128]{1,0:T(8,128)(2,1)S(1)}, u32[]{:S(2)}, u32[]{:S(2)}) collective-permute-start(bf16[496,128]{1,0:T(8,128)(2,1)S(1)} %message.9.refs_0_), channel_id=1, source_target_pairs={{0,9},{1,24},{2,27},{3,10},{4,29},{5,12},{6,15},{7,30},{8,17},{9,0... | collective-permute-start | bytes 380936 | tf_op jit(solution)/shard_map/ppermute | solution.py:402
  31.2 2.8 %collective-permute-done.7.refs_1_.refs_0_ = bf16[496,128]{1,0:T(8,128)(2,1)S(1)} collective-permute-done((bf16[496,128]{1,0:T(8,128)(2,1)S(1)}, bf16[496,128]{1,0:T(8,128)(2,1)S(1)}, u32[]{:S(2)}, u32[]{:S(2)}) %collective-permute-start.7) | collective-permute-done | bytes 127008 | tf_op jit(solution)/shard_map/ppermute | solution.py:402
  34.1 3.8 %collective-permute-start.8 = (bf16[496,128]{1,0:T(8,128)(2,1)S(1)}, bf16[496,128]{1,0:T(8,128)(2,1)S(1)}, u32[]{:S(2)}, u32[]{:S(2)}) collective-permute-start(bf16[496,128]{1,0:T(8,128)(2,1)S(1)} %message.10.refs_0_), channel_id=1, source_target_pairs={{0,25},{1,8},{2,11},{3,26},{4,13},{5,28},{6,31},{7,14},{8,1},{9,16... | collective-permute-start | bytes 380936 | tf_op jit(solution)/shard_map/ppermute | solution.py:402
  37.9 2.7 %collective-permute-done.8.refs_1_ = bf16[496,128]{1,0:T(8,128)(2,1)S(1)} collective-permute-done((bf16[496,128]{1,0:T(8,128)(2,1)S(1)}, bf16[496,128]{1,0:T(8,128)(2,1)S(1)}, u32[]{:S(2)}, u32[]{:S(2)}) %collective-permute-start.8) | collective-permute-done | bytes 127008 | tf_op jit(solution)/shard_map/ppermute | solution.py:402
  40.7 2.8 %collective-permute-start.9 = (bf16[512,128]{1,0:T(8,128)(2,1)S(1)}, bf16[512,128]{1,0:T(8,128)(2,1)S(1)}, u32[]{:S(2)}, u32[]{:S(2)}) collective-permute-start(bf16[512,128]{1,0:T(8,128)(2,1)S(1)} %message.11.refs_0_), channel_id=1, source_target_pairs={{0,5},{1,2},{2,1},{3,6},{4,7},{5,0},{6,3},{7,4},{8,11},{9,12},{10,... | collective-permute-start | bytes 393224 | tf_op jit(solution)/shard_map/ppermute | solution.py:402
  43.4 2.7 %collective-permute-done.9.refs_1_.line_ref = bf16[512,128]{1,0:T(8,128)(2,1)S(1)} collective-permute-done((bf16[512,128]{1,0:T(8,128)(2,1)S(1)}, bf16[512,128]{1,0:T(8,128)(2,1)S(1)}, u32[]{:S(2)}, u32[]{:S(2)}) %collective-permute-start.9) | collective-permute-done | bytes 131104 | tf_op jit(solution)/shard_map/ppermute | solution.py:402
  46.1 1.2 %collective-permute-start.11 = (bf16[944,128]{1,0:T(8,128)(2,1)S(1)}, bf16[944,128]{1,0:T(8,128)(2,1)S(1)}, u32[]{:S(2)}, u32[]{:S(2)}) collective-permute-start(bf16[944,128]{1,0:T(8,128)(2,1)S(1)} %get-tuple-element.46.refs_0_.near_ref), channel_id=1, source_target_pairs={{0,3},{1,4},{2,7},{3,0},{4,1},{5,6},{6,5},{7,2},{8,13},{9,10},{10,... | collective-permute-start | bytes 725000 | tf_op jit(solution)/shard_map/ppermute | solution.py:402
  47.3 1.1 %back.1.refs_2_.part_ref = f32[512,128]{1,0:T(8,128)S(1)} custom-call(bf16[8,64,128]{2,1,0:T(8,128)(2,1)S(1)} %get-tuple-element.44.grad_ref, bf16[2,64,128]{2,1,0:T(8,128)(2,1)S(1)} %get-tuple-element.45.planes_ref, bf16[27,128,128]{2,1,0:T(8,128)(2,1)S(1)} %get-tuple-element.34.weight_ref), custom_call_target="tpu_custom_call" | custom-call | tf_op jit(solution)/shard_map/back/pallas_call | solution.py:31
  48.5 0.9 %collective-permute-start.10 = (bf16[944,128]{1,0:T(8,128)(2,1)S(1)}, bf16[944,128]{1,0:T(8,128)(2,1)S(1)}, u32[]{:S(2)}, u32[]{:S(2)}) collective-permute-start(bf16[944,128]{1,0:T(8,128)(2,1)S(1)} %message.13), channel_id=1, source_target_pairs={{0,1},{1,0},{2,3},{3,2},{4,5},{5,4},{6,7},{7,6},{8,9},{9,8},{10,11... | collective-permute-start | bytes 725000 | tf_op jit(solution)/shard_map/ppermute | solution.py:402
  49.4 2.3 %collective-permute-done.11.far_ref = bf16[944,128]{1,0:T(8,128)(2,1)S(1)} collective-permute-done((bf16[944,128]{1,0:T(8,128)(2,1)S(1)}, bf16[944,128]{1,0:T(8,128)(2,1)S(1)}, u32[]{:S(2)}, u32[]{:S(2)}) %collective-permute-start.11) | collective-permute-done | bytes 241696 | tf_op jit(solution)/shard_map/ppermute | solution.py:402
  51.8 0.9 %collective-permute-start.12 = (bf16[944,128]{1,0:T(8,128)(2,1)S(1)}, bf16[944,128]{1,0:T(8,128)(2,1)S(1)}, u32[]{:S(2)}, u32[]{:S(2)}) collective-permute-start(bf16[944,128]{1,0:T(8,128)(2,1)S(1)} %collective-permute-done.11.far_ref), channel_id=1, source_target_pairs={{0,1},{1,0},{2,3},{3,2},{4,5},{5,4},{6,7},{7,6},{8,9},{9,8},{10,11... | collective-permute-start | bytes 725000 | tf_op jit(solution)/shard_map/ppermute | solution.py:402
  52.7 0.0 collective-permute-done.10.near_ref.got_near_ref
  52.7 1.0 %y_faces.1 = (bf16[4,128,128]{2,1,0:T(8,128)(2,1)}, f32[8,128]{1,0:T(8,128)S(1)}) custom-call(f32[512,128]{1,0:T(8,128)S(1)} %back.1.refs_2_.part_ref, f32[8,64,128]{2,1,0:T(8,128)S(1)} %get-tuple-element.31.mask_ref, bf16[27,128,128]{2,1,0:T(8,128)(2,1)S(1)} %get-tuple-element.34.weight_ref, ...), custom_call_target="tpu_custom_call" | custom-call | tf_op jit(solution)/shard_map/y_faces/pallas_call | solution.py:31
  53.7 0.1 collective-permute-done.12.got_far_ref
  53.8 1.6 %normalise.1 = f32[27,128,128]{2,1,0:T(8,128)} custom-call(bf16[944,128]{1,0:T(8,128)(2,1)S(1)} %get-tuple-element.46.refs_0_.near_ref, bf16[944,128]{1,0:T(8,128)(2,1)S(1)} %collective-permute-done.11.far_ref, bf16[944,128]{1,0:T(8,128)(2,1)S(1)} %collective-permute-done.10.near_ref.got_near_ref, bf16[944,128]{1,0:T(8,128)(2,1)S(1)} %collective-permute-done.12.got_far_ref, ...), custom_call_target="tpu_custom_call" | custom-call | tf_op jit(solution)/shard_map/normalise/pallas_call | solution.py:31
  (9 shorter events, 0.3 us)
Async XLA Ops:
  1.8 5.1 %collective-permute-start = (bf16[64,128]{1,0:T(8,128)(2,1)S(1)}, bf16[64,128]{1,0:T(8,128)(2,1)S(1)}, u32[]{:S(2)}, u32[]{:S(2)}) collective-permute-start(bf16[64,128]{1,0:T(8,128)(2,1)S(1)} %get-tuple-element.27), channel_id=1, source_target_pairs={{1,2},{2,1},{5,6},{6,5},{9,10},{10,9},{13,14},{14,13},{17,18},{18,... | collective-permute-start | bytes 49160 | tf_op jit(solution)/shard_map/ppermute | solution.py:378
  2.5 5.2 %collective-permute-start.1 = (bf16[64,128]{1,0:T(8,128)(2,1)S(1)}, bf16[64,128]{1,0:T(8,128)(2,1)S(1)}, u32[]{:S(2)}, u32[]{:S(2)}) collective-permute-start(bf16[64,128]{1,0:T(8,128)(2,1)S(1)} %get-tuple-element.28), channel_id=1, source_target_pairs={{0,1},{1,0},{2,3},{3,2},{4,5},{5,4},{6,7},{7,6},{8,9},{9,8},{10,11... | collective-permute-start | bytes 49160 | tf_op jit(solution)/shard_map/ppermute | solution.py:379
  7.7 7.3 %collective-permute-start.2 = (bf16[80,128]{1,0:T(8,128)(2,1)S(1)}, bf16[80,128]{1,0:T(8,128)(2,1)S(1)}, u32[]{:S(2)}, u32[]{:S(2)}) collective-permute-start(bf16[80,128]{1,0:T(8,128)(2,1)S(1)} %get-tuple-element.36), channel_id=1, source_target_pairs={{4,8},{8,4},{12,16},{16,12},{20,24},{24,20},{5,9},{9,5},{13,17},{1... | collective-permute-start | bytes 61448 | tf_op jit(solution)/shard_map/ppermute | solution.py:499
  8.4 6.6 %collective-permute-start.3 = (bf16[80,128]{1,0:T(8,128)(2,1)S(1)}, bf16[80,128]{1,0:T(8,128)(2,1)S(1)}, u32[]{:S(2)}, u32[]{:S(2)}) collective-permute-start(bf16[80,128]{1,0:T(8,128)(2,1)S(1)} %get-tuple-element.37), channel_id=1, source_target_pairs={{0,4},{4,0},{8,12},{12,8},{16,20},{20,16},{24,28},{28,24},{1,5},{5... | collective-permute-start | bytes 61448 | tf_op jit(solution)/shard_map/ppermute | solution.py:500
  17.1 1.9 %collective-permute-start.4 = (bf16[1792,128]{1,0:T(8,128)(2,1)S(1)}, bf16[1792,128]{1,0:T(8,128)(2,1)S(1)}, u32[]{:S(2)}, u32[]{:S(2)}) collective-permute-start(bf16[1792,128]{1,0:T(8,128)(2,1)S(1)} %get-tuple-element.39), channel_id=1, source_target_pairs={{0,1},{1,0},{2,3},{3,2},{4,5},{5,4},{6,7},{7,6},{8,9},{9,8},{10,11... | collective-permute-start | bytes 1376264 | tf_op jit(solution)/shard_map/ppermute | solution.py:402
  19.0 5.9 %collective-permute-start.5 = (bf16[992,128]{1,0:T(8,128)(2,1)S(1)}, bf16[992,128]{1,0:T(8,128)(2,1)S(1)}, u32[]{:S(2)}, u32[]{:S(2)}) collective-permute-start(bf16[992,128]{1,0:T(8,128)(2,1)S(1)} %message.7), channel_id=1, source_target_pairs={{0,3},{1,4},{2,7},{3,0},{4,1},{5,6},{6,5},{7,2},{8,13},{9,10},{10,... | collective-permute-start | bytes 761864 | tf_op jit(solution)/shard_map/ppermute | solution.py:402
  25.0 4.6 %collective-permute-start.6 = (bf16[560,128]{1,0:T(8,128)(2,1)S(1)}, bf16[560,128]{1,0:T(8,128)(2,1)S(1)}, u32[]{:S(2)}, u32[]{:S(2)}) collective-permute-start(bf16[560,128]{1,0:T(8,128)(2,1)S(1)} %message.8), channel_id=1, source_target_pairs={{0,5},{1,2},{2,1},{3,6},{4,7},{5,0},{6,3},{7,4},{8,11},{9,12},{10,... | collective-permute-start | bytes 430088 | tf_op jit(solution)/shard_map/ppermute | solution.py:402
  29.6 4.4 %collective-permute-start.7 = (bf16[496,128]{1,0:T(8,128)(2,1)S(1)}, bf16[496,128]{1,0:T(8,128)(2,1)S(1)}, u32[]{:S(2)}, u32[]{:S(2)}) collective-permute-start(bf16[496,128]{1,0:T(8,128)(2,1)S(1)} %message.9.refs_0_), channel_id=1, source_target_pairs={{0,9},{1,24},{2,27},{3,10},{4,29},{5,12},{6,15},{7,30},{8,17},{9,0... | collective-permute-start | bytes 380936 | tf_op jit(solution)/shard_map/ppermute | solution.py:402
  34.1 6.5 %collective-permute-start.8 = (bf16[496,128]{1,0:T(8,128)(2,1)S(1)}, bf16[496,128]{1,0:T(8,128)(2,1)S(1)}, u32[]{:S(2)}, u32[]{:S(2)}) collective-permute-start(bf16[496,128]{1,0:T(8,128)(2,1)S(1)} %message.10.refs_0_), channel_id=1, source_target_pairs={{0,25},{1,8},{2,11},{3,26},{4,13},{5,28},{6,31},{7,14},{8,1},{9,16... | collective-permute-start | bytes 380936 | tf_op jit(solution)/shard_map/ppermute | solution.py:402
  40.7 5.4 %collective-permute-start.9 = (bf16[512,128]{1,0:T(8,128)(2,1)S(1)}, bf16[512,128]{1,0:T(8,128)(2,1)S(1)}, u32[]{:S(2)}, u32[]{:S(2)}) collective-permute-start(bf16[512,128]{1,0:T(8,128)(2,1)S(1)} %message.11.refs_0_), channel_id=1, source_target_pairs={{0,5},{1,2},{2,1},{3,6},{4,7},{5,0},{6,3},{7,4},{8,11},{9,12},{10,... | collective-permute-start | bytes 393224 | tf_op jit(solution)/shard_map/ppermute | solution.py:402
  46.1 5.6 %collective-permute-start.11 = (bf16[944,128]{1,0:T(8,128)(2,1)S(1)}, bf16[944,128]{1,0:T(8,128)(2,1)S(1)}, u32[]{:S(2)}, u32[]{:S(2)}) collective-permute-start(bf16[944,128]{1,0:T(8,128)(2,1)S(1)} %get-tuple-element.46.refs_0_.near_ref), channel_id=1, source_target_pairs={{0,3},{1,4},{2,7},{3,0},{4,1},{5,6},{6,5},{7,2},{8,13},{9,10},{10,... | collective-permute-start | bytes 725000 | tf_op jit(solution)/shard_map/ppermute | solution.py:402
  48.5 4.1 %collective-permute-start.10 = (bf16[944,128]{1,0:T(8,128)(2,1)S(1)}, bf16[944,128]{1,0:T(8,128)(2,1)S(1)}, u32[]{:S(2)}, u32[]{:S(2)}) collective-permute-start(bf16[944,128]{1,0:T(8,128)(2,1)S(1)} %message.13), channel_id=1, source_target_pairs={{0,1},{1,0},{2,3},{3,2},{4,5},{5,4},{6,7},{7,6},{8,9},{9,8},{10,11... | collective-permute-start | bytes 725000 | tf_op jit(solution)/shard_map/ppermute | solution.py:402
  51.8 2.0 %collective-permute-start.12 = (bf16[944,128]{1,0:T(8,128)(2,1)S(1)}, bf16[944,128]{1,0:T(8,128)(2,1)S(1)}, u32[]{:S(2)}, u32[]{:S(2)}) collective-permute-start(bf16[944,128]{1,0:T(8,128)(2,1)S(1)} %collective-permute-done.11.far_ref), channel_id=1, source_target_pairs={{0,1},{1,0},{2,3},{3,2},{4,5},{5,4},{6,7},{7,6},{8,9},{9,8},{10,11... | collective-permute-start | bytes 725000 | tf_op jit(solution)/shard_map/ppermute | solution.py:402

commit v4 on v3

--- a/solution.py
+++ b/solution.py
@@ -235,7 +235,7 @@
 
 def tile_kernel(
     cols_ref, pre_ref, mask_ref, sums_ref, head_ref, weight_ref, x_next_ref, x_pair_ref,
-    grad_ref, next_ref, edge_ref, keep_ref, send_ref,
+    grad_ref, next_ref, edge_ref, keep_ref, first_ref, rest_ref,
     ends_ref, terms_ref,
 ):
     channels = cols_ref.shape[2] // TAPS
@@ -268,28 +268,28 @@
     grad_ref[...] = rounded.reshape(SIDE, PLANE, channels)
     low_y, high_y = y_faces(lambda x: gradient[x * PLANE : (x + 1) * PLANE])
     ends = gradient[:PLANE], gradient[voxels - PLANE :]
-    pair_ref = send_ref.at[send_ref.shape[0] - PLANE :]
+    pair_ref = rest_ref.at[rest_ref.shape[0] - PLANE :]
     store_faces(*ends, low_y, high_y, pair_ref, next_ref, edge_ref)
 
     def term(planes, gradient):
-        return contract(planes.reshape(-1, wide), gradient, 0, 0).reshape(TAPS, channels, channels)
-
-    terms_ref[:TAPS] = term(cols_ref[: SIDE - 1], rounded[PLANE:]) + term(
+        return contract(planes.reshape(-1, wide), gradient, 0, 0)
+
+    terms_ref[:wide] = term(cols_ref[: SIDE - 1], rounded[PLANE:]) + term(
         ends_ref[0], rounded[:PLANE]
     )
-    terms_ref[TAPS : 2 * TAPS] = term(cols_ref[...], rounded)
-    terms_ref[2 * TAPS :] = term(cols_ref[1:], rounded[:inner]) + term(
+    terms_ref[wide : 2 * wide] = term(cols_ref[...], rounded)
+    terms_ref[2 * wide :] = term(cols_ref[1:], rounded[:inner]) + term(
         ends_ref[1], rounded[inner:]
     )
-    length = channels // PARTS
+    length = terms_ref.shape[0] // PARTS
     for r in range(PARTS):
-        first = pl.multiple_of(part_index(r) * length, length)
-        part = terms_ref[:, pl.ds(first, length), :].reshape(-1, channels)
-        row = (r % (PARTS // 2)) * part.shape[0]
+        part = terms_ref[pl.ds(pl.multiple_of(part_index(r) * length, 16), length)]
+        row = (r % 2) * length
         if r < PARTS // 2:
-            keep_ref[row : row + part.shape[0]] = part
+            keep_ref[r * length : (r + 1) * length] = part
         else:
-            send_ref[row : row + part.shape[0]] = part.astype(BF16)
+            send_ref = rest_ref if r < PARTS - 2 else first_ref
+            send_ref[row : row + length] = part.astype(BF16)
 
 
 def lane_of(tx, ty):
@@ -322,10 +322,19 @@
     part_ref[...] = total
 
 
-def y_faces_kernel(extra_ref, part_ref, mask_ref, weight_ref, near_ref, far_ref, line_ref, out_ref, token_ref, cols_ref):
+def squares(ref, rows):
+    value = ref[:rows].astype(F32)
+    return jnp.sum(value * value, axis=0, keepdims=True)
+
+
+def y_faces_kernel(
+    extra_ref, part_ref, mask_ref, weight_ref, near_ref, far_ref, line_ref, *refs
+):
+    pieces, (out_ref, squares_ref, cols_ref) = refs[:-3], refs[-3:]
     channels, rows = part_ref.shape[1], (SIDE + 2) * SIDE
     tx, ty = lax.axis_index("tx"), lax.axis_index("ty")
-    token_ref[...] = jnp.zeros(token_ref.shape, F32)
+    total = sum(squares(ref, near_ref.shape[0] - rows) for ref in pieces)
+    squares_ref[...] = jnp.broadcast_to(total, squares_ref.shape)
     by_first, by_second = far_ref[far_ref.shape[0] - rows :], line_ref[line_ref.shape[0] - rows :]
     other = jnp.where(lane_of(tx, ty) == 0, by_first.astype(F32), by_second.astype(F32))
     beyond = jnp.zeros(other.shape, F32) if extra_ref is None else extra_ref[...].astype(F32)
@@ -350,23 +359,23 @@
             out_ref[slot, a * rows : (a + 1) * rows, :] = total[j * rows : (j + 1) * rows]
 
 
-def norm_kernel(near_ref, far_ref, got_near_ref, got_far_ref, token_ref, out_ref):
-    del token_ref
-    kernels, channels = out_ref.shape[0], out_ref.shape[2]
-    length = channels // PARTS
-    refs = (near_ref, far_ref, got_near_ref, got_far_ref)
-    rows = kernels * length
-    pieces = [ref.at[i * rows : (i + 1) * rows] for ref in refs for i in range(2)]
-    squares = jnp.zeros((kernels * length, channels), F32)
-    for piece in pieces:
-        value = piece[...].astype(F32)
-        squares = squares + value * value
-    mean = jnp.sum(squares) / (kernels * channels * channels)
-    scale = 1.0 / jnp.sqrt(jnp.broadcast_to(mean, (1, channels)) + 1e-06)
+def norm_kernel(*refs):
+    pieces, refs = refs[:PARTS], refs[PARTS:]
+    squares_ref, grad_ref, out_hbm, grad_hbm, out_ref, semaphores = refs
+    copies = [pltpu.make_async_copy(grad_ref, grad_hbm, semaphores.at[PARTS])]
+    copies[0].start()
+    rows, channels = out_ref.shape[1:]
+    total = squares_ref[:1] + squares(pieces[-1], rows)
+    mean = jnp.sum(total, axis=1, keepdims=True) / (PARTS * rows * channels)
+    scale = jnp.broadcast_to(1.0 / jnp.sqrt(mean + 1e-06), (1, channels))
     for r, piece in enumerate(pieces):
-        value = piece[...].astype(F32) * scale
-        first = pl.multiple_of(part_index(r) * length, length)
-        out_ref[:, pl.ds(first, length), :] = value.reshape(kernels, length, channels)
+        out_ref[r] = piece[:rows].astype(F32) * scale
+        first = pl.multiple_of(part_index(r) * rows, 16)
+        target = out_hbm.at[pl.ds(first, rows)]
+        copies.append(pltpu.make_async_copy(out_ref.at[r], target, semaphores.at[r]))
+        copies[-1].start()
+    for copy in copies:
+        copy.wait()
 
 
 def swap_pairs(first, count):
@@ -514,32 +523,37 @@
         fetched=len(fetched),
     )
     part = kernels * channels // PARTS
-    gradient, g_next, g_edges, keep, send = call(
+    gradient, g_next, g_edges, keep, first, rest = call(
         tile_kernel,
         (
             shape((SIDE, PLANE, channels), BF16),
             face,
             edges,
             shape((PARTS // 2 * part, channels), F32),
-            shape((PARTS // 2 * part + PLANE, channels), BF16),
+            shape((2 * part, channels), BF16),
+            shape((2 * part + PLANE, channels), BF16),
         ),
         (tile_cols, pre, mask, sums, head, weight, x_next, x_pair),
         (
             pltpu.VMEM((2, PLANE, TAPS * channels), BF16),
-            pltpu.VMEM((kernels, channels, channels), F32),
+            pltpu.VMEM((kernels * channels, channels), F32),
         ),
         name="tile",
     )
 
-    got0 = exchange_with(send, by_core)
-    faces = [(PLANE, add, (got0, 4 * part)), (PLANE, add, (g_next, 0))]
-    kept = [(2 * part, add, (keep, 2 * part), (got0, 2 * part))]
-    got1 = exchange_with(message(kept + faces), first_way)
-    kept = [(part, add, (keep, part), (got0, part), (got1, part))]
+    got_first = exchange_with(first, by_core)
+    got_rest = exchange_with(rest, by_core)
+    onward = message([(part, add, (keep, 3 * part), (got_first, part))])
+    got_onward = exchange_with(onward, first_way)
+    faces = [(PLANE, add, (got_rest, 2 * part)), (PLANE, add, (g_next, 0))]
+    got1 = exchange_with(
+        message([(part, add, (keep, 2 * part), (got_first, 0)), *faces]), first_way
+    )
+    kept = [(part, add, (keep, part), (got_rest, part), (got_onward, 0))]
     got2 = exchange_with(message(kept + faces), second_way)
-    at = (2 * part, part, part)
-    hand_on = (PLANE, picked_face, (got1, at[0] + PLANE), (got2, at[1] + PLANE))
-    total = [(part, add, (keep, 0), (got0, 0), (got1, 0), (got2, 0))]
+    at = (part, part, part)
+    hand_on = (PLANE, picked_face, (got1, part + PLANE), (got2, part + PLANE))
+    total = [(part, add, (keep, 0), (got_rest, 0), (got1, 0), (got2, 0))]
     flips, lines = [], []
     while 2 ** len(flips) < n_tx // 2:
         flips.append(2 ** (len(flips) + 1) - 1)
@@ -560,10 +574,10 @@
     g_a, g_b, planes = edge_faces(kernel, g_edges, (got1, got2, *lines))
     rows = g_a.shape[0]
     total = message(total + [(rows, add, (g_b, 0))])
-    got3 = exchange_with(total, second_way)
-    near = [(part, add, (total, 0)), (part, add, (got3, 0)), (rows, add, (g_b, 0))]
-    near, gradient = message(near, (), (gradient,))
-    far = exchange_with(near, first_way)
+    piece1 = exchange_with(total, second_way)
+    piece2 = exchange_with(total, first_way)
+    onward, gradient = message([(part, add, (piece1, 0))], (), (gradient,))
+    piece3 = exchange_with(onward, first_way)
     back_part = call(
         back_kernel,
         shape((SIDE * PLANE, channels), F32),
@@ -571,30 +585,38 @@
         (cols,),
         name="back",
     )
-    got_near = exchange_with(
-        message([(2 * part, add, (near, 0)), (rows, add, (g_a, 0))], (back_part,)), by_core
-    )
-    got_far = exchange_with(far, by_core)
-    faces = (back_part, mask, weight, got_near, far, got3)
+    near = message([(part, add, (piece2, 0)), (rows, add, (g_a, 0))], (back_part,))
+    pieces = (total, piece1, near, piece3)
+    others = [exchange_with(piece, by_core) for piece in pieces]
+    faces = (back_part, mask, weight, others[2], piece2, piece1, *pieces, *others[:3])
     kernel = functools.partial(y_faces_kernel, None)
     if n_ty > 4:
         pairs = [pair for i in range(3, n_ty - 1, 4) for pair in ((i, i + 1), (i + 1, i))]
         faces = (lax.ppermute(g_b, "ty", pairs), *faces)
         kernel = y_faces_kernel
-    grad_features, token = call(
+    grad_features, squares_of = call(
         kernel,
         (shape((slots, brick, channels), BF16), shape((8, channels), F32)),
         faces,
         (pltpu.VMEM((PLANE, TAPS * channels), BF16),),
         name="y_faces",
     )
-    grad_weight = call(
+    grad_weight, grad_features = pl.pallas_call(
         norm_kernel,
-        shape((kernels, channels, channels), F32),
-        (near, far, got_near, got_far, token),
+        out_shape=(
+            shape((kernels * channels, channels), F32),
+            shape((slots, brick, channels), BF16),
+        ),
+        in_specs=vmem(PARTS + 2),
+        out_specs=(pl.BlockSpec(memory_space=pltpu.HBM),) * 2,
+        scratch_shapes=[
+            pltpu.VMEM((PARTS, part, channels), F32),
+            pltpu.SemaphoreType.DMA((PARTS + 1,)),
+        ],
+        compiler_params=pltpu.CompilerParams(vmem_limit_bytes=16 * 2**20),
         name="normalise",
-    )
-    return (grad_features, grad_weight)
+    )(*pieces, *others, squares_of, grad_features)
+    return (grad_features, grad_weight.reshape(conv_weight.shape))
 
 
 def solution(mesh):

time: 55.6 us -> 53 us (0.953)
  waiting for transfers between devices: 20.3 us -> 14.4 us
  starting transfers between devices: 24.8 us -> 28.8 us
  Pallas kernels: 9.62 us -> 8.92 us
    ppermute x9 -> x14, waiting for transfers between devices: 19.4 us -> 13.5 us  [exchange_with(): return lax.ppermute(value, ('tx', 'ty'), pairs)]
    ppermute x9 -> x14, starting transfers between devices: 14.7 us -> 18.7 us  [exchange_with(): return lax.ppermute(value, ('tx', 'ty'), pairs)]
    pallas_call x7 -> x6, Pallas kernels: 9.3 us -> 7.17 us  [call(): pl.pallas_call(body, out_shape=outs, in_specs=[pl.BlockSpec(memory_space=...]
    pallas_call x0 -> x1, Pallas kernels: none -> 1.45 us  [on_device(): pl.pallas_call(norm_kernel, out_shape=(shape((kernels * channels, channel...]
  transfers between devices with their start and end apart: 13 -> 18, of which waited for: 9 -> 12; matrix products, arithmetic and copies ran while one was open for 0% -> 0% of each run, Pallas kernels for 8% -> 8%
where the time goes in v4:
time: 53 us; the launch traced here: 52.8 us
  starting transfers between devices  28.8 us (54%)
  waiting for transfers between devices  14.4 us (27%)
  Pallas kernels  8.92 us (17%)
  between operations  0.77 us (1%)
    ppermute x14, starting transfers between devices, exchange_with(): return lax.ppermute(value, ('tx', 'ty'), pairs)  18.7 us
    ppermute x14, waiting for transfers between devices, exchange_with(): return lax.ppermute(value, ('tx', 'ty'), pairs)  13.5 us
    pallas_call x6, Pallas kernels, call(): pl.pallas_call(body, out_shape=outs, in_specs=[pl.BlockSpec(memory_space=...  7.17 us
    ppermute x1, starting transfers between devices, swap_along_y(): return (got_b, lax.ppermute(a, 'ty', swap_pairs(0, count)))  4.39 us
    ppermute x1, starting transfers between devices, on_device(): x_pair = lax.ppermute(x_pair, 'tx', swap_pairs(0, n_tx))  4.35 us
    pallas_call x1, Pallas kernels, on_device(): pl.pallas_call(norm_kernel, out_shape=(shape((kernels * channels, channel...  1.45 us
  transfers between devices with their start and end apart: 18, of which 12 were waited for; matrix products, arithmetic and copies ran while one was open for 0% of the time, Pallas kernels for 8%

profile of v4, /device:TPU:0, one launch (start us, length us, event | category | flops | bytes accessed | tf_op | source)
XLA Modules:
  0.0 52.8 jit_solution(13935276824647882797)
XLA Ops:
  0.6 1.2 %first_faces.1 = (bf16[64,128]{1,0:T(8,128)(2,1)S(1)}, bf16[64,128]{1,0:T(8,128)(2,1)S(1)}, bf16[2,64,128]{2,1,0:T(8,128)(2,1)S(1)}, f32[8,64,128]{2,1,0:T(8,128)S(1)}, f32[8,64,128]{2,1,0:T(8,128)S(1)}) custom-call(bf16[4,128,128]{2,1,0:T(8,128)(2,1)} %feat_hbm.1, s32[4,128]{1,0:T(4,128)} %occ_hbm.1), custom_call_target="tpu_custom_call" | custom-call | tf_op jit(solution)/shard_map/first_faces/pallas_call | solution.py:31
  1.8 0.7 %collective-permute-start = (bf16[64,128]{1,0:T(8,128)(2,1)S(1)}, bf16[64,128]{1,0:T(8,128)(2,1)S(1)}, u32[]{:S(2)}, u32[]{:S(2)}) collective-permute-start(bf16[64,128]{1,0:T(8,128)(2,1)S(1)} %get-tuple-element.30), channel_id=1, source_target_pairs={{1,2},{2,1},{5,6},{6,5},{9,10},{10,9},{13,14},{14,13},{17,18},{18,... | collective-permute-start | bytes 49160 | tf_op jit(solution)/shard_map/ppermute | solution.py:387
  2.5 4.4 %collective-permute-start.1 = (bf16[64,128]{1,0:T(8,128)(2,1)S(1)}, bf16[64,128]{1,0:T(8,128)(2,1)S(1)}, u32[]{:S(2)}, u32[]{:S(2)}) collective-permute-start(bf16[64,128]{1,0:T(8,128)(2,1)S(1)} %get-tuple-element.31), channel_id=1, source_target_pairs={{0,1},{1,0},{2,3},{3,2},{4,5},{5,4},{6,7},{7,6},{8,9},{9,8},{10,11... | collective-permute-start | bytes 49160 | tf_op jit(solution)/shard_map/ppermute | solution.py:388
  6.9 0.8 %collective-permute-done.1.y_a_ref = bf16[64,128]{1,0:T(8,128)(2,1)S(1)} collective-permute-done((bf16[64,128]{1,0:T(8,128)(2,1)S(1)}, bf16[64,128]{1,0:T(8,128)(2,1)S(1)}, u32[]{:S(2)}, u32[]{:S(2)}) %collective-permute-start.1) | collective-permute-done | bytes 16416 | tf_op jit(solution)/shard_map/ppermute | solution.py:388
  7.7 0.7 %collective-permute-start.2 = (bf16[80,128]{1,0:T(8,128)(2,1)S(1)}, bf16[80,128]{1,0:T(8,128)(2,1)S(1)}, u32[]{:S(2)}, u32[]{:S(2)}) collective-permute-start(bf16[80,128]{1,0:T(8,128)(2,1)S(1)} %get-tuple-element.39), channel_id=1, source_target_pairs={{4,8},{8,4},{12,16},{16,12},{20,24},{24,20},{5,9},{9,5},{13,17},{1... | collective-permute-start | bytes 61448 | tf_op jit(solution)/shard_map/ppermute | solution.py:508
  8.4 4.3 %collective-permute-start.3 = (bf16[80,128]{1,0:T(8,128)(2,1)S(1)}, bf16[80,128]{1,0:T(8,128)(2,1)S(1)}, u32[]{:S(2)}, u32[]{:S(2)}) collective-permute-start(bf16[80,128]{1,0:T(8,128)(2,1)S(1)} %get-tuple-element.40), channel_id=1, source_target_pairs={{0,4},{4,0},{8,12},{12,8},{16,20},{20,16},{24,28},{28,24},{1,5},{5... | collective-permute-start | bytes 61448 | tf_op jit(solution)/shard_map/ppermute | solution.py:509
  12.8 2.3 %main.1 = (bf16[8,64,1152]{2,1,0:T(8,128)(2,1)S(1)}, f32[512,128]{1,0:T(8,128)S(1)}, f32[32,512]{1,0:T(8,128)S(1)}, bf16[16,128]{1,0:T(8,128)(2,1)S(1)}, bf16[27,128,128]{2,1,0:T(8,128)(2,1)S(1)}) custom-call(s32[1,1024]{1,0:T(1,128)} %bitcast.2, bf16[16,1024]{1,0:T(8,128)(2,1)} %teach_hbm.1, bf16[16,128]{1,0:T(8,128)(2,1)} %head_hbm.1, ...), custom_call_target="tpu_custom_call" | custom-call | tf_op jit(solution)/shard_map/main/pallas_call | solution.py:31
  15.1 2.0 %tile.1 = (bf16[8,64,128]{2,1,0:T(8,128)(2,1)S(1)}, bf16[64,128]{1,0:T(8,128)(2,1)S(1)}, bf16[2,64,128]{2,1,0:T(8,128)(2,1)S(1)}, f32[1728,128]{1,0:T(8,128)S(1)...) custom-call(bf16[8,64,1152]{2,1,0:T(8,128)(2,1)S(1)} %get-tuple-element.32.cols_ref, ...), custom_call_target="tpu_custom_call" | custom-call | tf_op jit(solution)/shard_map/tile/pallas_call | solution.py:31
  17.2 0.5 collective-permute-start.4
  17.7 1.0 %collective-permute-done.5.refs_1_ = bf16[864,128]{1,0:T(8,128)(2,1)S(1)} collective-permute-done((bf16[864,128]{1,0:T(8,128)(2,1)S(1)}, bf16[864,128]{1,0:T(8,128)(2,1)S(1)}, u32[]{:S(2)}, u32[]{:S(2)}) %collective-permute-start.5) | collective-permute-done | bytes 221216 | tf_op jit(solution)/shard_map/ppermute | solution.py:411
  18.7 1.9 %collective-permute-start.7 = (bf16[432,128]{1,0:T(8,128)(2,1)S(1)}, bf16[432,128]{1,0:T(8,128)(2,1)S(1)}, u32[]{:S(2)}, u32[]{:S(2)}) collective-permute-start(bf16[432,128]{1,0:T(8,128)(2,1)S(1)} %message.9), channel_id=1, source_target_pairs={{0,3},{1,4},{2,7},{3,0},{4,1},{5,6},{6,5},{7,2},{8,13},{9,10},{10,... | collective-permute-start | bytes 331784 | tf_op jit(solution)/shard_map/ppermute | solution.py:411
  20.7 0.4 collective-permute-start.6
  21.0 2.0 %collective-permute-done.7.refs_2_ = bf16[432,128]{1,0:T(8,128)(2,1)S(1)} collective-permute-done((bf16[432,128]{1,0:T(8,128)(2,1)S(1)}, bf16[432,128]{1,0:T(8,128)(2,1)S(1)}, u32[]{:S(2)}, u32[]{:S(2)}) %collective-permute-start.7) | collective-permute-done | bytes 110624 | tf_op jit(solution)/shard_map/ppermute | solution.py:411
  23.1 1.8 %collective-permute-start.8 = (bf16[560,128]{1,0:T(8,128)(2,1)S(1)}, bf16[560,128]{1,0:T(8,128)(2,1)S(1)}, u32[]{:S(2)}, u32[]{:S(2)}) collective-permute-start(bf16[560,128]{1,0:T(8,128)(2,1)S(1)} %message.10), channel_id=1, source_target_pairs={{0,5},{1,2},{2,1},{3,6},{4,7},{5,0},{6,3},{7,4},{8,11},{9,12},{10,... | collective-permute-start | bytes 430088 | tf_op jit(solution)/shard_map/ppermute | solution.py:411
  24.9 0.3 collective-permute-done.6.refs_2_.got1_ref
  25.2 2.4 %collective-permute-done.8.refs_3_.got2_ref = bf16[560,128]{1,0:T(8,128)(2,1)S(1)} collective-permute-done((bf16[560,128]{1,0:T(8,128)(2,1)S(1)}, bf16[560,128]{1,0:T(8,128)(2,1)S(1)}, u32[]{:S(2)}, u32[]{:S(2)}) %collective-permute-start.8) | collective-permute-done | bytes 143392 | tf_op jit(solution)/shard_map/ppermute | solution.py:411
  27.8 1.9 %collective-permute-start.9 = (bf16[496,128]{1,0:T(8,128)(2,1)S(1)}, bf16[496,128]{1,0:T(8,128)(2,1)S(1)}, u32[]{:S(2)}, u32[]{:S(2)}) collective-permute-start(bf16[496,128]{1,0:T(8,128)(2,1)S(1)} %message.11.refs_0_), channel_id=1, source_target_pairs={{0,9},{1,24},{2,27},{3,10},{4,29},{5,12},{6,15},{7,30},{8,17},{9,0... | collective-permute-start | bytes 380936 | tf_op jit(solution)/shard_map/ppermute | solution.py:411
  29.7 2.6 %collective-permute-done.9.refs_1_.refs_0_ = bf16[496,128]{1,0:T(8,128)(2,1)S(1)} collective-permute-done((bf16[496,128]{1,0:T(8,128)(2,1)S(1)}, bf16[496,128]{1,0:T(8,128)(2,1)S(1)}, u32[]{:S(2)}, u32[]{:S(2)}) %collective-permute-start.9) | collective-permute-done | bytes 127008 | tf_op jit(solution)/shard_map/ppermute | solution.py:411
  32.3 4.0 %collective-permute-start.10 = (bf16[496,128]{1,0:T(8,128)(2,1)S(1)}, bf16[496,128]{1,0:T(8,128)(2,1)S(1)}, u32[]{:S(2)}, u32[]{:S(2)}) collective-permute-start(bf16[496,128]{1,0:T(8,128)(2,1)S(1)} %message.12.refs_0_), channel_id=1, source_target_pairs={{0,25},{1,8},{2,11},{3,26},{4,13},{5,28},{6,31},{7,14},{8,1},{9,16... | collective-permute-start | bytes 380936 | tf_op jit(solution)/shard_map/ppermute | solution.py:411
  36.3 2.7 %collective-permute-done.10.refs_1_ = bf16[496,128]{1,0:T(8,128)(2,1)S(1)} collective-permute-done((bf16[496,128]{1,0:T(8,128)(2,1)S(1)}, bf16[496,128]{1,0:T(8,128)(2,1)S(1)}, u32[]{:S(2)}, u32[]{:S(2)}) %collective-permute-start.10) | collective-permute-done | bytes 127008 | tf_op jit(solution)/shard_map/ppermute | solution.py:411
  39.1 2.4 %collective-permute-start.11 = (bf16[512,128]{1,0:T(8,128)(2,1)S(1)}, bf16[512,128]{1,0:T(8,128)(2,1)S(1)}, u32[]{:S(2)}, u32[]{:S(2)}) collective-permute-start(bf16[512,128]{1,0:T(8,128)(2,1)S(1)} %message.13.refs_0_), channel_id=1, source_target_pairs={{0,5},{1,2},{2,1},{3,6},{4,7},{5,0},{6,3},{7,4},{8,11},{9,12},{10,... | collective-permute-start | bytes 393224 | tf_op jit(solution)/shard_map/ppermute | solution.py:411
  41.5 1.6 %collective-permute-start.12 = (bf16[512,128]{1,0:T(8,128)(2,1)S(1)}, bf16[512,128]{1,0:T(8,128)(2,1)S(1)}, u32[]{:S(2)}, u32[]{:S(2)}) collective-permute-start(bf16[512,128]{1,0:T(8,128)(2,1)S(1)} %message.13.refs_0_), channel_id=1, source_target_pairs={{0,3},{1,4},{2,7},{3,0},{4,1},{5,6},{6,5},{7,2},{8,13},{9,10},{10,... | collective-permute-start | bytes 393224 | tf_op jit(solution)/shard_map/ppermute | solution.py:411
  43.1 1.0 %collective-permute-done.11.refs_0_.line_ref.refs_1_ = bf16[512,128]{1,0:T(8,128)(2,1)S(1)} collective-permute-done((bf16[512,128]{1,0:T(8,128)(2,1)S(1)}, bf16[512,128]{1,0:T(8,128)(2,1)S(1)}, u32[]{:S(2)}, u32[]{:S(2)}) %collective-permute-start.11) | collective-permute-done | bytes 131104 | tf_op jit(solution)/shard_map/ppermute | solution.py:411
  44.2 3.4 %collective-permute-start.13 = (bf16[432,128]{1,0:T(8,128)(2,1)S(1)}, bf16[432,128]{1,0:T(8,128)(2,1)S(1)}, u32[]{:S(2)}, u32[]{:S(2)}) collective-permute-start(bf16[432,128]{1,0:T(8,128)(2,1)S(1)} %get-tuple-element.51), channel_id=1, source_target_pairs={{0,3},{1,4},{2,7},{3,0},{4,1},{5,6},{6,5},{7,2},{8,13},{9,10},{10,... | collective-permute-start | bytes 331784 | tf_op jit(solution)/shard_map/ppermute | solution.py:411
  47.6 1.1 %back.1.refs_2_.part_ref = f32[512,128]{1,0:T(8,128)S(1)} custom-call(bf16[8,64,128]{2,1,0:T(8,128)(2,1)S(1)} %get-tuple-element.49.grad_ref, bf16[2,64,128]{2,1,0:T(8,128)(2,1)S(1)} %get-tuple-element.50.planes_ref, bf16[27,128,128]{2,1,0:T(8,128)(2,1)S(1)} %get-tuple-element.37.weight_ref), custom_call_target="tpu_custom_call" | custom-call | tf_op jit(solution)/shard_map/back/pallas_call | solution.py:31
  48.8 0.6 %collective-permute-start.16 = (bf16[512,128]{1,0:T(8,128)(2,1)S(1)}, bf16[512,128]{1,0:T(8,128)(2,1)S(1)}, u32[]{:S(2)}, u32[]{:S(2)}) collective-permute-start(bf16[512,128]{1,0:T(8,128)(2,1)S(1)} %message.15.refs_2_), channel_id=1, source_target_pairs={{0,1},{1,0},{2,3},{3,2},{4,5},{5,4},{6,7},{7,6},{8,9},{9,8},{10,11... | collective-permute-start | bytes 393224 | tf_op jit(solution)/shard_map/ppermute | solution.py:411
  49.5 0.6 %collective-permute-done.13.refs_3_ = bf16[432,128]{1,0:T(8,128)(2,1)S(1)} collective-permute-done((bf16[432,128]{1,0:T(8,128)(2,1)S(1)}, bf16[432,128]{1,0:T(8,128)(2,1)S(1)}, u32[]{:S(2)}, u32[]{:S(2)}) %collective-permute-start.13) | collective-permute-done | bytes 110624 | tf_op jit(solution)/shard_map/ppermute | solution.py:411
  50.0 0.3 collective-permute-done.16.near_ref.refs_6_
  50.4 0.4 collective-permute-done.15.refs_5_
  50.7 0.5 %y_faces.1 = (bf16[4,128,128]{2,1,0:T(8,128)(2,1)S(1)}, f32[8,128]{1,0:T(8,128)S(1)}) custom-call(f32[512,128]{1,0:T(8,128)S(1)} %back.1.refs_2_.part_ref, f32[8,64,128]{2,1,0:T(8,128)S(1)} %get-tuple-element.34.mask_ref, bf16[27,128,128]{2,1,0:T(8,128)(2,1)S(1)} %get-tuple-element.37.weight_ref, ...), custom_call_target="tpu_custom_call" | custom-call | tf_op jit(solution)/shard_map/y_faces/pallas_call | solution.py:31
  51.3 0.1 collective-permute-done.17.refs_7_
  51.4 1.4 %normalise.1 = (f32[3456,128]{1,0:T(8,128)}, bf16[4,128,128]{2,1,0:T(8,128)(2,1)}) custom-call(bf16[512,128]{1,0:T(8,128)(2,1)S(1)} %message.13.refs_0_, bf16[512,128]{1,0:T(8,128)(2,1)S(1)} %collective-permute-done.11.refs_0_.line_ref.refs_1_, bf16[512,128]{1,0:T(8,128)(2,1)S(1)} %message.15.refs_2_, bf16[432,128]{1,0:T(8,128)(2,1)S(1)} %collective-permute-done.13.refs_3_, ...), custom_call_target="tpu_custom_call" | custom-call | tf_op jit(solution)/shard_map/normalise/pallas_call | solution.py:604
  (20 shorter events, 0.5 us)
Async XLA Ops:
  1.8 5.1 %collective-permute-start = (bf16[64,128]{1,0:T(8,128)(2,1)S(1)}, bf16[64,128]{1,0:T(8,128)(2,1)S(1)}, u32[]{:S(2)}, u32[]{:S(2)}) collective-permute-start(bf16[64,128]{1,0:T(8,128)(2,1)S(1)} %get-tuple-element.30), channel_id=1, source_target_pairs={{1,2},{2,1},{5,6},{6,5},{9,10},{10,9},{13,14},{14,13},{17,18},{18,... | collective-permute-start | bytes 49160 | tf_op jit(solution)/shard_map/ppermute | solution.py:387
  2.5 5.2 %collective-permute-start.1 = (bf16[64,128]{1,0:T(8,128)(2,1)S(1)}, bf16[64,128]{1,0:T(8,128)(2,1)S(1)}, u32[]{:S(2)}, u32[]{:S(2)}) collective-permute-start(bf16[64,128]{1,0:T(8,128)(2,1)S(1)} %get-tuple-element.31), channel_id=1, source_target_pairs={{0,1},{1,0},{2,3},{3,2},{4,5},{5,4},{6,7},{7,6},{8,9},{9,8},{10,11... | collective-permute-start | bytes 49160 | tf_op jit(solution)/shard_map/ppermute | solution.py:388
  7.7 7.3 %collective-permute-start.2 = (bf16[80,128]{1,0:T(8,128)(2,1)S(1)}, bf16[80,128]{1,0:T(8,128)(2,1)S(1)}, u32[]{:S(2)}, u32[]{:S(2)}) collective-permute-start(bf16[80,128]{1,0:T(8,128)(2,1)S(1)} %get-tuple-element.39), channel_id=1, source_target_pairs={{4,8},{8,4},{12,16},{16,12},{20,24},{24,20},{5,9},{9,5},{13,17},{1... | collective-permute-start | bytes 61448 | tf_op jit(solution)/shard_map/ppermute | solution.py:508
  8.4 6.6 %collective-permute-start.3 = (bf16[80,128]{1,0:T(8,128)(2,1)S(1)}, bf16[80,128]{1,0:T(8,128)(2,1)S(1)}, u32[]{:S(2)}, u32[]{:S(2)}) collective-permute-start(bf16[80,128]{1,0:T(8,128)(2,1)S(1)} %get-tuple-element.40), channel_id=1, source_target_pairs={{0,4},{4,0},{8,12},{12,8},{16,20},{20,16},{24,28},{28,24},{1,5},{5... | collective-permute-start | bytes 61448 | tf_op jit(solution)/shard_map/ppermute | solution.py:509
  17.1 1.5 %collective-permute-start.5 = (bf16[864,128]{1,0:T(8,128)(2,1)S(1)}, bf16[864,128]{1,0:T(8,128)(2,1)S(1)}, u32[]{:S(2)}, u32[]{:S(2)}) collective-permute-start(bf16[864,128]{1,0:T(8,128)(2,1)S(1)} %get-tuple-element.43), channel_id=1, source_target_pairs={{0,1},{1,0},{2,3},{3,2},{4,5},{5,4},{6,7},{7,6},{8,9},{9,8},{10,11... | collective-permute-start | bytes 663560 | tf_op jit(solution)/shard_map/ppermute | solution.py:411
  17.2 3.4 %collective-permute-start.4 = (bf16[928,128]{1,0:T(8,128)(2,1)S(1)}, bf16[928,128]{1,0:T(8,128)(2,1)S(1)}, u32[]{:S(2)}, u32[]{:S(2)}) collective-permute-start(bf16[928,128]{1,0:T(8,128)(2,1)S(1)} %get-tuple-element.42), channel_id=1, source_target_pairs={{0,1},{1,0},{2,3},{3,2},{4,5},{5,4},{6,7},{7,6},{8,9},{9,8},{10,11... | collective-permute-start | bytes 712712 | tf_op jit(solution)/shard_map/ppermute | solution.py:411
  18.7 4.4 %collective-permute-start.7 = (bf16[432,128]{1,0:T(8,128)(2,1)S(1)}, bf16[432,128]{1,0:T(8,128)(2,1)S(1)}, u32[]{:S(2)}, u32[]{:S(2)}) collective-permute-start(bf16[432,128]{1,0:T(8,128)(2,1)S(1)} %message.9), channel_id=1, source_target_pairs={{0,3},{1,4},{2,7},{3,0},{4,1},{5,6},{6,5},{7,2},{8,13},{9,10},{10,... | collective-permute-start | bytes 331784 | tf_op jit(solution)/shard_map/ppermute | solution.py:411
  20.7 4.6 %collective-permute-start.6 = (bf16[560,128]{1,0:T(8,128)(2,1)S(1)}, bf16[560,128]{1,0:T(8,128)(2,1)S(1)}, u32[]{:S(2)}, u32[]{:S(2)}) collective-permute-start(bf16[560,128]{1,0:T(8,128)(2,1)S(1)} %message.8), channel_id=1, source_target_pairs={{0,3},{1,4},{2,7},{3,0},{4,1},{5,6},{6,5},{7,2},{8,13},{9,10},{10,... | collective-permute-start | bytes 430088 | tf_op jit(solution)/shard_map/ppermute | solution.py:411
  23.1 4.6 %collective-permute-start.8 = (bf16[560,128]{1,0:T(8,128)(2,1)S(1)}, bf16[560,128]{1,0:T(8,128)(2,1)S(1)}, u32[]{:S(2)}, u32[]{:S(2)}) collective-permute-start(bf16[560,128]{1,0:T(8,128)(2,1)S(1)} %message.10), channel_id=1, source_target_pairs={{0,5},{1,2},{2,1},{3,6},{4,7},{5,0},{6,3},{7,4},{8,11},{9,12},{10,... | collective-permute-start | bytes 430088 | tf_op jit(solution)/shard_map/ppermute | solution.py:411
  27.8 4.5 %collective-permute-start.9 = (bf16[496,128]{1,0:T(8,128)(2,1)S(1)}, bf16[496,128]{1,0:T(8,128)(2,1)S(1)}, u32[]{:S(2)}, u32[]{:S(2)}) collective-permute-start(bf16[496,128]{1,0:T(8,128)(2,1)S(1)} %message.11.refs_0_), channel_id=1, source_target_pairs={{0,9},{1,24},{2,27},{3,10},{4,29},{5,12},{6,15},{7,30},{8,17},{9,0... | collective-permute-start | bytes 380936 | tf_op jit(solution)/shard_map/ppermute | solution.py:411
  32.3 6.7 %collective-permute-start.10 = (bf16[496,128]{1,0:T(8,128)(2,1)S(1)}, bf16[496,128]{1,0:T(8,128)(2,1)S(1)}, u32[]{:S(2)}, u32[]{:S(2)}) collective-permute-start(bf16[496,128]{1,0:T(8,128)(2,1)S(1)} %message.12.refs_0_), channel_id=1, source_target_pairs={{0,25},{1,8},{2,11},{3,26},{4,13},{5,28},{6,31},{7,14},{8,1},{9,16... | collective-permute-start | bytes 380936 | tf_op jit(solution)/shard_map/ppermute | solution.py:411
  39.1 5.0 %collective-permute-start.11 = (bf16[512,128]{1,0:T(8,128)(2,1)S(1)}, bf16[512,128]{1,0:T(8,128)(2,1)S(1)}, u32[]{:S(2)}, u32[]{:S(2)}) collective-permute-start(bf16[512,128]{1,0:T(8,128)(2,1)S(1)} %message.13.refs_0_), channel_id=1, source_target_pairs={{0,5},{1,2},{2,1},{3,6},{4,7},{5,0},{6,3},{7,4},{8,11},{9,12},{10,... | collective-permute-start | bytes 393224 | tf_op jit(solution)/shard_map/ppermute | solution.py:411
  41.5 7.3 %collective-permute-start.12 = (bf16[512,128]{1,0:T(8,128)(2,1)S(1)}, bf16[512,128]{1,0:T(8,128)(2,1)S(1)}, u32[]{:S(2)}, u32[]{:S(2)}) collective-permute-start(bf16[512,128]{1,0:T(8,128)(2,1)S(1)} %message.13.refs_0_), channel_id=1, source_target_pairs={{0,3},{1,4},{2,7},{3,0},{4,1},{5,6},{6,5},{7,2},{8,13},{9,10},{10,... | collective-permute-start | bytes 393224 | tf_op jit(solution)/shard_map/ppermute | solution.py:411
  44.2 5.9 %collective-permute-start.13 = (bf16[432,128]{1,0:T(8,128)(2,1)S(1)}, bf16[432,128]{1,0:T(8,128)(2,1)S(1)}, u32[]{:S(2)}, u32[]{:S(2)}) collective-permute-start(bf16[432,128]{1,0:T(8,128)(2,1)S(1)} %get-tuple-element.51), channel_id=1, source_target_pairs={{0,3},{1,4},{2,7},{3,0},{4,1},{5,6},{6,5},{7,2},{8,13},{9,10},{10,... | collective-permute-start | bytes 331784 | tf_op jit(solution)/shard_map/ppermute | solution.py:411
  47.6 2.4 %collective-permute-start.14 = (bf16[512,128]{1,0:T(8,128)(2,1)S(1)}, bf16[512,128]{1,0:T(8,128)(2,1)S(1)}, u32[]{:S(2)}, u32[]{:S(2)}) collective-permute-start(bf16[512,128]{1,0:T(8,128)(2,1)S(1)} %message.13.refs_0_), channel_id=1, source_target_pairs={{0,1},{1,0},{2,3},{3,2},{4,5},{5,4},{6,7},{7,6},{8,9},{9,8},{10,11... | collective-permute-start | bytes 393224 | tf_op jit(solution)/shard_map/ppermute | solution.py:411
  48.8 1.6 %collective-permute-start.16 = (bf16[512,128]{1,0:T(8,128)(2,1)S(1)}, bf16[512,128]{1,0:T(8,128)(2,1)S(1)}, u32[]{:S(2)}, u32[]{:S(2)}) collective-permute-start(bf16[512,128]{1,0:T(8,128)(2,1)S(1)} %message.15.refs_2_), channel_id=1, source_target_pairs={{0,1},{1,0},{2,3},{3,2},{4,5},{5,4},{6,7},{7,6},{8,9},{9,8},{10,11... | collective-permute-start | bytes 393224 | tf_op jit(solution)/shard_map/ppermute | solution.py:411
  49.4 1.3 %collective-permute-start.15 = (bf16[512,128]{1,0:T(8,128)(2,1)S(1)}, bf16[512,128]{1,0:T(8,128)(2,1)S(1)}, u32[]{:S(2)}, u32[]{:S(2)}) collective-permute-start(bf16[512,128]{1,0:T(8,128)(2,1)S(1)} %collective-permute-done.11.refs_0_.line_ref.refs_1_), channel_id=1, source_target_pairs={{0,1},{1,0},{2,3},{3,2},{4,5},{5,4},{6,7},{7,6},{8,9},{9,8},{10,11... | collective-permute-start | bytes 393224 | tf_op jit(solution)/shard_map/ppermute | solution.py:411
  50.0 1.3 %collective-permute-start.17 = (bf16[432,128]{1,0:T(8,128)(2,1)S(1)}, bf16[432,128]{1,0:T(8,128)(2,1)S(1)}, u32[]{:S(2)}, u32[]{:S(2)}) collective-permute-start(bf16[432,128]{1,0:T(8,128)(2,1)S(1)} %collective-permute-done.13.refs_3_), channel_id=1, source_target_pairs={{0,1},{1,0},{2,3},{3,2},{4,5},{5,4},{6,7},{7,6},{8,9},{9,8},{10,11... | collective-permute-start | bytes 331784 | tf_op jit(solution)/shard_map/ppermute | solution.py:411

commit v5 on v4

--- a/solution.py
+++ b/solution.py
@@ -233,10 +233,38 @@
     pre_ref[...] = pre + jnp.concatenate([product(slice(1, SIDE), 2), edge], axis=0)
 
 
+def write_terms(cols_ref, ends_ref, gradient, start, stop, terms_ref, first=0):
+    channels = gradient.shape[1]
+    inner = (SIDE - 1) * PLANE
+    for dx in range(3):
+        low, high = max(start, TAPS * dx), min(stop, TAPS * (dx + 1))
+        if low >= high:
+            continue
+        lanes = slice((low - TAPS * dx) * channels, (high - TAPS * dx) * channels)
+
+        def term(planes, gradient):
+            return contract(planes.reshape(gradient.shape[0], -1), gradient, 0, 0)
+
+        if dx == 0:
+            total = term(cols_ref[: SIDE - 1, :, lanes], gradient[PLANE:])
+            total = total + term(ends_ref[0, :, lanes], gradient[:PLANE])
+        elif dx == 1:
+            total = term(cols_ref[:, :, lanes], gradient)
+        else:
+            total = term(cols_ref[1:, :, lanes], gradient[:inner])
+            total = total + term(ends_ref[1, :, lanes], gradient[inner:])
+        terms_ref[(low - first) * channels : (high - first) * channels] = total
+
+
+def for_quarter(body):
+    for i in range(PARTS // 2):
+        pl.when((part_index(PARTS - 2) >> 1) == i)(functools.partial(body, i))
+
+
 def tile_kernel(
     cols_ref, pre_ref, mask_ref, sums_ref, head_ref, weight_ref, x_next_ref, x_pair_ref,
-    grad_ref, next_ref, edge_ref, keep_ref, first_ref, rest_ref,
-    ends_ref, terms_ref,
+    grad_ref, ends_ref, first_ref,
+    terms_ref,
 ):
     channels = cols_ref.shape[2] // TAPS
     classes = head_ref.shape[0]
@@ -263,33 +291,47 @@
     heads = jnp.concatenate([head_ref[...]] * 3, axis=0)
     pieces = jnp.concatenate([piece.astype(F32) for piece in split3(slope_logits)], axis=0)
     dhidden = contract(pieces.T.astype(BF16), heads, 1, 0)
-    gradient = dhidden * slope
-    rounded = gradient.astype(BF16)
+    rounded = (dhidden * slope).astype(BF16)
     grad_ref[...] = rounded.reshape(SIDE, PLANE, channels)
-    low_y, high_y = y_faces(lambda x: gradient[x * PLANE : (x + 1) * PLANE])
-    ends = gradient[:PLANE], gradient[voxels - PLANE :]
+    length = first_ref.shape[0] // 2
+
+    def parts(i):
+        start = 2 * length * i // channels
+        stop = -(-2 * length * (i + 1) // channels)
+        write_terms(cols_ref, ends_ref, rounded, start, stop, terms_ref, start)
+        for r in range(2):
+            row = 2 * length * i - start * channels + (part_index(PARTS - 2 + r) & 1) * length
+            part = terms_ref[pl.ds(pl.multiple_of(row, 16), length)]
+            first_ref[r * length : (r + 1) * length] = part.astype(BF16)
+
+    for_quarter(parts)
+
+
+def terms_kernel(
+    cols_ref, ends_ref, grad_ref, next_ref, edge_ref, keep_ref, rest_ref, terms_ref
+):
+    channels = grad_ref.shape[2]
+    length = terms_ref.shape[0] // PARTS
+    gradient = grad_ref[...].reshape(-1, channels)
+    low_y, high_y = y_faces(lambda x: grad_ref[x].astype(F32))
+    ends = grad_ref[0].astype(F32), grad_ref[SIDE - 1].astype(F32)
     pair_ref = rest_ref.at[rest_ref.shape[0] - PLANE :]
     store_faces(*ends, low_y, high_y, pair_ref, next_ref, edge_ref)
 
-    def term(planes, gradient):
-        return contract(planes.reshape(-1, wide), gradient, 0, 0)
-
-    terms_ref[:wide] = term(cols_ref[: SIDE - 1], rounded[PLANE:]) + term(
-        ends_ref[0], rounded[:PLANE]
-    )
-    terms_ref[wide : 2 * wide] = term(cols_ref[...], rounded)
-    terms_ref[2 * wide :] = term(cols_ref[1:], rounded[:inner]) + term(
-        ends_ref[1], rounded[inner:]
-    )
-    length = terms_ref.shape[0] // PARTS
-    for r in range(PARTS):
+    def parts(i):
+        stop = -(-2 * length * i // channels)
+        start = 2 * length * (i + 1) // channels
+        write_terms(cols_ref, ends_ref, gradient, 0, stop, terms_ref)
+        write_terms(cols_ref, ends_ref, gradient, start, 3 * TAPS, terms_ref)
+
+    for_quarter(parts)
+    for r in range(PARTS - 2):
         part = terms_ref[pl.ds(pl.multiple_of(part_index(r) * length, 16), length)]
-        row = (r % 2) * length
         if r < PARTS // 2:
             keep_ref[r * length : (r + 1) * length] = part
         else:
-            send_ref = rest_ref if r < PARTS - 2 else first_ref
-            send_ref[row : row + length] = part.astype(BF16)
+            row = (r - PARTS // 2) * length
+            rest_ref[row : row + length] = part.astype(BF16)
 
 
 def lane_of(tx, ty):
@@ -523,22 +565,25 @@
         fetched=len(fetched),
     )
     part = kernels * channels // PARTS
-    gradient, g_next, g_edges, keep, first, rest = call(
+    ends = shape((2, PLANE, TAPS * channels), BF16)
+    gradient, ends, first = call(
         tile_kernel,
+        (shape((SIDE, PLANE, channels), BF16), ends, shape((2 * part, channels), BF16)),
+        (tile_cols, pre, mask, sums, head, weight, x_next, x_pair),
+        (pltpu.VMEM((2 * part + 2 * channels, channels), F32),),
+        name="tile",
+    )
+    g_next, g_edges, keep, rest = call(
+        terms_kernel,
         (
-            shape((SIDE, PLANE, channels), BF16),
             face,
             edges,
             shape((PARTS // 2 * part, channels), F32),
-            shape((2 * part, channels), BF16),
             shape((2 * part + PLANE, channels), BF16),
         ),
-        (tile_cols, pre, mask, sums, head, weight, x_next, x_pair),
-        (
-            pltpu.VMEM((2, PLANE, TAPS * channels), BF16),
-            pltpu.VMEM((kernels * channels, channels), F32),
-        ),
-        name="tile",
+        (tile_cols, ends, gradient),
+        (pltpu.VMEM((kernels * channels, channels), F32),),
+        name="terms",
     )
 
     got_first = exchange_with(first, by_core)
@@ -573,11 +618,8 @@
     kernel = functools.partial(hand_on_edge_kernel, flips, at)
     g_a, g_b, planes = edge_faces(kernel, g_edges, (got1, got2, *lines))
     rows = g_a.shape[0]
-    total = message(total + [(rows, add, (g_b, 0))])
+    total, gradient = message(total + [(rows, add, (g_b, 0))], (), (gradient,))
     piece1 = exchange_with(total, second_way)
-    piece2 = exchange_with(total, first_way)
-    onward, gradient = message([(part, add, (piece1, 0))], (), (gradient,))
-    piece3 = exchange_with(onward, first_way)
     back_part = call(
         back_kernel,
         shape((SIDE * PLANE, channels), F32),
@@ -585,7 +627,9 @@
         (cols,),
         name="back",
     )
-    near = message([(part, add, (piece2, 0)), (rows, add, (g_a, 0))], (back_part,))
+    piece2 = exchange_with(message([(part + rows, add, (total, 0))], (back_part,)), first_way)
+    piece3 = exchange_with(message([(part, add, (piece1, 0))]), first_way)
+    near = message([(part, add, (piece2, 0)), (rows, add, (g_a, 0))])
     pieces = (total, piece1, near, piece3)
     others = [exchange_with(piece, by_core) for piece in pieces]
     faces = (back_part, mask, weight, others[2], piece2, piece1, *pieces, *others[:3])

time: 53 us -> 52.1 us (0.983)
  starting transfers between devices: 28.8 us -> 28 us
  waiting for transfers between devices: 14.4 us -> 13.7 us
    ppermute x14, starting transfers between devices: 18.7 us -> 18 us  [exchange_with(): return lax.ppermute(value, ('tx', 'ty'), pairs)]
    ppermute x14, waiting for transfers between devices: 13.5 us -> 12.8 us  [exchange_with(): return lax.ppermute(value, ('tx', 'ty'), pairs)]
    pallas_call x6 -> x7, Pallas kernels: 7.17 us -> 7.6 us  [call(): pl.pallas_call(body, out_shape=outs, in_specs=[pl.BlockSpec(memory_space=...]
  transfers between devices with their start and end apart: 18 -> 18, of which waited for: 12 -> 11; matrix products, arithmetic and copies ran while one was open for 0% -> 0% of each run, Pallas kernels for 8% -> 10%
where the time goes in v5:
time: 52.1 us; the launch traced here: 51.8 us
  starting transfers between devices  28 us (54%)
  waiting for transfers between devices  13.7 us (26%)
  Pallas kernels  9.35 us (18%)
  between operations  0.77 us (1%)
    ppermute x14, starting transfers between devices, exchange_with(): return lax.ppermute(value, ('tx', 'ty'), pairs)  18 us
    ppermute x14, waiting for transfers between devices, exchange_with(): return lax.ppermute(value, ('tx', 'ty'), pairs)  12.8 us
    pallas_call x7, Pallas kernels, call(): pl.pallas_call(body, out_shape=outs, in_specs=[pl.BlockSpec(memory_space=...  7.6 us
    ppermute x1, starting transfers between devices, swap_along_y(): return (got_b, lax.ppermute(a, 'ty', swap_pairs(0, count)))  4.39 us
    ppermute x1, starting transfers between devices, on_device(): x_pair = lax.ppermute(x_pair, 'tx', swap_pairs(0, n_tx))  4.35 us
    pallas_call x1, Pallas kernels, on_device(): pl.pallas_call(norm_kernel, out_shape=(shape((kernels * channels, channel...  1.45 us
  transfers between devices with their start and end apart: 18, of which 11 were waited for; matrix products, arithmetic and copies ran while one was open for 0% of the time, Pallas kernels for 10%

profile of v5, /device:TPU:0, one launch (start us, length us, event | category | flops | bytes accessed | tf_op | source)
XLA Modules:
  0.0 51.8 jit_solution(5592387152131858768)
XLA Ops:
  0.6 1.2 %first_faces.1 = (bf16[64,128]{1,0:T(8,128)(2,1)S(1)}, bf16[64,128]{1,0:T(8,128)(2,1)S(1)}, bf16[2,64,128]{2,1,0:T(8,128)(2,1)S(1)}, f32[8,64,128]{2,1,0:T(8,128)S(1)}, f32[8,64,128]{2,1,0:T(8,128)S(1)}) custom-call(bf16[4,128,128]{2,1,0:T(8,128)(2,1)} %feat_hbm.1, s32[4,128]{1,0:T(4,128)} %occ_hbm.1), custom_call_target="tpu_custom_call" | custom-call | tf_op jit(solution)/shard_map/first_faces/pallas_call | solution.py:31
  1.8 0.7 %collective-permute-start = (bf16[64,128]{1,0:T(8,128)(2,1)S(1)}, bf16[64,128]{1,0:T(8,128)(2,1)S(1)}, u32[]{:S(2)}, u32[]{:S(2)}) collective-permute-start(bf16[64,128]{1,0:T(8,128)(2,1)S(1)} %get-tuple-element.31), channel_id=1, source_target_pairs={{1,2},{2,1},{5,6},{6,5},{9,10},{10,9},{13,14},{14,13},{17,18},{18,... | collective-permute-start | bytes 49160 | tf_op jit(solution)/shard_map/ppermute | solution.py:429
  2.5 4.4 %collective-permute-start.1 = (bf16[64,128]{1,0:T(8,128)(2,1)S(1)}, bf16[64,128]{1,0:T(8,128)(2,1)S(1)}, u32[]{:S(2)}, u32[]{:S(2)}) collective-permute-start(bf16[64,128]{1,0:T(8,128)(2,1)S(1)} %get-tuple-element.32), channel_id=1, source_target_pairs={{0,1},{1,0},{2,3},{3,2},{4,5},{5,4},{6,7},{7,6},{8,9},{9,8},{10,11... | collective-permute-start | bytes 49160 | tf_op jit(solution)/shard_map/ppermute | solution.py:430
  6.9 0.8 %collective-permute-done.1.y_a_ref = bf16[64,128]{1,0:T(8,128)(2,1)S(1)} collective-permute-done((bf16[64,128]{1,0:T(8,128)(2,1)S(1)}, bf16[64,128]{1,0:T(8,128)(2,1)S(1)}, u32[]{:S(2)}, u32[]{:S(2)}) %collective-permute-start.1) | collective-permute-done | bytes 16416 | tf_op jit(solution)/shard_map/ppermute | solution.py:430
  7.7 0.7 %collective-permute-start.2 = (bf16[80,128]{1,0:T(8,128)(2,1)S(1)}, bf16[80,128]{1,0:T(8,128)(2,1)S(1)}, u32[]{:S(2)}, u32[]{:S(2)}) collective-permute-start(bf16[80,128]{1,0:T(8,128)(2,1)S(1)} %get-tuple-element.40), channel_id=1, source_target_pairs={{4,8},{8,4},{12,16},{16,12},{20,24},{24,20},{5,9},{9,5},{13,17},{1... | collective-permute-start | bytes 61448 | tf_op jit(solution)/shard_map/ppermute | solution.py:550
  8.4 4.3 %collective-permute-start.3 = (bf16[80,128]{1,0:T(8,128)(2,1)S(1)}, bf16[80,128]{1,0:T(8,128)(2,1)S(1)}, u32[]{:S(2)}, u32[]{:S(2)}) collective-permute-start(bf16[80,128]{1,0:T(8,128)(2,1)S(1)} %get-tuple-element.41), channel_id=1, source_target_pairs={{0,4},{4,0},{8,12},{12,8},{16,20},{20,16},{24,28},{28,24},{1,5},{5... | collective-permute-start | bytes 61448 | tf_op jit(solution)/shard_map/ppermute | solution.py:551
  12.8 2.3 %main.1 = (bf16[8,64,1152]{2,1,0:T(8,128)(2,1)S(1)}, f32[512,128]{1,0:T(8,128)S(1)}, f32[32,512]{1,0:T(8,128)S(1)}, bf16[16,128]{1,0:T(8,128)(2,1)S(1)}, bf16[27,128,128]{2,1,0:T(8,128)(2,1)S(1)}) custom-call(s32[1,1024]{1,0:T(1,128)} %bitcast.2, bf16[16,1024]{1,0:T(8,128)(2,1)} %teach_hbm.1, bf16[16,128]{1,0:T(8,128)(2,1)} %head_hbm.1, ...), custom_call_target="tpu_custom_call" | custom-call | tf_op jit(solution)/shard_map/main/pallas_call | solution.py:31
  15.1 1.3 %tile.1 = (bf16[8,64,128]{2,1,0:T(8,128)(2,1)S(1)}, bf16[2,64,1152]{2,1,0:T(8,128)(2,1)S(1)}, bf16[864,128]{1,0:T(8,128)(2,1)S(1)}) custom-call(bf16[8,64,1152]{2,1,0:T(8,128)(2,1)S(1)} %get-tuple-element.33.cols_ref, f32[512,128]{1,0:T(8,128)S(1)} %get-tuple-element.34.pre_ref, f32[8,64,128]{2,1,0:T(8,128)S(1)} %get-tuple-element.35.mask_ref, ...), custom_call_target="tpu_custom_call" | custom-call | tf_op jit(solution)/shard_map/tile/pallas_call | solution.py:31
  16.4 1.2 %terms.1 = (bf16[64,128]{1,0:T(8,128)(2,1)S(1)}, bf16[2,64,128]{2,1,0:T(8,128)(2,1)S(1)}, f32[1728,128]{1,0:T(8,128)S(1)}, bf16[928,128]{1,0:T(8,128)(2,1)S(1)}) custom-call(bf16[8,64,1152]{2,1,0:T(8,128)(2,1)S(1)} %get-tuple-element.33.cols_ref, bf16[2,64,1152]{2,1,0:T(8,128)(2,1)S(1)} %get-tuple-element.42.ends_ref, ...), custom_call_target="tpu_custom_call" | custom-call | tf_op jit(solution)/shard_map/terms/pallas_call | solution.py:31
  17.6 0.6 %collective-permute-start.4 = (bf16[928,128]{1,0:T(8,128)(2,1)S(1)}, bf16[928,128]{1,0:T(8,128)(2,1)S(1)}, u32[]{:S(2)}, u32[]{:S(2)}) collective-permute-start(bf16[928,128]{1,0:T(8,128)(2,1)S(1)} %get-tuple-element.45), channel_id=1, source_target_pairs={{0,1},{1,0},{2,3},{3,2},{4,5},{5,4},{6,7},{7,6},{8,9},{9,8},{10,11... | collective-permute-start | bytes 712712 | tf_op jit(solution)/shard_map/ppermute | solution.py:453
  18.2 1.8 %collective-permute-start.7 = (bf16[432,128]{1,0:T(8,128)(2,1)S(1)}, bf16[432,128]{1,0:T(8,128)(2,1)S(1)}, u32[]{:S(2)}, u32[]{:S(2)}) collective-permute-start(bf16[432,128]{1,0:T(8,128)(2,1)S(1)} %message.10), channel_id=1, source_target_pairs={{0,3},{1,4},{2,7},{3,0},{4,1},{5,6},{6,5},{7,2},{8,13},{9,10},{10,... | collective-permute-start | bytes 331784 | tf_op jit(solution)/shard_map/ppermute | solution.py:453
  20.0 1.4 %collective-permute-start.6 = (bf16[560,128]{1,0:T(8,128)(2,1)S(1)}, bf16[560,128]{1,0:T(8,128)(2,1)S(1)}, u32[]{:S(2)}, u32[]{:S(2)}) collective-permute-start(bf16[560,128]{1,0:T(8,128)(2,1)S(1)} %message.9), channel_id=1, source_target_pairs={{0,3},{1,4},{2,7},{3,0},{4,1},{5,6},{6,5},{7,2},{8,13},{9,10},{10,... | collective-permute-start | bytes 430088 | tf_op jit(solution)/shard_map/ppermute | solution.py:453
  21.5 1.0 %collective-permute-done.7.refs_2_ = bf16[432,128]{1,0:T(8,128)(2,1)S(1)} collective-permute-done((bf16[432,128]{1,0:T(8,128)(2,1)S(1)}, bf16[432,128]{1,0:T(8,128)(2,1)S(1)}, u32[]{:S(2)}, u32[]{:S(2)}) %collective-permute-start.7) | collective-permute-done | bytes 110624 | tf_op jit(solution)/shard_map/ppermute | solution.py:453
  22.5 1.9 %collective-permute-start.8 = (bf16[560,128]{1,0:T(8,128)(2,1)S(1)}, bf16[560,128]{1,0:T(8,128)(2,1)S(1)}, u32[]{:S(2)}, u32[]{:S(2)}) collective-permute-start(bf16[560,128]{1,0:T(8,128)(2,1)S(1)} %message.11), channel_id=1, source_target_pairs={{0,5},{1,2},{2,1},{3,6},{4,7},{5,0},{6,3},{7,4},{8,11},{9,12},{10,... | collective-permute-start | bytes 430088 | tf_op jit(solution)/shard_map/ppermute | solution.py:453
  24.4 0.2 collective-permute-done.6.refs_2_.got1_ref
  24.6 2.5 %collective-permute-done.8.refs_3_.got2_ref = bf16[560,128]{1,0:T(8,128)(2,1)S(1)} collective-permute-done((bf16[560,128]{1,0:T(8,128)(2,1)S(1)}, bf16[560,128]{1,0:T(8,128)(2,1)S(1)}, u32[]{:S(2)}, u32[]{:S(2)}) %collective-permute-start.8) | collective-permute-done | bytes 143392 | tf_op jit(solution)/shard_map/ppermute | solution.py:453
  27.2 1.9 %collective-permute-start.9 = (bf16[496,128]{1,0:T(8,128)(2,1)S(1)}, bf16[496,128]{1,0:T(8,128)(2,1)S(1)}, u32[]{:S(2)}, u32[]{:S(2)}) collective-permute-start(bf16[496,128]{1,0:T(8,128)(2,1)S(1)} %message.12.refs_0_), channel_id=1, source_target_pairs={{0,9},{1,24},{2,27},{3,10},{4,29},{5,12},{6,15},{7,30},{8,17},{9,0... | collective-permute-start | bytes 380936 | tf_op jit(solution)/shard_map/ppermute | solution.py:453
  29.2 2.6 %collective-permute-done.9.refs_1_.refs_0_ = bf16[496,128]{1,0:T(8,128)(2,1)S(1)} collective-permute-done((bf16[496,128]{1,0:T(8,128)(2,1)S(1)}, bf16[496,128]{1,0:T(8,128)(2,1)S(1)}, u32[]{:S(2)}, u32[]{:S(2)}) %collective-permute-start.9) | collective-permute-done | bytes 127008 | tf_op jit(solution)/shard_map/ppermute | solution.py:453
  31.8 4.1 %collective-permute-start.10 = (bf16[496,128]{1,0:T(8,128)(2,1)S(1)}, bf16[496,128]{1,0:T(8,128)(2,1)S(1)}, u32[]{:S(2)}, u32[]{:S(2)}) collective-permute-start(bf16[496,128]{1,0:T(8,128)(2,1)S(1)} %message.13.refs_0_), channel_id=1, source_target_pairs={{0,25},{1,8},{2,11},{3,26},{4,13},{5,28},{6,31},{7,14},{8,1},{9,16... | collective-permute-start | bytes 380936 | tf_op jit(solution)/shard_map/ppermute | solution.py:453
  35.9 2.8 %collective-permute-done.10.refs_1_ = bf16[496,128]{1,0:T(8,128)(2,1)S(1)} collective-permute-done((bf16[496,128]{1,0:T(8,128)(2,1)S(1)}, bf16[496,128]{1,0:T(8,128)(2,1)S(1)}, u32[]{:S(2)}, u32[]{:S(2)}) %collective-permute-start.10) | collective-permute-done | bytes 127008 | tf_op jit(solution)/shard_map/ppermute | solution.py:453
  38.7 3.4 %collective-permute-start.11 = (bf16[512,128]{1,0:T(8,128)(2,1)S(1)}, bf16[512,128]{1,0:T(8,128)(2,1)S(1)}, u32[]{:S(2)}, u32[]{:S(2)}) collective-permute-start(bf16[512,128]{1,0:T(8,128)(2,1)S(1)} %get-tuple-element.50.refs_0_), channel_id=1, source_target_pairs={{0,5},{1,2},{2,1},{3,6},{4,7},{5,0},{6,3},{7,4},{8,11},{9,12},{10,... | collective-permute-start | bytes 393224 | tf_op jit(solution)/shard_map/ppermute | solution.py:453
  42.1 1.1 %back.1.refs_1_.part_ref = f32[512,128]{1,0:T(8,128)S(1)} custom-call(bf16[8,64,128]{2,1,0:T(8,128)(2,1)S(1)} %get-tuple-element.51.grad_ref, bf16[2,64,128]{2,1,0:T(8,128)(2,1)S(1)} %get-tuple-element.52.planes_ref, bf16[27,128,128]{2,1,0:T(8,128)(2,1)S(1)} %get-tuple-element.38.weight_ref), custom_call_target="tpu_custom_call" | custom-call | tf_op jit(solution)/shard_map/back/pallas_call | solution.py:31
  43.4 1.4 %collective-permute-done.11.refs_0_.line_ref.refs_1_ = bf16[512,128]{1,0:T(8,128)(2,1)S(1)} collective-permute-done((bf16[512,128]{1,0:T(8,128)(2,1)S(1)}, bf16[512,128]{1,0:T(8,128)(2,1)S(1)}, u32[]{:S(2)}, u32[]{:S(2)}) %collective-permute-start.11) | collective-permute-done | bytes 131104 | tf_op jit(solution)/shard_map/ppermute | solution.py:453
  44.8 0.8 %collective-permute-start.13 = (bf16[432,128]{1,0:T(8,128)(2,1)S(1)}, bf16[432,128]{1,0:T(8,128)(2,1)S(1)}, u32[]{:S(2)}, u32[]{:S(2)}) collective-permute-start(bf16[432,128]{1,0:T(8,128)(2,1)S(1)} %message.17), channel_id=1, source_target_pairs={{0,3},{1,4},{2,7},{3,0},{4,1},{5,6},{6,5},{7,2},{8,13},{9,10},{10,... | collective-permute-start | bytes 331784 | tf_op jit(solution)/shard_map/ppermute | solution.py:453
  45.7 1.1 %collective-permute-start.14 = (bf16[512,128]{1,0:T(8,128)(2,1)S(1)}, bf16[512,128]{1,0:T(8,128)(2,1)S(1)}, u32[]{:S(2)}, u32[]{:S(2)}) collective-permute-start(bf16[512,128]{1,0:T(8,128)(2,1)S(1)} %get-tuple-element.50.refs_0_), channel_id=1, source_target_pairs={{0,1},{1,0},{2,3},{3,2},{4,5},{5,4},{6,7},{7,6},{8,9},{9,8},{10,11... | collective-permute-start | bytes 393224 | tf_op jit(solution)/shard_map/ppermute | solution.py:453
  46.8 1.0 %collective-permute-done.12.refs_0_.far_ref = bf16[512,128]{1,0:T(8,128)(2,1)S(1)} collective-permute-done((bf16[512,128]{1,0:T(8,128)(2,1)S(1)}, bf16[512,128]{1,0:T(8,128)(2,1)S(1)}, u32[]{:S(2)}, u32[]{:S(2)}) %collective-permute-start.12) | collective-permute-done | bytes 131104 | tf_op jit(solution)/shard_map/ppermute | solution.py:453
  47.8 0.4 collective-permute-start.16
  48.4 0.7 %collective-permute-done.13.refs_3_ = bf16[432,128]{1,0:T(8,128)(2,1)S(1)} collective-permute-done((bf16[432,128]{1,0:T(8,128)(2,1)S(1)}, bf16[432,128]{1,0:T(8,128)(2,1)S(1)}, u32[]{:S(2)}, u32[]{:S(2)}) %collective-permute-start.13) | collective-permute-done | bytes 110624 | tf_op jit(solution)/shard_map/ppermute | solution.py:453
  49.2 0.3 collective-permute-done.15.refs_5_
  49.6 0.5 %y_faces.1 = (bf16[4,128,128]{2,1,0:T(8,128)(2,1)S(1)}, f32[8,128]{1,0:T(8,128)S(1)}) custom-call(f32[512,128]{1,0:T(8,128)S(1)} %back.1.refs_1_.part_ref, f32[8,64,128]{2,1,0:T(8,128)S(1)} %get-tuple-element.35.mask_ref, bf16[27,128,128]{2,1,0:T(8,128)(2,1)S(1)} %get-tuple-element.38.weight_ref, ...), custom_call_target="tpu_custom_call" | custom-call | tf_op jit(solution)/shard_map/y_faces/pallas_call | solution.py:31
  50.1 0.3 collective-permute-done.17.refs_7_
  50.4 1.4 %normalise.1 = (f32[3456,128]{1,0:T(8,128)}, bf16[4,128,128]{2,1,0:T(8,128)(2,1)}) custom-call(bf16[512,128]{1,0:T(8,128)(2,1)S(1)} %get-tuple-element.50.refs_0_, bf16[512,128]{1,0:T(8,128)(2,1)S(1)} %collective-permute-done.11.refs_0_.line_ref.refs_1_, bf16[512,128]{1,0:T(8,128)(2,1)S(1)} %message.16.refs_2_, ...), custom_call_target="tpu_custom_call" | custom-call | tf_op jit(solution)/shard_map/normalise/pallas_call | solution.py:648
  (22 shorter events, 0.8 us)
Async XLA Ops:
  1.8 5.1 %collective-permute-start = (bf16[64,128]{1,0:T(8,128)(2,1)S(1)}, bf16[64,128]{1,0:T(8,128)(2,1)S(1)}, u32[]{:S(2)}, u32[]{:S(2)}) collective-permute-start(bf16[64,128]{1,0:T(8,128)(2,1)S(1)} %get-tuple-element.31), channel_id=1, source_target_pairs={{1,2},{2,1},{5,6},{6,5},{9,10},{10,9},{13,14},{14,13},{17,18},{18,... | collective-permute-start | bytes 49160 | tf_op jit(solution)/shard_map/ppermute | solution.py:429
  2.5 5.2 %collective-permute-start.1 = (bf16[64,128]{1,0:T(8,128)(2,1)S(1)}, bf16[64,128]{1,0:T(8,128)(2,1)S(1)}, u32[]{:S(2)}, u32[]{:S(2)}) collective-permute-start(bf16[64,128]{1,0:T(8,128)(2,1)S(1)} %get-tuple-element.32), channel_id=1, source_target_pairs={{0,1},{1,0},{2,3},{3,2},{4,5},{5,4},{6,7},{7,6},{8,9},{9,8},{10,11... | collective-permute-start | bytes 49160 | tf_op jit(solution)/shard_map/ppermute | solution.py:430
  7.7 7.3 %collective-permute-start.2 = (bf16[80,128]{1,0:T(8,128)(2,1)S(1)}, bf16[80,128]{1,0:T(8,128)(2,1)S(1)}, u32[]{:S(2)}, u32[]{:S(2)}) collective-permute-start(bf16[80,128]{1,0:T(8,128)(2,1)S(1)} %get-tuple-element.40), channel_id=1, source_target_pairs={{4,8},{8,4},{12,16},{16,12},{20,24},{24,20},{5,9},{9,5},{13,17},{1... | collective-permute-start | bytes 61448 | tf_op jit(solution)/shard_map/ppermute | solution.py:550
  8.4 6.6 %collective-permute-start.3 = (bf16[80,128]{1,0:T(8,128)(2,1)S(1)}, bf16[80,128]{1,0:T(8,128)(2,1)S(1)}, u32[]{:S(2)}, u32[]{:S(2)}) collective-permute-start(bf16[80,128]{1,0:T(8,128)(2,1)S(1)} %get-tuple-element.41), channel_id=1, source_target_pairs={{0,4},{4,0},{8,12},{12,8},{16,20},{20,16},{24,28},{28,24},{1,5},{5... | collective-permute-start | bytes 61448 | tf_op jit(solution)/shard_map/ppermute | solution.py:551
  16.3 1.9 %collective-permute-start.5 = (bf16[864,128]{1,0:T(8,128)(2,1)S(1)}, bf16[864,128]{1,0:T(8,128)(2,1)S(1)}, u32[]{:S(2)}, u32[]{:S(2)}) collective-permute-start(bf16[864,128]{1,0:T(8,128)(2,1)S(1)} %get-tuple-element.46), channel_id=1, source_target_pairs={{0,1},{1,0},{2,3},{3,2},{4,5},{5,4},{6,7},{7,6},{8,9},{9,8},{10,11... | collective-permute-start | bytes 663560 | tf_op jit(solution)/shard_map/ppermute | solution.py:453
  17.6 2.4 %collective-permute-start.4 = (bf16[928,128]{1,0:T(8,128)(2,1)S(1)}, bf16[928,128]{1,0:T(8,128)(2,1)S(1)}, u32[]{:S(2)}, u32[]{:S(2)}) collective-permute-start(bf16[928,128]{1,0:T(8,128)(2,1)S(1)} %get-tuple-element.45), channel_id=1, source_target_pairs={{0,1},{1,0},{2,3},{3,2},{4,5},{5,4},{6,7},{7,6},{8,9},{9,8},{10,11... | collective-permute-start | bytes 712712 | tf_op jit(solution)/shard_map/ppermute | solution.py:453
  18.2 4.2 %collective-permute-start.7 = (bf16[432,128]{1,0:T(8,128)(2,1)S(1)}, bf16[432,128]{1,0:T(8,128)(2,1)S(1)}, u32[]{:S(2)}, u32[]{:S(2)}) collective-permute-start(bf16[432,128]{1,0:T(8,128)(2,1)S(1)} %message.10), channel_id=1, source_target_pairs={{0,3},{1,4},{2,7},{3,0},{4,1},{5,6},{6,5},{7,2},{8,13},{9,10},{10,... | collective-permute-start | bytes 331784 | tf_op jit(solution)/shard_map/ppermute | solution.py:453
  20.0 4.6 %collective-permute-start.6 = (bf16[560,128]{1,0:T(8,128)(2,1)S(1)}, bf16[560,128]{1,0:T(8,128)(2,1)S(1)}, u32[]{:S(2)}, u32[]{:S(2)}) collective-permute-start(bf16[560,128]{1,0:T(8,128)(2,1)S(1)} %message.9), channel_id=1, source_target_pairs={{0,3},{1,4},{2,7},{3,0},{4,1},{5,6},{6,5},{7,2},{8,13},{9,10},{10,... | collective-permute-start | bytes 430088 | tf_op jit(solution)/shard_map/ppermute | solution.py:453
  22.5 4.6 %collective-permute-start.8 = (bf16[560,128]{1,0:T(8,128)(2,1)S(1)}, bf16[560,128]{1,0:T(8,128)(2,1)S(1)}, u32[]{:S(2)}, u32[]{:S(2)}) collective-permute-start(bf16[560,128]{1,0:T(8,128)(2,1)S(1)} %message.11), channel_id=1, source_target_pairs={{0,5},{1,2},{2,1},{3,6},{4,7},{5,0},{6,3},{7,4},{8,11},{9,12},{10,... | collective-permute-start | bytes 430088 | tf_op jit(solution)/shard_map/ppermute | solution.py:453
  27.2 4.5 %collective-permute-start.9 = (bf16[496,128]{1,0:T(8,128)(2,1)S(1)}, bf16[496,128]{1,0:T(8,128)(2,1)S(1)}, u32[]{:S(2)}, u32[]{:S(2)}) collective-permute-start(bf16[496,128]{1,0:T(8,128)(2,1)S(1)} %message.12.refs_0_), channel_id=1, source_target_pairs={{0,9},{1,24},{2,27},{3,10},{4,29},{5,12},{6,15},{7,30},{8,17},{9,0... | collective-permute-start | bytes 380936 | tf_op jit(solution)/shard_map/ppermute | solution.py:453
  31.8 6.9 %collective-permute-start.10 = (bf16[496,128]{1,0:T(8,128)(2,1)S(1)}, bf16[496,128]{1,0:T(8,128)(2,1)S(1)}, u32[]{:S(2)}, u32[]{:S(2)}) collective-permute-start(bf16[496,128]{1,0:T(8,128)(2,1)S(1)} %message.13.refs_0_), channel_id=1, source_target_pairs={{0,25},{1,8},{2,11},{3,26},{4,13},{5,28},{6,31},{7,14},{8,1},{9,16... | collective-permute-start | bytes 380936 | tf_op jit(solution)/shard_map/ppermute | solution.py:453
  38.7 6.0 %collective-permute-start.11 = (bf16[512,128]{1,0:T(8,128)(2,1)S(1)}, bf16[512,128]{1,0:T(8,128)(2,1)S(1)}, u32[]{:S(2)}, u32[]{:S(2)}) collective-permute-start(bf16[512,128]{1,0:T(8,128)(2,1)S(1)} %get-tuple-element.50.refs_0_), channel_id=1, source_target_pairs={{0,5},{1,2},{2,1},{3,6},{4,7},{5,0},{6,3},{7,4},{8,11},{9,12},{10,... | collective-permute-start | bytes 393224 | tf_op jit(solution)/shard_map/ppermute | solution.py:453
  43.3 4.5 %collective-permute-start.12 = (bf16[512,128]{1,0:T(8,128)(2,1)S(1)}, bf16[512,128]{1,0:T(8,128)(2,1)S(1)}, u32[]{:S(2)}, u32[]{:S(2)}) collective-permute-start(bf16[512,128]{1,0:T(8,128)(2,1)S(1)} %message.15), channel_id=1, source_target_pairs={{0,3},{1,4},{2,7},{3,0},{4,1},{5,6},{6,5},{7,2},{8,13},{9,10},{10,... | collective-permute-start | bytes 393224 | tf_op jit(solution)/shard_map/ppermute | solution.py:453
  44.8 4.2 %collective-permute-start.13 = (bf16[432,128]{1,0:T(8,128)(2,1)S(1)}, bf16[432,128]{1,0:T(8,128)(2,1)S(1)}, u32[]{:S(2)}, u32[]{:S(2)}) collective-permute-start(bf16[432,128]{1,0:T(8,128)(2,1)S(1)} %message.17), channel_id=1, source_target_pairs={{0,3},{1,4},{2,7},{3,0},{4,1},{5,6},{6,5},{7,2},{8,13},{9,10},{10,... | collective-permute-start | bytes 331784 | tf_op jit(solution)/shard_map/ppermute | solution.py:453
  45.7 3.6 %collective-permute-start.14 = (bf16[512,128]{1,0:T(8,128)(2,1)S(1)}, bf16[512,128]{1,0:T(8,128)(2,1)S(1)}, u32[]{:S(2)}, u32[]{:S(2)}) collective-permute-start(bf16[512,128]{1,0:T(8,128)(2,1)S(1)} %get-tuple-element.50.refs_0_), channel_id=1, source_target_pairs={{0,1},{1,0},{2,3},{3,2},{4,5},{5,4},{6,7},{7,6},{8,9},{9,8},{10,11... | collective-permute-start | bytes 393224 | tf_op jit(solution)/shard_map/ppermute | solution.py:453
  47.8 1.4 %collective-permute-start.16 = (bf16[512,128]{1,0:T(8,128)(2,1)S(1)}, bf16[512,128]{1,0:T(8,128)(2,1)S(1)}, u32[]{:S(2)}, u32[]{:S(2)}) collective-permute-start(bf16[512,128]{1,0:T(8,128)(2,1)S(1)} %message.16.refs_2_), channel_id=1, source_target_pairs={{0,1},{1,0},{2,3},{3,2},{4,5},{5,4},{6,7},{7,6},{8,9},{9,8},{10,11... | collective-permute-start | bytes 393224 | tf_op jit(solution)/shard_map/ppermute | solution.py:453
  48.2 1.3 %collective-permute-start.15 = (bf16[512,128]{1,0:T(8,128)(2,1)S(1)}, bf16[512,128]{1,0:T(8,128)(2,1)S(1)}, u32[]{:S(2)}, u32[]{:S(2)}) collective-permute-start(bf16[512,128]{1,0:T(8,128)(2,1)S(1)} %collective-permute-done.11.refs_0_.line_ref.refs_1_), channel_id=1, source_target_pairs={{0,1},{1,0},{2,3},{3,2},{4,5},{5,4},{6,7},{7,6},{8,9},{9,8},{10,11... | collective-permute-start | bytes 393224 | tf_op jit(solution)/shard_map/ppermute | solution.py:453
  49.0 1.3 %collective-permute-start.17 = (bf16[432,128]{1,0:T(8,128)(2,1)S(1)}, bf16[432,128]{1,0:T(8,128)(2,1)S(1)}, u32[]{:S(2)}, u32[]{:S(2)}) collective-permute-start(bf16[432,128]{1,0:T(8,128)(2,1)S(1)} %collective-permute-done.13.refs_3_), channel_id=1, source_target_pairs={{0,1},{1,0},{2,3},{3,2},{4,5},{5,4},{6,7},{7,6},{8,9},{9,8},{10,11... | collective-permute-start | bytes 331784 | tf_op jit(solution)/shard_map/ppermute | solution.py:453

commit v6 on v5

--- a/solution.py
+++ b/solution.py
@@ -83,35 +83,38 @@
     return low, high
 
 
-def store_faces(low_plane, high_plane, low_y, high_y, pair_ref, next_ref, edge_ref):
-    even = parity("tx")
-    pair_ref[...] = jnp.where(even, high_plane, low_plane).astype(BF16)
-    next_ref[...] = jnp.where(even, low_plane, high_plane).astype(BF16)
-    edge_ref[0] = low_y.astype(BF16)
-    edge_ref[1] = high_y.astype(BF16)
+def occupancy_mask(columns, slot, first, rows, channels):
+    return jnp.broadcast_to(columns[first : first + rows, slot : slot + 1], (rows, channels))
 
 
 def first_faces_kernel(
-    feat_hbm, occ_hbm, b_ref, a_ref, ends_ref, masked_ref, mask_ref, feat_ref, occ_ref, semaphores
+    feat_hbm, occ_hbm, point_hbm, teach_hbm, head_hbm, weight_hbm,
+    b_ref, a_ref, ends_ref, feat_ref, occ_ref, point_ref, teach_ref, head_ref, weight_ref,
+    semaphores,
 ):
-    for copy in fetch((feat_hbm, occ_hbm), (feat_ref, occ_ref), semaphores):
+    sources = (feat_hbm, occ_hbm, point_hbm, teach_hbm, head_hbm, weight_hbm)
+    rooms = (feat_ref, occ_ref, point_ref, teach_ref, head_ref, weight_ref)
+    copies = fetch(sources, rooms, semaphores)
+    for copy in copies[:2]:
         copy.wait()
     columns = occupancy_columns(occ_ref, 8)
-    rows, channels = BY * SIDE, mask_ref.shape[2]
-    for slot in range(GX * GY):
-        x0, row0 = slot_planes(slot)
-        wide = jnp.broadcast_to(columns[:, slot : slot + 1], (columns.shape[0], channels))
-        for a in range(BX):
-            mask = wide[a * rows : (a + 1) * rows]
-            part = feat_ref[slot, a * rows : (a + 1) * rows, :].astype(F32)
-            mask_ref[x0 + a, row0 : row0 + rows, :] = mask
-            masked_ref[x0 + a, row0 : row0 + rows, :] = part * mask
-    low_y, high_y = y_faces(lambda x: masked_ref[x])
+    rows, channels = BY * SIDE, feat_ref.shape[2]
+
+    def masked(x, j, first, count):
+        slot, row = x // BX * GY + j, x % BX * rows + first
+        mask = occupancy_mask(columns, slot, row, count, channels)
+        return feat_ref[slot, row : row + count, :].astype(F32) * mask
+
+    low_y = jnp.concatenate([masked(x, 0, 0, SIDE) for x in range(SIDE)], axis=0)
+    high_y = jnp.concatenate([masked(x, GY - 1, rows - SIDE, SIDE) for x in range(SIDE)], axis=0)
     even = parity("ty")
     a_ref[...] = jnp.where(even, high_y, low_y).astype(BF16)
     b_ref[...] = jnp.where(even, low_y, high_y).astype(BF16)
-    ends_ref[0] = masked_ref[0].astype(BF16)
-    ends_ref[1] = masked_ref[SIDE - 1].astype(BF16)
+    for i, x in enumerate((0, SIDE - 1)):
+        plane = jnp.concatenate([masked(x, j, 0, rows) for j in range(GY)], axis=0)
+        ends_ref[i] = plane.astype(BF16)
+    for copy in copies[2:]:
+        copy.wait()
 
 
 def halo_along_y(b_ref, a_ref):
@@ -158,9 +161,9 @@
     store_edges(low, high, edge_ref, a_ref, b_ref, planes_ref)
 
 
-def picked_face(by_first_way, by_second_way):
+def picked_face(by_first_way, by_core):
     lane = lane_of(lax.axis_index("tx"), lax.axis_index("ty"))
-    return jnp.where(lane == 0, by_second_way.astype(F32), by_first_way.astype(F32))
+    return jnp.where(lane == 0, by_core.astype(F32), by_first_way.astype(F32))
 
 
 def write_columns(plane, cols_ref):
@@ -203,24 +206,23 @@
 
 
 def main_kernel(
-    point_hbm, teach_hbm, head_hbm, weight_hbm, masked_ref, y_b_ref, y_a_ref,
-    cols_ref, pre_ref, sums_ref, head_ref, weight_ref,
-    point_ref, teach_ref, semaphores,
+    feat_ref, occ_ref, point_ref, teach_ref, weight_ref, y_b_ref, y_a_ref,
+    cols_ref, pre_ref, mask_ref, sums_ref,
 ):
-    sources = (point_hbm, teach_hbm, head_hbm, weight_hbm)
-    copies = fetch(sources, (point_ref, teach_ref, head_ref, weight_ref), semaphores)
-    channels = masked_ref.shape[2]
+    rows, channels = BY * SIDE, feat_ref.shape[2]
+    columns = occupancy_columns(occ_ref, 8)
     low, high = halo_along_y(y_b_ref, y_a_ref)
     for x in range(SIDE):
-        rows = slice(x * SIDE, (x + 1) * SIDE)
-        plane = jnp.concatenate([low[rows], masked_ref[x], high[rows]], axis=0)
-        write_columns(plane, cols_ref.at[x])
+        plane = []
+        for j in range(GY):
+            slot, row = x // BX * GY + j, x % BX * rows
+            mask = occupancy_mask(columns, slot, row, rows, channels)
+            mask_ref[x, j * rows : (j + 1) * rows, :] = mask
+            plane.append(feat_ref[slot, row : row + rows, :].astype(F32) * mask)
+        here = slice(x * SIDE, (x + 1) * SIDE)
+        write_columns(jnp.concatenate([low[here], *plane, high[here]], axis=0), cols_ref.at[x])
     wide, inner = TAPS * channels, SIDE - 1
-    for copy in copies[:2]:
-        copy.wait()
     sums_ref[...] = voxel_sums(point_ref, teach_ref)
-    for copy in copies[2:]:
-        copy.wait()
 
     def product(planes, dx):
         window = cols_ref[planes].reshape(-1, wide)
@@ -293,7 +295,11 @@
     dhidden = contract(pieces.T.astype(BF16), heads, 1, 0)
     rounded = (dhidden * slope).astype(BF16)
     grad_ref[...] = rounded.reshape(SIDE, PLANE, channels)
-    length = first_ref.shape[0] // 2
+    length = 3 * TAPS * channels // PARTS
+    even = parity("tx")
+    low, high = rounded[:PLANE].astype(F32), rounded[inner:].astype(F32)
+    first_ref[2 * length : 2 * length + PLANE] = jnp.where(even, high, low).astype(BF16)
+    first_ref[2 * length + PLANE :] = jnp.where(even, low, high).astype(BF16)
 
     def parts(i):
         start = 2 * length * i // channels
@@ -308,15 +314,14 @@
 
 
 def terms_kernel(
-    cols_ref, ends_ref, grad_ref, next_ref, edge_ref, keep_ref, rest_ref, terms_ref
+    cols_ref, ends_ref, grad_ref, edge_ref, keep_ref, rest_ref, terms_ref
 ):
     channels = grad_ref.shape[2]
     length = terms_ref.shape[0] // PARTS
     gradient = grad_ref[...].reshape(-1, channels)
     low_y, high_y = y_faces(lambda x: grad_ref[x].astype(F32))
-    ends = grad_ref[0].astype(F32), grad_ref[SIDE - 1].astype(F32)
-    pair_ref = rest_ref.at[rest_ref.shape[0] - PLANE :]
-    store_faces(*ends, low_y, high_y, pair_ref, next_ref, edge_ref)
+    edge_ref[0] = low_y.astype(BF16)
+    edge_ref[1] = high_y.astype(BF16)
 
     def parts(i):
         stop = -(-2 * length * i // channels)
@@ -535,13 +540,19 @@
     grid = pltpu.VMEM(ext, F32)
     cols = pltpu.VMEM((SIDE + 2, PLANE, TAPS * channels), BF16)
 
-    fetched = (features, occupancy)
+    points = point_voxel.reshape(1, -1)
+    fetched = (features, occupancy, points, teacher, head_weight, conv_weight)
     face = shape((PLANE, channels), BF16)
     planes = shape((SIDE, PLANE, channels), F32)
-    y_b, y_a, x_ends, masked, mask = call(
-        first_faces_kernel, (face, face, edges, planes, planes), fetched, buffers(*fetched),
-        name="first_faces", fetched=2,
-    )
+    y_b, y_a, x_ends, *rooms = call(
+        first_faces_kernel,
+        (face, face, edges, *[shape(x.shape, x.dtype) for x in fetched]),
+        fetched,
+        (pltpu.SemaphoreType.DMA((len(fetched),)),),
+        name="first_faces",
+        fetched=len(fetched),
+    )
+    feat, occ, point, teach, head, weight = rooms
     y_b, y_a = swap_along_y(y_b, y_a)
     wide_face = shape(((SIDE + 2) * SIDE, channels), BF16)
     x_pair, x_next = call(
@@ -549,37 +560,32 @@
     )
     x_next = lax.ppermute(x_next, "tx", swap_pairs(1, n_tx))
     x_pair = lax.ppermute(x_pair, "tx", swap_pairs(0, n_tx))
-    fetched = (point_voxel.reshape(1, -1), teacher, head_weight, conv_weight)
-    tile_cols, pre, sums, head, weight = call(
+    tile_cols, pre, mask, sums = call(
         main_kernel,
         (
             shape((SIDE, PLANE, TAPS * channels), BF16),
             shape((SIDE * PLANE, channels), F32),
+            planes,
             shape((2 * head_weight.shape[0], SIDE * PLANE), F32),
-            shape(head_weight.shape, BF16),
-            shape(conv_weight.shape, BF16),
         ),
-        (*fetched, masked, y_b, y_a),
-        (*buffers(*fetched[:2])[:-1], pltpu.SemaphoreType.DMA((len(fetched),))),
+        (feat, occ, point, teach, weight, y_b, y_a),
         name="main",
-        fetched=len(fetched),
     )
     part = kernels * channels // PARTS
     ends = shape((2, PLANE, TAPS * channels), BF16)
     gradient, ends, first = call(
         tile_kernel,
-        (shape((SIDE, PLANE, channels), BF16), ends, shape((2 * part, channels), BF16)),
+        (shape((SIDE, PLANE, channels), BF16), ends, shape((2 * part + 2 * PLANE, channels), BF16)),
         (tile_cols, pre, mask, sums, head, weight, x_next, x_pair),
         (pltpu.VMEM((2 * part + 2 * channels, channels), F32),),
         name="tile",
     )
-    g_next, g_edges, keep, rest = call(
+    g_edges, keep, rest = call(
         terms_kernel,
         (
-            face,
             edges,
             shape((PARTS // 2 * part, channels), F32),
-            shape((2 * part + PLANE, channels), BF16),
+            shape((2 * part, channels), BF16),
         ),
         (tile_cols, ends, gradient),
         (pltpu.VMEM((kernels * channels, channels), F32),),
@@ -590,19 +596,25 @@
     got_rest = exchange_with(rest, by_core)
     onward = message([(part, add, (keep, 3 * part), (got_first, part))])
     got_onward = exchange_with(onward, first_way)
-    faces = [(PLANE, add, (got_rest, 2 * part)), (PLANE, add, (g_next, 0))]
+    pair, following = 2 * part, 2 * part + PLANE
+    planes = [(got_first, pair), (first, following), (first, pair), (got_first, following)]
     got1 = exchange_with(
-        message([(part, add, (keep, 2 * part), (got_first, 0)), *faces]), first_way
+        message(
+            [(part, add, (keep, 2 * part), (got_first, 0))]
+            + [(PLANE, add, plane) for plane in planes]
+        ),
+        first_way,
     )
     kept = [(part, add, (keep, part), (got_rest, part), (got_onward, 0))]
-    got2 = exchange_with(message(kept + faces), second_way)
-    at = (part, part, part)
-    hand_on = (PLANE, picked_face, (got1, part + PLANE), (got2, part + PLANE))
+    got2 = exchange_with(message(kept), second_way)
+    x_faces = exchange_with(message([(2 * PLANE, add, (got1, part + 2 * PLANE))]), by_core)
+    at = (part, 0, part)
+    hand_on = (PLANE, picked_face, (got1, part + PLANE), (x_faces, PLANE))
     total = [(part, add, (keep, 0), (got_rest, 0), (got1, 0), (got2, 0))]
     flips, lines = [], []
     while 2 ** len(flips) < n_tx // 2:
         flips.append(2 ** (len(flips) + 1) - 1)
-    flips = list(zip(flips, flips[::-1]))
+    flips = list(zip(flips[::-1], flips))
     for both in flips:
         own = message(total + [hand_on])
         lines.append(exchange_with(own, along_line(both)))
@@ -616,7 +628,7 @@
         total = [(part, add, (own, 0), (got, 0))]
         bit *= 2
     kernel = functools.partial(hand_on_edge_kernel, flips, at)
-    g_a, g_b, planes = edge_faces(kernel, g_edges, (got1, got2, *lines))
+    g_a, g_b, planes = edge_faces(kernel, g_edges, (got1, x_faces, *lines))
     rows = g_a.shape[0]
     total, gradient = message(total + [(rows, add, (g_b, 0))], (), (gradient,))
     piece1 = exchange_with(total, second_way)
@@ -628,10 +640,12 @@
         name="back",
     )
     piece2 = exchange_with(message([(part + rows, add, (total, 0))], (back_part,)), first_way)
-    piece3 = exchange_with(message([(part, add, (piece1, 0))]), first_way)
+    onward = message([(part, add, (piece1, 0))])
+    piece3 = exchange_with(onward, first_way)
     near = message([(part, add, (piece2, 0)), (rows, add, (g_a, 0))])
     pieces = (total, piece1, near, piece3)
-    others = [exchange_with(piece, by_core) for piece in pieces]
+    late = message([(part, add, (total, 0))], (near,))
+    others = [exchange_with(piece, by_core) for piece in (late, *pieces[1:])]
     faces = (back_part, mask, weight, others[2], piece2, piece1, *pieces, *others[:3])
     kernel = functools.partial(y_faces_kernel, None)
     if n_ty > 4:

time: 52.1 us -> 51.8 us (level)
  waiting for transfers between devices: 13.7 us -> 16.2 us
  starting transfers between devices: 28 us -> 25.6 us
  Pallas kernels: 9.35 us -> 8.77 us
    ppermute x14 -> x15, starting transfers between devices: 18 us -> 15.5 us  [exchange_with(): return lax.ppermute(value, ('tx', 'ty'), pairs)]
    ppermute x14 -> x15, waiting for transfers between devices: 12.8 us -> 15.1 us  [exchange_with(): return lax.ppermute(value, ('tx', 'ty'), pairs)]
    pallas_call x7, Pallas kernels: 7.6 us -> 6.98 us  [call(): pl.pallas_call(body, out_shape=outs, in_specs=[pl.BlockSpec(memory_space=...]
  transfers between devices with their start and end apart: 18 -> 19, of which waited for: 11 -> 12; matrix products, arithmetic and copies ran while one was open for 0% -> 0% of each run, Pallas kernels for 10% -> 9%
where the time goes in v6:
time: 51.8 us; the launch traced here: 51.4 us
  starting transfers between devices  25.6 us (49%)
  waiting for transfers between devices  16.2 us (31%)
  Pallas kernels  8.77 us (17%)
  between operations  0.77 us (1%)
    ppermute x15, starting transfers between devices, exchange_with(): return lax.ppermute(value, ('tx', 'ty'), pairs)  15.5 us
    ppermute x15, waiting for transfers between devices, exchange_with(): return lax.ppermute(value, ('tx', 'ty'), pairs)  15.1 us
    pallas_call x7, Pallas kernels, call(): pl.pallas_call(body, out_shape=outs, in_specs=[pl.BlockSpec(memory_space=...  6.98 us
    ppermute x1, starting transfers between devices, swap_along_y(): return (got_b, lax.ppermute(a, 'ty', swap_pairs(0, count)))  4.39 us
    ppermute x1, starting transfers between devices, on_device(): x_pair = lax.ppermute(x_pair, 'tx', swap_pairs(0, n_tx))  4.35 us
    pallas_call x1, Pallas kernels, on_device(): pl.pallas_call(norm_kernel, out_shape=(shape((kernels * channels, channel...  1.45 us
  transfers between devices with their start and end apart: 19, of which 12 were waited for; matrix products, arithmetic and copies ran while one was open for 0% of the time, Pallas kernels for 9%

profile of v6, /device:TPU:0, one launch (start us, length us, event | category | flops | bytes accessed | tf_op | source)
XLA Modules:
  0.0 51.4 jit_solution(14646188926255991898)
XLA Ops:
  0.6 1.4 %first_faces.1 = (bf16[64,128]{1,0:T(8,128)(2,1)S(1)}, bf16[64,128]{1,0:T(8,128)(2,1)S(1)}, bf16[2,64,128]{2,1,0:T(8,128)(2,1)S(1)}, bf16[4,128,128]{2,1,0:T(8,1...) custom-call(bf16[4,128,128]{2,1,0:T(8,128)(2,1)} %feat_hbm.1, ...), custom_call_target="tpu_custom_call" | custom-call | tf_op jit(solution)/shard_map/first_faces/pallas_call | solution.py:31
  2.0 0.7 %collective-permute-start = (bf16[64,128]{1,0:T(8,128)(2,1)S(1)}, bf16[64,128]{1,0:T(8,128)(2,1)S(1)}, u32[]{:S(2)}, u32[]{:S(2)}) collective-permute-start(bf16[64,128]{1,0:T(8,128)(2,1)S(1)} %get-tuple-element.37), channel_id=1, source_target_pairs={{1,2},{2,1},{5,6},{6,5},{9,10},{10,9},{13,14},{14,13},{17,18},{18,... | collective-permute-start | bytes 49160 | tf_op jit(solution)/shard_map/ppermute | solution.py:434
  2.7 4.4 %collective-permute-start.1 = (bf16[64,128]{1,0:T(8,128)(2,1)S(1)}, bf16[64,128]{1,0:T(8,128)(2,1)S(1)}, u32[]{:S(2)}, u32[]{:S(2)}) collective-permute-start(bf16[64,128]{1,0:T(8,128)(2,1)S(1)} %get-tuple-element.38), channel_id=1, source_target_pairs={{0,1},{1,0},{2,3},{3,2},{4,5},{5,4},{6,7},{7,6},{8,9},{9,8},{10,11... | collective-permute-start | bytes 49160 | tf_op jit(solution)/shard_map/ppermute | solution.py:435
  7.1 0.8 %collective-permute-done.1.y_a_ref = bf16[64,128]{1,0:T(8,128)(2,1)S(1)} collective-permute-done((bf16[64,128]{1,0:T(8,128)(2,1)S(1)}, bf16[64,128]{1,0:T(8,128)(2,1)S(1)}, u32[]{:S(2)}, u32[]{:S(2)}) %collective-permute-start.1) | collective-permute-done | bytes 16416 | tf_op jit(solution)/shard_map/ppermute | solution.py:435
  7.9 0.7 %collective-permute-start.2 = (bf16[80,128]{1,0:T(8,128)(2,1)S(1)}, bf16[80,128]{1,0:T(8,128)(2,1)S(1)}, u32[]{:S(2)}, u32[]{:S(2)}) collective-permute-start(bf16[80,128]{1,0:T(8,128)(2,1)S(1)} %get-tuple-element.45), channel_id=1, source_target_pairs={{4,8},{8,4},{12,16},{16,12},{20,24},{24,20},{5,9},{9,5},{13,17},{1... | collective-permute-start | bytes 61448 | tf_op jit(solution)/shard_map/ppermute | solution.py:561
  8.6 4.3 %collective-permute-start.3 = (bf16[80,128]{1,0:T(8,128)(2,1)S(1)}, bf16[80,128]{1,0:T(8,128)(2,1)S(1)}, u32[]{:S(2)}, u32[]{:S(2)}) collective-permute-start(bf16[80,128]{1,0:T(8,128)(2,1)S(1)} %get-tuple-element.46), channel_id=1, source_target_pairs={{0,4},{4,0},{8,12},{12,8},{16,20},{20,16},{24,28},{28,24},{1,5},{5... | collective-permute-start | bytes 61448 | tf_op jit(solution)/shard_map/ppermute | solution.py:562
  12.9 1.5 %main.1 = (bf16[8,64,1152]{2,1,0:T(8,128)(2,1)S(1)}, f32[512,128]{1,0:T(8,128)S(1)}, f32[8,64,128]{2,1,0:T(8,128)S(1)}, f32[32,512]{1,0:T(8,128)S(1)}) custom-call(bf16[4,128,128]{2,1,0:T(8,128)(2,1)S(1)} %get-tuple-element.32.feat_ref, s32[4,128]{1,0:T(4,128)S(1)} %get-tuple-element.33.occ_ref, s32[1,1024]{1,0:T(1,128)S(1)} %get-tuple-element.34.point_ref, ...), custom_call_target="tpu_custom_call" | custom-call | tf_op jit(solution)/shard_map/main/pallas_call | solution.py:31
  14.7 1.3 %tile.1 = (bf16[8,64,128]{2,1,0:T(8,128)(2,1)S(1)}, bf16[2,64,1152]{2,1,0:T(8,128)(2,1)S(1)}, bf16[992,128]{1,0:T(8,128)(2,1)S(1)}) custom-call(bf16[8,64,1152]{2,1,0:T(8,128)(2,1)S(1)} %get-tuple-element.39.cols_ref, f32[512,128]{1,0:T(8,128)S(1)} %get-tuple-element.40.pre_ref, f32[8,64,128]{2,1,0:T(8,128)S(1)} %get-tuple-element.41.mask_ref, ...), custom_call_target="tpu_custom_call" | custom-call | tf_op jit(solution)/shard_map/tile/pallas_call | solution.py:31
  16.1 1.2 %terms.1 = (bf16[2,64,128]{2,1,0:T(8,128)(2,1)S(1)}, f32[1728,128]{1,0:T(8,128)S(1)}, bf16[864,128]{1,0:T(8,128)(2,1)S(1)}) custom-call(bf16[8,64,1152]{2,1,0:T(8,128)(2,1)S(1)} %get-tuple-element.39.cols_ref, bf16[2,64,1152]{2,1,0:T(8,128)(2,1)S(1)} %get-tuple-element.47.ends_ref, bf16[8,64,128]{2,1,0:T(8,128)(2,1)S(1)} %get-tuple-element.48.grad_ref.refs_3_), custom_call_target="tpu_custom_call" | custom-call | tf_op jit(solution)/shard_map/terms/pallas_call | solution.py:31
  17.3 0.6 %collective-permute-start.4 = (bf16[864,128]{1,0:T(8,128)(2,1)S(1)}, bf16[864,128]{1,0:T(8,128)(2,1)S(1)}, u32[]{:S(2)}, u32[]{:S(2)}) collective-permute-start(bf16[864,128]{1,0:T(8,128)(2,1)S(1)} %get-tuple-element.50), channel_id=1, source_target_pairs={{0,1},{1,0},{2,3},{3,2},{4,5},{5,4},{6,7},{7,6},{8,9},{9,8},{10,11... | collective-permute-start | bytes 663560 | tf_op jit(solution)/shard_map/ppermute | solution.py:458
  17.9 1.8 %collective-permute-start.7 = (bf16[432,128]{1,0:T(8,128)(2,1)S(1)}, bf16[432,128]{1,0:T(8,128)(2,1)S(1)}, u32[]{:S(2)}, u32[]{:S(2)}) collective-permute-start(bf16[432,128]{1,0:T(8,128)(2,1)S(1)} %message.12), channel_id=1, source_target_pairs={{0,3},{1,4},{2,7},{3,0},{4,1},{5,6},{6,5},{7,2},{8,13},{9,10},{10,... | collective-permute-start | bytes 331784 | tf_op jit(solution)/shard_map/ppermute | solution.py:458
  19.8 2.3 %collective-permute-done.7.refs_2_ = bf16[432,128]{1,0:T(8,128)(2,1)S(1)} collective-permute-done((bf16[432,128]{1,0:T(8,128)(2,1)S(1)}, bf16[432,128]{1,0:T(8,128)(2,1)S(1)}, u32[]{:S(2)}, u32[]{:S(2)}) %collective-permute-start.7) | collective-permute-done | bytes 110624 | tf_op jit(solution)/shard_map/ppermute | solution.py:458
  22.2 2.4 %collective-permute-start.8 = (bf16[432,128]{1,0:T(8,128)(2,1)S(1)}, bf16[432,128]{1,0:T(8,128)(2,1)S(1)}, u32[]{:S(2)}, u32[]{:S(2)}) collective-permute-start(bf16[432,128]{1,0:T(8,128)(2,1)S(1)} %message.13), channel_id=1, source_target_pairs={{0,5},{1,2},{2,1},{3,6},{4,7},{5,0},{6,3},{7,4},{8,11},{9,12},{10,... | collective-permute-start | bytes 331784 | tf_op jit(solution)/shard_map/ppermute | solution.py:458
  24.7 0.4 collective-permute-start.9
  25.1 0.9 %collective-permute-done.9.refs_4_.got2_ref = bf16[128,128]{1,0:T(8,128)(2,1)S(1)} collective-permute-done((bf16[128,128]{1,0:T(8,128)(2,1)S(1)}, bf16[128,128]{1,0:T(8,128)(2,1)S(1)}, u32[]{:S(2)}, u32[]{:S(2)}) %collective-permute-start.9) | collective-permute-done | bytes 32800 | tf_op jit(solution)/shard_map/ppermute | solution.py:458
  26.0 1.1 %collective-permute-done.8.refs_3_ = bf16[432,128]{1,0:T(8,128)(2,1)S(1)} collective-permute-done((bf16[432,128]{1,0:T(8,128)(2,1)S(1)}, bf16[432,128]{1,0:T(8,128)(2,1)S(1)}, u32[]{:S(2)}, u32[]{:S(2)}) %collective-permute-start.8) | collective-permute-done | bytes 110624 | tf_op jit(solution)/shard_map/ppermute | solution.py:458
  27.1 3.8 %collective-permute-start.10 = (bf16[496,128]{1,0:T(8,128)(2,1)S(1)}, bf16[496,128]{1,0:T(8,128)(2,1)S(1)}, u32[]{:S(2)}, u32[]{:S(2)}) collective-permute-start(bf16[496,128]{1,0:T(8,128)(2,1)S(1)} %message.15.refs_0_), channel_id=1, source_target_pairs={{0,25},{1,8},{2,11},{3,26},{4,13},{5,28},{6,31},{7,14},{8,1},{9,16... | collective-permute-start | bytes 380936 | tf_op jit(solution)/shard_map/ppermute | solution.py:458
  30.9 3.6 %collective-permute-done.10.refs_1_.refs_0_ = bf16[496,128]{1,0:T(8,128)(2,1)S(1)} collective-permute-done((bf16[496,128]{1,0:T(8,128)(2,1)S(1)}, bf16[496,128]{1,0:T(8,128)(2,1)S(1)}, u32[]{:S(2)}, u32[]{:S(2)}) %collective-permute-start.10) | collective-permute-done | bytes 127008 | tf_op jit(solution)/shard_map/ppermute | solution.py:458
  34.6 5.0 %collective-permute-done.11.refs_1_ = bf16[496,128]{1,0:T(8,128)(2,1)S(1)} collective-permute-done((bf16[496,128]{1,0:T(8,128)(2,1)S(1)}, bf16[496,128]{1,0:T(8,128)(2,1)S(1)}, u32[]{:S(2)}, u32[]{:S(2)}) %collective-permute-start.11) | collective-permute-done | bytes 127008 | tf_op jit(solution)/shard_map/ppermute | solution.py:458
  39.7 1.4 %collective-permute-start.12 = (bf16[512,128]{1,0:T(8,128)(2,1)S(1)}, bf16[512,128]{1,0:T(8,128)(2,1)S(1)}, u32[]{:S(2)}, u32[]{:S(2)}) collective-permute-start(bf16[512,128]{1,0:T(8,128)(2,1)S(1)} %get-tuple-element.54.refs_0_), channel_id=1, source_target_pairs={{0,5},{1,2},{2,1},{3,6},{4,7},{5,0},{6,3},{7,4},{8,11},{9,12},{10,... | collective-permute-start | bytes 393224 | tf_op jit(solution)/shard_map/ppermute | solution.py:458
  41.0 1.1 %back.1.refs_1_.part_ref = f32[512,128]{1,0:T(8,128)S(1)} custom-call(bf16[8,64,128]{2,1,0:T(8,128)(2,1)S(1)} %get-tuple-element.55.grad_ref, bf16[2,64,128]{2,1,0:T(8,128)(2,1)S(1)} %get-tuple-element.56.planes_ref, bf16[27,128,128]{2,1,0:T(8,128)(2,1)S(1)} %get-tuple-element.36.weight_ref), custom_call_target="tpu_custom_call" | custom-call | tf_op jit(solution)/shard_map/back/pallas_call | solution.py:31
  42.2 1.5 %collective-permute-start.13 = (bf16[512,128]{1,0:T(8,128)(2,1)S(1)}, bf16[512,128]{1,0:T(8,128)(2,1)S(1)}, u32[]{:S(2)}, u32[]{:S(2)}) collective-permute-start(bf16[512,128]{1,0:T(8,128)(2,1)S(1)} %message.18), channel_id=1, source_target_pairs={{0,3},{1,4},{2,7},{3,0},{4,1},{5,6},{6,5},{7,2},{8,13},{9,10},{10,... | collective-permute-start | bytes 393224 | tf_op jit(solution)/shard_map/ppermute | solution.py:458
  43.7 0.4 collective-permute-done.12.refs_0_.line_ref.refs_1_
  44.1 1.9 %collective-permute-start.14 = (bf16[432,128]{1,0:T(8,128)(2,1)S(1)}, bf16[432,128]{1,0:T(8,128)(2,1)S(1)}, u32[]{:S(2)}, u32[]{:S(2)}) collective-permute-start(bf16[432,128]{1,0:T(8,128)(2,1)S(1)} %message.20), channel_id=1, source_target_pairs={{0,3},{1,4},{2,7},{3,0},{4,1},{5,6},{6,5},{7,2},{8,13},{9,10},{10,... | collective-permute-start | bytes 331784 | tf_op jit(solution)/shard_map/ppermute | solution.py:458
  46.1 0.6 %collective-permute-done.13.refs_0_.far_ref = bf16[512,128]{1,0:T(8,128)(2,1)S(1)} collective-permute-done((bf16[512,128]{1,0:T(8,128)(2,1)S(1)}, bf16[512,128]{1,0:T(8,128)(2,1)S(1)}, u32[]{:S(2)}, u32[]{:S(2)}) %collective-permute-start.13) | collective-permute-done | bytes 131104 | tf_op jit(solution)/shard_map/ppermute | solution.py:458
  46.7 0.4 collective-permute-start.17
  47.3 0.4 collective-permute-start.15
  47.7 0.8 %collective-permute-done.14.refs_3_ = bf16[432,128]{1,0:T(8,128)(2,1)S(1)} collective-permute-done((bf16[432,128]{1,0:T(8,128)(2,1)S(1)}, bf16[432,128]{1,0:T(8,128)(2,1)S(1)}, u32[]{:S(2)}, u32[]{:S(2)}) %collective-permute-start.14) | collective-permute-done | bytes 110624 | tf_op jit(solution)/shard_map/ppermute | solution.py:458
  48.5 0.5 collective-permute-start.18
  49.0 0.5 %y_faces.1 = (bf16[4,128,128]{2,1,0:T(8,128)(2,1)S(1)}, f32[8,128]{1,0:T(8,128)S(1)}) custom-call(f32[512,128]{1,0:T(8,128)S(1)} %back.1.refs_1_.part_ref, f32[8,64,128]{2,1,0:T(8,128)S(1)} %get-tuple-element.41.mask_ref, bf16[27,128,128]{2,1,0:T(8,128)(2,1)S(1)} %get-tuple-element.36.weight_ref, ...), custom_call_target="tpu_custom_call" | custom-call | tf_op jit(solution)/shard_map/y_faces/pallas_call | solution.py:31
  49.5 0.4 collective-permute-done.18.refs_7_
  49.9 1.4 %normalise.1 = (f32[3456,128]{1,0:T(8,128)}, bf16[4,128,128]{2,1,0:T(8,128)(2,1)}) custom-call(bf16[512,128]{1,0:T(8,128)(2,1)S(1)} %get-tuple-element.54.refs_0_, bf16[512,128]{1,0:T(8,128)(2,1)S(1)} %collective-permute-done.12.refs_0_.line_ref.refs_1_, bf16[512,128]{1,0:T(8,128)(2,1)S(1)} %message.19.refs_1_.refs_2_, ...), custom_call_target="tpu_custom_call" | custom-call | tf_op jit(solution)/shard_map/normalise/pallas_call | solution.py:662
  (26 shorter events, 1.3 us)
Async XLA Ops:
  2.0 5.1 %collective-permute-start = (bf16[64,128]{1,0:T(8,128)(2,1)S(1)}, bf16[64,128]{1,0:T(8,128)(2,1)S(1)}, u32[]{:S(2)}, u32[]{:S(2)}) collective-permute-start(bf16[64,128]{1,0:T(8,128)(2,1)S(1)} %get-tuple-element.37), channel_id=1, source_target_pairs={{1,2},{2,1},{5,6},{6,5},{9,10},{10,9},{13,14},{14,13},{17,18},{18,... | collective-permute-start | bytes 49160 | tf_op jit(solution)/shard_map/ppermute | solution.py:434
  2.7 5.2 %collective-permute-start.1 = (bf16[64,128]{1,0:T(8,128)(2,1)S(1)}, bf16[64,128]{1,0:T(8,128)(2,1)S(1)}, u32[]{:S(2)}, u32[]{:S(2)}) collective-permute-start(bf16[64,128]{1,0:T(8,128)(2,1)S(1)} %get-tuple-element.38), channel_id=1, source_target_pairs={{0,1},{1,0},{2,3},{3,2},{4,5},{5,4},{6,7},{7,6},{8,9},{9,8},{10,11... | collective-permute-start | bytes 49160 | tf_op jit(solution)/shard_map/ppermute | solution.py:435
  7.9 6.5 %collective-permute-start.2 = (bf16[80,128]{1,0:T(8,128)(2,1)S(1)}, bf16[80,128]{1,0:T(8,128)(2,1)S(1)}, u32[]{:S(2)}, u32[]{:S(2)}) collective-permute-start(bf16[80,128]{1,0:T(8,128)(2,1)S(1)} %get-tuple-element.45), channel_id=1, source_target_pairs={{4,8},{8,4},{12,16},{16,12},{20,24},{24,20},{5,9},{9,5},{13,17},{1... | collective-permute-start | bytes 61448 | tf_op jit(solution)/shard_map/ppermute | solution.py:561
  8.6 6.1 %collective-permute-start.3 = (bf16[80,128]{1,0:T(8,128)(2,1)S(1)}, bf16[80,128]{1,0:T(8,128)(2,1)S(1)}, u32[]{:S(2)}, u32[]{:S(2)}) collective-permute-start(bf16[80,128]{1,0:T(8,128)(2,1)S(1)} %get-tuple-element.46), channel_id=1, source_target_pairs={{0,4},{4,0},{8,12},{12,8},{16,20},{20,16},{24,28},{28,24},{1,5},{5... | collective-permute-start | bytes 61448 | tf_op jit(solution)/shard_map/ppermute | solution.py:562
  16.0 1.9 %collective-permute-start.5 = (bf16[992,128]{1,0:T(8,128)(2,1)S(1)}, bf16[992,128]{1,0:T(8,128)(2,1)S(1)}, u32[]{:S(2)}, u32[]{:S(2)}) collective-permute-start(bf16[992,128]{1,0:T(8,128)(2,1)S(1)} %get-tuple-element.51.refs_2_), channel_id=1, source_target_pairs={{0,1},{1,0},{2,3},{3,2},{4,5},{5,4},{6,7},{7,6},{8,9},{9,8},{10,11... | collective-permute-start | bytes 761864 | tf_op jit(solution)/shard_map/ppermute | solution.py:458
  17.3 2.6 %collective-permute-start.4 = (bf16[864,128]{1,0:T(8,128)(2,1)S(1)}, bf16[864,128]{1,0:T(8,128)(2,1)S(1)}, u32[]{:S(2)}, u32[]{:S(2)}) collective-permute-start(bf16[864,128]{1,0:T(8,128)(2,1)S(1)} %get-tuple-element.50), channel_id=1, source_target_pairs={{0,1},{1,0},{2,3},{3,2},{4,5},{5,4},{6,7},{7,6},{8,9},{9,8},{10,11... | collective-permute-start | bytes 663560 | tf_op jit(solution)/shard_map/ppermute | solution.py:458
  17.9 4.2 %collective-permute-start.7 = (bf16[432,128]{1,0:T(8,128)(2,1)S(1)}, bf16[432,128]{1,0:T(8,128)(2,1)S(1)}, u32[]{:S(2)}, u32[]{:S(2)}) collective-permute-start(bf16[432,128]{1,0:T(8,128)(2,1)S(1)} %message.12), channel_id=1, source_target_pairs={{0,3},{1,4},{2,7},{3,0},{4,1},{5,6},{6,5},{7,2},{8,13},{9,10},{10,... | collective-permute-start | bytes 331784 | tf_op jit(solution)/shard_map/ppermute | solution.py:458
  19.7 4.9 %collective-permute-start.6 = (bf16[688,128]{1,0:T(8,128)(2,1)S(1)}, bf16[688,128]{1,0:T(8,128)(2,1)S(1)}, u32[]{:S(2)}, u32[]{:S(2)}) collective-permute-start(bf16[688,128]{1,0:T(8,128)(2,1)S(1)} %message.11), channel_id=1, source_target_pairs={{0,3},{1,4},{2,7},{3,0},{4,1},{5,6},{6,5},{7,2},{8,13},{9,10},{10,... | collective-permute-start | bytes 528392 | tf_op jit(solution)/shard_map/ppermute | solution.py:458
  22.2 4.8 %collective-permute-start.8 = (bf16[432,128]{1,0:T(8,128)(2,1)S(1)}, bf16[432,128]{1,0:T(8,128)(2,1)S(1)}, u32[]{:S(2)}, u32[]{:S(2)}) collective-permute-start(bf16[432,128]{1,0:T(8,128)(2,1)S(1)} %message.13), channel_id=1, source_target_pairs={{0,5},{1,2},{2,1},{3,6},{4,7},{5,0},{6,3},{7,4},{8,11},{9,12},{10,... | collective-permute-start | bytes 331784 | tf_op jit(solution)/shard_map/ppermute | solution.py:458
  24.7 1.3 %collective-permute-start.9 = (bf16[128,128]{1,0:T(8,128)(2,1)S(1)}, bf16[128,128]{1,0:T(8,128)(2,1)S(1)}, u32[]{:S(2)}, u32[]{:S(2)}) collective-permute-start(bf16[128,128]{1,0:T(8,128)(2,1)S(1)} %message.14), channel_id=1, source_target_pairs={{0,1},{1,0},{2,3},{3,2},{4,5},{5,4},{6,7},{7,6},{8,9},{9,8},{10,11... | collective-permute-start | bytes 98312 | tf_op jit(solution)/shard_map/ppermute | solution.py:458
  27.1 7.3 %collective-permute-start.10 = (bf16[496,128]{1,0:T(8,128)(2,1)S(1)}, bf16[496,128]{1,0:T(8,128)(2,1)S(1)}, u32[]{:S(2)}, u32[]{:S(2)}) collective-permute-start(bf16[496,128]{1,0:T(8,128)(2,1)S(1)} %message.15.refs_0_), channel_id=1, source_target_pairs={{0,25},{1,8},{2,11},{3,26},{4,13},{5,28},{6,31},{7,14},{8,1},{9,16... | collective-permute-start | bytes 380936 | tf_op jit(solution)/shard_map/ppermute | solution.py:458
  34.5 5.1 %collective-permute-start.11 = (bf16[496,128]{1,0:T(8,128)(2,1)S(1)}, bf16[496,128]{1,0:T(8,128)(2,1)S(1)}, u32[]{:S(2)}, u32[]{:S(2)}) collective-permute-start(bf16[496,128]{1,0:T(8,128)(2,1)S(1)} %message.16.refs_0_), channel_id=1, source_target_pairs={{0,9},{1,24},{2,27},{3,10},{4,29},{5,12},{6,15},{7,30},{8,17},{9,0... | collective-permute-start | bytes 380936 | tf_op jit(solution)/shard_map/ppermute | solution.py:458
  39.7 4.5 %collective-permute-start.12 = (bf16[512,128]{1,0:T(8,128)(2,1)S(1)}, bf16[512,128]{1,0:T(8,128)(2,1)S(1)}, u32[]{:S(2)}, u32[]{:S(2)}) collective-permute-start(bf16[512,128]{1,0:T(8,128)(2,1)S(1)} %get-tuple-element.54.refs_0_), channel_id=1, source_target_pairs={{0,5},{1,2},{2,1},{3,6},{4,7},{5,0},{6,3},{7,4},{8,11},{9,12},{10,... | collective-permute-start | bytes 393224 | tf_op jit(solution)/shard_map/ppermute | solution.py:458
  42.2 4.5 %collective-permute-start.13 = (bf16[512,128]{1,0:T(8,128)(2,1)S(1)}, bf16[512,128]{1,0:T(8,128)(2,1)S(1)}, u32[]{:S(2)}, u32[]{:S(2)}) collective-permute-start(bf16[512,128]{1,0:T(8,128)(2,1)S(1)} %message.18), channel_id=1, source_target_pairs={{0,3},{1,4},{2,7},{3,0},{4,1},{5,6},{6,5},{7,2},{8,13},{9,10},{10,... | collective-permute-start | bytes 393224 | tf_op jit(solution)/shard_map/ppermute | solution.py:458
  44.1 4.3 %collective-permute-start.14 = (bf16[432,128]{1,0:T(8,128)(2,1)S(1)}, bf16[432,128]{1,0:T(8,128)(2,1)S(1)}, u32[]{:S(2)}, u32[]{:S(2)}) collective-permute-start(bf16[432,128]{1,0:T(8,128)(2,1)S(1)} %message.20), channel_id=1, source_target_pairs={{0,3},{1,4},{2,7},{3,0},{4,1},{5,6},{6,5},{7,2},{8,13},{9,10},{10,... | collective-permute-start | bytes 331784 | tf_op jit(solution)/shard_map/ppermute | solution.py:458
  46.7 2.3 %collective-permute-start.17 = (bf16[512,128]{1,0:T(8,128)(2,1)S(1)}, bf16[512,128]{1,0:T(8,128)(2,1)S(1)}, u32[]{:S(2)}, u32[]{:S(2)}) collective-permute-start(bf16[512,128]{1,0:T(8,128)(2,1)S(1)} %message.19.refs_1_.refs_2_), channel_id=1, source_target_pairs={{0,1},{1,0},{2,3},{3,2},{4,5},{5,4},{6,7},{7,6},{8,9},{9,8},{10,11... | collective-permute-start | bytes 393224 | tf_op jit(solution)/shard_map/ppermute | solution.py:458
  47.1 1.9 %collective-permute-start.16 = (bf16[512,128]{1,0:T(8,128)(2,1)S(1)}, bf16[512,128]{1,0:T(8,128)(2,1)S(1)}, u32[]{:S(2)}, u32[]{:S(2)}) collective-permute-start(bf16[512,128]{1,0:T(8,128)(2,1)S(1)} %collective-permute-done.12.refs_0_.line_ref.refs_1_), channel_id=1, source_target_pairs={{0,1},{1,0},{2,3},{3,2},{4,5},{5,4},{6,7},{7,6},{8,9},{9,8},{10,11... | collective-permute-start | bytes 393224 | tf_op jit(solution)/shard_map/ppermute | solution.py:458
  47.3 1.7 %collective-permute-start.15 = (bf16[432,128]{1,0:T(8,128)(2,1)S(1)}, bf16[432,128]{1,0:T(8,128)(2,1)S(1)}, u32[]{:S(2)}, u32[]{:S(2)}) collective-permute-start(bf16[432,128]{1,0:T(8,128)(2,1)S(1)} %message.21), channel_id=1, source_target_pairs={{0,1},{1,0},{2,3},{3,2},{4,5},{5,4},{6,7},{7,6},{8,9},{9,8},{10,11... | collective-permute-start | bytes 331784 | tf_op jit(solution)/shard_map/ppermute | solution.py:458
  48.5 1.4 %collective-permute-start.18 = (bf16[432,128]{1,0:T(8,128)(2,1)S(1)}, bf16[432,128]{1,0:T(8,128)(2,1)S(1)}, u32[]{:S(2)}, u32[]{:S(2)}) collective-permute-start(bf16[432,128]{1,0:T(8,128)(2,1)S(1)} %collective-permute-done.14.refs_3_), channel_id=1, source_target_pairs={{0,1},{1,0},{2,3},{3,2},{4,5},{5,4},{6,7},{7,6},{8,9},{9,8},{10,11... | collective-permute-start | bytes 331784 | tf_op jit(solution)/shard_map/ppermute | solution.py:458

commit v7 on v6

--- a/solution.py
+++ b/solution.py
@@ -39,11 +39,6 @@
     )(*[pin(array) for array in inputs[:fetched]], *inputs[fetched:])
 
 
-def buffers(*arrays):
-    rooms = [pltpu.VMEM(array.shape, array.dtype) for array in arrays]
-    return (*rooms, pltpu.SemaphoreType.DMA((len(arrays),)))
-
-
 def fetch(sources, rooms, semaphores):
     copies = [
         pltpu.make_async_copy(source, room, semaphores.at[i])
@@ -58,10 +53,6 @@
     return jax.ShapeDtypeStruct(dims, dtype)
 
 
-def slot_planes(slot):
-    return BX * (slot // GY), (slot % GY) * BY * SIDE
-
-
 def parity(axis):
     return lax.rem(lax.axis_index(axis), 2) == 0
 
@@ -72,11 +63,6 @@
     return padded.T
 
 
-def write_grid(grid_ref, planes):
-    for x in range(SIDE):
-        grid_ref[x + 1, SIDE : SIDE + PLANE, :] = planes(x)
-
-
 def y_faces(planes):
     low = jnp.concatenate([planes(x)[:SIDE] for x in range(SIDE)], axis=0)
     high = jnp.concatenate([planes(x)[PLANE - SIDE :] for x in range(SIDE)], axis=0)
@@ -88,14 +74,9 @@
 
 
 def first_faces_kernel(
-    feat_hbm, occ_hbm, point_hbm, teach_hbm, head_hbm, weight_hbm,
-    b_ref, a_ref, ends_ref, feat_ref, occ_ref, point_ref, teach_ref, head_ref, weight_ref,
-    semaphores,
+    feat_hbm, occ_hbm, b_ref, a_ref, ends_ref, feat_ref, occ_ref, semaphores
 ):
-    sources = (feat_hbm, occ_hbm, point_hbm, teach_hbm, head_hbm, weight_hbm)
-    rooms = (feat_ref, occ_ref, point_ref, teach_ref, head_ref, weight_ref)
-    copies = fetch(sources, rooms, semaphores)
-    for copy in copies[:2]:
+    for copy in fetch((feat_hbm, occ_hbm), (feat_ref, occ_ref), semaphores):
         copy.wait()
     columns = occupancy_columns(occ_ref, 8)
     rows, channels = BY * SIDE, feat_ref.shape[2]
@@ -113,7 +94,11 @@
     for i, x in enumerate((0, SIDE - 1)):
         plane = jnp.concatenate([masked(x, j, 0, rows) for j in range(GY)], axis=0)
         ends_ref[i] = plane.astype(BF16)
-    for copy in copies[2:]:
+
+
+def fetch_kernel(*refs):
+    count = len(refs) // 2 - 1
+    for copy in fetch(refs[:count], refs[count + 1 : -1], refs[-1]):
         copy.wait()
 
 
@@ -123,7 +108,7 @@
     return jnp.where(even, b, a), jnp.where(even, a, b)
 
 
-def x_faces_kernel(ends_ref, y_b_ref, y_a_ref, *refs):
+def x_faces_kernel(ends_ref, y_a_ref, y_b_ref, *refs):
     pair_ref, next_ref = refs[-2:]
     low, high = halo_along_y(y_b_ref, y_a_ref)
     last = PLANE - SIDE
@@ -206,7 +191,7 @@
 
 
 def main_kernel(
-    feat_ref, occ_ref, point_ref, teach_ref, weight_ref, y_b_ref, y_a_ref,
+    feat_ref, occ_ref, point_ref, teach_ref, weight_ref, y_a_ref, y_b_ref,
     cols_ref, pre_ref, mask_ref, sums_ref,
 ):
     rows, channels = BY * SIDE, feat_ref.shape[2]
@@ -431,8 +416,8 @@
 
 def swap_along_y(b, a):
     count = lax.axis_size("ty")
-    got_b = lax.ppermute(b, "ty", swap_pairs(1, count))
-    return got_b, lax.ppermute(a, "ty", swap_pairs(0, count))
+    got_a = lax.ppermute(a, "ty", swap_pairs(0, count))
+    return lax.ppermute(b, "ty", swap_pairs(1, count)), got_a
 
 
 def edge_faces(kernel, edges, faces, waits=()):
@@ -536,15 +521,14 @@
     kernels = conv_weight.shape[0]
     n_tx, n_ty = lax.axis_size("tx"), lax.axis_size("ty")
     edges = shape((2, PLANE, channels), BF16)
-    ext = (SIDE + 2, (SIDE + 2) * SIDE, channels)
-    grid = pltpu.VMEM(ext, F32)
     cols = pltpu.VMEM((SIDE + 2, PLANE, TAPS * channels), BF16)
 
     points = point_voxel.reshape(1, -1)
-    fetched = (features, occupancy, points, teacher, head_weight, conv_weight)
+    fetched = (features, occupancy)
     face = shape((PLANE, channels), BF16)
+    wide_face = shape(((SIDE + 2) * SIDE, channels), BF16)
     planes = shape((SIDE, PLANE, channels), F32)
-    y_b, y_a, x_ends, *rooms = call(
+    y_b, y_a, x_ends, feat, occ = call(
         first_faces_kernel,
         (face, face, edges, *[shape(x.shape, x.dtype) for x in fetched]),
         fetched,
@@ -552,12 +536,24 @@
         name="first_faces",
         fetched=len(fetched),
     )
-    feat, occ, point, teach, head, weight = rooms
+    fetched = (points, teacher, head_weight, conv_weight)
+    point, teach, head, weight = call(
+        fetch_kernel,
+        tuple(shape(x.shape, x.dtype) for x in fetched),
+        (*fetched, x_ends),
+        (pltpu.SemaphoreType.DMA((len(fetched),)),),
+        name="fetch",
+        fetched=len(fetched),
+    )
     y_b, y_a = swap_along_y(y_b, y_a)
-    wide_face = shape(((SIDE + 2) * SIDE, channels), BF16)
-    x_pair, x_next = call(
-        x_faces_kernel, (wide_face, wide_face), (x_ends, y_b, y_a), name="x_faces"
-    )
+    x_pair, x_next = pl.pallas_call(
+        x_faces_kernel,
+        out_shape=(wide_face, wide_face),
+        in_specs=vmem(3) + [pl.BlockSpec(memory_space=pl.ANY)],
+        out_specs=tuple(vmem(2)),
+        compiler_params=pltpu.CompilerParams(vmem_limit_bytes=16 * 2**20),
+        name="x_faces",
+    )(x_ends, y_a, y_b, weight)
     x_next = lax.ppermute(x_next, "tx", swap_pairs(1, n_tx))
     x_pair = lax.ppermute(x_pair, "tx", swap_pairs(0, n_tx))
     tile_cols, pre, mask, sums = call(
@@ -568,7 +564,7 @@
             planes,
             shape((2 * head_weight.shape[0], SIDE * PLANE), F32),
         ),
-        (feat, occ, point, teach, weight, y_b, y_a),
+        (feat, occ, point, teach, weight, y_a, y_b),
         name="main",
     )
     part = kernels * channels // PARTS

time: 51.8 us -> 51.7 us (level)
  Pallas kernels: 8.77 us -> 9.79 us
  starting transfers between devices: 25.6 us -> 24.8 us
    ppermute x2, starting transfers between devices: 5.06 us -> 1.17 us  [the longest x1 0.65 us: swap_along_y(): return (lax.ppermute(b, 'ty', swap_pairs(1, count)), got_a)]
    ppermute x15, starting transfers between devices: 15.5 us -> 17.6 us  [exchange_with(): return lax.ppermute(value, ('tx', 'ty'), pairs)]
    ppermute x1, starting transfers between devices: 4.35 us -> 5.37 us  [on_device(): x_pair = lax.ppermute(x_pair, 'tx', swap_pairs(0, n_tx))]
    pallas_call x7, Pallas kernels: 6.98 us -> 7.98 us  [call(): pl.pallas_call(body, out_shape=outs, in_specs=[pl.BlockSpec(memory_space=...]
    ppermute x2, waiting for transfers between devices: 0.84 us -> 0.01 us  [the longest x1 0.01 us: swap_along_y(): got_a = lax.ppermute(a, 'ty', swap_pairs(0, count))]
  transfers between devices with their start and end apart: 19 -> 19, of which waited for: 12 -> 11; matrix products, arithmetic and copies ran while one was open for 0% -> 0% of each run, Pallas kernels for 9% -> 11%
where the time goes in v7:
time: 51.7 us; the launch traced here: 51.2 us
  starting transfers between devices  24.8 us (48%)
  waiting for transfers between devices  15.7 us (30%)
  Pallas kernels  9.79 us (19%)
  between operations  0.8 us (2%)
    ppermute x15, starting transfers between devices, exchange_with(): return lax.ppermute(value, ('tx', 'ty'), pairs)  17.6 us
    ppermute x15, waiting for transfers between devices, exchange_with(): return lax.ppermute(value, ('tx', 'ty'), pairs)  15.4 us
    pallas_call x7, Pallas kernels, call(): pl.pallas_call(body, out_shape=outs, in_specs=[pl.BlockSpec(memory_space=...  7.98 us
    ppermute x1, starting transfers between devices, on_device(): x_pair = lax.ppermute(x_pair, 'tx', swap_pairs(0, n_tx))  5.37 us
    pallas_call x1, Pallas kernels, on_device(): pl.pallas_call(norm_kernel, out_shape=(shape((kernels * channels, channel...  1.45 us
  transfers between devices with their start and end apart: 19, of which 11 were waited for; matrix products, arithmetic and copies ran while one was open for 0% of the time, Pallas kernels for 11%

profile of v7, /device:TPU:0, one launch (start us, length us, event | category | flops | bytes accessed | tf_op | source)
XLA Modules:
  0.0 51.2 jit_solution(4049340052235663784)
XLA Ops:
  0.6 1.1 %first_faces.1 = (bf16[64,128]{1,0:T(8,128)(2,1)S(1)}, bf16[64,128]{1,0:T(8,128)(2,1)S(1)}, bf16[2,64,128]{2,1,0:T(8,128)(2,1)S(1)}, bf16[4,128,128]{2,1,0:T(8,128)(2,1)S(1)}, s32[4,128]{1,0:T(4,128)S(1)}) custom-call(bf16[4,128,128]{2,1,0:T(8,128)(2,1)} %feat_hbm.1, s32[4,128]{1,0:T(4,128)} %occ_hbm.1), custom_call_target="tpu_custom_call" | custom-call | tf_op jit(solution)/shard_map/first_faces/pallas_call | solution.py:31
  1.8 0.5 %collective-permute-start = (bf16[64,128]{1,0:T(8,128)(2,1)S(1)}, bf16[64,128]{1,0:T(8,128)(2,1)S(1)}, u32[]{:S(2)}, u32[]{:S(2)}) collective-permute-start(bf16[64,128]{1,0:T(8,128)(2,1)S(1)} %get-tuple-element.38), channel_id=1, source_target_pairs={{0,1},{1,0},{2,3},{3,2},{4,5},{5,4},{6,7},{7,6},{8,9},{9,8},{10,11... | collective-permute-start | bytes 49160 | tf_op jit(solution)/shard_map/ppermute | solution.py:419
  2.3 0.7 %collective-permute-start.1 = (bf16[64,128]{1,0:T(8,128)(2,1)S(1)}, bf16[64,128]{1,0:T(8,128)(2,1)S(1)}, u32[]{:S(2)}, u32[]{:S(2)}) collective-permute-start(bf16[64,128]{1,0:T(8,128)(2,1)S(1)} %get-tuple-element.39), channel_id=1, source_target_pairs={{1,2},{2,1},{5,6},{6,5},{9,10},{10,9},{13,14},{14,13},{17,18},{18,... | collective-permute-start | bytes 49160 | tf_op jit(solution)/shard_map/ppermute | solution.py:420
  2.9 1.3 %fetch.1 = (s32[1,1024]{1,0:T(1,128)S(1)}, bf16[16,1024]{1,0:T(8,128)(2,1)S(1)}, bf16[16,128]{1,0:T(8,128)(2,1)S(1)}, bf16[27,128,128]{2,1,0:T(8,128)(2,1)S(1)}) custom-call(s32[1,1024]{1,0:T(1,128)} %bitcast.2, bf16[16,1024]{1,0:T(8,128)(2,1)} %refs_1_.1, bf16[16,128]{1,0:T(8,128)(2,1)} %refs_2_.1, bf16[27,128,128]{2,1,0:T(8,128)(2,1)} %refs_3_.1, ...), custom_call_target="tpu_custom_call" | custom-call | tf_op jit(solution)/shard_map/fetch/pallas_call | solution.py:31
  4.3 0.7 %collective-permute-start.2 = (bf16[80,128]{1,0:T(8,128)(2,1)S(1)}, bf16[80,128]{1,0:T(8,128)(2,1)S(1)}, u32[]{:S(2)}, u32[]{:S(2)}) collective-permute-start(bf16[80,128]{1,0:T(8,128)(2,1)S(1)} %get-tuple-element.45), channel_id=1, source_target_pairs={{4,8},{8,4},{12,16},{16,12},{20,24},{24,20},{5,9},{9,5},{13,17},{1... | collective-permute-start | bytes 61448 | tf_op jit(solution)/shard_map/ppermute | solution.py:557
  4.9 5.4 %collective-permute-start.3 = (bf16[80,128]{1,0:T(8,128)(2,1)S(1)}, bf16[80,128]{1,0:T(8,128)(2,1)S(1)}, u32[]{:S(2)}, u32[]{:S(2)}) collective-permute-start(bf16[80,128]{1,0:T(8,128)(2,1)S(1)} %get-tuple-element.46), channel_id=1, source_target_pairs={{0,4},{4,0},{8,12},{12,8},{16,20},{20,16},{24,28},{28,24},{1,5},{5... | collective-permute-start | bytes 61448 | tf_op jit(solution)/shard_map/ppermute | solution.py:558
  10.3 1.5 %main.1 = (bf16[8,64,1152]{2,1,0:T(8,128)(2,1)S(1)}, f32[512,128]{1,0:T(8,128)S(1)}, f32[8,64,128]{2,1,0:T(8,128)S(1)}, f32[32,512]{1,0:T(8,128)S(1)}) custom-call(bf16[4,128,128]{2,1,0:T(8,128)(2,1)S(1)} %get-tuple-element.32.feat_ref, s32[4,128]{1,0:T(4,128)S(1)} %get-tuple-element.33.occ_ref, s32[1,1024]{1,0:T(1,128)S(1)} %get-tuple-element.35.point_ref, ...), custom_call_target="tpu_custom_call" | custom-call | tf_op jit(solution)/shard_map/main/pallas_call | solution.py:31
  11.8 0.3 collective-permute-done.3.x_pair_ref
  12.1 1.3 %tile.1 = (bf16[8,64,128]{2,1,0:T(8,128)(2,1)S(1)}, bf16[2,64,1152]{2,1,0:T(8,128)(2,1)S(1)}, bf16[992,128]{1,0:T(8,128)(2,1)S(1)}) custom-call(bf16[8,64,1152]{2,1,0:T(8,128)(2,1)S(1)} %get-tuple-element.40.cols_ref, f32[512,128]{1,0:T(8,128)S(1)} %get-tuple-element.41.pre_ref, f32[8,64,128]{2,1,0:T(8,128)S(1)} %get-tuple-element.42.mask_ref, ...), custom_call_target="tpu_custom_call" | custom-call | tf_op jit(solution)/shard_map/tile/pallas_call | solution.py:31
  13.3 2.8 %collective-permute-start.5 = (bf16[992,128]{1,0:T(8,128)(2,1)S(1)}, bf16[992,128]{1,0:T(8,128)(2,1)S(1)}, u32[]{:S(2)}, u32[]{:S(2)}) collective-permute-start(bf16[992,128]{1,0:T(8,128)(2,1)S(1)} %get-tuple-element.51.refs_2_), channel_id=1, source_target_pairs={{0,1},{1,0},{2,3},{3,2},{4,5},{5,4},{6,7},{7,6},{8,9},{9,8},{10,11... | collective-permute-start | bytes 761864 | tf_op jit(solution)/shard_map/ppermute | solution.py:443
  16.1 1.2 %terms.1 = (bf16[2,64,128]{2,1,0:T(8,128)(2,1)S(1)}, f32[1728,128]{1,0:T(8,128)S(1)}, bf16[864,128]{1,0:T(8,128)(2,1)S(1)}) custom-call(bf16[8,64,1152]{2,1,0:T(8,128)(2,1)S(1)} %get-tuple-element.40.cols_ref, bf16[2,64,1152]{2,1,0:T(8,128)(2,1)S(1)} %get-tuple-element.47.ends_ref, bf16[8,64,128]{2,1,0:T(8,128)(2,1)S(1)} %get-tuple-element.48.grad_ref.refs_3_), custom_call_target="tpu_custom_call" | custom-call | tf_op jit(solution)/shard_map/terms/pallas_call | solution.py:31
  17.5 2.0 %collective-permute-start.7 = (bf16[432,128]{1,0:T(8,128)(2,1)S(1)}, bf16[432,128]{1,0:T(8,128)(2,1)S(1)}, u32[]{:S(2)}, u32[]{:S(2)}) collective-permute-start(bf16[432,128]{1,0:T(8,128)(2,1)S(1)} %message.12), channel_id=1, source_target_pairs={{0,3},{1,4},{2,7},{3,0},{4,1},{5,6},{6,5},{7,2},{8,13},{9,10},{10,... | collective-permute-start | bytes 331784 | tf_op jit(solution)/shard_map/ppermute | solution.py:443
  19.6 2.3 %collective-permute-done.7.refs_2_ = bf16[432,128]{1,0:T(8,128)(2,1)S(1)} collective-permute-done((bf16[432,128]{1,0:T(8,128)(2,1)S(1)}, bf16[432,128]{1,0:T(8,128)(2,1)S(1)}, u32[]{:S(2)}, u32[]{:S(2)}) %collective-permute-start.7) | collective-permute-done | bytes 110624 | tf_op jit(solution)/shard_map/ppermute | solution.py:443
  22.0 2.4 %collective-permute-start.8 = (bf16[432,128]{1,0:T(8,128)(2,1)S(1)}, bf16[432,128]{1,0:T(8,128)(2,1)S(1)}, u32[]{:S(2)}, u32[]{:S(2)}) collective-permute-start(bf16[432,128]{1,0:T(8,128)(2,1)S(1)} %message.13), channel_id=1, source_target_pairs={{0,5},{1,2},{2,1},{3,6},{4,7},{5,0},{6,3},{7,4},{8,11},{9,12},{10,... | collective-permute-start | bytes 331784 | tf_op jit(solution)/shard_map/ppermute | solution.py:443
  24.6 1.2 %collective-permute-done.9.refs_4_.got2_ref = bf16[128,128]{1,0:T(8,128)(2,1)S(1)} collective-permute-done((bf16[128,128]{1,0:T(8,128)(2,1)S(1)}, bf16[128,128]{1,0:T(8,128)(2,1)S(1)}, u32[]{:S(2)}, u32[]{:S(2)}) %collective-permute-start.9) | collective-permute-done | bytes 32800 | tf_op jit(solution)/shard_map/ppermute | solution.py:443
  25.8 1.1 %collective-permute-done.8.refs_3_ = bf16[432,128]{1,0:T(8,128)(2,1)S(1)} collective-permute-done((bf16[432,128]{1,0:T(8,128)(2,1)S(1)}, bf16[432,128]{1,0:T(8,128)(2,1)S(1)}, u32[]{:S(2)}, u32[]{:S(2)}) %collective-permute-start.8) | collective-permute-done | bytes 110624 | tf_op jit(solution)/shard_map/ppermute | solution.py:443
  26.9 3.8 %collective-permute-start.10 = (bf16[496,128]{1,0:T(8,128)(2,1)S(1)}, bf16[496,128]{1,0:T(8,128)(2,1)S(1)}, u32[]{:S(2)}, u32[]{:S(2)}) collective-permute-start(bf16[496,128]{1,0:T(8,128)(2,1)S(1)} %message.15.refs_0_), channel_id=1, source_target_pairs={{0,25},{1,8},{2,11},{3,26},{4,13},{5,28},{6,31},{7,14},{8,1},{9,16... | collective-permute-start | bytes 380936 | tf_op jit(solution)/shard_map/ppermute | solution.py:443
  30.7 3.6 %collective-permute-done.10.refs_1_.refs_0_ = bf16[496,128]{1,0:T(8,128)(2,1)S(1)} collective-permute-done((bf16[496,128]{1,0:T(8,128)(2,1)S(1)}, bf16[496,128]{1,0:T(8,128)(2,1)S(1)}, u32[]{:S(2)}, u32[]{:S(2)}) %collective-permute-start.10) | collective-permute-done | bytes 127008 | tf_op jit(solution)/shard_map/ppermute | solution.py:443
  34.5 5.0 %collective-permute-done.11.refs_1_ = bf16[496,128]{1,0:T(8,128)(2,1)S(1)} collective-permute-done((bf16[496,128]{1,0:T(8,128)(2,1)S(1)}, bf16[496,128]{1,0:T(8,128)(2,1)S(1)}, u32[]{:S(2)}, u32[]{:S(2)}) %collective-permute-start.11) | collective-permute-done | bytes 127008 | tf_op jit(solution)/shard_map/ppermute | solution.py:443
  39.5 1.4 %collective-permute-start.12 = (bf16[512,128]{1,0:T(8,128)(2,1)S(1)}, bf16[512,128]{1,0:T(8,128)(2,1)S(1)}, u32[]{:S(2)}, u32[]{:S(2)}) collective-permute-start(bf16[512,128]{1,0:T(8,128)(2,1)S(1)} %get-tuple-element.54.refs_0_), channel_id=1, source_target_pairs={{0,5},{1,2},{2,1},{3,6},{4,7},{5,0},{6,3},{7,4},{8,11},{9,12},{10,... | collective-permute-start | bytes 393224 | tf_op jit(solution)/shard_map/ppermute | solution.py:443
  40.9 1.1 %back.1.refs_1_.part_ref = f32[512,128]{1,0:T(8,128)S(1)} custom-call(bf16[8,64,128]{2,1,0:T(8,128)(2,1)S(1)} %get-tuple-element.55.grad_ref, bf16[2,64,128]{2,1,0:T(8,128)(2,1)S(1)} %get-tuple-element.56.planes_ref, bf16[27,128,128]{2,1,0:T(8,128)(2,1)S(1)} %get-tuple-element.37.weight_ref.refs_0_), custom_call_target="tpu_custom_call" | custom-call | tf_op jit(solution)/shard_map/back/pallas_call | solution.py:31
  42.0 1.5 %collective-permute-start.13 = (bf16[512,128]{1,0:T(8,128)(2,1)S(1)}, bf16[512,128]{1,0:T(8,128)(2,1)S(1)}, u32[]{:S(2)}, u32[]{:S(2)}) collective-permute-start(bf16[512,128]{1,0:T(8,128)(2,1)S(1)} %message.18), channel_id=1, source_target_pairs={{0,3},{1,4},{2,7},{3,0},{4,1},{5,6},{6,5},{7,2},{8,13},{9,10},{10,... | collective-permute-start | bytes 393224 | tf_op jit(solution)/shard_map/ppermute | solution.py:443
  43.6 0.4 collective-permute-done.12.refs_0_.line_ref.refs_1_
  44.0 1.9 %collective-permute-start.14 = (bf16[432,128]{1,0:T(8,128)(2,1)S(1)}, bf16[432,128]{1,0:T(8,128)(2,1)S(1)}, u32[]{:S(2)}, u32[]{:S(2)}) collective-permute-start(bf16[432,128]{1,0:T(8,128)(2,1)S(1)} %message.20), channel_id=1, source_target_pairs={{0,3},{1,4},{2,7},{3,0},{4,1},{5,6},{6,5},{7,2},{8,13},{9,10},{10,... | collective-permute-start | bytes 331784 | tf_op jit(solution)/shard_map/ppermute | solution.py:443
  45.9 0.6 %collective-permute-done.13.refs_0_.far_ref = bf16[512,128]{1,0:T(8,128)(2,1)S(1)} collective-permute-done((bf16[512,128]{1,0:T(8,128)(2,1)S(1)}, bf16[512,128]{1,0:T(8,128)(2,1)S(1)}, u32[]{:S(2)}, u32[]{:S(2)}) %collective-permute-start.13) | collective-permute-done | bytes 131104 | tf_op jit(solution)/shard_map/ppermute | solution.py:443
  46.5 0.4 collective-permute-start.17
  47.1 0.4 collective-permute-start.15
  47.5 0.8 %collective-permute-done.14.refs_3_ = bf16[432,128]{1,0:T(8,128)(2,1)S(1)} collective-permute-done((bf16[432,128]{1,0:T(8,128)(2,1)S(1)}, bf16[432,128]{1,0:T(8,128)(2,1)S(1)}, u32[]{:S(2)}, u32[]{:S(2)}) %collective-permute-start.14) | collective-permute-done | bytes 110624 | tf_op jit(solution)/shard_map/ppermute | solution.py:443
  48.3 0.4 collective-permute-start.18
  48.8 0.5 %y_faces.1 = (bf16[4,128,128]{2,1,0:T(8,128)(2,1)S(1)}, f32[8,128]{1,0:T(8,128)S(1)}) custom-call(f32[512,128]{1,0:T(8,128)S(1)} %back.1.refs_1_.part_ref, f32[8,64,128]{2,1,0:T(8,128)S(1)} %get-tuple-element.42.mask_ref, bf16[27,128,128]{2,1,0:T(8,128)(2,1)S(1)} %get-tuple-element.37.weight_ref.refs_0_, ...), custom_call_target="tpu_custom_call" | custom-call | tf_op jit(solution)/shard_map/y_faces/pallas_call | solution.py:31
  49.3 0.4 collective-permute-done.18.refs_7_
  49.7 1.4 %normalise.1 = (f32[3456,128]{1,0:T(8,128)}, bf16[4,128,128]{2,1,0:T(8,128)(2,1)}) custom-call(bf16[512,128]{1,0:T(8,128)(2,1)S(1)} %get-tuple-element.54.refs_0_, bf16[512,128]{1,0:T(8,128)(2,1)S(1)} %collective-permute-done.12.refs_0_.line_ref.refs_1_, bf16[512,128]{1,0:T(8,128)(2,1)S(1)} %message.19.refs_1_.refs_2_, ...), custom_call_target="tpu_custom_call" | custom-call | tf_op jit(solution)/shard_map/normalise/pallas_call | solution.py:658
  (27 shorter events, 1.1 us)
Async XLA Ops:
  1.8 2.4 %collective-permute-start = (bf16[64,128]{1,0:T(8,128)(2,1)S(1)}, bf16[64,128]{1,0:T(8,128)(2,1)S(1)}, u32[]{:S(2)}, u32[]{:S(2)}) collective-permute-start(bf16[64,128]{1,0:T(8,128)(2,1)S(1)} %get-tuple-element.38), channel_id=1, source_target_pairs={{0,1},{1,0},{2,3},{3,2},{4,5},{5,4},{6,7},{7,6},{8,9},{9,8},{10,11... | collective-permute-start | bytes 49160 | tf_op jit(solution)/shard_map/ppermute | solution.py:419
  2.3 1.9 %collective-permute-start.1 = (bf16[64,128]{1,0:T(8,128)(2,1)S(1)}, bf16[64,128]{1,0:T(8,128)(2,1)S(1)}, u32[]{:S(2)}, u32[]{:S(2)}) collective-permute-start(bf16[64,128]{1,0:T(8,128)(2,1)S(1)} %get-tuple-element.39), channel_id=1, source_target_pairs={{1,2},{2,1},{5,6},{6,5},{9,10},{10,9},{13,14},{14,13},{17,18},{18,... | collective-permute-start | bytes 49160 | tf_op jit(solution)/shard_map/ppermute | solution.py:420
  4.3 7.5 %collective-permute-start.2 = (bf16[80,128]{1,0:T(8,128)(2,1)S(1)}, bf16[80,128]{1,0:T(8,128)(2,1)S(1)}, u32[]{:S(2)}, u32[]{:S(2)}) collective-permute-start(bf16[80,128]{1,0:T(8,128)(2,1)S(1)} %get-tuple-element.45), channel_id=1, source_target_pairs={{4,8},{8,4},{12,16},{16,12},{20,24},{24,20},{5,9},{9,5},{13,17},{1... | collective-permute-start | bytes 61448 | tf_op jit(solution)/shard_map/ppermute | solution.py:557
  4.9 7.1 %collective-permute-start.3 = (bf16[80,128]{1,0:T(8,128)(2,1)S(1)}, bf16[80,128]{1,0:T(8,128)(2,1)S(1)}, u32[]{:S(2)}, u32[]{:S(2)}) collective-permute-start(bf16[80,128]{1,0:T(8,128)(2,1)S(1)} %get-tuple-element.46), channel_id=1, source_target_pairs={{0,4},{4,0},{8,12},{12,8},{16,20},{20,16},{24,28},{28,24},{1,5},{5... | collective-permute-start | bytes 61448 | tf_op jit(solution)/shard_map/ppermute | solution.py:558
  13.3 4.1 %collective-permute-start.5 = (bf16[992,128]{1,0:T(8,128)(2,1)S(1)}, bf16[992,128]{1,0:T(8,128)(2,1)S(1)}, u32[]{:S(2)}, u32[]{:S(2)}) collective-permute-start(bf16[992,128]{1,0:T(8,128)(2,1)S(1)} %get-tuple-element.51.refs_2_), channel_id=1, source_target_pairs={{0,1},{1,0},{2,3},{3,2},{4,5},{5,4},{6,7},{7,6},{8,9},{9,8},{10,11... | collective-permute-start | bytes 761864 | tf_op jit(solution)/shard_map/ppermute | solution.py:443
  17.3 2.3 %collective-permute-start.4 = (bf16[864,128]{1,0:T(8,128)(2,1)S(1)}, bf16[864,128]{1,0:T(8,128)(2,1)S(1)}, u32[]{:S(2)}, u32[]{:S(2)}) collective-permute-start(bf16[864,128]{1,0:T(8,128)(2,1)S(1)} %get-tuple-element.50), channel_id=1, source_target_pairs={{0,1},{1,0},{2,3},{3,2},{4,5},{5,4},{6,7},{7,6},{8,9},{9,8},{10,11... | collective-permute-start | bytes 663560 | tf_op jit(solution)/shard_map/ppermute | solution.py:443
  17.5 4.5 %collective-permute-start.7 = (bf16[432,128]{1,0:T(8,128)(2,1)S(1)}, bf16[432,128]{1,0:T(8,128)(2,1)S(1)}, u32[]{:S(2)}, u32[]{:S(2)}) collective-permute-start(bf16[432,128]{1,0:T(8,128)(2,1)S(1)} %message.12), channel_id=1, source_target_pairs={{0,3},{1,4},{2,7},{3,0},{4,1},{5,6},{6,5},{7,2},{8,13},{9,10},{10,... | collective-permute-start | bytes 331784 | tf_op jit(solution)/shard_map/ppermute | solution.py:443
  19.6 4.9 %collective-permute-start.6 = (bf16[688,128]{1,0:T(8,128)(2,1)S(1)}, bf16[688,128]{1,0:T(8,128)(2,1)S(1)}, u32[]{:S(2)}, u32[]{:S(2)}) collective-permute-start(bf16[688,128]{1,0:T(8,128)(2,1)S(1)} %message.11), channel_id=1, source_target_pairs={{0,3},{1,4},{2,7},{3,0},{4,1},{5,6},{6,5},{7,2},{8,13},{9,10},{10,... | collective-permute-start | bytes 528392 | tf_op jit(solution)/shard_map/ppermute | solution.py:443
  22.0 4.9 %collective-permute-start.8 = (bf16[432,128]{1,0:T(8,128)(2,1)S(1)}, bf16[432,128]{1,0:T(8,128)(2,1)S(1)}, u32[]{:S(2)}, u32[]{:S(2)}) collective-permute-start(bf16[432,128]{1,0:T(8,128)(2,1)S(1)} %message.13), channel_id=1, source_target_pairs={{0,5},{1,2},{2,1},{3,6},{4,7},{5,0},{6,3},{7,4},{8,11},{9,12},{10,... | collective-permute-start | bytes 331784 | tf_op jit(solution)/shard_map/ppermute | solution.py:443
  24.5 1.3 %collective-permute-start.9 = (bf16[128,128]{1,0:T(8,128)(2,1)S(1)}, bf16[128,128]{1,0:T(8,128)(2,1)S(1)}, u32[]{:S(2)}, u32[]{:S(2)}) collective-permute-start(bf16[128,128]{1,0:T(8,128)(2,1)S(1)} %message.14), channel_id=1, source_target_pairs={{0,1},{1,0},{2,3},{3,2},{4,5},{5,4},{6,7},{7,6},{8,9},{9,8},{10,11... | collective-permute-start | bytes 98312 | tf_op jit(solution)/shard_map/ppermute | solution.py:443
  26.9 7.4 %collective-permute-start.10 = (bf16[496,128]{1,0:T(8,128)(2,1)S(1)}, bf16[496,128]{1,0:T(8,128)(2,1)S(1)}, u32[]{:S(2)}, u32[]{:S(2)}) collective-permute-start(bf16[496,128]{1,0:T(8,128)(2,1)S(1)} %message.15.refs_0_), channel_id=1, source_target_pairs={{0,25},{1,8},{2,11},{3,26},{4,13},{5,28},{6,31},{7,14},{8,1},{9,16... | collective-permute-start | bytes 380936 | tf_op jit(solution)/shard_map/ppermute | solution.py:443
  34.3 5.1 %collective-permute-start.11 = (bf16[496,128]{1,0:T(8,128)(2,1)S(1)}, bf16[496,128]{1,0:T(8,128)(2,1)S(1)}, u32[]{:S(2)}, u32[]{:S(2)}) collective-permute-start(bf16[496,128]{1,0:T(8,128)(2,1)S(1)} %message.16.refs_0_), channel_id=1, source_target_pairs={{0,9},{1,24},{2,27},{3,10},{4,29},{5,12},{6,15},{7,30},{8,17},{9,0... | collective-permute-start | bytes 380936 | tf_op jit(solution)/shard_map/ppermute | solution.py:443
  39.5 4.5 %collective-permute-start.12 = (bf16[512,128]{1,0:T(8,128)(2,1)S(1)}, bf16[512,128]{1,0:T(8,128)(2,1)S(1)}, u32[]{:S(2)}, u32[]{:S(2)}) collective-permute-start(bf16[512,128]{1,0:T(8,128)(2,1)S(1)} %get-tuple-element.54.refs_0_), channel_id=1, source_target_pairs={{0,5},{1,2},{2,1},{3,6},{4,7},{5,0},{6,3},{7,4},{8,11},{9,12},{10,... | collective-permute-start | bytes 393224 | tf_op jit(solution)/shard_map/ppermute | solution.py:443
  42.0 4.5 %collective-permute-start.13 = (bf16[512,128]{1,0:T(8,128)(2,1)S(1)}, bf16[512,128]{1,0:T(8,128)(2,1)S(1)}, u32[]{:S(2)}, u32[]{:S(2)}) collective-permute-start(bf16[512,128]{1,0:T(8,128)(2,1)S(1)} %message.18), channel_id=1, source_target_pairs={{0,3},{1,4},{2,7},{3,0},{4,1},{5,6},{6,5},{7,2},{8,13},{9,10},{10,... | collective-permute-start | bytes 393224 | tf_op jit(solution)/shard_map/ppermute | solution.py:443
  44.0 4.4 %collective-permute-start.14 = (bf16[432,128]{1,0:T(8,128)(2,1)S(1)}, bf16[432,128]{1,0:T(8,128)(2,1)S(1)}, u32[]{:S(2)}, u32[]{:S(2)}) collective-permute-start(bf16[432,128]{1,0:T(8,128)(2,1)S(1)} %message.20), channel_id=1, source_target_pairs={{0,3},{1,4},{2,7},{3,0},{4,1},{5,6},{6,5},{7,2},{8,13},{9,10},{10,... | collective-permute-start | bytes 331784 | tf_op jit(solution)/shard_map/ppermute | solution.py:443
  46.5 2.2 %collective-permute-start.17 = (bf16[512,128]{1,0:T(8,128)(2,1)S(1)}, bf16[512,128]{1,0:T(8,128)(2,1)S(1)}, u32[]{:S(2)}, u32[]{:S(2)}) collective-permute-start(bf16[512,128]{1,0:T(8,128)(2,1)S(1)} %message.19.refs_1_.refs_2_), channel_id=1, source_target_pairs={{0,1},{1,0},{2,3},{3,2},{4,5},{5,4},{6,7},{7,6},{8,9},{9,8},{10,11... | collective-permute-start | bytes 393224 | tf_op jit(solution)/shard_map/ppermute | solution.py:443
  46.9 1.9 %collective-permute-start.16 = (bf16[512,128]{1,0:T(8,128)(2,1)S(1)}, bf16[512,128]{1,0:T(8,128)(2,1)S(1)}, u32[]{:S(2)}, u32[]{:S(2)}) collective-permute-start(bf16[512,128]{1,0:T(8,128)(2,1)S(1)} %collective-permute-done.12.refs_0_.line_ref.refs_1_), channel_id=1, source_target_pairs={{0,1},{1,0},{2,3},{3,2},{4,5},{5,4},{6,7},{7,6},{8,9},{9,8},{10,11... | collective-permute-start | bytes 393224 | tf_op jit(solution)/shard_map/ppermute | solution.py:443
  47.1 1.6 %collective-permute-start.15 = (bf16[432,128]{1,0:T(8,128)(2,1)S(1)}, bf16[432,128]{1,0:T(8,128)(2,1)S(1)}, u32[]{:S(2)}, u32[]{:S(2)}) collective-permute-start(bf16[432,128]{1,0:T(8,128)(2,1)S(1)} %message.21), channel_id=1, source_target_pairs={{0,1},{1,0},{2,3},{3,2},{4,5},{5,4},{6,7},{7,6},{8,9},{9,8},{10,11... | collective-permute-start | bytes 331784 | tf_op jit(solution)/shard_map/ppermute | solution.py:443
  48.3 1.4 %collective-permute-start.18 = (bf16[432,128]{1,0:T(8,128)(2,1)S(1)}, bf16[432,128]{1,0:T(8,128)(2,1)S(1)}, u32[]{:S(2)}, u32[]{:S(2)}) collective-permute-start(bf16[432,128]{1,0:T(8,128)(2,1)S(1)} %collective-permute-done.14.refs_3_), channel_id=1, source_target_pairs={{0,1},{1,0},{2,3},{3,2},{4,5},{5,4},{6,7},{7,6},{8,9},{9,8},{10,11... | collective-permute-start | bytes 331784 | tf_op jit(solution)/shard_map/ppermute | solution.py:443

commit v8 on v7

--- a/solution.py
+++ b/solution.py
@@ -360,18 +360,19 @@
 
 
 def y_faces_kernel(
-    extra_ref, part_ref, mask_ref, weight_ref, near_ref, far_ref, line_ref, *refs
+    extra_ref, part_ref, mask_ref, weight_ref, near_ref, far_ref, *refs
 ):
     pieces, (out_ref, squares_ref, cols_ref) = refs[:-3], refs[-3:]
     channels, rows = part_ref.shape[1], (SIDE + 2) * SIDE
     tx, ty = lax.axis_index("tx"), lax.axis_index("ty")
-    total = sum(squares(ref, near_ref.shape[0] - rows) for ref in pieces)
+    part = near_ref.shape[0] - 2 * rows
+    total = sum(squares(ref, part) for ref in pieces)
     squares_ref[...] = jnp.broadcast_to(total, squares_ref.shape)
-    by_first, by_second = far_ref[far_ref.shape[0] - rows :], line_ref[line_ref.shape[0] - rows :]
-    other = jnp.where(lane_of(tx, ty) == 0, by_first.astype(F32), by_second.astype(F32))
+    own, by_core = far_ref[part:].astype(F32), near_ref[part + rows :].astype(F32)
+    other = jnp.where(lane_of(tx, ty) == 0, own, by_core)
     beyond = jnp.zeros(other.shape, F32) if extra_ref is None else extra_ref[...].astype(F32)
     other = jnp.where(((ty + 1) & 2) == 2, other, beyond)
-    pair = near_ref[near_ref.shape[0] - rows :].astype(F32)
+    pair = near_ref[part : part + rows].astype(F32)
     even = parity("ty")
     added = []
     for dy, face in ((0, jnp.where(even, other, pair)), (2, jnp.where(even, pair, other))):
@@ -463,6 +464,11 @@
 
 def along_line(flips):
     return lambda tx, ty: same_lane(tx, ty, tx ^ (2 * flips[lane_of(tx, ty)]), ty)
+
+
+def inner_face(own, other):
+    inner = ((lax.axis_index("ty") + 1) & 2) == 2
+    return jnp.where(inner, own, other)
 
 
 def add(*terms):
@@ -626,7 +632,7 @@
     kernel = functools.partial(hand_on_edge_kernel, flips, at)
     g_a, g_b, planes = edge_faces(kernel, g_edges, (got1, x_faces, *lines))
     rows = g_a.shape[0]
-    total, gradient = message(total + [(rows, add, (g_b, 0))], (), (gradient,))
+    total, gradient = message(total, (), (gradient,))
     piece1 = exchange_with(total, second_way)
     back_part = call(
         back_kernel,
@@ -635,14 +641,15 @@
         (cols,),
         name="back",
     )
-    piece2 = exchange_with(message([(part + rows, add, (total, 0))], (back_part,)), first_way)
-    onward = message([(part, add, (piece1, 0))])
-    piece3 = exchange_with(onward, first_way)
-    near = message([(part, add, (piece2, 0)), (rows, add, (g_a, 0))])
+    other_b = exchange_with(g_b, by_core)
+    face = (rows, inner_face, (g_b, 0), (other_b, 0))
+    piece2 = exchange_with(message([(part, add, (total, 0)), face], (back_part,)), first_way)
+    piece3 = exchange_with(piece1, first_way)
+    near = message([(part, add, (piece2, 0)), (rows, add, (g_a, 0)), (rows, add, (piece2, part))])
     pieces = (total, piece1, near, piece3)
     late = message([(part, add, (total, 0))], (near,))
     others = [exchange_with(piece, by_core) for piece in (late, *pieces[1:])]
-    faces = (back_part, mask, weight, others[2], piece2, piece1, *pieces, *others[:3])
+    faces = (back_part, mask, weight, others[2], piece2, *pieces, *others[:3])
     kernel = functools.partial(y_faces_kernel, None)
     if n_ty > 4:
         pairs = [pair for i in range(3, n_ty - 1, 4) for pair in ((i, i + 1), (i + 1, i))]

time: 51.7 us -> 51.3 us (level)
    ppermute x15 -> x16, starting transfers between devices: 17.6 us -> 17.4 us  [exchange_with(): return lax.ppermute(value, ('tx', 'ty'), pairs)]
    ppermute x15 -> x16, waiting for transfers between devices: 15.4 us -> 15.5 us  [exchange_with(): return lax.ppermute(value, ('tx', 'ty'), pairs)]
  transfers between devices with their start and end apart: 19 -> 20, of which waited for: 11 -> 10; matrix products, arithmetic and copies ran while one was open for 0% -> 0% of each run, Pallas kernels for 11% -> 11%
where the time goes in v8:
time: 51.3 us; the launch traced here: 51.1 us
  starting transfers between devices  24.6 us (48%)
  waiting for transfers between devices  15.8 us (31%)
  Pallas kernels  9.8 us (19%)
  between operations  0.8 us (2%)
    ppermute x16, starting transfers between devices, exchange_with(): return lax.ppermute(value, ('tx', 'ty'), pairs)  17.4 us
    ppermute x16, waiting for transfers between devices, exchange_with(): return lax.ppermute(value, ('tx', 'ty'), pairs)  15.5 us
    pallas_call x7, Pallas kernels, call(): pl.pallas_call(body, out_shape=outs, in_specs=[pl.BlockSpec(memory_space=...  7.97 us
    ppermute x1, starting transfers between devices, on_device(): x_pair = lax.ppermute(x_pair, 'tx', swap_pairs(0, n_tx))  5.37 us
    pallas_call x1, Pallas kernels, on_device(): pl.pallas_call(norm_kernel, out_shape=(shape((kernels * channels, channel...  1.46 us
  transfers between devices with their start and end apart: 20, of which 10 were waited for; matrix products, arithmetic and copies ran while one was open for 0% of the time, Pallas kernels for 11%

profile of v8, /device:TPU:0, one launch (start us, length us, event | category | flops | bytes accessed | tf_op | source)
XLA Modules:
  0.0 51.1 jit_solution(15123314673302667765)
XLA Ops:
  0.6 1.1 %first_faces.1 = (bf16[64,128]{1,0:T(8,128)(2,1)S(1)}, bf16[64,128]{1,0:T(8,128)(2,1)S(1)}, bf16[2,64,128]{2,1,0:T(8,128)(2,1)S(1)}, bf16[4,128,128]{2,1,0:T(8,128)(2,1)S(1)}, s32[4,128]{1,0:T(4,128)S(1)}) custom-call(bf16[4,128,128]{2,1,0:T(8,128)(2,1)} %feat_hbm.1, s32[4,128]{1,0:T(4,128)} %occ_hbm.1), custom_call_target="tpu_custom_call" | custom-call | tf_op jit(solution)/shard_map/first_faces/pallas_call | solution.py:31
  1.8 0.5 %collective-permute-start = (bf16[64,128]{1,0:T(8,128)(2,1)S(1)}, bf16[64,128]{1,0:T(8,128)(2,1)S(1)}, u32[]{:S(2)}, u32[]{:S(2)}) collective-permute-start(bf16[64,128]{1,0:T(8,128)(2,1)S(1)} %get-tuple-element.38), channel_id=1, source_target_pairs={{0,1},{1,0},{2,3},{3,2},{4,5},{5,4},{6,7},{7,6},{8,9},{9,8},{10,11... | collective-permute-start | bytes 49160 | tf_op jit(solution)/shard_map/ppermute | solution.py:420
  2.3 0.7 %collective-permute-start.1 = (bf16[64,128]{1,0:T(8,128)(2,1)S(1)}, bf16[64,128]{1,0:T(8,128)(2,1)S(1)}, u32[]{:S(2)}, u32[]{:S(2)}) collective-permute-start(bf16[64,128]{1,0:T(8,128)(2,1)S(1)} %get-tuple-element.39), channel_id=1, source_target_pairs={{1,2},{2,1},{5,6},{6,5},{9,10},{10,9},{13,14},{14,13},{17,18},{18,... | collective-permute-start | bytes 49160 | tf_op jit(solution)/shard_map/ppermute | solution.py:421
  2.9 1.3 %fetch.1 = (s32[1,1024]{1,0:T(1,128)S(1)}, bf16[16,1024]{1,0:T(8,128)(2,1)S(1)}, bf16[16,128]{1,0:T(8,128)(2,1)S(1)}, bf16[27,128,128]{2,1,0:T(8,128)(2,1)S(1)}) custom-call(s32[1,1024]{1,0:T(1,128)} %bitcast.2, bf16[16,1024]{1,0:T(8,128)(2,1)} %refs_1_.1, bf16[16,128]{1,0:T(8,128)(2,1)} %refs_2_.1, bf16[27,128,128]{2,1,0:T(8,128)(2,1)} %refs_3_.1, ...), custom_call_target="tpu_custom_call" | custom-call | tf_op jit(solution)/shard_map/fetch/pallas_call | solution.py:31
  4.3 0.7 %collective-permute-start.2 = (bf16[80,128]{1,0:T(8,128)(2,1)S(1)}, bf16[80,128]{1,0:T(8,128)(2,1)S(1)}, u32[]{:S(2)}, u32[]{:S(2)}) collective-permute-start(bf16[80,128]{1,0:T(8,128)(2,1)S(1)} %get-tuple-element.45), channel_id=1, source_target_pairs={{4,8},{8,4},{12,16},{16,12},{20,24},{24,20},{5,9},{9,5},{13,17},{1... | collective-permute-start | bytes 61448 | tf_op jit(solution)/shard_map/ppermute | solution.py:563
  4.9 5.4 %collective-permute-start.3 = (bf16[80,128]{1,0:T(8,128)(2,1)S(1)}, bf16[80,128]{1,0:T(8,128)(2,1)S(1)}, u32[]{:S(2)}, u32[]{:S(2)}) collective-permute-start(bf16[80,128]{1,0:T(8,128)(2,1)S(1)} %get-tuple-element.46), channel_id=1, source_target_pairs={{0,4},{4,0},{8,12},{12,8},{16,20},{20,16},{24,28},{28,24},{1,5},{5... | collective-permute-start | bytes 61448 | tf_op jit(solution)/shard_map/ppermute | solution.py:564
  10.3 1.5 %main.1 = (bf16[8,64,1152]{2,1,0:T(8,128)(2,1)S(1)}, f32[512,128]{1,0:T(8,128)S(1)}, f32[8,64,128]{2,1,0:T(8,128)S(1)}, f32[32,512]{1,0:T(8,128)S(1)}) custom-call(bf16[4,128,128]{2,1,0:T(8,128)(2,1)S(1)} %get-tuple-element.32.feat_ref, s32[4,128]{1,0:T(4,128)S(1)} %get-tuple-element.33.occ_ref, s32[1,1024]{1,0:T(1,128)S(1)} %get-tuple-element.35.point_ref, ...), custom_call_target="tpu_custom_call" | custom-call | tf_op jit(solution)/shard_map/main/pallas_call | solution.py:31
  11.8 0.3 collective-permute-done.3.x_pair_ref
  12.1 1.3 %tile.1 = (bf16[8,64,128]{2,1,0:T(8,128)(2,1)S(1)}, bf16[2,64,1152]{2,1,0:T(8,128)(2,1)S(1)}, bf16[992,128]{1,0:T(8,128)(2,1)S(1)}) custom-call(bf16[8,64,1152]{2,1,0:T(8,128)(2,1)S(1)} %get-tuple-element.40.cols_ref, f32[512,128]{1,0:T(8,128)S(1)} %get-tuple-element.41.pre_ref, f32[8,64,128]{2,1,0:T(8,128)S(1)} %get-tuple-element.42.mask_ref, ...), custom_call_target="tpu_custom_call" | custom-call | tf_op jit(solution)/shard_map/tile/pallas_call | solution.py:31
  13.3 2.8 %collective-permute-start.5 = (bf16[992,128]{1,0:T(8,128)(2,1)S(1)}, bf16[992,128]{1,0:T(8,128)(2,1)S(1)}, u32[]{:S(2)}, u32[]{:S(2)}) collective-permute-start(bf16[992,128]{1,0:T(8,128)(2,1)S(1)} %get-tuple-element.51.refs_2_), channel_id=1, source_target_pairs={{0,1},{1,0},{2,3},{3,2},{4,5},{5,4},{6,7},{7,6},{8,9},{9,8},{10,11... | collective-permute-start | bytes 761864 | tf_op jit(solution)/shard_map/ppermute | solution.py:444
  16.1 1.2 %terms.1 = (bf16[2,64,128]{2,1,0:T(8,128)(2,1)S(1)}, f32[1728,128]{1,0:T(8,128)S(1)}, bf16[864,128]{1,0:T(8,128)(2,1)S(1)}) custom-call(bf16[8,64,1152]{2,1,0:T(8,128)(2,1)S(1)} %get-tuple-element.40.cols_ref, bf16[2,64,1152]{2,1,0:T(8,128)(2,1)S(1)} %get-tuple-element.47.ends_ref, bf16[8,64,128]{2,1,0:T(8,128)(2,1)S(1)} %get-tuple-element.48.grad_ref.refs_2_), custom_call_target="tpu_custom_call" | custom-call | tf_op jit(solution)/shard_map/terms/pallas_call | solution.py:31
  17.5 2.0 %collective-permute-start.7 = (bf16[432,128]{1,0:T(8,128)(2,1)S(1)}, bf16[432,128]{1,0:T(8,128)(2,1)S(1)}, u32[]{:S(2)}, u32[]{:S(2)}) collective-permute-start(bf16[432,128]{1,0:T(8,128)(2,1)S(1)} %message.11), channel_id=1, source_target_pairs={{0,3},{1,4},{2,7},{3,0},{4,1},{5,6},{6,5},{7,2},{8,13},{9,10},{10,... | collective-permute-start | bytes 331784 | tf_op jit(solution)/shard_map/ppermute | solution.py:444
  19.6 2.3 %collective-permute-done.7.refs_2_ = bf16[432,128]{1,0:T(8,128)(2,1)S(1)} collective-permute-done((bf16[432,128]{1,0:T(8,128)(2,1)S(1)}, bf16[432,128]{1,0:T(8,128)(2,1)S(1)}, u32[]{:S(2)}, u32[]{:S(2)}) %collective-permute-start.7) | collective-permute-done | bytes 110624 | tf_op jit(solution)/shard_map/ppermute | solution.py:444
  22.0 2.4 %collective-permute-start.8 = (bf16[432,128]{1,0:T(8,128)(2,1)S(1)}, bf16[432,128]{1,0:T(8,128)(2,1)S(1)}, u32[]{:S(2)}, u32[]{:S(2)}) collective-permute-start(bf16[432,128]{1,0:T(8,128)(2,1)S(1)} %message.12), channel_id=1, source_target_pairs={{0,5},{1,2},{2,1},{3,6},{4,7},{5,0},{6,3},{7,4},{8,11},{9,12},{10,... | collective-permute-start | bytes 331784 | tf_op jit(solution)/shard_map/ppermute | solution.py:444
  24.6 1.2 %collective-permute-done.9.refs_4_.got2_ref = bf16[128,128]{1,0:T(8,128)(2,1)S(1)} collective-permute-done((bf16[128,128]{1,0:T(8,128)(2,1)S(1)}, bf16[128,128]{1,0:T(8,128)(2,1)S(1)}, u32[]{:S(2)}, u32[]{:S(2)}) %collective-permute-start.9) | collective-permute-done | bytes 32800 | tf_op jit(solution)/shard_map/ppermute | solution.py:444
  25.8 1.1 %collective-permute-done.8.refs_3_ = bf16[432,128]{1,0:T(8,128)(2,1)S(1)} collective-permute-done((bf16[432,128]{1,0:T(8,128)(2,1)S(1)}, bf16[432,128]{1,0:T(8,128)(2,1)S(1)}, u32[]{:S(2)}, u32[]{:S(2)}) %collective-permute-start.8) | collective-permute-done | bytes 110624 | tf_op jit(solution)/shard_map/ppermute | solution.py:444
  26.9 3.8 %collective-permute-start.10 = (bf16[496,128]{1,0:T(8,128)(2,1)S(1)}, bf16[496,128]{1,0:T(8,128)(2,1)S(1)}, u32[]{:S(2)}, u32[]{:S(2)}) collective-permute-start(bf16[496,128]{1,0:T(8,128)(2,1)S(1)} %message.14.refs_0_), channel_id=1, source_target_pairs={{0,25},{1,8},{2,11},{3,26},{4,13},{5,28},{6,31},{7,14},{8,1},{9,16... | collective-permute-start | bytes 380936 | tf_op jit(solution)/shard_map/ppermute | solution.py:444
  30.7 3.6 %collective-permute-done.10.refs_1_.refs_0_ = bf16[496,128]{1,0:T(8,128)(2,1)S(1)} collective-permute-done((bf16[496,128]{1,0:T(8,128)(2,1)S(1)}, bf16[496,128]{1,0:T(8,128)(2,1)S(1)}, u32[]{:S(2)}, u32[]{:S(2)}) %collective-permute-start.10) | collective-permute-done | bytes 127008 | tf_op jit(solution)/shard_map/ppermute | solution.py:444
  34.3 0.2 collective-permute-start.11
  34.5 5.0 %collective-permute-done.11.refs_1_ = bf16[496,128]{1,0:T(8,128)(2,1)S(1)} collective-permute-done((bf16[496,128]{1,0:T(8,128)(2,1)S(1)}, bf16[496,128]{1,0:T(8,128)(2,1)S(1)}, u32[]{:S(2)}, u32[]{:S(2)}) %collective-permute-start.11) | collective-permute-done | bytes 127008 | tf_op jit(solution)/shard_map/ppermute | solution.py:444
  39.5 1.4 %collective-permute-start.12 = (bf16[432,128]{1,0:T(8,128)(2,1)S(1)}, bf16[432,128]{1,0:T(8,128)(2,1)S(1)}, u32[]{:S(2)}, u32[]{:S(2)}) collective-permute-start(bf16[432,128]{1,0:T(8,128)(2,1)S(1)} %get-tuple-element.52.refs_0_), channel_id=1, source_target_pairs={{0,5},{1,2},{2,1},{3,6},{4,7},{5,0},{6,3},{7,4},{8,11},{9,12},{10,... | collective-permute-start | bytes 331784 | tf_op jit(solution)/shard_map/ppermute | solution.py:444
  41.0 1.1 %back.1.refs_3_.part_ref = f32[512,128]{1,0:T(8,128)S(1)} custom-call(bf16[8,64,128]{2,1,0:T(8,128)(2,1)S(1)} %get-tuple-element.55.grad_ref, bf16[2,64,128]{2,1,0:T(8,128)(2,1)S(1)} %get-tuple-element.56.planes_ref, bf16[27,128,128]{2,1,0:T(8,128)(2,1)S(1)} %get-tuple-element.37.weight_ref.refs_0_), custom_call_target="tpu_custom_call" | custom-call | tf_op jit(solution)/shard_map/back/pallas_call | solution.py:31
  42.2 1.6 %collective-permute-start.14 = (bf16[512,128]{1,0:T(8,128)(2,1)S(1)}, bf16[512,128]{1,0:T(8,128)(2,1)S(1)}, u32[]{:S(2)}, u32[]{:S(2)}) collective-permute-start(bf16[512,128]{1,0:T(8,128)(2,1)S(1)} %message.17), channel_id=1, source_target_pairs={{0,3},{1,4},{2,7},{3,0},{4,1},{5,6},{6,5},{7,2},{8,13},{9,10},{10,... | collective-permute-start | bytes 393224 | tf_op jit(solution)/shard_map/ppermute | solution.py:444
  43.8 1.1 %collective-permute-start.15 = (bf16[432,128]{1,0:T(8,128)(2,1)S(1)}, bf16[432,128]{1,0:T(8,128)(2,1)S(1)}, u32[]{:S(2)}, u32[]{:S(2)}) collective-permute-start(bf16[432,128]{1,0:T(8,128)(2,1)S(1)} %collective-permute-done.12.refs_1_), channel_id=1, source_target_pairs={{0,3},{1,4},{2,7},{3,0},{4,1},{5,6},{6,5},{7,2},{8,13},{9,10},{10,... | collective-permute-start | bytes 331784 | tf_op jit(solution)/shard_map/ppermute | solution.py:444
  44.9 1.7 %collective-permute-done.14.refs_0_.far_ref = bf16[512,128]{1,0:T(8,128)(2,1)S(1)} collective-permute-done((bf16[512,128]{1,0:T(8,128)(2,1)S(1)}, bf16[512,128]{1,0:T(8,128)(2,1)S(1)}, u32[]{:S(2)}, u32[]{:S(2)}) %collective-permute-start.14) | collective-permute-done | bytes 131104 | tf_op jit(solution)/shard_map/ppermute | solution.py:444
  46.7 0.8 %collective-permute-start.18 = (bf16[592,128]{1,0:T(8,128)(2,1)S(1)}, bf16[592,128]{1,0:T(8,128)(2,1)S(1)}, u32[]{:S(2)}, u32[]{:S(2)}) collective-permute-start(bf16[592,128]{1,0:T(8,128)(2,1)S(1)} %message.18.refs_1_.refs_2_), channel_id=1, source_target_pairs={{0,1},{1,0},{2,3},{3,2},{4,5},{5,4},{6,7},{7,6},{8,9},{9,8},{10,11... | collective-permute-start | bytes 454664 | tf_op jit(solution)/shard_map/ppermute | solution.py:444
  47.6 0.5 collective-permute-start.16
  48.1 0.4 collective-permute-start.19
  48.5 0.3 collective-permute-done.17.refs_5_
  48.8 0.2 collective-permute-done.16.refs_4_
  49.1 0.5 %y_faces.1 = (bf16[4,128,128]{2,1,0:T(8,128)(2,1)S(1)}, f32[8,128]{1,0:T(8,128)S(1)}) custom-call(f32[512,128]{1,0:T(8,128)S(1)} %back.1.refs_3_.part_ref, f32[8,64,128]{2,1,0:T(8,128)S(1)} %get-tuple-element.42.mask_ref, bf16[27,128,128]{2,1,0:T(8,128)(2,1)S(1)} %get-tuple-element.37.weight_ref.refs_0_, ...), custom_call_target="tpu_custom_call" | custom-call | tf_op jit(solution)/shard_map/y_faces/pallas_call | solution.py:31
  49.6 1.5 %normalise.1 = (f32[3456,128]{1,0:T(8,128)}, bf16[4,128,128]{2,1,0:T(8,128)(2,1)}) custom-call(bf16[432,128]{1,0:T(8,128)(2,1)S(1)} %get-tuple-element.52.refs_0_, bf16[432,128]{1,0:T(8,128)(2,1)S(1)} %collective-permute-done.12.refs_1_, bf16[592,128]{1,0:T(8,128)(2,1)S(1)} %message.18.refs_1_.refs_2_, bf16[432,128]{1,0:T(8,128)(2,1)S(1)} %collective-permute-done.15.refs_3_, ...), custom_call_target="tpu_custom_call" | custom-call | tf_op jit(solution)/shard_map/normalise/pallas_call | solution.py:665
  (28 shorter events, 0.9 us)
Async XLA Ops:
  1.8 2.4 %collective-permute-start = (bf16[64,128]{1,0:T(8,128)(2,1)S(1)}, bf16[64,128]{1,0:T(8,128)(2,1)S(1)}, u32[]{:S(2)}, u32[]{:S(2)}) collective-permute-start(bf16[64,128]{1,0:T(8,128)(2,1)S(1)} %get-tuple-element.38), channel_id=1, source_target_pairs={{0,1},{1,0},{2,3},{3,2},{4,5},{5,4},{6,7},{7,6},{8,9},{9,8},{10,11... | collective-permute-start | bytes 49160 | tf_op jit(solution)/shard_map/ppermute | solution.py:420
  2.3 1.9 %collective-permute-start.1 = (bf16[64,128]{1,0:T(8,128)(2,1)S(1)}, bf16[64,128]{1,0:T(8,128)(2,1)S(1)}, u32[]{:S(2)}, u32[]{:S(2)}) collective-permute-start(bf16[64,128]{1,0:T(8,128)(2,1)S(1)} %get-tuple-element.39), channel_id=1, source_target_pairs={{1,2},{2,1},{5,6},{6,5},{9,10},{10,9},{13,14},{14,13},{17,18},{18,... | collective-permute-start | bytes 49160 | tf_op jit(solution)/shard_map/ppermute | solution.py:421
  4.3 7.5 %collective-permute-start.2 = (bf16[80,128]{1,0:T(8,128)(2,1)S(1)}, bf16[80,128]{1,0:T(8,128)(2,1)S(1)}, u32[]{:S(2)}, u32[]{:S(2)}) collective-permute-start(bf16[80,128]{1,0:T(8,128)(2,1)S(1)} %get-tuple-element.45), channel_id=1, source_target_pairs={{4,8},{8,4},{12,16},{16,12},{20,24},{24,20},{5,9},{9,5},{13,17},{1... | collective-permute-start | bytes 61448 | tf_op jit(solution)/shard_map/ppermute | solution.py:563
  4.9 7.1 %collective-permute-start.3 = (bf16[80,128]{1,0:T(8,128)(2,1)S(1)}, bf16[80,128]{1,0:T(8,128)(2,1)S(1)}, u32[]{:S(2)}, u32[]{:S(2)}) collective-permute-start(bf16[80,128]{1,0:T(8,128)(2,1)S(1)} %get-tuple-element.46), channel_id=1, source_target_pairs={{0,4},{4,0},{8,12},{12,8},{16,20},{20,16},{24,28},{28,24},{1,5},{5... | collective-permute-start | bytes 61448 | tf_op jit(solution)/shard_map/ppermute | solution.py:564
  13.3 4.1 %collective-permute-start.5 = (bf16[992,128]{1,0:T(8,128)(2,1)S(1)}, bf16[992,128]{1,0:T(8,128)(2,1)S(1)}, u32[]{:S(2)}, u32[]{:S(2)}) collective-permute-start(bf16[992,128]{1,0:T(8,128)(2,1)S(1)} %get-tuple-element.51.refs_2_), channel_id=1, source_target_pairs={{0,1},{1,0},{2,3},{3,2},{4,5},{5,4},{6,7},{7,6},{8,9},{9,8},{10,11... | collective-permute-start | bytes 761864 | tf_op jit(solution)/shard_map/ppermute | solution.py:444
  17.3 2.3 %collective-permute-start.4 = (bf16[864,128]{1,0:T(8,128)(2,1)S(1)}, bf16[864,128]{1,0:T(8,128)(2,1)S(1)}, u32[]{:S(2)}, u32[]{:S(2)}) collective-permute-start(bf16[864,128]{1,0:T(8,128)(2,1)S(1)} %get-tuple-element.50), channel_id=1, source_target_pairs={{0,1},{1,0},{2,3},{3,2},{4,5},{5,4},{6,7},{7,6},{8,9},{9,8},{10,11... | collective-permute-start | bytes 663560 | tf_op jit(solution)/shard_map/ppermute | solution.py:444
  17.5 4.5 %collective-permute-start.7 = (bf16[432,128]{1,0:T(8,128)(2,1)S(1)}, bf16[432,128]{1,0:T(8,128)(2,1)S(1)}, u32[]{:S(2)}, u32[]{:S(2)}) collective-permute-start(bf16[432,128]{1,0:T(8,128)(2,1)S(1)} %message.11), channel_id=1, source_target_pairs={{0,3},{1,4},{2,7},{3,0},{4,1},{5,6},{6,5},{7,2},{8,13},{9,10},{10,... | collective-permute-start | bytes 331784 | tf_op jit(solution)/shard_map/ppermute | solution.py:444
  19.5 4.9 %collective-permute-start.6 = (bf16[688,128]{1,0:T(8,128)(2,1)S(1)}, bf16[688,128]{1,0:T(8,128)(2,1)S(1)}, u32[]{:S(2)}, u32[]{:S(2)}) collective-permute-start(bf16[688,128]{1,0:T(8,128)(2,1)S(1)} %message.10), channel_id=1, source_target_pairs={{0,3},{1,4},{2,7},{3,0},{4,1},{5,6},{6,5},{7,2},{8,13},{9,10},{10,... | collective-permute-start | bytes 528392 | tf_op jit(solution)/shard_map/ppermute | solution.py:444
  22.0 4.9 %collective-permute-start.8 = (bf16[432,128]{1,0:T(8,128)(2,1)S(1)}, bf16[432,128]{1,0:T(8,128)(2,1)S(1)}, u32[]{:S(2)}, u32[]{:S(2)}) collective-permute-start(bf16[432,128]{1,0:T(8,128)(2,1)S(1)} %message.12), channel_id=1, source_target_pairs={{0,5},{1,2},{2,1},{3,6},{4,7},{5,0},{6,3},{7,4},{8,11},{9,12},{10,... | collective-permute-start | bytes 331784 | tf_op jit(solution)/shard_map/ppermute | solution.py:444
  24.5 1.3 %collective-permute-start.9 = (bf16[128,128]{1,0:T(8,128)(2,1)S(1)}, bf16[128,128]{1,0:T(8,128)(2,1)S(1)}, u32[]{:S(2)}, u32[]{:S(2)}) collective-permute-start(bf16[128,128]{1,0:T(8,128)(2,1)S(1)} %message.13), channel_id=1, source_target_pairs={{0,1},{1,0},{2,3},{3,2},{4,5},{5,4},{6,7},{7,6},{8,9},{9,8},{10,11... | collective-permute-start | bytes 98312 | tf_op jit(solution)/shard_map/ppermute | solution.py:444
  26.9 7.4 %collective-permute-start.10 = (bf16[496,128]{1,0:T(8,128)(2,1)S(1)}, bf16[496,128]{1,0:T(8,128)(2,1)S(1)}, u32[]{:S(2)}, u32[]{:S(2)}) collective-permute-start(bf16[496,128]{1,0:T(8,128)(2,1)S(1)} %message.14.refs_0_), channel_id=1, source_target_pairs={{0,25},{1,8},{2,11},{3,26},{4,13},{5,28},{6,31},{7,14},{8,1},{9,16... | collective-permute-start | bytes 380936 | tf_op jit(solution)/shard_map/ppermute | solution.py:444
  34.3 5.1 %collective-permute-start.11 = (bf16[496,128]{1,0:T(8,128)(2,1)S(1)}, bf16[496,128]{1,0:T(8,128)(2,1)S(1)}, u32[]{:S(2)}, u32[]{:S(2)}) collective-permute-start(bf16[496,128]{1,0:T(8,128)(2,1)S(1)} %message.15.refs_0_), channel_id=1, source_target_pairs={{0,9},{1,24},{2,27},{3,10},{4,29},{5,12},{6,15},{7,30},{8,17},{9,0... | collective-permute-start | bytes 380936 | tf_op jit(solution)/shard_map/ppermute | solution.py:444
  39.5 4.3 %collective-permute-start.12 = (bf16[432,128]{1,0:T(8,128)(2,1)S(1)}, bf16[432,128]{1,0:T(8,128)(2,1)S(1)}, u32[]{:S(2)}, u32[]{:S(2)}) collective-permute-start(bf16[432,128]{1,0:T(8,128)(2,1)S(1)} %get-tuple-element.52.refs_0_), channel_id=1, source_target_pairs={{0,5},{1,2},{2,1},{3,6},{4,7},{5,0},{6,3},{7,4},{8,11},{9,12},{10,... | collective-permute-start | bytes 331784 | tf_op jit(solution)/shard_map/ppermute | solution.py:444
  40.9 1.3 %collective-permute-start.13 = (bf16[80,128]{1,0:T(8,128)(2,1)S(1)}, bf16[80,128]{1,0:T(8,128)(2,1)S(1)}, u32[]{:S(2)}, u32[]{:S(2)}) collective-permute-start(bf16[80,128]{1,0:T(8,128)(2,1)S(1)} %get-tuple-element.54.refs_1_), channel_id=1, source_target_pairs={{0,1},{1,0},{2,3},{3,2},{4,5},{5,4},{6,7},{7,6},{8,9},{9,8},{10,11... | collective-permute-start | bytes 61448 | tf_op jit(solution)/shard_map/ppermute | solution.py:444
  42.2 4.5 %collective-permute-start.14 = (bf16[512,128]{1,0:T(8,128)(2,1)S(1)}, bf16[512,128]{1,0:T(8,128)(2,1)S(1)}, u32[]{:S(2)}, u32[]{:S(2)}) collective-permute-start(bf16[512,128]{1,0:T(8,128)(2,1)S(1)} %message.17), channel_id=1, source_target_pairs={{0,3},{1,4},{2,7},{3,0},{4,1},{5,6},{6,5},{7,2},{8,13},{9,10},{10,... | collective-permute-start | bytes 393224 | tf_op jit(solution)/shard_map/ppermute | solution.py:444
  43.8 4.3 %collective-permute-start.15 = (bf16[432,128]{1,0:T(8,128)(2,1)S(1)}, bf16[432,128]{1,0:T(8,128)(2,1)S(1)}, u32[]{:S(2)}, u32[]{:S(2)}) collective-permute-start(bf16[432,128]{1,0:T(8,128)(2,1)S(1)} %collective-permute-done.12.refs_1_), channel_id=1, source_target_pairs={{0,3},{1,4},{2,7},{3,0},{4,1},{5,6},{6,5},{7,2},{8,13},{9,10},{10,... | collective-permute-start | bytes 331784 | tf_op jit(solution)/shard_map/ppermute | solution.py:444
  46.7 2.4 %collective-permute-start.18 = (bf16[592,128]{1,0:T(8,128)(2,1)S(1)}, bf16[592,128]{1,0:T(8,128)(2,1)S(1)}, u32[]{:S(2)}, u32[]{:S(2)}) collective-permute-start(bf16[592,128]{1,0:T(8,128)(2,1)S(1)} %message.18.refs_1_.refs_2_), channel_id=1, source_target_pairs={{0,1},{1,0},{2,3},{3,2},{4,5},{5,4},{6,7},{7,6},{8,9},{9,8},{10,11... | collective-permute-start | bytes 454664 | tf_op jit(solution)/shard_map/ppermute | solution.py:444
  47.5 1.3 %collective-permute-start.17 = (bf16[432,128]{1,0:T(8,128)(2,1)S(1)}, bf16[432,128]{1,0:T(8,128)(2,1)S(1)}, u32[]{:S(2)}, u32[]{:S(2)}) collective-permute-start(bf16[432,128]{1,0:T(8,128)(2,1)S(1)} %collective-permute-done.12.refs_1_), channel_id=1, source_target_pairs={{0,1},{1,0},{2,3},{3,2},{4,5},{5,4},{6,7},{7,6},{8,9},{9,8},{10,11... | collective-permute-start | bytes 331784 | tf_op jit(solution)/shard_map/ppermute | solution.py:444
  47.6 1.5 %collective-permute-start.16 = (bf16[432,128]{1,0:T(8,128)(2,1)S(1)}, bf16[432,128]{1,0:T(8,128)(2,1)S(1)}, u32[]{:S(2)}, u32[]{:S(2)}) collective-permute-start(bf16[432,128]{1,0:T(8,128)(2,1)S(1)} %message.19), channel_id=1, source_target_pairs={{0,1},{1,0},{2,3},{3,2},{4,5},{5,4},{6,7},{7,6},{8,9},{9,8},{10,11... | collective-permute-start | bytes 331784 | tf_op jit(solution)/shard_map/ppermute | solution.py:444
  48.1 1.5 %collective-permute-start.19 = (bf16[432,128]{1,0:T(8,128)(2,1)S(1)}, bf16[432,128]{1,0:T(8,128)(2,1)S(1)}, u32[]{:S(2)}, u32[]{:S(2)}) collective-permute-start(bf16[432,128]{1,0:T(8,128)(2,1)S(1)} %collective-permute-done.15.refs_3_), channel_id=1, source_target_pairs={{0,1},{1,0},{2,3},{3,2},{4,5},{5,4},{6,7},{7,6},{8,9},{9,8},{10,11... | collective-permute-start | bytes 331784 | tf_op jit(solution)/shard_map/ppermute | solution.py:444

commit v9 on v8

--- a/solution.py
+++ b/solution.py
@@ -647,8 +647,7 @@
     piece3 = exchange_with(piece1, first_way)
     near = message([(part, add, (piece2, 0)), (rows, add, (g_a, 0)), (rows, add, (piece2, part))])
     pieces = (total, piece1, near, piece3)
-    late = message([(part, add, (total, 0))], (near,))
-    others = [exchange_with(piece, by_core) for piece in (late, *pieces[1:])]
+    others = [exchange_with(piece, by_core) for piece in pieces]
     faces = (back_part, mask, weight, others[2], piece2, *pieces, *others[:3])
     kernel = functools.partial(y_faces_kernel, None)
     if n_ty > 4:

time: 51.3 us -> 51.2 us (level)
  no operation moved by 1% of the time
where the time goes in v9:
time: 51.2 us; the launch traced here: 51 us
  starting transfers between devices  24.7 us (48%)
  waiting for transfers between devices  15.8 us (31%)
  Pallas kernels  9.78 us (19%)
  between operations  0.8 us (2%)
    ppermute x16, starting transfers between devices, exchange_with(): return lax.ppermute(value, ('tx', 'ty'), pairs)  17.5 us
    ppermute x16, waiting for transfers between devices, exchange_with(): return lax.ppermute(value, ('tx', 'ty'), pairs)  15.5 us
    pallas_call x7, Pallas kernels, call(): pl.pallas_call(body, out_shape=outs, in_specs=[pl.BlockSpec(memory_space=...  7.98 us
    ppermute x1, starting transfers between devices, on_device(): x_pair = lax.ppermute(x_pair, 'tx', swap_pairs(0, n_tx))  5.37 us
    pallas_call x1, Pallas kernels, on_device(): pl.pallas_call(norm_kernel, out_shape=(shape((kernels * channels, channel...  1.46 us
  transfers between devices with their start and end apart: 20, of which 10 were waited for; matrix products, arithmetic and copies ran while one was open for 0% of the time, Pallas kernels for 11%

profile of v9, /device:TPU:0, one launch (start us, length us, event | category | flops | bytes accessed | tf_op | source)
XLA Modules:
  0.0 51.0 jit_solution(12577897987162864433)
XLA Ops:
  0.6 1.1 %first_faces.1 = (bf16[64,128]{1,0:T(8,128)(2,1)S(1)}, bf16[64,128]{1,0:T(8,128)(2,1)S(1)}, bf16[2,64,128]{2,1,0:T(8,128)(2,1)S(1)}, bf16[4,128,128]{2,1,0:T(8,128)(2,1)S(1)}, s32[4,128]{1,0:T(4,128)S(1)}) custom-call(bf16[4,128,128]{2,1,0:T(8,128)(2,1)} %feat_hbm.1, s32[4,128]{1,0:T(4,128)} %occ_hbm.1), custom_call_target="tpu_custom_call" | custom-call | tf_op jit(solution)/shard_map/first_faces/pallas_call | solution.py:31
  1.8 0.5 %collective-permute-start = (bf16[64,128]{1,0:T(8,128)(2,1)S(1)}, bf16[64,128]{1,0:T(8,128)(2,1)S(1)}, u32[]{:S(2)}, u32[]{:S(2)}) collective-permute-start(bf16[64,128]{1,0:T(8,128)(2,1)S(1)} %get-tuple-element.38), channel_id=1, source_target_pairs={{0,1},{1,0},{2,3},{3,2},{4,5},{5,4},{6,7},{7,6},{8,9},{9,8},{10,11... | collective-permute-start | bytes 49160 | tf_op jit(solution)/shard_map/ppermute | solution.py:420
  2.3 0.7 %collective-permute-start.1 = (bf16[64,128]{1,0:T(8,128)(2,1)S(1)}, bf16[64,128]{1,0:T(8,128)(2,1)S(1)}, u32[]{:S(2)}, u32[]{:S(2)}) collective-permute-start(bf16[64,128]{1,0:T(8,128)(2,1)S(1)} %get-tuple-element.39), channel_id=1, source_target_pairs={{1,2},{2,1},{5,6},{6,5},{9,10},{10,9},{13,14},{14,13},{17,18},{18,... | collective-permute-start | bytes 49160 | tf_op jit(solution)/shard_map/ppermute | solution.py:421
  2.9 1.3 %fetch.1 = (s32[1,1024]{1,0:T(1,128)S(1)}, bf16[16,1024]{1,0:T(8,128)(2,1)S(1)}, bf16[16,128]{1,0:T(8,128)(2,1)S(1)}, bf16[27,128,128]{2,1,0:T(8,128)(2,1)S(1)}) custom-call(s32[1,1024]{1,0:T(1,128)} %bitcast.2, bf16[16,1024]{1,0:T(8,128)(2,1)} %refs_1_.1, bf16[16,128]{1,0:T(8,128)(2,1)} %refs_2_.1, bf16[27,128,128]{2,1,0:T(8,128)(2,1)} %refs_3_.1, ...), custom_call_target="tpu_custom_call" | custom-call | tf_op jit(solution)/shard_map/fetch/pallas_call | solution.py:31
  4.3 0.7 %collective-permute-start.2 = (bf16[80,128]{1,0:T(8,128)(2,1)S(1)}, bf16[80,128]{1,0:T(8,128)(2,1)S(1)}, u32[]{:S(2)}, u32[]{:S(2)}) collective-permute-start(bf16[80,128]{1,0:T(8,128)(2,1)S(1)} %get-tuple-element.45), channel_id=1, source_target_pairs={{4,8},{8,4},{12,16},{16,12},{20,24},{24,20},{5,9},{9,5},{13,17},{1... | collective-permute-start | bytes 61448 | tf_op jit(solution)/shard_map/ppermute | solution.py:563
  4.9 5.4 %collective-permute-start.3 = (bf16[80,128]{1,0:T(8,128)(2,1)S(1)}, bf16[80,128]{1,0:T(8,128)(2,1)S(1)}, u32[]{:S(2)}, u32[]{:S(2)}) collective-permute-start(bf16[80,128]{1,0:T(8,128)(2,1)S(1)} %get-tuple-element.46), channel_id=1, source_target_pairs={{0,4},{4,0},{8,12},{12,8},{16,20},{20,16},{24,28},{28,24},{1,5},{5... | collective-permute-start | bytes 61448 | tf_op jit(solution)/shard_map/ppermute | solution.py:564
  10.3 1.5 %main.1 = (bf16[8,64,1152]{2,1,0:T(8,128)(2,1)S(1)}, f32[512,128]{1,0:T(8,128)S(1)}, f32[8,64,128]{2,1,0:T(8,128)S(1)}, f32[32,512]{1,0:T(8,128)S(1)}) custom-call(bf16[4,128,128]{2,1,0:T(8,128)(2,1)S(1)} %get-tuple-element.32.feat_ref, s32[4,128]{1,0:T(4,128)S(1)} %get-tuple-element.33.occ_ref, s32[1,1024]{1,0:T(1,128)S(1)} %get-tuple-element.35.point_ref, ...), custom_call_target="tpu_custom_call" | custom-call | tf_op jit(solution)/shard_map/main/pallas_call | solution.py:31
  11.8 0.3 collective-permute-done.3.x_pair_ref
  12.1 1.3 %tile.1 = (bf16[8,64,128]{2,1,0:T(8,128)(2,1)S(1)}, bf16[2,64,1152]{2,1,0:T(8,128)(2,1)S(1)}, bf16[992,128]{1,0:T(8,128)(2,1)S(1)}) custom-call(bf16[8,64,1152]{2,1,0:T(8,128)(2,1)S(1)} %get-tuple-element.40.cols_ref, f32[512,128]{1,0:T(8,128)S(1)} %get-tuple-element.41.pre_ref, f32[8,64,128]{2,1,0:T(8,128)S(1)} %get-tuple-element.42.mask_ref, ...), custom_call_target="tpu_custom_call" | custom-call | tf_op jit(solution)/shard_map/tile/pallas_call | solution.py:31
  13.3 2.8 %collective-permute-start.5 = (bf16[992,128]{1,0:T(8,128)(2,1)S(1)}, bf16[992,128]{1,0:T(8,128)(2,1)S(1)}, u32[]{:S(2)}, u32[]{:S(2)}) collective-permute-start(bf16[992,128]{1,0:T(8,128)(2,1)S(1)} %get-tuple-element.51.refs_2_), channel_id=1, source_target_pairs={{0,1},{1,0},{2,3},{3,2},{4,5},{5,4},{6,7},{7,6},{8,9},{9,8},{10,11... | collective-permute-start | bytes 761864 | tf_op jit(solution)/shard_map/ppermute | solution.py:444
  16.1 1.2 %terms.1 = (bf16[2,64,128]{2,1,0:T(8,128)(2,1)S(1)}, f32[1728,128]{1,0:T(8,128)S(1)}, bf16[864,128]{1,0:T(8,128)(2,1)S(1)}) custom-call(bf16[8,64,1152]{2,1,0:T(8,128)(2,1)S(1)} %get-tuple-element.40.cols_ref, bf16[2,64,1152]{2,1,0:T(8,128)(2,1)S(1)} %get-tuple-element.47.ends_ref, bf16[8,64,128]{2,1,0:T(8,128)(2,1)S(1)} %get-tuple-element.48.grad_ref.refs_2_), custom_call_target="tpu_custom_call" | custom-call | tf_op jit(solution)/shard_map/terms/pallas_call | solution.py:31
  17.5 2.0 %collective-permute-start.7 = (bf16[432,128]{1,0:T(8,128)(2,1)S(1)}, bf16[432,128]{1,0:T(8,128)(2,1)S(1)}, u32[]{:S(2)}, u32[]{:S(2)}) collective-permute-start(bf16[432,128]{1,0:T(8,128)(2,1)S(1)} %message.10), channel_id=1, source_target_pairs={{0,3},{1,4},{2,7},{3,0},{4,1},{5,6},{6,5},{7,2},{8,13},{9,10},{10,... | collective-permute-start | bytes 331784 | tf_op jit(solution)/shard_map/ppermute | solution.py:444
  19.6 2.3 %collective-permute-done.7.refs_2_ = bf16[432,128]{1,0:T(8,128)(2,1)S(1)} collective-permute-done((bf16[432,128]{1,0:T(8,128)(2,1)S(1)}, bf16[432,128]{1,0:T(8,128)(2,1)S(1)}, u32[]{:S(2)}, u32[]{:S(2)}) %collective-permute-start.7) | collective-permute-done | bytes 110624 | tf_op jit(solution)/shard_map/ppermute | solution.py:444
  22.0 2.4 %collective-permute-start.8 = (bf16[432,128]{1,0:T(8,128)(2,1)S(1)}, bf16[432,128]{1,0:T(8,128)(2,1)S(1)}, u32[]{:S(2)}, u32[]{:S(2)}) collective-permute-start(bf16[432,128]{1,0:T(8,128)(2,1)S(1)} %message.11), channel_id=1, source_target_pairs={{0,5},{1,2},{2,1},{3,6},{4,7},{5,0},{6,3},{7,4},{8,11},{9,12},{10,... | collective-permute-start | bytes 331784 | tf_op jit(solution)/shard_map/ppermute | solution.py:444
  24.6 1.2 %collective-permute-done.9.refs_4_.got2_ref = bf16[128,128]{1,0:T(8,128)(2,1)S(1)} collective-permute-done((bf16[128,128]{1,0:T(8,128)(2,1)S(1)}, bf16[128,128]{1,0:T(8,128)(2,1)S(1)}, u32[]{:S(2)}, u32[]{:S(2)}) %collective-permute-start.9) | collective-permute-done | bytes 32800 | tf_op jit(solution)/shard_map/ppermute | solution.py:444
  25.8 1.1 %collective-permute-done.8.refs_3_ = bf16[432,128]{1,0:T(8,128)(2,1)S(1)} collective-permute-done((bf16[432,128]{1,0:T(8,128)(2,1)S(1)}, bf16[432,128]{1,0:T(8,128)(2,1)S(1)}, u32[]{:S(2)}, u32[]{:S(2)}) %collective-permute-start.8) | collective-permute-done | bytes 110624 | tf_op jit(solution)/shard_map/ppermute | solution.py:444
  26.9 3.8 %collective-permute-start.10 = (bf16[496,128]{1,0:T(8,128)(2,1)S(1)}, bf16[496,128]{1,0:T(8,128)(2,1)S(1)}, u32[]{:S(2)}, u32[]{:S(2)}) collective-permute-start(bf16[496,128]{1,0:T(8,128)(2,1)S(1)} %message.13.refs_0_), channel_id=1, source_target_pairs={{0,25},{1,8},{2,11},{3,26},{4,13},{5,28},{6,31},{7,14},{8,1},{9,16... | collective-permute-start | bytes 380936 | tf_op jit(solution)/shard_map/ppermute | solution.py:444
  30.7 3.6 %collective-permute-done.10.refs_1_.refs_0_ = bf16[496,128]{1,0:T(8,128)(2,1)S(1)} collective-permute-done((bf16[496,128]{1,0:T(8,128)(2,1)S(1)}, bf16[496,128]{1,0:T(8,128)(2,1)S(1)}, u32[]{:S(2)}, u32[]{:S(2)}) %collective-permute-start.10) | collective-permute-done | bytes 127008 | tf_op jit(solution)/shard_map/ppermute | solution.py:444
  34.3 0.2 collective-permute-start.11
  34.5 5.0 %collective-permute-done.11.refs_1_ = bf16[496,128]{1,0:T(8,128)(2,1)S(1)} collective-permute-done((bf16[496,128]{1,0:T(8,128)(2,1)S(1)}, bf16[496,128]{1,0:T(8,128)(2,1)S(1)}, u32[]{:S(2)}, u32[]{:S(2)}) %collective-permute-start.11) | collective-permute-done | bytes 127008 | tf_op jit(solution)/shard_map/ppermute | solution.py:444
  39.5 1.4 %collective-permute-start.12 = (bf16[432,128]{1,0:T(8,128)(2,1)S(1)}, bf16[432,128]{1,0:T(8,128)(2,1)S(1)}, u32[]{:S(2)}, u32[]{:S(2)}) collective-permute-start(bf16[432,128]{1,0:T(8,128)(2,1)S(1)} %get-tuple-element.52.refs_0_), channel_id=1, source_target_pairs={{0,5},{1,2},{2,1},{3,6},{4,7},{5,0},{6,3},{7,4},{8,11},{9,12},{10,... | collective-permute-start | bytes 331784 | tf_op jit(solution)/shard_map/ppermute | solution.py:444
  41.0 1.1 %back.1.refs_3_.part_ref = f32[512,128]{1,0:T(8,128)S(1)} custom-call(bf16[8,64,128]{2,1,0:T(8,128)(2,1)S(1)} %get-tuple-element.55.grad_ref, bf16[2,64,128]{2,1,0:T(8,128)(2,1)S(1)} %get-tuple-element.56.planes_ref, bf16[27,128,128]{2,1,0:T(8,128)(2,1)S(1)} %get-tuple-element.37.weight_ref.refs_0_), custom_call_target="tpu_custom_call" | custom-call | tf_op jit(solution)/shard_map/back/pallas_call | solution.py:31
  42.2 1.6 %collective-permute-start.14 = (bf16[512,128]{1,0:T(8,128)(2,1)S(1)}, bf16[512,128]{1,0:T(8,128)(2,1)S(1)}, u32[]{:S(2)}, u32[]{:S(2)}) collective-permute-start(bf16[512,128]{1,0:T(8,128)(2,1)S(1)} %message.16), channel_id=1, source_target_pairs={{0,3},{1,4},{2,7},{3,0},{4,1},{5,6},{6,5},{7,2},{8,13},{9,10},{10,... | collective-permute-start | bytes 393224 | tf_op jit(solution)/shard_map/ppermute | solution.py:444
  43.8 1.1 %collective-permute-start.15 = (bf16[432,128]{1,0:T(8,128)(2,1)S(1)}, bf16[432,128]{1,0:T(8,128)(2,1)S(1)}, u32[]{:S(2)}, u32[]{:S(2)}) collective-permute-start(bf16[432,128]{1,0:T(8,128)(2,1)S(1)} %collective-permute-done.12.refs_1_), channel_id=1, source_target_pairs={{0,3},{1,4},{2,7},{3,0},{4,1},{5,6},{6,5},{7,2},{8,13},{9,10},{10,... | collective-permute-start | bytes 331784 | tf_op jit(solution)/shard_map/ppermute | solution.py:444
  44.9 1.7 %collective-permute-done.14.refs_0_.far_ref = bf16[512,128]{1,0:T(8,128)(2,1)S(1)} collective-permute-done((bf16[512,128]{1,0:T(8,128)(2,1)S(1)}, bf16[512,128]{1,0:T(8,128)(2,1)S(1)}, u32[]{:S(2)}, u32[]{:S(2)}) %collective-permute-start.14) | collective-permute-done | bytes 131104 | tf_op jit(solution)/shard_map/ppermute | solution.py:444
  46.7 0.8 %collective-permute-start.18 = (bf16[592,128]{1,0:T(8,128)(2,1)S(1)}, bf16[592,128]{1,0:T(8,128)(2,1)S(1)}, u32[]{:S(2)}, u32[]{:S(2)}) collective-permute-start(bf16[592,128]{1,0:T(8,128)(2,1)S(1)} %message.17.refs_2_), channel_id=1, source_target_pairs={{0,1},{1,0},{2,3},{3,2},{4,5},{5,4},{6,7},{7,6},{8,9},{9,8},{10,11... | collective-permute-start | bytes 454664 | tf_op jit(solution)/shard_map/ppermute | solution.py:444
  47.6 0.4 collective-permute-start.17
  48.0 0.5 collective-permute-start.19
  48.5 0.3 collective-permute-done.16.refs_4_
  48.8 0.2 collective-permute-done.17.refs_5_
  49.0 0.5 %y_faces.1 = (bf16[4,128,128]{2,1,0:T(8,128)(2,1)S(1)}, f32[8,128]{1,0:T(8,128)S(1)}) custom-call(f32[512,128]{1,0:T(8,128)S(1)} %back.1.refs_3_.part_ref, f32[8,64,128]{2,1,0:T(8,128)S(1)} %get-tuple-element.42.mask_ref, bf16[27,128,128]{2,1,0:T(8,128)(2,1)S(1)} %get-tuple-element.37.weight_ref.refs_0_, ...), custom_call_target="tpu_custom_call" | custom-call | tf_op jit(solution)/shard_map/y_faces/pallas_call | solution.py:31
  49.5 1.5 %normalise.1 = (f32[3456,128]{1,0:T(8,128)}, bf16[4,128,128]{2,1,0:T(8,128)(2,1)}) custom-call(bf16[432,128]{1,0:T(8,128)(2,1)S(1)} %get-tuple-element.52.refs_0_, bf16[432,128]{1,0:T(8,128)(2,1)S(1)} %collective-permute-done.12.refs_1_, bf16[592,128]{1,0:T(8,128)(2,1)S(1)} %message.17.refs_2_, bf16[432,128]{1,0:T(8,128)(2,1)S(1)} %collective-permute-done.15.refs_3_, ...), custom_call_target="tpu_custom_call" | custom-call | tf_op jit(solution)/shard_map/normalise/pallas_call | solution.py:664
  (27 shorter events, 0.9 us)
Async XLA Ops:
  1.8 2.4 %collective-permute-start = (bf16[64,128]{1,0:T(8,128)(2,1)S(1)}, bf16[64,128]{1,0:T(8,128)(2,1)S(1)}, u32[]{:S(2)}, u32[]{:S(2)}) collective-permute-start(bf16[64,128]{1,0:T(8,128)(2,1)S(1)} %get-tuple-element.38), channel_id=1, source_target_pairs={{0,1},{1,0},{2,3},{3,2},{4,5},{5,4},{6,7},{7,6},{8,9},{9,8},{10,11... | collective-permute-start | bytes 49160 | tf_op jit(solution)/shard_map/ppermute | solution.py:420
  2.3 1.9 %collective-permute-start.1 = (bf16[64,128]{1,0:T(8,128)(2,1)S(1)}, bf16[64,128]{1,0:T(8,128)(2,1)S(1)}, u32[]{:S(2)}, u32[]{:S(2)}) collective-permute-start(bf16[64,128]{1,0:T(8,128)(2,1)S(1)} %get-tuple-element.39), channel_id=1, source_target_pairs={{1,2},{2,1},{5,6},{6,5},{9,10},{10,9},{13,14},{14,13},{17,18},{18,... | collective-permute-start | bytes 49160 | tf_op jit(solution)/shard_map/ppermute | solution.py:421
  4.3 7.5 %collective-permute-start.2 = (bf16[80,128]{1,0:T(8,128)(2,1)S(1)}, bf16[80,128]{1,0:T(8,128)(2,1)S(1)}, u32[]{:S(2)}, u32[]{:S(2)}) collective-permute-start(bf16[80,128]{1,0:T(8,128)(2,1)S(1)} %get-tuple-element.45), channel_id=1, source_target_pairs={{4,8},{8,4},{12,16},{16,12},{20,24},{24,20},{5,9},{9,5},{13,17},{1... | collective-permute-start | bytes 61448 | tf_op jit(solution)/shard_map/ppermute | solution.py:563
  4.9 7.1 %collective-permute-start.3 = (bf16[80,128]{1,0:T(8,128)(2,1)S(1)}, bf16[80,128]{1,0:T(8,128)(2,1)S(1)}, u32[]{:S(2)}, u32[]{:S(2)}) collective-permute-start(bf16[80,128]{1,0:T(8,128)(2,1)S(1)} %get-tuple-element.46), channel_id=1, source_target_pairs={{0,4},{4,0},{8,12},{12,8},{16,20},{20,16},{24,28},{28,24},{1,5},{5... | collective-permute-start | bytes 61448 | tf_op jit(solution)/shard_map/ppermute | solution.py:564
  13.3 4.1 %collective-permute-start.5 = (bf16[992,128]{1,0:T(8,128)(2,1)S(1)}, bf16[992,128]{1,0:T(8,128)(2,1)S(1)}, u32[]{:S(2)}, u32[]{:S(2)}) collective-permute-start(bf16[992,128]{1,0:T(8,128)(2,1)S(1)} %get-tuple-element.51.refs_2_), channel_id=1, source_target_pairs={{0,1},{1,0},{2,3},{3,2},{4,5},{5,4},{6,7},{7,6},{8,9},{9,8},{10,11... | collective-permute-start | bytes 761864 | tf_op jit(solution)/shard_map/ppermute | solution.py:444
  17.3 2.3 %collective-permute-start.4 = (bf16[864,128]{1,0:T(8,128)(2,1)S(1)}, bf16[864,128]{1,0:T(8,128)(2,1)S(1)}, u32[]{:S(2)}, u32[]{:S(2)}) collective-permute-start(bf16[864,128]{1,0:T(8,128)(2,1)S(1)} %get-tuple-element.50), channel_id=1, source_target_pairs={{0,1},{1,0},{2,3},{3,2},{4,5},{5,4},{6,7},{7,6},{8,9},{9,8},{10,11... | collective-permute-start | bytes 663560 | tf_op jit(solution)/shard_map/ppermute | solution.py:444
  17.5 4.5 %collective-permute-start.7 = (bf16[432,128]{1,0:T(8,128)(2,1)S(1)}, bf16[432,128]{1,0:T(8,128)(2,1)S(1)}, u32[]{:S(2)}, u32[]{:S(2)}) collective-permute-start(bf16[432,128]{1,0:T(8,128)(2,1)S(1)} %message.10), channel_id=1, source_target_pairs={{0,3},{1,4},{2,7},{3,0},{4,1},{5,6},{6,5},{7,2},{8,13},{9,10},{10,... | collective-permute-start | bytes 331784 | tf_op jit(solution)/shard_map/ppermute | solution.py:444
  19.5 4.9 %collective-permute-start.6 = (bf16[688,128]{1,0:T(8,128)(2,1)S(1)}, bf16[688,128]{1,0:T(8,128)(2,1)S(1)}, u32[]{:S(2)}, u32[]{:S(2)}) collective-permute-start(bf16[688,128]{1,0:T(8,128)(2,1)S(1)} %message.9), channel_id=1, source_target_pairs={{0,3},{1,4},{2,7},{3,0},{4,1},{5,6},{6,5},{7,2},{8,13},{9,10},{10,... | collective-permute-start | bytes 528392 | tf_op jit(solution)/shard_map/ppermute | solution.py:444
  22.0 4.9 %collective-permute-start.8 = (bf16[432,128]{1,0:T(8,128)(2,1)S(1)}, bf16[432,128]{1,0:T(8,128)(2,1)S(1)}, u32[]{:S(2)}, u32[]{:S(2)}) collective-permute-start(bf16[432,128]{1,0:T(8,128)(2,1)S(1)} %message.11), channel_id=1, source_target_pairs={{0,5},{1,2},{2,1},{3,6},{4,7},{5,0},{6,3},{7,4},{8,11},{9,12},{10,... | collective-permute-start | bytes 331784 | tf_op jit(solution)/shard_map/ppermute | solution.py:444
  24.5 1.3 %collective-permute-start.9 = (bf16[128,128]{1,0:T(8,128)(2,1)S(1)}, bf16[128,128]{1,0:T(8,128)(2,1)S(1)}, u32[]{:S(2)}, u32[]{:S(2)}) collective-permute-start(bf16[128,128]{1,0:T(8,128)(2,1)S(1)} %message.12), channel_id=1, source_target_pairs={{0,1},{1,0},{2,3},{3,2},{4,5},{5,4},{6,7},{7,6},{8,9},{9,8},{10,11... | collective-permute-start | bytes 98312 | tf_op jit(solution)/shard_map/ppermute | solution.py:444
  26.9 7.4 %collective-permute-start.10 = (bf16[496,128]{1,0:T(8,128)(2,1)S(1)}, bf16[496,128]{1,0:T(8,128)(2,1)S(1)}, u32[]{:S(2)}, u32[]{:S(2)}) collective-permute-start(bf16[496,128]{1,0:T(8,128)(2,1)S(1)} %message.13.refs_0_), channel_id=1, source_target_pairs={{0,25},{1,8},{2,11},{3,26},{4,13},{5,28},{6,31},{7,14},{8,1},{9,16... | collective-permute-start | bytes 380936 | tf_op jit(solution)/shard_map/ppermute | solution.py:444
  34.3 5.1 %collective-permute-start.11 = (bf16[496,128]{1,0:T(8,128)(2,1)S(1)}, bf16[496,128]{1,0:T(8,128)(2,1)S(1)}, u32[]{:S(2)}, u32[]{:S(2)}) collective-permute-start(bf16[496,128]{1,0:T(8,128)(2,1)S(1)} %message.14.refs_0_), channel_id=1, source_target_pairs={{0,9},{1,24},{2,27},{3,10},{4,29},{5,12},{6,15},{7,30},{8,17},{9,0... | collective-permute-start | bytes 380936 | tf_op jit(solution)/shard_map/ppermute | solution.py:444
  39.5 4.3 %collective-permute-start.12 = (bf16[432,128]{1,0:T(8,128)(2,1)S(1)}, bf16[432,128]{1,0:T(8,128)(2,1)S(1)}, u32[]{:S(2)}, u32[]{:S(2)}) collective-permute-start(bf16[432,128]{1,0:T(8,128)(2,1)S(1)} %get-tuple-element.52.refs_0_), channel_id=1, source_target_pairs={{0,5},{1,2},{2,1},{3,6},{4,7},{5,0},{6,3},{7,4},{8,11},{9,12},{10,... | collective-permute-start | bytes 331784 | tf_op jit(solution)/shard_map/ppermute | solution.py:444
  40.9 1.3 %collective-permute-start.13 = (bf16[80,128]{1,0:T(8,128)(2,1)S(1)}, bf16[80,128]{1,0:T(8,128)(2,1)S(1)}, u32[]{:S(2)}, u32[]{:S(2)}) collective-permute-start(bf16[80,128]{1,0:T(8,128)(2,1)S(1)} %get-tuple-element.54.refs_1_), channel_id=1, source_target_pairs={{0,1},{1,0},{2,3},{3,2},{4,5},{5,4},{6,7},{7,6},{8,9},{9,8},{10,11... | collective-permute-start | bytes 61448 | tf_op jit(solution)/shard_map/ppermute | solution.py:444
  42.2 4.5 %collective-permute-start.14 = (bf16[512,128]{1,0:T(8,128)(2,1)S(1)}, bf16[512,128]{1,0:T(8,128)(2,1)S(1)}, u32[]{:S(2)}, u32[]{:S(2)}) collective-permute-start(bf16[512,128]{1,0:T(8,128)(2,1)S(1)} %message.16), channel_id=1, source_target_pairs={{0,3},{1,4},{2,7},{3,0},{4,1},{5,6},{6,5},{7,2},{8,13},{9,10},{10,... | collective-permute-start | bytes 393224 | tf_op jit(solution)/shard_map/ppermute | solution.py:444
  43.8 4.2 %collective-permute-start.15 = (bf16[432,128]{1,0:T(8,128)(2,1)S(1)}, bf16[432,128]{1,0:T(8,128)(2,1)S(1)}, u32[]{:S(2)}, u32[]{:S(2)}) collective-permute-start(bf16[432,128]{1,0:T(8,128)(2,1)S(1)} %collective-permute-done.12.refs_1_), channel_id=1, source_target_pairs={{0,3},{1,4},{2,7},{3,0},{4,1},{5,6},{6,5},{7,2},{8,13},{9,10},{10,... | collective-permute-start | bytes 331784 | tf_op jit(solution)/shard_map/ppermute | solution.py:444
  46.7 2.3 %collective-permute-start.18 = (bf16[592,128]{1,0:T(8,128)(2,1)S(1)}, bf16[592,128]{1,0:T(8,128)(2,1)S(1)}, u32[]{:S(2)}, u32[]{:S(2)}) collective-permute-start(bf16[592,128]{1,0:T(8,128)(2,1)S(1)} %message.17.refs_2_), channel_id=1, source_target_pairs={{0,1},{1,0},{2,3},{3,2},{4,5},{5,4},{6,7},{7,6},{8,9},{9,8},{10,11... | collective-permute-start | bytes 454664 | tf_op jit(solution)/shard_map/ppermute | solution.py:444
  47.5 1.3 %collective-permute-start.16 = (bf16[432,128]{1,0:T(8,128)(2,1)S(1)}, bf16[432,128]{1,0:T(8,128)(2,1)S(1)}, u32[]{:S(2)}, u32[]{:S(2)}) collective-permute-start(bf16[432,128]{1,0:T(8,128)(2,1)S(1)} %get-tuple-element.52.refs_0_), channel_id=1, source_target_pairs={{0,1},{1,0},{2,3},{3,2},{4,5},{5,4},{6,7},{7,6},{8,9},{9,8},{10,11... | collective-permute-start | bytes 331784 | tf_op jit(solution)/shard_map/ppermute | solution.py:444
  47.6 1.4 %collective-permute-start.17 = (bf16[432,128]{1,0:T(8,128)(2,1)S(1)}, bf16[432,128]{1,0:T(8,128)(2,1)S(1)}, u32[]{:S(2)}, u32[]{:S(2)}) collective-permute-start(bf16[432,128]{1,0:T(8,128)(2,1)S(1)} %collective-permute-done.12.refs_1_), channel_id=1, source_target_pairs={{0,1},{1,0},{2,3},{3,2},{4,5},{5,4},{6,7},{7,6},{8,9},{9,8},{10,11... | collective-permute-start | bytes 331784 | tf_op jit(solution)/shard_map/ppermute | solution.py:444
  48.0 1.5 %collective-permute-start.19 = (bf16[432,128]{1,0:T(8,128)(2,1)S(1)}, bf16[432,128]{1,0:T(8,128)(2,1)S(1)}, u32[]{:S(2)}, u32[]{:S(2)}) collective-permute-start(bf16[432,128]{1,0:T(8,128)(2,1)S(1)} %collective-permute-done.15.refs_3_), channel_id=1, source_target_pairs={{0,1},{1,0},{2,3},{3,2},{4,5},{5,4},{6,7},{7,6},{8,9},{9,8},{10,11... | collective-permute-start | bytes 331784 | tf_op jit(solution)/shard_map/ppermute | solution.py:444

commit v10 on v9

--- a/solution.py
+++ b/solution.py
@@ -268,7 +268,7 @@
     mask = mask_ref[...].reshape(voxels, channels)
     logistic = 1.0 / (1.0 + jnp.exp(-pre))
     slope = logistic * (1.0 + pre * (1.0 - logistic)) * mask
-    hidden = (pre / (1.0 + jnp.exp(-pre)) * mask).astype(BF16)
+    hidden = (pre * logistic * mask).astype(BF16)
 
     logits = contract(head_ref[...], hidden, 1, 1)
     student = jnp.exp(logits)

time: 51.2 us -> 51.2 us (level)
  no operation moved by 1% of the time
where the time goes in v10:
time: 51.2 us; the launch traced here: 51 us
  starting transfers between devices  24.7 us (48%)
  waiting for transfers between devices  15.8 us (31%)
  Pallas kernels  9.78 us (19%)
  between operations  0.8 us (2%)
    ppermute x16, starting transfers between devices, exchange_with(): return lax.ppermute(value, ('tx', 'ty'), pairs)  17.5 us
    ppermute x16, waiting for transfers between devices, exchange_with(): return lax.ppermute(value, ('tx', 'ty'), pairs)  15.5 us
    pallas_call x7, Pallas kernels, call(): pl.pallas_call(body, out_shape=outs, in_specs=[pl.BlockSpec(memory_space=...  7.98 us
    ppermute x1, starting transfers between devices, on_device(): x_pair = lax.ppermute(x_pair, 'tx', swap_pairs(0, n_tx))  5.37 us
    pallas_call x1, Pallas kernels, on_device(): pl.pallas_call(norm_kernel, out_shape=(shape((kernels * channels, channel...  1.46 us
  transfers between devices with their start and end apart: 20, of which 10 were waited for; matrix products, arithmetic and copies ran while one was open for 0% of the time, Pallas kernels for 11%

profile of v10, /device:TPU:0, one launch (start us, length us, event | category | flops | bytes accessed | tf_op | source)
XLA Modules:
  0.0 51.0 jit_solution(12577897987162864433)
XLA Ops:
  0.6 1.1 %first_faces.1 = (bf16[64,128]{1,0:T(8,128)(2,1)S(1)}, bf16[64,128]{1,0:T(8,128)(2,1)S(1)}, bf16[2,64,128]{2,1,0:T(8,128)(2,1)S(1)}, bf16[4,128,128]{2,1,0:T(8,128)(2,1)S(1)}, s32[4,128]{1,0:T(4,128)S(1)}) custom-call(bf16[4,128,128]{2,1,0:T(8,128)(2,1)} %feat_hbm.1, s32[4,128]{1,0:T(4,128)} %occ_hbm.1), custom_call_target="tpu_custom_call" | custom-call | tf_op jit(solution)/shard_map/first_faces/pallas_call | solution.py:31
  1.8 0.5 %collective-permute-start = (bf16[64,128]{1,0:T(8,128)(2,1)S(1)}, bf16[64,128]{1,0:T(8,128)(2,1)S(1)}, u32[]{:S(2)}, u32[]{:S(2)}) collective-permute-start(bf16[64,128]{1,0:T(8,128)(2,1)S(1)} %get-tuple-element.38), channel_id=1, source_target_pairs={{0,1},{1,0},{2,3},{3,2},{4,5},{5,4},{6,7},{7,6},{8,9},{9,8},{10,11... | collective-permute-start | bytes 49160 | tf_op jit(solution)/shard_map/ppermute | solution.py:420
  2.3 0.7 %collective-permute-start.1 = (bf16[64,128]{1,0:T(8,128)(2,1)S(1)}, bf16[64,128]{1,0:T(8,128)(2,1)S(1)}, u32[]{:S(2)}, u32[]{:S(2)}) collective-permute-start(bf16[64,128]{1,0:T(8,128)(2,1)S(1)} %get-tuple-element.39), channel_id=1, source_target_pairs={{1,2},{2,1},{5,6},{6,5},{9,10},{10,9},{13,14},{14,13},{17,18},{18,... | collective-permute-start | bytes 49160 | tf_op jit(solution)/shard_map/ppermute | solution.py:421
  2.9 1.3 %fetch.1 = (s32[1,1024]{1,0:T(1,128)S(1)}, bf16[16,1024]{1,0:T(8,128)(2,1)S(1)}, bf16[16,128]{1,0:T(8,128)(2,1)S(1)}, bf16[27,128,128]{2,1,0:T(8,128)(2,1)S(1)}) custom-call(s32[1,1024]{1,0:T(1,128)} %bitcast.2, bf16[16,1024]{1,0:T(8,128)(2,1)} %refs_1_.1, bf16[16,128]{1,0:T(8,128)(2,1)} %refs_2_.1, bf16[27,128,128]{2,1,0:T(8,128)(2,1)} %refs_3_.1, ...), custom_call_target="tpu_custom_call" | custom-call | tf_op jit(solution)/shard_map/fetch/pallas_call | solution.py:31
  4.3 0.7 %collective-permute-start.2 = (bf16[80,128]{1,0:T(8,128)(2,1)S(1)}, bf16[80,128]{1,0:T(8,128)(2,1)S(1)}, u32[]{:S(2)}, u32[]{:S(2)}) collective-permute-start(bf16[80,128]{1,0:T(8,128)(2,1)S(1)} %get-tuple-element.45), channel_id=1, source_target_pairs={{4,8},{8,4},{12,16},{16,12},{20,24},{24,20},{5,9},{9,5},{13,17},{1... | collective-permute-start | bytes 61448 | tf_op jit(solution)/shard_map/ppermute | solution.py:563
  4.9 5.4 %collective-permute-start.3 = (bf16[80,128]{1,0:T(8,128)(2,1)S(1)}, bf16[80,128]{1,0:T(8,128)(2,1)S(1)}, u32[]{:S(2)}, u32[]{:S(2)}) collective-permute-start(bf16[80,128]{1,0:T(8,128)(2,1)S(1)} %get-tuple-element.46), channel_id=1, source_target_pairs={{0,4},{4,0},{8,12},{12,8},{16,20},{20,16},{24,28},{28,24},{1,5},{5... | collective-permute-start | bytes 61448 | tf_op jit(solution)/shard_map/ppermute | solution.py:564
  10.3 1.5 %main.1 = (bf16[8,64,1152]{2,1,0:T(8,128)(2,1)S(1)}, f32[512,128]{1,0:T(8,128)S(1)}, f32[8,64,128]{2,1,0:T(8,128)S(1)}, f32[32,512]{1,0:T(8,128)S(1)}) custom-call(bf16[4,128,128]{2,1,0:T(8,128)(2,1)S(1)} %get-tuple-element.32.feat_ref, s32[4,128]{1,0:T(4,128)S(1)} %get-tuple-element.33.occ_ref, s32[1,1024]{1,0:T(1,128)S(1)} %get-tuple-element.35.point_ref, ...), custom_call_target="tpu_custom_call" | custom-call | tf_op jit(solution)/shard_map/main/pallas_call | solution.py:31
  11.8 0.3 collective-permute-done.3.x_pair_ref
  12.1 1.3 %tile.1 = (bf16[8,64,128]{2,1,0:T(8,128)(2,1)S(1)}, bf16[2,64,1152]{2,1,0:T(8,128)(2,1)S(1)}, bf16[992,128]{1,0:T(8,128)(2,1)S(1)}) custom-call(bf16[8,64,1152]{2,1,0:T(8,128)(2,1)S(1)} %get-tuple-element.40.cols_ref, f32[512,128]{1,0:T(8,128)S(1)} %get-tuple-element.41.pre_ref, f32[8,64,128]{2,1,0:T(8,128)S(1)} %get-tuple-element.42.mask_ref, ...), custom_call_target="tpu_custom_call" | custom-call | tf_op jit(solution)/shard_map/tile/pallas_call | solution.py:31
  13.3 2.8 %collective-permute-start.5 = (bf16[992,128]{1,0:T(8,128)(2,1)S(1)}, bf16[992,128]{1,0:T(8,128)(2,1)S(1)}, u32[]{:S(2)}, u32[]{:S(2)}) collective-permute-start(bf16[992,128]{1,0:T(8,128)(2,1)S(1)} %get-tuple-element.51.refs_2_), channel_id=1, source_target_pairs={{0,1},{1,0},{2,3},{3,2},{4,5},{5,4},{6,7},{7,6},{8,9},{9,8},{10,11... | collective-permute-start | bytes 761864 | tf_op jit(solution)/shard_map/ppermute | solution.py:444
  16.1 1.2 %terms.1 = (bf16[2,64,128]{2,1,0:T(8,128)(2,1)S(1)}, f32[1728,128]{1,0:T(8,128)S(1)}, bf16[864,128]{1,0:T(8,128)(2,1)S(1)}) custom-call(bf16[8,64,1152]{2,1,0:T(8,128)(2,1)S(1)} %get-tuple-element.40.cols_ref, bf16[2,64,1152]{2,1,0:T(8,128)(2,1)S(1)} %get-tuple-element.47.ends_ref, bf16[8,64,128]{2,1,0:T(8,128)(2,1)S(1)} %get-tuple-element.48.grad_ref.refs_2_), custom_call_target="tpu_custom_call" | custom-call | tf_op jit(solution)/shard_map/terms/pallas_call | solution.py:31
  17.5 2.0 %collective-permute-start.7 = (bf16[432,128]{1,0:T(8,128)(2,1)S(1)}, bf16[432,128]{1,0:T(8,128)(2,1)S(1)}, u32[]{:S(2)}, u32[]{:S(2)}) collective-permute-start(bf16[432,128]{1,0:T(8,128)(2,1)S(1)} %message.10), channel_id=1, source_target_pairs={{0,3},{1,4},{2,7},{3,0},{4,1},{5,6},{6,5},{7,2},{8,13},{9,10},{10,... | collective-permute-start | bytes 331784 | tf_op jit(solution)/shard_map/ppermute | solution.py:444
  19.6 2.3 %collective-permute-done.7.refs_2_ = bf16[432,128]{1,0:T(8,128)(2,1)S(1)} collective-permute-done((bf16[432,128]{1,0:T(8,128)(2,1)S(1)}, bf16[432,128]{1,0:T(8,128)(2,1)S(1)}, u32[]{:S(2)}, u32[]{:S(2)}) %collective-permute-start.7) | collective-permute-done | bytes 110624 | tf_op jit(solution)/shard_map/ppermute | solution.py:444
  22.0 2.4 %collective-permute-start.8 = (bf16[432,128]{1,0:T(8,128)(2,1)S(1)}, bf16[432,128]{1,0:T(8,128)(2,1)S(1)}, u32[]{:S(2)}, u32[]{:S(2)}) collective-permute-start(bf16[432,128]{1,0:T(8,128)(2,1)S(1)} %message.11), channel_id=1, source_target_pairs={{0,5},{1,2},{2,1},{3,6},{4,7},{5,0},{6,3},{7,4},{8,11},{9,12},{10,... | collective-permute-start | bytes 331784 | tf_op jit(solution)/shard_map/ppermute | solution.py:444
  24.6 1.2 %collective-permute-done.9.refs_4_.got2_ref = bf16[128,128]{1,0:T(8,128)(2,1)S(1)} collective-permute-done((bf16[128,128]{1,0:T(8,128)(2,1)S(1)}, bf16[128,128]{1,0:T(8,128)(2,1)S(1)}, u32[]{:S(2)}, u32[]{:S(2)}) %collective-permute-start.9) | collective-permute-done | bytes 32800 | tf_op jit(solution)/shard_map/ppermute | solution.py:444
  25.8 1.1 %collective-permute-done.8.refs_3_ = bf16[432,128]{1,0:T(8,128)(2,1)S(1)} collective-permute-done((bf16[432,128]{1,0:T(8,128)(2,1)S(1)}, bf16[432,128]{1,0:T(8,128)(2,1)S(1)}, u32[]{:S(2)}, u32[]{:S(2)}) %collective-permute-start.8) | collective-permute-done | bytes 110624 | tf_op jit(solution)/shard_map/ppermute | solution.py:444
  26.9 3.8 %collective-permute-start.10 = (bf16[496,128]{1,0:T(8,128)(2,1)S(1)}, bf16[496,128]{1,0:T(8,128)(2,1)S(1)}, u32[]{:S(2)}, u32[]{:S(2)}) collective-permute-start(bf16[496,128]{1,0:T(8,128)(2,1)S(1)} %message.13.refs_0_), channel_id=1, source_target_pairs={{0,25},{1,8},{2,11},{3,26},{4,13},{5,28},{6,31},{7,14},{8,1},{9,16... | collective-permute-start | bytes 380936 | tf_op jit(solution)/shard_map/ppermute | solution.py:444
  30.7 3.6 %collective-permute-done.10.refs_1_.refs_0_ = bf16[496,128]{1,0:T(8,128)(2,1)S(1)} collective-permute-done((bf16[496,128]{1,0:T(8,128)(2,1)S(1)}, bf16[496,128]{1,0:T(8,128)(2,1)S(1)}, u32[]{:S(2)}, u32[]{:S(2)}) %collective-permute-start.10) | collective-permute-done | bytes 127008 | tf_op jit(solution)/shard_map/ppermute | solution.py:444
  34.3 0.2 collective-permute-start.11
  34.5 5.0 %collective-permute-done.11.refs_1_ = bf16[496,128]{1,0:T(8,128)(2,1)S(1)} collective-permute-done((bf16[496,128]{1,0:T(8,128)(2,1)S(1)}, bf16[496,128]{1,0:T(8,128)(2,1)S(1)}, u32[]{:S(2)}, u32[]{:S(2)}) %collective-permute-start.11) | collective-permute-done | bytes 127008 | tf_op jit(solution)/shard_map/ppermute | solution.py:444
  39.5 1.4 %collective-permute-start.12 = (bf16[432,128]{1,0:T(8,128)(2,1)S(1)}, bf16[432,128]{1,0:T(8,128)(2,1)S(1)}, u32[]{:S(2)}, u32[]{:S(2)}) collective-permute-start(bf16[432,128]{1,0:T(8,128)(2,1)S(1)} %get-tuple-element.52.refs_0_), channel_id=1, source_target_pairs={{0,5},{1,2},{2,1},{3,6},{4,7},{5,0},{6,3},{7,4},{8,11},{9,12},{10,... | collective-permute-start | bytes 331784 | tf_op jit(solution)/shard_map/ppermute | solution.py:444
  41.0 1.1 %back.1.refs_3_.part_ref = f32[512,128]{1,0:T(8,128)S(1)} custom-call(bf16[8,64,128]{2,1,0:T(8,128)(2,1)S(1)} %get-tuple-element.55.grad_ref, bf16[2,64,128]{2,1,0:T(8,128)(2,1)S(1)} %get-tuple-element.56.planes_ref, bf16[27,128,128]{2,1,0:T(8,128)(2,1)S(1)} %get-tuple-element.37.weight_ref.refs_0_), custom_call_target="tpu_custom_call" | custom-call | tf_op jit(solution)/shard_map/back/pallas_call | solution.py:31
  42.2 1.6 %collective-permute-start.14 = (bf16[512,128]{1,0:T(8,128)(2,1)S(1)}, bf16[512,128]{1,0:T(8,128)(2,1)S(1)}, u32[]{:S(2)}, u32[]{:S(2)}) collective-permute-start(bf16[512,128]{1,0:T(8,128)(2,1)S(1)} %message.16), channel_id=1, source_target_pairs={{0,3},{1,4},{2,7},{3,0},{4,1},{5,6},{6,5},{7,2},{8,13},{9,10},{10,... | collective-permute-start | bytes 393224 | tf_op jit(solution)/shard_map/ppermute | solution.py:444
  43.8 1.1 %collective-permute-start.15 = (bf16[432,128]{1,0:T(8,128)(2,1)S(1)}, bf16[432,128]{1,0:T(8,128)(2,1)S(1)}, u32[]{:S(2)}, u32[]{:S(2)}) collective-permute-start(bf16[432,128]{1,0:T(8,128)(2,1)S(1)} %collective-permute-done.12.refs_1_), channel_id=1, source_target_pairs={{0,3},{1,4},{2,7},{3,0},{4,1},{5,6},{6,5},{7,2},{8,13},{9,10},{10,... | collective-permute-start | bytes 331784 | tf_op jit(solution)/shard_map/ppermute | solution.py:444
  44.9 1.7 %collective-permute-done.14.refs_0_.far_ref = bf16[512,128]{1,0:T(8,128)(2,1)S(1)} collective-permute-done((bf16[512,128]{1,0:T(8,128)(2,1)S(1)}, bf16[512,128]{1,0:T(8,128)(2,1)S(1)}, u32[]{:S(2)}, u32[]{:S(2)}) %collective-permute-start.14) | collective-permute-done | bytes 131104 | tf_op jit(solution)/shard_map/ppermute | solution.py:444
  46.7 0.8 %collective-permute-start.18 = (bf16[592,128]{1,0:T(8,128)(2,1)S(1)}, bf16[592,128]{1,0:T(8,128)(2,1)S(1)}, u32[]{:S(2)}, u32[]{:S(2)}) collective-permute-start(bf16[592,128]{1,0:T(8,128)(2,1)S(1)} %message.17.refs_2_), channel_id=1, source_target_pairs={{0,1},{1,0},{2,3},{3,2},{4,5},{5,4},{6,7},{7,6},{8,9},{9,8},{10,11... | collective-permute-start | bytes 454664 | tf_op jit(solution)/shard_map/ppermute | solution.py:444
  47.6 0.4 collective-permute-start.17
  48.0 0.5 collective-permute-start.19
  48.5 0.3 collective-permute-done.16.refs_4_
  48.8 0.2 collective-permute-done.17.refs_5_
  49.0 0.5 %y_faces.1 = (bf16[4,128,128]{2,1,0:T(8,128)(2,1)S(1)}, f32[8,128]{1,0:T(8,128)S(1)}) custom-call(f32[512,128]{1,0:T(8,128)S(1)} %back.1.refs_3_.part_ref, f32[8,64,128]{2,1,0:T(8,128)S(1)} %get-tuple-element.42.mask_ref, bf16[27,128,128]{2,1,0:T(8,128)(2,1)S(1)} %get-tuple-element.37.weight_ref.refs_0_, ...), custom_call_target="tpu_custom_call" | custom-call | tf_op jit(solution)/shard_map/y_faces/pallas_call | solution.py:31
  49.5 1.5 %normalise.1 = (f32[3456,128]{1,0:T(8,128)}, bf16[4,128,128]{2,1,0:T(8,128)(2,1)}) custom-call(bf16[432,128]{1,0:T(8,128)(2,1)S(1)} %get-tuple-element.52.refs_0_, bf16[432,128]{1,0:T(8,128)(2,1)S(1)} %collective-permute-done.12.refs_1_, bf16[592,128]{1,0:T(8,128)(2,1)S(1)} %message.17.refs_2_, bf16[432,128]{1,0:T(8,128)(2,1)S(1)} %collective-permute-done.15.refs_3_, ...), custom_call_target="tpu_custom_call" | custom-call | tf_op jit(solution)/shard_map/normalise/pallas_call | solution.py:664
  (27 shorter events, 0.9 us)
Async XLA Ops:
  1.8 2.4 %collective-permute-start = (bf16[64,128]{1,0:T(8,128)(2,1)S(1)}, bf16[64,128]{1,0:T(8,128)(2,1)S(1)}, u32[]{:S(2)}, u32[]{:S(2)}) collective-permute-start(bf16[64,128]{1,0:T(8,128)(2,1)S(1)} %get-tuple-element.38), channel_id=1, source_target_pairs={{0,1},{1,0},{2,3},{3,2},{4,5},{5,4},{6,7},{7,6},{8,9},{9,8},{10,11... | collective-permute-start | bytes 49160 | tf_op jit(solution)/shard_map/ppermute | solution.py:420
  2.3 1.9 %collective-permute-start.1 = (bf16[64,128]{1,0:T(8,128)(2,1)S(1)}, bf16[64,128]{1,0:T(8,128)(2,1)S(1)}, u32[]{:S(2)}, u32[]{:S(2)}) collective-permute-start(bf16[64,128]{1,0:T(8,128)(2,1)S(1)} %get-tuple-element.39), channel_id=1, source_target_pairs={{1,2},{2,1},{5,6},{6,5},{9,10},{10,9},{13,14},{14,13},{17,18},{18,... | collective-permute-start | bytes 49160 | tf_op jit(solution)/shard_map/ppermute | solution.py:421
  4.3 7.5 %collective-permute-start.2 = (bf16[80,128]{1,0:T(8,128)(2,1)S(1)}, bf16[80,128]{1,0:T(8,128)(2,1)S(1)}, u32[]{:S(2)}, u32[]{:S(2)}) collective-permute-start(bf16[80,128]{1,0:T(8,128)(2,1)S(1)} %get-tuple-element.45), channel_id=1, source_target_pairs={{4,8},{8,4},{12,16},{16,12},{20,24},{24,20},{5,9},{9,5},{13,17},{1... | collective-permute-start | bytes 61448 | tf_op jit(solution)/shard_map/ppermute | solution.py:563
  4.9 7.1 %collective-permute-start.3 = (bf16[80,128]{1,0:T(8,128)(2,1)S(1)}, bf16[80,128]{1,0:T(8,128)(2,1)S(1)}, u32[]{:S(2)}, u32[]{:S(2)}) collective-permute-start(bf16[80,128]{1,0:T(8,128)(2,1)S(1)} %get-tuple-element.46), channel_id=1, source_target_pairs={{0,4},{4,0},{8,12},{12,8},{16,20},{20,16},{24,28},{28,24},{1,5},{5... | collective-permute-start | bytes 61448 | tf_op jit(solution)/shard_map/ppermute | solution.py:564
  13.3 4.1 %collective-permute-start.5 = (bf16[992,128]{1,0:T(8,128)(2,1)S(1)}, bf16[992,128]{1,0:T(8,128)(2,1)S(1)}, u32[]{:S(2)}, u32[]{:S(2)}) collective-permute-start(bf16[992,128]{1,0:T(8,128)(2,1)S(1)} %get-tuple-element.51.refs_2_), channel_id=1, source_target_pairs={{0,1},{1,0},{2,3},{3,2},{4,5},{5,4},{6,7},{7,6},{8,9},{9,8},{10,11... | collective-permute-start | bytes 761864 | tf_op jit(solution)/shard_map/ppermute | solution.py:444
  17.3 2.3 %collective-permute-start.4 = (bf16[864,128]{1,0:T(8,128)(2,1)S(1)}, bf16[864,128]{1,0:T(8,128)(2,1)S(1)}, u32[]{:S(2)}, u32[]{:S(2)}) collective-permute-start(bf16[864,128]{1,0:T(8,128)(2,1)S(1)} %get-tuple-element.50), channel_id=1, source_target_pairs={{0,1},{1,0},{2,3},{3,2},{4,5},{5,4},{6,7},{7,6},{8,9},{9,8},{10,11... | collective-permute-start | bytes 663560 | tf_op jit(solution)/shard_map/ppermute | solution.py:444
  17.5 4.5 %collective-permute-start.7 = (bf16[432,128]{1,0:T(8,128)(2,1)S(1)}, bf16[432,128]{1,0:T(8,128)(2,1)S(1)}, u32[]{:S(2)}, u32[]{:S(2)}) collective-permute-start(bf16[432,128]{1,0:T(8,128)(2,1)S(1)} %message.10), channel_id=1, source_target_pairs={{0,3},{1,4},{2,7},{3,0},{4,1},{5,6},{6,5},{7,2},{8,13},{9,10},{10,... | collective-permute-start | bytes 331784 | tf_op jit(solution)/shard_map/ppermute | solution.py:444
  19.5 4.9 %collective-permute-start.6 = (bf16[688,128]{1,0:T(8,128)(2,1)S(1)}, bf16[688,128]{1,0:T(8,128)(2,1)S(1)}, u32[]{:S(2)}, u32[]{:S(2)}) collective-permute-start(bf16[688,128]{1,0:T(8,128)(2,1)S(1)} %message.9), channel_id=1, source_target_pairs={{0,3},{1,4},{2,7},{3,0},{4,1},{5,6},{6,5},{7,2},{8,13},{9,10},{10,... | collective-permute-start | bytes 528392 | tf_op jit(solution)/shard_map/ppermute | solution.py:444
  22.0 4.9 %collective-permute-start.8 = (bf16[432,128]{1,0:T(8,128)(2,1)S(1)}, bf16[432,128]{1,0:T(8,128)(2,1)S(1)}, u32[]{:S(2)}, u32[]{:S(2)}) collective-permute-start(bf16[432,128]{1,0:T(8,128)(2,1)S(1)} %message.11), channel_id=1, source_target_pairs={{0,5},{1,2},{2,1},{3,6},{4,7},{5,0},{6,3},{7,4},{8,11},{9,12},{10,... | collective-permute-start | bytes 331784 | tf_op jit(solution)/shard_map/ppermute | solution.py:444
  24.5 1.3 %collective-permute-start.9 = (bf16[128,128]{1,0:T(8,128)(2,1)S(1)}, bf16[128,128]{1,0:T(8,128)(2,1)S(1)}, u32[]{:S(2)}, u32[]{:S(2)}) collective-permute-start(bf16[128,128]{1,0:T(8,128)(2,1)S(1)} %message.12), channel_id=1, source_target_pairs={{0,1},{1,0},{2,3},{3,2},{4,5},{5,4},{6,7},{7,6},{8,9},{9,8},{10,11... | collective-permute-start | bytes 98312 | tf_op jit(solution)/shard_map/ppermute | solution.py:444
  26.9 7.4 %collective-permute-start.10 = (bf16[496,128]{1,0:T(8,128)(2,1)S(1)}, bf16[496,128]{1,0:T(8,128)(2,1)S(1)}, u32[]{:S(2)}, u32[]{:S(2)}) collective-permute-start(bf16[496,128]{1,0:T(8,128)(2,1)S(1)} %message.13.refs_0_), channel_id=1, source_target_pairs={{0,25},{1,8},{2,11},{3,26},{4,13},{5,28},{6,31},{7,14},{8,1},{9,16... | collective-permute-start | bytes 380936 | tf_op jit(solution)/shard_map/ppermute | solution.py:444
  34.3 5.1 %collective-permute-start.11 = (bf16[496,128]{1,0:T(8,128)(2,1)S(1)}, bf16[496,128]{1,0:T(8,128)(2,1)S(1)}, u32[]{:S(2)}, u32[]{:S(2)}) collective-permute-start(bf16[496,128]{1,0:T(8,128)(2,1)S(1)} %message.14.refs_0_), channel_id=1, source_target_pairs={{0,9},{1,24},{2,27},{3,10},{4,29},{5,12},{6,15},{7,30},{8,17},{9,0... | collective-permute-start | bytes 380936 | tf_op jit(solution)/shard_map/ppermute | solution.py:444
  39.5 4.3 %collective-permute-start.12 = (bf16[432,128]{1,0:T(8,128)(2,1)S(1)}, bf16[432,128]{1,0:T(8,128)(2,1)S(1)}, u32[]{:S(2)}, u32[]{:S(2)}) collective-permute-start(bf16[432,128]{1,0:T(8,128)(2,1)S(1)} %get-tuple-element.52.refs_0_), channel_id=1, source_target_pairs={{0,5},{1,2},{2,1},{3,6},{4,7},{5,0},{6,3},{7,4},{8,11},{9,12},{10,... | collective-permute-start | bytes 331784 | tf_op jit(solution)/shard_map/ppermute | solution.py:444
  40.9 1.3 %collective-permute-start.13 = (bf16[80,128]{1,0:T(8,128)(2,1)S(1)}, bf16[80,128]{1,0:T(8,128)(2,1)S(1)}, u32[]{:S(2)}, u32[]{:S(2)}) collective-permute-start(bf16[80,128]{1,0:T(8,128)(2,1)S(1)} %get-tuple-element.54.refs_1_), channel_id=1, source_target_pairs={{0,1},{1,0},{2,3},{3,2},{4,5},{5,4},{6,7},{7,6},{8,9},{9,8},{10,11... | collective-permute-start | bytes 61448 | tf_op jit(solution)/shard_map/ppermute | solution.py:444
  42.2 4.5 %collective-permute-start.14 = (bf16[512,128]{1,0:T(8,128)(2,1)S(1)}, bf16[512,128]{1,0:T(8,128)(2,1)S(1)}, u32[]{:S(2)}, u32[]{:S(2)}) collective-permute-start(bf16[512,128]{1,0:T(8,128)(2,1)S(1)} %message.16), channel_id=1, source_target_pairs={{0,3},{1,4},{2,7},{3,0},{4,1},{5,6},{6,5},{7,2},{8,13},{9,10},{10,... | collective-permute-start | bytes 393224 | tf_op jit(solution)/shard_map/ppermute | solution.py:444
  43.8 4.2 %collective-permute-start.15 = (bf16[432,128]{1,0:T(8,128)(2,1)S(1)}, bf16[432,128]{1,0:T(8,128)(2,1)S(1)}, u32[]{:S(2)}, u32[]{:S(2)}) collective-permute-start(bf16[432,128]{1,0:T(8,128)(2,1)S(1)} %collective-permute-done.12.refs_1_), channel_id=1, source_target_pairs={{0,3},{1,4},{2,7},{3,0},{4,1},{5,6},{6,5},{7,2},{8,13},{9,10},{10,... | collective-permute-start | bytes 331784 | tf_op jit(solution)/shard_map/ppermute | solution.py:444
  46.7 2.3 %collective-permute-start.18 = (bf16[592,128]{1,0:T(8,128)(2,1)S(1)}, bf16[592,128]{1,0:T(8,128)(2,1)S(1)}, u32[]{:S(2)}, u32[]{:S(2)}) collective-permute-start(bf16[592,128]{1,0:T(8,128)(2,1)S(1)} %message.17.refs_2_), channel_id=1, source_target_pairs={{0,1},{1,0},{2,3},{3,2},{4,5},{5,4},{6,7},{7,6},{8,9},{9,8},{10,11... | collective-permute-start | bytes 454664 | tf_op jit(solution)/shard_map/ppermute | solution.py:444
  47.5 1.3 %collective-permute-start.16 = (bf16[432,128]{1,0:T(8,128)(2,1)S(1)}, bf16[432,128]{1,0:T(8,128)(2,1)S(1)}, u32[]{:S(2)}, u32[]{:S(2)}) collective-permute-start(bf16[432,128]{1,0:T(8,128)(2,1)S(1)} %get-tuple-element.52.refs_0_), channel_id=1, source_target_pairs={{0,1},{1,0},{2,3},{3,2},{4,5},{5,4},{6,7},{7,6},{8,9},{9,8},{10,11... | collective-permute-start | bytes 331784 | tf_op jit(solution)/shard_map/ppermute | solution.py:444
  47.6 1.4 %collective-permute-start.17 = (bf16[432,128]{1,0:T(8,128)(2,1)S(1)}, bf16[432,128]{1,0:T(8,128)(2,1)S(1)}, u32[]{:S(2)}, u32[]{:S(2)}) collective-permute-start(bf16[432,128]{1,0:T(8,128)(2,1)S(1)} %collective-permute-done.12.refs_1_), channel_id=1, source_target_pairs={{0,1},{1,0},{2,3},{3,2},{4,5},{5,4},{6,7},{7,6},{8,9},{9,8},{10,11... | collective-permute-start | bytes 331784 | tf_op jit(solution)/shard_map/ppermute | solution.py:444
  48.0 1.5 %collective-permute-start.19 = (bf16[432,128]{1,0:T(8,128)(2,1)S(1)}, bf16[432,128]{1,0:T(8,128)(2,1)S(1)}, u32[]{:S(2)}, u32[]{:S(2)}) collective-permute-start(bf16[432,128]{1,0:T(8,128)(2,1)S(1)} %collective-permute-done.15.refs_3_), channel_id=1, source_target_pairs={{0,1},{1,0},{2,3},{3,2},{4,5},{5,4},{6,7},{7,6},{8,9},{9,8},{10,11... | collective-permute-start | bytes 331784 | tf_op jit(solution)/shard_map/ppermute | solution.py:444
